TPU v7x, 32 devices: a whole 2x2x4 slice. The times are simulated.
32 devices in a mesh: region: 8 (over z, x), neuron: 4 (over y, core).
Axes of the slice: x: 2, y: 2, z: 4, core: 2. Of those that a mesh axis runs over, the one named last changes fastest.
Arguments:
- counts: bfloat16 [8, 5120, 1024], P('region', 'neuron'), may hold values from 0 to 3, as said below
- latents: bfloat16 [64, 1024], P(None, 'neuron'), may hold values from -5 to 5
- loadings: bfloat16 [8, 64, 5120], P('region', None, 'neuron'), may hold values from -0.75 to 0.75
- bias: float32 [8, 5120], P('region', 'neuron'), may hold values from -3 to 3
- delays: int32 [8, 64], P('region'), may hold values from 0 to 128
- recorded: int32 [8], P('region'), may hold values from 256 to 1024, as said below
Outputs:
- grad_latents: float32 [64, 1024], P(None, 'neuron')
- grad_loadings: float32 [8, 64, 5120], P('region', None, 'neuron')
- grad_bias: float32 [8, 5120], P('region', 'neuron')
Inputs may be any that keep to these rules, and one draw needn't show every extreme that they name: At least one region is recorded over all 1024 bins. `counts`: whole numbers.
All inputs are finite; a program needn't handle non-finite values.
Results may differ from a plain program's by a relative error of at most 0.0021.
Values may be sent and summed in bfloat16 or wider, within the bound.
No kernel may reach another device: no remote copies, remote signals or barrier semaphores. Data moves between devices by JAX's collectives and lax.ppermute only.
A program may use at most 64 MiB of HBM per device.

v0:
```python
import jax
import jax.numpy as jnp
from jax import lax
from jax.sharding import PartitionSpec as P


def move_rows(source, delay_row, levels, forward):
    current = source
    for level in range(levels):
        amount = 1 << level
        if forward:
            displaced = jnp.pad(current[:, :-amount], ((0, 0), (amount, 0)))
        else:
            displaced = jnp.pad(current[:, amount:], ((0, 0), (0, amount)))
        chosen = delay_row // amount % 2 == 1
        current = jnp.where(chosen[:, None], displaced, current)
    return current


def delay_rows(source, delay_row, offset, span):
    result = move_rows(source, delay_row, offset.bit_length(), True)
    return result[:, offset : offset + span]


def advance_rows(source, delay_row, span, largest):
    result = move_rows(source, delay_row, largest.bit_length(), False)
    return result[:, :span]


def per_device(counts, latents, loadings, bias, delays, recorded):
    count_rows = counts[0]
    load = loadings[0]
    bias_row = bias[0]
    delay_row = delays[0]
    length = recorded[0]
    width = latents.shape[1]
    total = count_rows.shape[1]
    reach = width // 2
    lat_count = latents.shape[0]
    neu_count = count_rows.shape[0]

    def accumulate(carry, piece, start):
        grad_load, grad_bias, grad_shift = carry
        span = piece.shape[1]
        observed = lax.dynamic_slice_in_dim(count_rows, start, span, 1).astype(jnp.float32)
        eta = lax.dot_general(
            load, piece, (((0,), (0,)), ((), ())), preferred_element_type=jnp.float32
        )
        eta = eta + bias_row[:, None]
        bins = start + jnp.arange(span, dtype=jnp.int32)
        resid = jnp.where((bins < length)[None, :], jnp.exp(eta) - observed, 0.0)
        resid_low = resid.astype(jnp.bfloat16)
        grad_load = grad_load + lax.dot_general(
            piece, resid_low, (((1,), (1,)), ((), ())), preferred_element_type=jnp.float32
        )
        grad_bias = grad_bias + jnp.sum(resid, axis=1)
        block = jnp.dot(load, resid_low, preferred_element_type=jnp.float32)
        grad_shift = lax.dynamic_update_slice_in_dim(grad_shift, block, start, 1)
        return (grad_load, grad_bias, grad_shift)

    initial = (
        jnp.zeros((lat_count, neu_count), jnp.float32),
        jnp.zeros((neu_count,), jnp.float32),
        jnp.zeros((lat_count, total), jnp.float32),
    )
    whole = lax.all_gather(latents, "neuron", axis=1, tiled=True)
    shifted = delay_rows(jnp.pad(whole, ((0, 0), (reach, 0))), delay_row, reach, total)

    def visit(step, carry):
        begin = (step * width).astype(jnp.int32)
        return accumulate(carry, lax.dynamic_slice_in_dim(shifted, begin, width, 1), begin)

    grad_load, grad_bias, grad_shift = lax.fori_loop(0, total // width, visit, initial)
    source = advance_rows(jnp.pad(grad_shift, ((0, 0), (0, reach))), delay_row, total, reach)
    summed = lax.psum_scatter(source, "neuron", scatter_dimension=1, tiled=True)
    grad_latents = lax.psum(summed, "region")
    return (grad_latents, grad_load[None], grad_bias[None])


def solution(mesh):
    placed = (
        P("region", "neuron", None),
        P(None, "neuron"),
        P("region", None, "neuron"),
        P("region", "neuron"),
        P("region", None),
        P("region"),
    )
    return jax.shard_map(
        per_device,
        mesh=mesh,
        in_specs=placed,
        out_specs=(P(None, "neuron"), P("region", None, "neuron"), P("region", "neuron")),
        check_vma=False,
    )
```

profile of v0, /device:TPU:0, one launch (start us, length us, event | category | flops | bytes accessed | tf_op | source)
XLA Modules:
  0.0 136.6 jit_solution(10153982143903372193)
XLA Ops:
  7.2 0.7 fusion.11
  7.9 6.7 %all_gather.3 = bf16[64,1024]{1,0:T(8,128)(2,1)S(1)} all-gather(bf16[64,256]{1,0:T(8,128)(2,1)} %param.9), channel_id=1, replica_groups=mesh['region'=8,'neuron'=4] {'neuron'}, dimensions={1}, use_global_device_ids=true | all-gather | bytes 163840 | tf_op jit(solution)/shard_map/all_gather | solution.py:66
  14.7 0.1 pad_select_fusion.13
  14.8 0.1 pad_select_fusion.12
  14.9 0.1 pad_select_fusion.11
  15.0 0.1 pad_select_fusion.10
  15.2 0.1 pad_select_fusion.9
  15.3 0.1 pad_select_fusion.8
  15.4 0.1 pad_select_fusion.7
  15.6 1.0 copy-done.2
  16.5 2.7 %copy.9 = bf16[1,1280,1024]{1,2,0:T(8,128)(2,1)} copy(bf16[1,1280,1024]{2,1,0:T(8,128)(2,1)S(1)} %copy-done.2) | data formatting | bytes 5242880 | tf_op args[0]
  19.4 11.9 %while.18 = (s32[]{:T(128)}, f32[64,1280]{1,0:T(8,128)S(1)}, f32[1280]{0:T(1024)S(1)}, f32[64,1024]{1,0:T(8,128)S(1)}, bf16[64,1024]{1,0:T(8,128)(2,1)S(1)}, /*i...) while((s32[]{:T(128)}, f32[64,1280]{1,0:T(8,128)S(1)}, ...), condition=%wide.region_2.3_spmd.clone, body=%wide.region_0.2_spmd.clone.sunk | while | flops 127960832 | bytes 3776474 | solution.py:73
  19.4 0.7 add_compare_fusion.2
  20.1 1.6 %fusion.44 = (f32[1280]{0:T(1024)S(1)}, bf16[1280,256]{0,1:T(8,128)(2,1)S(1)}) fusion(bf16[1280,1024]{0,1:T(8,128)(2,1)} %get-tuple-element.317, s32[]{:T(128)S(6)} %select_n.307, f32[1280]{0:T(1024)S(1)} %reduce.2, bf16[64,1280]{1,0:T(8,128)(2,1)S(1)} %get-tuple-element.315, bf16[64,1024]{1,0:T(8,128)(2,1)S(1)} %get-tuple-element.313, ...), kind=kOutput, calls=%fused_computation.96.clone.1 | convolution fusion | flops 43907840 | bytes 1522176 | tf_op jit(solution)/shard_map/while/body/eval_jaxpr/dot_general | solution.py:46
  21.7 0.3 fusion.45
  22.0 0.3 convolution_add_fusion.3
  22.4 0.7 add_compare_fusion.2
  23.0 1.6 %fusion.44 = (f32[1280]{0:T(1024)S(1)}, bf16[1280,256]{0,1:T(8,128)(2,1)S(1)}) fusion(bf16[1280,1024]{0,1:T(8,128)(2,1)} %get-tuple-element.317, s32[]{:T(128)S(6)} %select_n.307, f32[1280]{0:T(1024)S(1)} %reduce.2, bf16[64,1280]{1,0:T(8,128)(2,1)S(1)} %get-tuple-element.315, bf16[64,1024]{1,0:T(8,128)(2,1)S(1)} %get-tuple-element.313, ...), kind=kOutput, calls=%fused_computation.96.clone.1 | convolution fusion | flops 43907840 | bytes 1522176 | tf_op jit(solution)/shard_map/while/body/eval_jaxpr/dot_general | solution.py:46
  24.7 0.3 fusion.45
  25.0 0.3 convolution_add_fusion.3
  25.3 0.7 add_compare_fusion.2
  26.0 1.6 %fusion.44 = (f32[1280]{0:T(1024)S(1)}, bf16[1280,256]{0,1:T(8,128)(2,1)S(1)}) fusion(bf16[1280,1024]{0,1:T(8,128)(2,1)} %get-tuple-element.317, s32[]{:T(128)S(6)} %select_n.307, f32[1280]{0:T(1024)S(1)} %reduce.2, bf16[64,1280]{1,0:T(8,128)(2,1)S(1)} %get-tuple-element.315, bf16[64,1024]{1,0:T(8,128)(2,1)S(1)} %get-tuple-element.313, ...), kind=kOutput, calls=%fused_computation.96.clone.1 | convolution fusion | flops 43907840 | bytes 1522176 | tf_op jit(solution)/shard_map/while/body/eval_jaxpr/dot_general | solution.py:46
  27.7 0.3 fusion.45
  28.0 0.3 convolution_add_fusion.3
  28.3 0.7 add_compare_fusion.2
  29.0 1.6 %fusion.44 = (f32[1280]{0:T(1024)S(1)}, bf16[1280,256]{0,1:T(8,128)(2,1)S(1)}) fusion(bf16[1280,1024]{0,1:T(8,128)(2,1)} %get-tuple-element.317, s32[]{:T(128)S(6)} %select_n.307, f32[1280]{0:T(1024)S(1)} %reduce.2, bf16[64,1280]{1,0:T(8,128)(2,1)S(1)} %get-tuple-element.315, bf16[64,1024]{1,0:T(8,128)(2,1)S(1)} %get-tuple-element.313, ...), kind=kOutput, calls=%fused_computation.96.clone.1 | convolution fusion | flops 43907840 | bytes 1522176 | tf_op jit(solution)/shard_map/while/body/eval_jaxpr/dot_general | solution.py:46
  30.7 0.3 fusion.45
  31.0 0.3 convolution_add_fusion.3
  31.3 0.1 pad_slice_fusion
  31.4 0.1 pad_select_fusion.6
  31.5 0.1 slice.80
  31.7 0.1 pad_select_fusion.5
  31.8 0.2 copy-done
  32.0 0.1 slice.81
  32.2 0.1 pad_select_fusion.4
  32.3 0.1 slice.82
  32.4 0.1 pad_select_fusion.3
  32.5 0.1 slice.83
  32.7 0.1 pad_select_fusion.2
  32.8 0.1 slice.84
  32.9 0.1 pad_select_fusion.1
  33.0 0.1 slice.85
  33.1 0.1 pad_select_fusion
  33.3 0.8 slice_select_fusion
  34.1 21.8 %reduce-scatter.2.cloned.1.call-done = f32[64,256]{1,0:T(8,128)} async-done(((f32[64,1024]{1,0:T(8,128)}), f32[64,256]{1,0:T(8,128)}) %reduce-scatter.2.cloned.1.call-update) | async-done | bytes 65552 | tf_op jit(solution)/shard_map/reduce_scatter | solution.py:75
  56.0 0.6 broadcast_in_dim.142
  56.6 71.7 %all-reduce.20.cloned.1.call-done = f32[64,256]{1,0:T(8,128)} async-done(((f32[64,256]{1,0:T(8,128)}), f32[64,256]{1,0:T(8,128)}) %all-reduce.20.cloned.1.call-update) | async-done | bytes 65552 | tf_op jit(solution)/shard_map/psum | solution.py:76
  128.3 1.5 %copy.24 = f32[64,256]{1,0:T(8,128)} copy(f32[64,256]{1,0:T(8,128)} %all-reduce.20.cloned.1.call-done) | data formatting | bytes 131072
  (25 shorter events, 0.4 us)
Async XLA Ops:
  7.2 48.8 %reduce-scatter.2.cloned.1.call-start = ((), (), s32[]{:S(2)}) async-start(), calls=%async_computation.1 | async-start | bytes 327680 | tf_op jit(solution)/shard_map/reduce_scatter | solution.py:75
  14.8 1.7 %copy-start.2 = (bf16[1,1280,1024]{2,1,0:T(8,128)(2,1)S(1)}, bf16[1,1280,1024]{2,1,0:T(8,128)(2,1)}, u32[]{:S(2)}) copy-start(bf16[1,1280,1024]{2,1,0:T(8,128)(2,1)} %param.8) | copy-start | bytes 7864324
  16.5 2.8 %copy-start.1 = (bf16[1,64,1280]{2,1,0:T(8,128)(2,1)S(1)}, bf16[1,64,1280]{2,1,0:T(8,128)(2,1)}, u32[]{:S(2)}) copy-start(bf16[1,64,1280]{2,1,0:T(8,128)(2,1)} %param.10) | copy-start | bytes 491524
  16.5 2.8 %copy-start.3 = (f32[1,1280]{1,0:T(1,128)S(1)}, f32[1,1280]{1,0:T(1,128)}, u32[]{:S(2)}) copy-start(f32[1,1280]{1,0:T(1,128)} %param.11) | copy-start | bytes 15364
  31.3 0.7 copy-start
  34.1 94.2 %all-reduce.20.cloned.1.call-start = ((), (), s32[]{:S(2)}) async-start(), calls=%async_computation.2 | async-start | bytes 131072 | tf_op jit(solution)/shard_map/psum | solution.py:76
Sparse Core Ops, SparseCore 0:
  34.2 21.6 reduce-scatter.1
  59.7 68.4 all-reduce.19
where the time goes:
time: 137 us
  waiting for transfers between devices  93.5 us (68%)
  between operations  14.3 us (10%)
  matrix products  8.99 us (7%)
  local copies, waits for them, and re-layouts  6.96 us (5%)
  blocking collectives  6.72 us (5%)
  other arithmetic  5.78 us (4%)
    psum x1, waiting for transfers between devices, per_device(): grad_latents = lax.psum(summed, 'region')  71.7 us
    reduce_scatter x1, waiting for transfers between devices, per_device(): summed = lax.psum_scatter(source, 'neuron', scatter_dimension=1, tiled=True)  21.8 us
    all_gather x1, blocking collectives, per_device(): whole = lax.all_gather(latents, 'neuron', axis=1, tiled=True)  6.72 us
    dot_general x4, matrix products, accumulate(): lax.dot_general(load, piece, (((0,), (0,)), ((), ())), preferred_element_...  6.56 us
    unnamed x10, local copies, waits for them, and re-layouts  5.39 us
  transfers between devices with their start and end apart: 2, of which 2 were waited for; matrix products, arithmetic and copies ran while one was open for 0% of the time, Pallas kernels for 0%

commit v1 on v0

v1 whole, which is shorter than its diff:
```python
import functools

import jax
import jax.numpy as jnp
from jax import lax
from jax.experimental import pallas as pl
from jax.experimental.pallas import tpu as pltpu
from jax.sharding import PartitionSpec as P

LANES = 128
EXTRA = 16
F32 = jnp.float32
BF16 = jnp.bfloat16


def shift_tiles(tiles, delay, forward):
    lane = lax.broadcasted_iota(jnp.int32, delay.shape, 1)
    nothing = jnp.zeros_like(tiles[0])
    for level in range(7):
        amount = 1 << level
        chosen = (delay & amount) != 0
        if forward:
            turned = [pltpu.roll(tile, amount, 1) for tile in tiles]
            before = [nothing] + turned[:-1]
            moved = [jnp.where(lane < amount, b, t) for b, t in zip(before, turned)]
        else:
            turned = [pltpu.roll(tile, LANES - amount, 1) for tile in tiles]
            after = turned[1:] + [nothing]
            moved = [jnp.where(lane < LANES - amount, t, a) for t, a in zip(turned, after)]
        tiles = [jnp.where(chosen, m, tile) for m, tile in zip(moved, tiles)]
    chosen = delay >= LANES
    other = [nothing] + tiles[:-1] if forward else tiles[1:] + [nothing]
    return [jnp.where(chosen, o, tile) for o, tile in zip(other, tiles)]


def main_kernel(parts, axis, chunk, step, *refs):
    recorded_ref, delays_ref, bias_ref, load_ref, counts_ref = refs[:5]
    blocks = refs[5 : 5 + parts]
    grad_load_ref, grad_bias_ref = refs[5 + parts : 7 + parts]
    outs = refs[7 + parts : 7 + 2 * parts]
    whole, shifted, load_ext, grad_shift = refs[7 + 2 * parts :]
    lats, total = grad_shift.shape
    neurons = counts_ref.shape[0]
    width = total // parts
    me = lax.axis_index(axis)
    length = recorded_ref[0]

    diagonal = lax.broadcasted_iota(jnp.int32, (lats, lats), 0) == lax.broadcasted_iota(jnp.int32, (lats, lats), 1)
    spread = jnp.broadcast_to(delays_ref[...].astype(F32), (lats, lats))
    column = jnp.sum(jnp.where(diagonal, spread, 0.0), axis=1, keepdims=True)
    delay = jnp.broadcast_to(column, (lats, LANES)).astype(jnp.int32)

    load_ext[0:lats, :] = load_ref[...]
    bias = bias_ref[...]
    high = bias.astype(BF16).astype(F32)
    middle = (bias - high).astype(BF16).astype(F32)
    low = bias - high - middle
    row = lax.broadcasted_iota(jnp.int32, (EXTRA, neurons), 0)
    below = jnp.where(row == 0, high, jnp.where(row == 1, middle, jnp.where(row == 2, low, 0.0)))
    load_ext[lats:, :] = below.astype(BF16)

    for k in range(parts):
        start = lax.rem(me + parts - k, parts) * width
        whole[:, pl.ds(pl.multiple_of(start, width), width)] = blocks[k][...]
    tiles = [whole[:, j * LANES : (j + 1) * LANES].astype(F32) for j in range(total // LANES)]
    for j, tile in enumerate(shift_tiles(tiles, delay, True)):
        shifted[0:lats, j * LANES : (j + 1) * LANES] = tile.astype(BF16)
    row = lax.broadcasted_iota(jnp.int32, (EXTRA, total), 0)
    shifted[lats:, :] = jnp.where(row < 3, 1.0, 0.0).astype(BF16)

    grad_shift[...] = jnp.zeros_like(grad_shift)
    bins = lax.broadcasted_iota(jnp.int32, (1, total), 1)

    def visit(index, carry):
        rows = pl.ds(pl.multiple_of(index * chunk, chunk), chunk)
        load_part = load_ext[:, rows]
        grad_load = jnp.zeros((lats, chunk), F32)
        sums = jnp.zeros((chunk, LANES), F32)
        for begin in range(0, total, step):
            span = slice(begin, begin + step)
            piece = shifted[:, span]
            eta = lax.dot_general(load_part, piece, (((0,), (0,)), ((), ())), preferred_element_type=F32)
            observed = counts_ref[rows, span].astype(F32)
            resid = jnp.where(bins[:, span] < length, jnp.exp(eta) - observed, 0.0)
            resid_low = resid.astype(BF16)
            for j in range(step // LANES):
                sums = sums + resid[:, j * LANES : (j + 1) * LANES]
            grad_load = grad_load + lax.dot_general(
                piece[0:lats], resid_low, (((1,), (1,)), ((), ())), preferred_element_type=F32
            )
            grad_shift[:, span] += jnp.dot(load_part[0:lats], resid_low, preferred_element_type=F32)
        grad_load_ref[:, rows] = grad_load
        grad_bias_ref[:, rows] = jnp.sum(sums.T, axis=0, keepdims=True)
        return carry

    lax.fori_loop(0, neurons // chunk, visit, 0, unroll=total <= 1024)

    tiles = [grad_shift[:, j * LANES : (j + 1) * LANES] for j in range(total // LANES)]
    for j, tile in enumerate(shift_tiles(tiles, delay, False)):
        grad_shift[:, j * LANES : (j + 1) * LANES] = tile
    for k in range(parts):
        start = lax.rem(me + k, parts) * width
        outs[k][...] = grad_shift[:, pl.ds(pl.multiple_of(start, width), width)]


def split_kernel(parts, axis, *refs):
    pieces, outs, held = refs[: -parts - 1], refs[-parts - 1 : -1], refs[-1]
    me = lax.axis_index(axis)
    rows = held.shape[1]
    value = pieces[0][...]
    for piece in pieces[1:]:
        value = value + piece[...]
    for j in range(parts):
        held[j] = value[j * rows : (j + 1) * rows]
    for k in range(parts):
        outs[k][...] = held[lax.rem(me + k, parts)]


def join_kernel(parts, axis, *refs):
    pieces, out, held = refs[:parts], refs[parts], refs[parts + 1]
    me = lax.axis_index(axis)
    rows = held.shape[1]
    for k in range(parts):
        held[lax.rem(me + parts - k, parts)] = pieces[k][...]
    for j in range(parts):
        out[j * rows : (j + 1) * rows, :] = held[j]


def per_device(region_count, neuron_count, counts, latents, loadings, bias, delays, recorded):
    neurons, total = counts.shape[1:]
    lats, width = latents.shape
    vmem = pl.BlockSpec(memory_space=pltpu.VMEM)
    smem = pl.BlockSpec(memory_space=pltpu.SMEM)

    def send(value, axis, count, k):
        return lax.ppermute(value, axis, [(i, (i + k) % count) for i in range(count)])

    blocks = [latents] + [send(latents, "neuron", neuron_count, k) for k in range(1, neuron_count)]
    results = pl.pallas_call(
        functools.partial(main_kernel, neuron_count, "neuron", 256, 512),
        out_shape=[jax.ShapeDtypeStruct((lats, neurons), F32), jax.ShapeDtypeStruct((1, neurons), F32)]
        + [jax.ShapeDtypeStruct((lats, width), F32)] * neuron_count,
        in_specs=[smem] + [vmem] * (4 + neuron_count),
        out_specs=[vmem] * (2 + neuron_count),
        scratch_shapes=[
            pltpu.VMEM((lats, total), BF16),
            pltpu.VMEM((lats + EXTRA, total), BF16),
            pltpu.VMEM((lats + EXTRA, neurons), BF16),
            pltpu.VMEM((lats, total), F32),
        ],
        compiler_params=pltpu.CompilerParams(vmem_limit_bytes=40 * 1024 * 1024),
    )(recorded, delays, bias, loadings[0], counts[0], *blocks)
    grad_load, grad_bias = results[:2]
    parts = results[2:]
    arrived = [parts[0]] + [send(parts[k], "neuron", neuron_count, k) for k in range(1, neuron_count)]

    rows = lats // region_count
    pieces = pl.pallas_call(
        functools.partial(split_kernel, region_count, "region"),
        out_shape=[jax.ShapeDtypeStruct((rows, width), F32)] * region_count,
        in_specs=[vmem] * neuron_count,
        out_specs=[vmem] * region_count,
        scratch_shapes=[pltpu.VMEM((region_count, rows, width), F32)],
    )(*arrived)
    arrived = [pieces[0]] + [send(pieces[k], "region", region_count, k) for k in range(1, region_count)]
    mine = functools.reduce(jnp.add, arrived)
    arrived = [mine] + [send(mine, "region", region_count, k) for k in range(1, region_count)]
    grad_latents = pl.pallas_call(
        functools.partial(join_kernel, region_count, "region"),
        out_shape=jax.ShapeDtypeStruct((lats, width), F32),
        in_specs=[vmem] * region_count,
        out_specs=vmem,
        scratch_shapes=[pltpu.VMEM((region_count, rows, width), F32)],
    )(*arrived)
    return (grad_latents, grad_load[None], grad_bias)


def solution(mesh):
    placed = (
        P("region", "neuron", None),
        P(None, "neuron"),
        P("region", None, "neuron"),
        P("region", "neuron"),
        P("region", None),
        P("region"),
    )
    return jax.shard_map(
        functools.partial(per_device, mesh.shape["region"], mesh.shape["neuron"]),
        mesh=mesh,
        in_specs=placed,
        out_specs=(P(None, "neuron"), P("region", None, "neuron"), P("region", "neuron")),
        check_vma=False,
    )
```

time: 137 us -> 58 us (0.42)
  waiting for transfers between devices: 93.5 us -> 11.5 us
  starting transfers between devices: 0.08 us -> 29.8 us
  between operations: 14.3 us -> 1.39 us
  matrix products: 8.99 us -> 0 us
  Pallas kernels: 0 us -> 7.54 us
  blocking collectives: 6.72 us -> 0 us
  other arithmetic: 5.78 us -> 0.71 us
    psum x1 -> x0, waiting for transfers between devices: 71.7 us -> none  [per_device(): grad_latents = lax.psum(summed, 'region')]
    ppermute x0 -> x20, starting transfers between devices: none -> 29.8 us  [send(): lax.ppermute(value, axis, [(i, (i + k) % count) for i in range(count)])]
    reduce_scatter x1 -> x0, waiting for transfers between devices: 21.8 us -> none  [per_device(): summed = lax.psum_scatter(source, 'neuron', scatter_dimension=1, tiled=True)]
    ppermute x0 -> x20, waiting for transfers between devices: none -> 11.5 us  [send(): lax.ppermute(value, axis, [(i, (i + k) % count) for i in range(count)])]
    dot_general x12 -> x0, matrix products: 8.99 us -> none  [the longest x4 6.56 us: accumulate(): lax.dot_general(load, piece, (((0,), (0,)), ((), ())), preferred_element_...]
    pallas_call x0 -> x3, Pallas kernels: none -> 7.54 us  [the longest x1 4.49 us: per_device(): pl.pallas_call(functools.partial(main_kernel, neuron_count, 'neuron', 256...]
    all_gather x1 -> x0, blocking collectives: 6.72 us -> none  [per_device(): whole = lax.all_gather(latents, 'neuron', axis=1, tiled=True)]
    lt x4 -> x0, other arithmetic: 2.61 us -> none  [accumulate(): resid = jnp.where((bins < length)[None, :], jnp.exp(eta) - observed, 0.0)]
  transfers between devices with their start and end apart: 2 -> 20, of which waited for: 2 -> 9; matrix products, arithmetic and copies ran while one was open for 0% -> 0% of each run, Pallas kernels for 0% -> 0%
where the time goes in v1:
time: 58 us; the launch traced here: 57.6 us
  starting transfers between devices  29.8 us (51%)
  waiting for transfers between devices  11.5 us (20%)
  Pallas kernels  7.54 us (13%)
  local copies, waits for them, and re-layouts  6.61 us (11%)
  between operations  1.39 us (2%)
  other arithmetic  0.71 us (1%)
    ppermute x20, starting transfers between devices, send(): lax.ppermute(value, axis, [(i, (i + k) % count) for i in range(count)])  29.8 us
    ppermute x20, waiting for transfers between devices, send(): lax.ppermute(value, axis, [(i, (i + k) % count) for i in range(count)])  11.5 us
    unnamed x34, local copies, waits for them, and re-layouts  6.61 us
    pallas_call x1, Pallas kernels, per_device(): pl.pallas_call(functools.partial(main_kernel, neuron_count, 'neuron', 256...  4.49 us
    pallas_call x1, Pallas kernels, per_device(): pl.pallas_call(functools.partial(split_kernel, region_count, 'region'), o...  1.59 us
    pallas_call x1, Pallas kernels, per_device(): pl.pallas_call(functools.partial(join_kernel, region_count, 'region'), ou...  1.46 us
  transfers between devices with their start and end apart: 20, of which 9 were waited for; matrix products, arithmetic and copies ran while one was open for 0% of the time, Pallas kernels for 0%

profile of v1, /device:TPU:0, one launch (start us, length us, event | category | flops | bytes accessed | tf_op | source)
XLA Modules:
  0.0 57.6 jit_solution(14003330928867333107)
XLA Ops:
  0.6 3.0 %collective-permute-start.1 = (bf16[64,256]{1,0:T(8,128)(2,1)}, bf16[64,256]{1,0:T(8,128)(2,1)S(1)}, u32[]{:S(2)}, u32[]{:S(2)}) collective-permute-start(bf16[64,256]{1,0:T(8,128)(2,1)} %refs_5_.1), channel_id=1, source_target_pairs={{0,2},{1,3},{2,0},{3,1},{4,6},{5,7},{6,4},{7,5},{8,10},{9,11},{10,... | collective-permute-start | bytes 98312 | tf_op jit(solution)/shard_map/ppermute | solution.py:136
  3.7 0.0 collective-permute-start
  3.7 1.7 %collective-permute-start.2 = (bf16[64,256]{1,0:T(8,128)(2,1)}, bf16[64,256]{1,0:T(8,128)(2,1)S(1)}, u32[]{:S(2)}, u32[]{:S(2)}) collective-permute-start(bf16[64,256]{1,0:T(8,128)(2,1)} %refs_5_.1), channel_id=1, source_target_pairs={{0,3},{1,0},{2,1},{3,2},{4,7},{5,4},{6,5},{7,6},{8,11},{9,8},{10,9... | collective-permute-start | bytes 98312 | tf_op jit(solution)/shard_map/ppermute | solution.py:136
  6.1 0.0 collective-permute-done.1.refs_7_
  6.1 1.1 %collective-permute-done.refs_6_ = bf16[64,256]{1,0:T(8,128)(2,1)S(1)} collective-permute-done((bf16[64,256]{1,0:T(8,128)(2,1)}, bf16[64,256]{1,0:T(8,128)(2,1)S(1)}, u32[]{:S(2)}, u32[]{:S(2)}) %collective-permute-start) | collective-permute-done | bytes 32800 | tf_op jit(solution)/shard_map/ppermute | solution.py:136
  7.2 0.1 collective-permute-done.2.refs_8_
  7.3 1.7 %copy-done = bf16[1,1280,1024]{2,1,0:T(8,128)(2,1)S(1)} copy-done((bf16[1,1280,1024]{2,1,0:T(8,128)(2,1)S(1)}, bf16[1,1280,1024]{2,1,0:T(8,128)(2,1)}, u32[]{:S(2)}) %copy-start) | copy-done | bytes 2621464
  9.1 0.9 %copy-done.1 = bf16[1,64,1280]{2,1,0:T(8,128)(2,1)S(1)} copy-done((bf16[1,64,1280]{2,1,0:T(8,128)(2,1)S(1)}, bf16[1,64,1280]{2,1,0:T(8,128)(2,1)}, u32[]{:S(2)}) %copy-start.1) | copy-done | bytes 163864
  10.0 0.8 %copy-done.3 = bf16[64,256]{1,0:T(8,128)(2,1)S(1)} copy-done((bf16[64,256]{1,0:T(8,128)(2,1)S(1)}, bf16[64,256]{1,0:T(8,128)(2,1)}, u32[]{:S(2)}) %copy-start.3) | copy-done | bytes 32792
  10.7 0.7 %copy-done.4 = f32[1,1280]{1,0:T(1,128)S(1)} copy-done((f32[1,1280]{1,0:T(1,128)S(1)}, f32[1,1280]{1,0:T(1,128)}, u32[]{:S(2)}) %copy-start.4) | copy-done | bytes 5144
  11.4 0.7 %copy-done.5 = s32[1,64]{1,0:T(1,128)S(1)} copy-done((s32[1,64]{1,0:T(1,128)S(1)}, s32[1,64]{1,0:T(1,128)}, u32[]{:S(2)}) %copy-start.5) | copy-done | bytes 280
  12.1 4.5 %shard_map.85 = (f32[64,1280]{1,0:T(8,128)}, f32[1,1280]{1,0:T(1,128)}, f32[64,256]{1,0:T(8,128)S(1)}, f32[64,256]{1,0:T(8,128)S(1)}, f32[64,256]{1,0:T(8,128)S(1)}, /*index=5*/f32[64,256]{1,0:T(8,128)S(1)}) custom-call(s32[1]{0:T(128)S(6)} %copy.9.refs_0_, s32[1,64]{1,0:T(1,128)S(1)} %copy-done.5, f32[1,1280]{1,0:T(1,128)S(1)} %copy-done.4, ...), custom_call_target="tpu_custom_call" | custom-call | tf_op jit(solution)/shard_map/pallas_call | solution.py:139
  16.6 0.6 %copy-done.2 = f32[64,256]{1,0:T(8,128)} copy-done((f32[64,256]{1,0:T(8,128)}, f32[64,256]{1,0:T(8,128)S(1)}, u32[]{:S(2)}) %copy-start.2) | copy-done | bytes 65560
  17.2 0.1 collective-permute-start.3
  17.3 2.0 %collective-permute-start.4 = (f32[64,256]{1,0:T(8,128)S(1)}, f32[64,256]{1,0:T(8,128)S(1)}, u32[]{:S(2)}, u32[]{:S(2)}) collective-permute-start(f32[64,256]{1,0:T(8,128)S(1)} %get-tuple-element.19), channel_id=1, source_target_pairs={{0,2},{1,3},{2,0},{3,1},{4,6},{5,7},{6,4},{7,5},{8,10},{9,11},{10,... | collective-permute-start | bytes 196616 | tf_op jit(solution)/shard_map/ppermute | solution.py:136
  19.2 0.0 collective-permute-start.5
  19.2 1.8 %collective-permute-done.3.refs_1_ = f32[64,256]{1,0:T(8,128)S(1)} collective-permute-done((f32[64,256]{1,0:T(8,128)S(1)}, f32[64,256]{1,0:T(8,128)S(1)}, u32[]{:S(2)}, u32[]{:S(2)}) %collective-permute-start.3) | collective-permute-done | bytes 65568 | tf_op jit(solution)/shard_map/ppermute | solution.py:136
  21.0 1.2 %collective-permute-done.4.refs_2_ = f32[64,256]{1,0:T(8,128)S(1)} collective-permute-done((f32[64,256]{1,0:T(8,128)S(1)}, f32[64,256]{1,0:T(8,128)S(1)}, u32[]{:S(2)}, u32[]{:S(2)}) %collective-permute-start.4) | collective-permute-done | bytes 65568 | tf_op jit(solution)/shard_map/ppermute | solution.py:136
  22.2 0.6 %copy-done.7 = f32[64,256]{1,0:T(8,128)} copy-done((f32[64,256]{1,0:T(8,128)}, f32[64,256]{1,0:T(8,128)S(1)}, u32[]{:S(2)}) %copy-start.7) | copy-done | bytes 65560
  22.8 0.0 copy-done.8
  22.8 1.6 %shard_map.86 = (f32[8,256]{1,0:T(8,128)}, f32[8,256]{1,0:T(8,128)}, f32[8,256]{1,0:T(8,128)}, f32[8,256]{1,0:T(8,128)}, f32[8,256]{1,0:T(8,128)}, /*index=5*/f3...) custom-call(f32[64,256]{1,0:T(8,128)} %copy-done.2, f32[64,256]{1,0:T(8,128)} %copy-done.6, f32[64,256]{1,0:T(8,128)} %copy-done.7, ...), custom_call_target="tpu_custom_call" | custom-call | tf_op jit(solution)/shard_map/pallas_call | solution.py:158
  24.4 1.6 %collective-permute-start.6 = (f32[8,256]{1,0:T(8,128)}, f32[8,256]{1,0:T(8,128)S(1)}, u32[]{:S(2)}, u32[]{:S(2)}) collective-permute-start(f32[8,256]{1,0:T(8,128)} %get-tuple-element.22), channel_id=1, source_target_pairs={{0,4},{4,8},{8,12},{12,16},{16,20},{20,24},{24,28},{28,0},{1,5},{5... | collective-permute-start | bytes 24584 | tf_op jit(solution)/shard_map/ppermute | solution.py:136
  26.1 1.6 %collective-permute-start.7 = (f32[8,256]{1,0:T(8,128)}, f32[8,256]{1,0:T(8,128)S(1)}, u32[]{:S(2)}, u32[]{:S(2)}) collective-permute-start(f32[8,256]{1,0:T(8,128)} %get-tuple-element.23), channel_id=1, source_target_pairs={{0,8},{4,12},{8,16},{12,20},{16,24},{20,28},{24,0},{28,4},{1,9},{5... | collective-permute-start | bytes 24584 | tf_op jit(solution)/shard_map/ppermute | solution.py:136
  27.6 2.6 %collective-permute-start.8 = (f32[8,256]{1,0:T(8,128)}, f32[8,256]{1,0:T(8,128)S(1)}, u32[]{:S(2)}, u32[]{:S(2)}) collective-permute-start(f32[8,256]{1,0:T(8,128)} %get-tuple-element.24), channel_id=1, source_target_pairs={{0,12},{4,16},{8,20},{12,24},{16,28},{20,0},{24,4},{28,8},{1,13},{... | collective-permute-start | bytes 24584 | tf_op jit(solution)/shard_map/ppermute | solution.py:136
  30.2 1.2 %collective-permute-start.9 = (f32[8,256]{1,0:T(8,128)}, f32[8,256]{1,0:T(8,128)S(1)}, u32[]{:S(2)}, u32[]{:S(2)}) collective-permute-start(f32[8,256]{1,0:T(8,128)} %get-tuple-element.25), channel_id=1, source_target_pairs={{0,16},{4,20},{8,24},{12,28},{16,0},{20,4},{24,8},{28,12},{1,17},{... | collective-permute-start | bytes 24584 | tf_op jit(solution)/shard_map/ppermute | solution.py:136
  31.4 2.6 %collective-permute-start.10 = (f32[8,256]{1,0:T(8,128)}, f32[8,256]{1,0:T(8,128)S(1)}, u32[]{:S(2)}, u32[]{:S(2)}) collective-permute-start(f32[8,256]{1,0:T(8,128)} %get-tuple-element.26), channel_id=1, source_target_pairs={{0,20},{4,24},{8,28},{12,0},{16,4},{20,8},{24,12},{28,16},{1,21},{... | collective-permute-start | bytes 24584 | tf_op jit(solution)/shard_map/ppermute | solution.py:136
  34.0 0.0 collective-permute-done.6
  34.0 1.4 %collective-permute-start.11 = (f32[8,256]{1,0:T(8,128)}, f32[8,256]{1,0:T(8,128)S(1)}, u32[]{:S(2)}, u32[]{:S(2)}) collective-permute-start(f32[8,256]{1,0:T(8,128)} %get-tuple-element.27), channel_id=1, source_target_pairs={{0,24},{4,28},{8,0},{12,4},{16,8},{20,12},{24,16},{28,20},{1,25},{... | collective-permute-start | bytes 24584 | tf_op jit(solution)/shard_map/ppermute | solution.py:136
  35.4 0.0 collective-permute-done.7
  35.4 1.4 %collective-permute-start.12 = (f32[8,256]{1,0:T(8,128)}, f32[8,256]{1,0:T(8,128)S(1)}, u32[]{:S(2)}, u32[]{:S(2)}) collective-permute-start(f32[8,256]{1,0:T(8,128)} %get-tuple-element.28), channel_id=1, source_target_pairs={{0,28},{4,0},{8,4},{12,8},{16,12},{20,16},{24,20},{28,24},{1,29},{... | collective-permute-start | bytes 24584 | tf_op jit(solution)/shard_map/ppermute | solution.py:136
  36.8 0.0 collective-permute-done.8
  36.8 0.0 collective-permute-done.9
  36.8 0.0 collective-permute-done.10
  36.9 1.1 %collective-permute-done.11 = f32[8,256]{1,0:T(8,128)S(1)} collective-permute-done((f32[8,256]{1,0:T(8,128)}, f32[8,256]{1,0:T(8,128)S(1)}, u32[]{:S(2)}, u32[]{:S(2)}) %collective-permute-start.11) | collective-permute-done | bytes 8224 | tf_op jit(solution)/shard_map/ppermute | solution.py:136
  37.9 1.4 %collective-permute-done.12 = f32[8,256]{1,0:T(8,128)S(1)} collective-permute-done((f32[8,256]{1,0:T(8,128)}, f32[8,256]{1,0:T(8,128)S(1)}, u32[]{:S(2)}, u32[]{:S(2)}) %collective-permute-start.12) | collective-permute-done | bytes 8224 | tf_op jit(solution)/shard_map/ppermute | solution.py:136
  39.3 0.7 %add_add_fusion.refs_0_ = f32[8,256]{1,0:T(8,128)S(1)} fusion(f32[8,256]{1,0:T(8,128)S(1)} %collective-permute-done.12, f32[8,256]{1,0:T(8,128)S(1)} %collective-permute-done.11, f32[8,256]{1,0:T(8,128)S(1)} %collective-permute-done.10, f32[8,256]{1,0:T(8,128)S(1)} %collective-permute-done.9, f32[8,256]{1,0:T(8,128)S(1)} %collective-permute-done.8, ...), kind=kLoop, calls=%fused_computation | loop fusion | flops 14336 | bytes 73728 | tf_op jit(solution)/shard_map/add | solution.py:166
  40.0 4.2 %collective-permute-start.19 = (f32[8,256]{1,0:T(8,128)S(1)}, f32[8,256]{1,0:T(8,128)S(1)}, u32[]{:S(2)}, u32[]{:S(2)}) collective-permute-start(f32[8,256]{1,0:T(8,128)S(1)} %add_add_fusion.refs_0_), channel_id=1, source_target_pairs={{0,28},{4,0},{8,4},{12,8},{16,12},{20,16},{24,20},{28,24},{1,29},{... | collective-permute-start | bytes 24584 | tf_op jit(solution)/shard_map/ppermute | solution.py:136
  44.2 3.0 %collective-permute-start.16 = (f32[8,256]{1,0:T(8,128)S(1)}, f32[8,256]{1,0:T(8,128)S(1)}, u32[]{:S(2)}, u32[]{:S(2)}) collective-permute-start(f32[8,256]{1,0:T(8,128)S(1)} %add_add_fusion.refs_0_), channel_id=1, source_target_pairs={{0,16},{4,20},{8,24},{12,28},{16,0},{20,4},{24,8},{28,12},{1,17},{... | collective-permute-start | bytes 24584 | tf_op jit(solution)/shard_map/ppermute | solution.py:136
  47.2 0.3 collective-permute-start.15
  47.4 1.7 %collective-permute-start.14 = (f32[8,256]{1,0:T(8,128)S(1)}, f32[8,256]{1,0:T(8,128)S(1)}, u32[]{:S(2)}, u32[]{:S(2)}) collective-permute-start(f32[8,256]{1,0:T(8,128)S(1)} %add_add_fusion.refs_0_), channel_id=1, source_target_pairs={{0,8},{4,12},{8,16},{12,20},{16,24},{20,28},{24,0},{28,4},{1,9},{5... | collective-permute-start | bytes 24584 | tf_op jit(solution)/shard_map/ppermute | solution.py:136
  49.1 1.5 %collective-permute-start.13 = (f32[8,256]{1,0:T(8,128)S(1)}, f32[8,256]{1,0:T(8,128)S(1)}, u32[]{:S(2)}, u32[]{:S(2)}) collective-permute-start(f32[8,256]{1,0:T(8,128)S(1)} %add_add_fusion.refs_0_), channel_id=1, source_target_pairs={{0,4},{4,8},{8,12},{12,16},{16,20},{20,24},{24,28},{28,0},{1,5},{5... | collective-permute-start | bytes 24584 | tf_op jit(solution)/shard_map/ppermute | solution.py:136
  50.6 0.0 collective-permute-done.17.refs_5_
  50.6 0.0 collective-permute-done.16.refs_4_
  50.6 2.0 %collective-permute-done.15.refs_3_ = f32[8,256]{1,0:T(8,128)S(1)} collective-permute-done((f32[8,256]{1,0:T(8,128)S(1)}, f32[8,256]{1,0:T(8,128)S(1)}, u32[]{:S(2)}, u32[]{:S(2)}) %collective-permute-start.15) | collective-permute-done | bytes 8224 | tf_op jit(solution)/shard_map/ppermute | solution.py:136
  52.6 1.5 %collective-permute-done.14.refs_2_ = f32[8,256]{1,0:T(8,128)S(1)} collective-permute-done((f32[8,256]{1,0:T(8,128)S(1)}, f32[8,256]{1,0:T(8,128)S(1)}, u32[]{:S(2)}, u32[]{:S(2)}) %collective-permute-start.14) | collective-permute-done | bytes 8224 | tf_op jit(solution)/shard_map/ppermute | solution.py:136
  54.1 1.4 %collective-permute-done.13.refs_1_ = f32[8,256]{1,0:T(8,128)S(1)} collective-permute-done((f32[8,256]{1,0:T(8,128)S(1)}, f32[8,256]{1,0:T(8,128)S(1)}, u32[]{:S(2)}, u32[]{:S(2)}) %collective-permute-start.13) | collective-permute-done | bytes 8224 | tf_op jit(solution)/shard_map/ppermute | solution.py:136
  55.5 0.6 copy-done.16
  56.1 1.5 %shard_map.87 = f32[64,256]{1,0:T(8,128)} custom-call(f32[8,256]{1,0:T(8,128)} %copy-done.9, f32[8,256]{1,0:T(8,128)} %copy-done.16, f32[8,256]{1,0:T(8,128)} %copy-done.15, f32[8,256]{1,0:T(8,128)} %copy-done.14, f32[8,256]{1,0:T(8,128)} %copy-done.13, f32[8,256]{1,0:T(8,128)} %copy-done.12, f32[8,256]{1,0:T(8,128)} %copy-done.11, f32[8,256]{1,0:T(8,128)} %copy-done.10), custom_call_target="tpu_custom_call" | custom-call | tf_op jit(solution)/shard_map/pallas_call | solution.py:168
  (30 shorter events, 0.1 us)
Async XLA Ops:
  0.6 5.4 %collective-permute-start.1 = (bf16[64,256]{1,0:T(8,128)(2,1)}, bf16[64,256]{1,0:T(8,128)(2,1)S(1)}, u32[]{:S(2)}, u32[]{:S(2)}) collective-permute-start(bf16[64,256]{1,0:T(8,128)(2,1)} %refs_5_.1), channel_id=1, source_target_pairs={{0,2},{1,3},{2,0},{3,1},{4,6},{5,7},{6,4},{7,5},{8,10},{9,11},{10,... | collective-permute-start | bytes 98312 | tf_op jit(solution)/shard_map/ppermute | solution.py:136
  3.7 3.6 %collective-permute-start = (bf16[64,256]{1,0:T(8,128)(2,1)}, bf16[64,256]{1,0:T(8,128)(2,1)S(1)}, u32[]{:S(2)}, u32[]{:S(2)}) collective-permute-start(bf16[64,256]{1,0:T(8,128)(2,1)} %refs_5_.1), channel_id=1, source_target_pairs={{0,1},{1,2},{2,3},{3,0},{4,5},{5,6},{6,7},{7,4},{8,9},{9,10},{10,1... | collective-permute-start | bytes 98312 | tf_op jit(solution)/shard_map/ppermute | solution.py:136
  3.7 3.7 %collective-permute-start.2 = (bf16[64,256]{1,0:T(8,128)(2,1)}, bf16[64,256]{1,0:T(8,128)(2,1)S(1)}, u32[]{:S(2)}, u32[]{:S(2)}) collective-permute-start(bf16[64,256]{1,0:T(8,128)(2,1)} %refs_5_.1), channel_id=1, source_target_pairs={{0,3},{1,0},{2,1},{3,2},{4,7},{5,4},{6,5},{7,6},{8,11},{9,8},{10,9... | collective-permute-start | bytes 98312 | tf_op jit(solution)/shard_map/ppermute | solution.py:136
  7.3 1.7 %copy-start = (bf16[1,1280,1024]{2,1,0:T(8,128)(2,1)S(1)}, bf16[1,1280,1024]{2,1,0:T(8,128)(2,1)}, u32[]{:S(2)}) copy-start(bf16[1,1280,1024]{2,1,0:T(8,128)(2,1)} %param.6) | copy-start | bytes 7864324
  9.1 0.9 %copy-start.1 = (bf16[1,64,1280]{2,1,0:T(8,128)(2,1)S(1)}, bf16[1,64,1280]{2,1,0:T(8,128)(2,1)}, u32[]{:S(2)}) copy-start(bf16[1,64,1280]{2,1,0:T(8,128)(2,1)} %param.8) | copy-start | bytes 491524
  10.0 0.8 %copy-start.3 = (bf16[64,256]{1,0:T(8,128)(2,1)S(1)}, bf16[64,256]{1,0:T(8,128)(2,1)}, u32[]{:S(2)}) copy-start(bf16[64,256]{1,0:T(8,128)(2,1)} %refs_5_.1) | copy-start | bytes 98308
  10.7 0.7 %copy-start.4 = (f32[1,1280]{1,0:T(1,128)S(1)}, f32[1,1280]{1,0:T(1,128)}, u32[]{:S(2)}) copy-start(f32[1,1280]{1,0:T(1,128)} %refs_2_.1) | copy-start | bytes 15364
  11.4 0.7 %copy-start.5 = (s32[1,64]{1,0:T(1,128)S(1)}, s32[1,64]{1,0:T(1,128)}, u32[]{:S(2)}) copy-start(s32[1,64]{1,0:T(1,128)} %refs_1_.1) | copy-start | bytes 772
  16.6 0.6 %copy-start.2 = (f32[64,256]{1,0:T(8,128)}, f32[64,256]{1,0:T(8,128)S(1)}, u32[]{:S(2)}) copy-start(f32[64,256]{1,0:T(8,128)S(1)} %get-tuple-element.17.refs_0_) | copy-start | bytes 196612
  17.2 3.8 %collective-permute-start.3 = (f32[64,256]{1,0:T(8,128)S(1)}, f32[64,256]{1,0:T(8,128)S(1)}, u32[]{:S(2)}, u32[]{:S(2)}) collective-permute-start(f32[64,256]{1,0:T(8,128)S(1)} %get-tuple-element.18), channel_id=1, source_target_pairs={{0,1},{1,2},{2,3},{3,0},{4,5},{5,6},{6,7},{7,4},{8,9},{9,10},{10,1... | collective-permute-start | bytes 196616 | tf_op jit(solution)/shard_map/ppermute | solution.py:136
  17.3 4.9 %collective-permute-start.4 = (f32[64,256]{1,0:T(8,128)S(1)}, f32[64,256]{1,0:T(8,128)S(1)}, u32[]{:S(2)}, u32[]{:S(2)}) collective-permute-start(f32[64,256]{1,0:T(8,128)S(1)} %get-tuple-element.19), channel_id=1, source_target_pairs={{0,2},{1,3},{2,0},{3,1},{4,6},{5,7},{6,4},{7,5},{8,10},{9,11},{10,... | collective-permute-start | bytes 196616 | tf_op jit(solution)/shard_map/ppermute | solution.py:136
  19.2 3.0 %collective-permute-start.5 = (f32[64,256]{1,0:T(8,128)S(1)}, f32[64,256]{1,0:T(8,128)S(1)}, u32[]{:S(2)}, u32[]{:S(2)}) collective-permute-start(f32[64,256]{1,0:T(8,128)S(1)} %get-tuple-element.20), channel_id=1, source_target_pairs={{0,3},{1,0},{2,1},{3,2},{4,7},{5,4},{6,5},{7,6},{8,11},{9,8},{10,9... | collective-permute-start | bytes 196616 | tf_op jit(solution)/shard_map/ppermute | solution.py:136
  21.0 1.2 %copy-start.6 = (f32[64,256]{1,0:T(8,128)}, f32[64,256]{1,0:T(8,128)S(1)}, u32[]{:S(2)}) copy-start(f32[64,256]{1,0:T(8,128)S(1)} %collective-permute-done.3.refs_1_) | copy-start | bytes 196612
  22.2 0.6 %copy-start.7 = (f32[64,256]{1,0:T(8,128)}, f32[64,256]{1,0:T(8,128)S(1)}, u32[]{:S(2)}) copy-start(f32[64,256]{1,0:T(8,128)S(1)} %collective-permute-done.4.refs_2_) | copy-start | bytes 196612
  22.2 0.6 %copy-start.8 = (f32[64,256]{1,0:T(8,128)}, f32[64,256]{1,0:T(8,128)S(1)}, u32[]{:S(2)}) copy-start(f32[64,256]{1,0:T(8,128)S(1)} %collective-permute-done.5.refs_3_) | copy-start | bytes 196612
  24.4 9.6 %collective-permute-start.6 = (f32[8,256]{1,0:T(8,128)}, f32[8,256]{1,0:T(8,128)S(1)}, u32[]{:S(2)}, u32[]{:S(2)}) collective-permute-start(f32[8,256]{1,0:T(8,128)} %get-tuple-element.22), channel_id=1, source_target_pairs={{0,4},{4,8},{8,12},{12,16},{16,20},{20,24},{24,28},{28,0},{1,5},{5... | collective-permute-start | bytes 24584 | tf_op jit(solution)/shard_map/ppermute | solution.py:136
  26.1 9.3 %collective-permute-start.7 = (f32[8,256]{1,0:T(8,128)}, f32[8,256]{1,0:T(8,128)S(1)}, u32[]{:S(2)}, u32[]{:S(2)}) collective-permute-start(f32[8,256]{1,0:T(8,128)} %get-tuple-element.23), channel_id=1, source_target_pairs={{0,8},{4,12},{8,16},{12,20},{16,24},{20,28},{24,0},{28,4},{1,9},{5... | collective-permute-start | bytes 24584 | tf_op jit(solution)/shard_map/ppermute | solution.py:136
  27.6 9.2 %collective-permute-start.8 = (f32[8,256]{1,0:T(8,128)}, f32[8,256]{1,0:T(8,128)S(1)}, u32[]{:S(2)}, u32[]{:S(2)}) collective-permute-start(f32[8,256]{1,0:T(8,128)} %get-tuple-element.24), channel_id=1, source_target_pairs={{0,12},{4,16},{8,20},{12,24},{16,28},{20,0},{24,4},{28,8},{1,13},{... | collective-permute-start | bytes 24584 | tf_op jit(solution)/shard_map/ppermute | solution.py:136
  30.2 6.7 %collective-permute-start.9 = (f32[8,256]{1,0:T(8,128)}, f32[8,256]{1,0:T(8,128)S(1)}, u32[]{:S(2)}, u32[]{:S(2)}) collective-permute-start(f32[8,256]{1,0:T(8,128)} %get-tuple-element.25), channel_id=1, source_target_pairs={{0,16},{4,20},{8,24},{12,28},{16,0},{20,4},{24,8},{28,12},{1,17},{... | collective-permute-start | bytes 24584 | tf_op jit(solution)/shard_map/ppermute | solution.py:136
  31.4 5.4 %collective-permute-start.10 = (f32[8,256]{1,0:T(8,128)}, f32[8,256]{1,0:T(8,128)S(1)}, u32[]{:S(2)}, u32[]{:S(2)}) collective-permute-start(f32[8,256]{1,0:T(8,128)} %get-tuple-element.26), channel_id=1, source_target_pairs={{0,20},{4,24},{8,28},{12,0},{16,4},{20,8},{24,12},{28,16},{1,21},{... | collective-permute-start | bytes 24584 | tf_op jit(solution)/shard_map/ppermute | solution.py:136
  34.0 3.9 %collective-permute-start.11 = (f32[8,256]{1,0:T(8,128)}, f32[8,256]{1,0:T(8,128)S(1)}, u32[]{:S(2)}, u32[]{:S(2)}) collective-permute-start(f32[8,256]{1,0:T(8,128)} %get-tuple-element.27), channel_id=1, source_target_pairs={{0,24},{4,28},{8,0},{12,4},{16,8},{20,12},{24,16},{28,20},{1,25},{... | collective-permute-start | bytes 24584 | tf_op jit(solution)/shard_map/ppermute | solution.py:136
  35.4 3.9 %collective-permute-start.12 = (f32[8,256]{1,0:T(8,128)}, f32[8,256]{1,0:T(8,128)S(1)}, u32[]{:S(2)}, u32[]{:S(2)}) collective-permute-start(f32[8,256]{1,0:T(8,128)} %get-tuple-element.28), channel_id=1, source_target_pairs={{0,28},{4,0},{8,4},{12,8},{16,12},{20,16},{24,20},{28,24},{1,29},{... | collective-permute-start | bytes 24584 | tf_op jit(solution)/shard_map/ppermute | solution.py:136
  40.0 15.5 %copy-start.9 = (f32[8,256]{1,0:T(8,128)}, f32[8,256]{1,0:T(8,128)S(1)}, u32[]{:S(2)}) copy-start(f32[8,256]{1,0:T(8,128)S(1)} %add_add_fusion.refs_0_) | copy-start | bytes 24580
  40.0 7.5 %collective-permute-start.19 = (f32[8,256]{1,0:T(8,128)S(1)}, f32[8,256]{1,0:T(8,128)S(1)}, u32[]{:S(2)}, u32[]{:S(2)}) collective-permute-start(f32[8,256]{1,0:T(8,128)S(1)} %add_add_fusion.refs_0_), channel_id=1, source_target_pairs={{0,28},{4,0},{8,4},{12,8},{16,12},{20,16},{24,20},{28,24},{1,29},{... | collective-permute-start | bytes 24584 | tf_op jit(solution)/shard_map/ppermute | solution.py:136
  44.2 5.0 %collective-permute-start.18 = (f32[8,256]{1,0:T(8,128)S(1)}, f32[8,256]{1,0:T(8,128)S(1)}, u32[]{:S(2)}, u32[]{:S(2)}) collective-permute-start(f32[8,256]{1,0:T(8,128)S(1)} %add_add_fusion.refs_0_), channel_id=1, source_target_pairs={{0,24},{4,28},{8,0},{12,4},{16,8},{20,12},{24,16},{28,20},{1,25},{... | collective-permute-start | bytes 24584 | tf_op jit(solution)/shard_map/ppermute | solution.py:136
  44.2 6.4 %collective-permute-start.17 = (f32[8,256]{1,0:T(8,128)S(1)}, f32[8,256]{1,0:T(8,128)S(1)}, u32[]{:S(2)}, u32[]{:S(2)}) collective-permute-start(f32[8,256]{1,0:T(8,128)S(1)} %add_add_fusion.refs_0_), channel_id=1, source_target_pairs={{0,20},{4,24},{8,28},{12,0},{16,4},{20,8},{24,12},{28,16},{1,21},{... | collective-permute-start | bytes 24584 | tf_op jit(solution)/shard_map/ppermute | solution.py:136
  44.2 6.4 %collective-permute-start.16 = (f32[8,256]{1,0:T(8,128)S(1)}, f32[8,256]{1,0:T(8,128)S(1)}, u32[]{:S(2)}, u32[]{:S(2)}) collective-permute-start(f32[8,256]{1,0:T(8,128)S(1)} %add_add_fusion.refs_0_), channel_id=1, source_target_pairs={{0,16},{4,20},{8,24},{12,28},{16,0},{20,4},{24,8},{28,12},{1,17},{... | collective-permute-start | bytes 24584 | tf_op jit(solution)/shard_map/ppermute | solution.py:136
  47.2 5.4 %collective-permute-start.15 = (f32[8,256]{1,0:T(8,128)S(1)}, f32[8,256]{1,0:T(8,128)S(1)}, u32[]{:S(2)}, u32[]{:S(2)}) collective-permute-start(f32[8,256]{1,0:T(8,128)S(1)} %add_add_fusion.refs_0_), channel_id=1, source_target_pairs={{0,12},{4,16},{8,20},{12,24},{16,28},{20,0},{24,4},{28,8},{1,13},{... | collective-permute-start | bytes 24584 | tf_op jit(solution)/shard_map/ppermute | solution.py:136
  47.4 8.1 %copy-start.10 = (f32[8,256]{1,0:T(8,128)}, f32[8,256]{1,0:T(8,128)S(1)}, u32[]{:S(2)}) copy-start(f32[8,256]{1,0:T(8,128)S(1)} %collective-permute-done.19.refs_7_) | copy-start | bytes 24580
  47.4 6.7 %collective-permute-start.14 = (f32[8,256]{1,0:T(8,128)S(1)}, f32[8,256]{1,0:T(8,128)S(1)}, u32[]{:S(2)}, u32[]{:S(2)}) collective-permute-start(f32[8,256]{1,0:T(8,128)S(1)} %add_add_fusion.refs_0_), channel_id=1, source_target_pairs={{0,8},{4,12},{8,16},{12,20},{16,24},{20,28},{24,0},{28,4},{1,9},{5... | collective-permute-start | bytes 24584 | tf_op jit(solution)/shard_map/ppermute | solution.py:136
  49.1 6.4 %copy-start.11 = (f32[8,256]{1,0:T(8,128)}, f32[8,256]{1,0:T(8,128)S(1)}, u32[]{:S(2)}) copy-start(f32[8,256]{1,0:T(8,128)S(1)} %collective-permute-done.18.refs_6_) | copy-start | bytes 24580
  49.1 6.3 %collective-permute-start.13 = (f32[8,256]{1,0:T(8,128)S(1)}, f32[8,256]{1,0:T(8,128)S(1)}, u32[]{:S(2)}, u32[]{:S(2)}) collective-permute-start(f32[8,256]{1,0:T(8,128)S(1)} %add_add_fusion.refs_0_), channel_id=1, source_target_pairs={{0,4},{4,8},{8,12},{12,16},{16,20},{20,24},{24,28},{28,0},{1,5},{5... | collective-permute-start | bytes 24584 | tf_op jit(solution)/shard_map/ppermute | solution.py:136
  50.6 4.9 %copy-start.12 = (f32[8,256]{1,0:T(8,128)}, f32[8,256]{1,0:T(8,128)S(1)}, u32[]{:S(2)}) copy-start(f32[8,256]{1,0:T(8,128)S(1)} %collective-permute-done.17.refs_5_) | copy-start | bytes 24580
  50.6 4.9 %copy-start.13 = (f32[8,256]{1,0:T(8,128)}, f32[8,256]{1,0:T(8,128)S(1)}, u32[]{:S(2)}) copy-start(f32[8,256]{1,0:T(8,128)S(1)} %collective-permute-done.16.refs_4_) | copy-start | bytes 24580
  52.6 2.9 %copy-start.14 = (f32[8,256]{1,0:T(8,128)}, f32[8,256]{1,0:T(8,128)S(1)}, u32[]{:S(2)}) copy-start(f32[8,256]{1,0:T(8,128)S(1)} %collective-permute-done.15.refs_3_) | copy-start | bytes 24580
  54.1 1.4 %copy-start.15 = (f32[8,256]{1,0:T(8,128)}, f32[8,256]{1,0:T(8,128)S(1)}, u32[]{:S(2)}) copy-start(f32[8,256]{1,0:T(8,128)S(1)} %collective-permute-done.14.refs_2_) | copy-start | bytes 24580
  55.5 0.6 copy-start.16

commit v2 on v1

v2 whole, which is shorter than its diff:
```python
import functools

import jax
import jax.numpy as jnp
from jax import lax
from jax.experimental import pallas as pl
from jax.experimental.pallas import tpu as pltpu
from jax.sharding import PartitionSpec as P

LANES = 128
EXTRA = 16
F32 = jnp.float32
BF16 = jnp.bfloat16


def shift_tiles(tiles, delay, forward):
    lane = lax.broadcasted_iota(jnp.int32, delay.shape, 1)
    nothing = jnp.zeros_like(tiles[0])
    for level in range(7):
        amount = 1 << level
        chosen = (delay & amount) != 0
        if forward:
            turned = [pltpu.roll(tile, amount, 1) for tile in tiles]
            before = [nothing] + turned[:-1]
            moved = [jnp.where(lane < amount, b, t) for b, t in zip(before, turned)]
        else:
            turned = [pltpu.roll(tile, LANES - amount, 1) for tile in tiles]
            after = turned[1:] + [nothing]
            moved = [jnp.where(lane < LANES - amount, t, a) for t, a in zip(turned, after)]
        tiles = [jnp.where(chosen, m, tile) for m, tile in zip(moved, tiles)]
    chosen = delay >= LANES
    other = [nothing] + tiles[:-1] if forward else tiles[1:] + [nothing]
    return [jnp.where(chosen, o, tile) for o, tile in zip(other, tiles)]


def main_kernel(parts, chunk, step, *refs):
    recorded_ref, latents_ref, delays_hbm, bias_hbm, load_hbm, counts_hbm, out, grad_load_hbm, grad_bias_hbm = refs[:9]
    delays_ref, bias_ref, counts_ref, shifted, load_ext, grad_shift, grad_load_ref, grad_bias_ref = refs[9:17]
    small_sems, counts_sems, out_sems = refs[17:]
    lats, total = grad_shift.shape
    neurons = counts_ref.shape[0]
    width = total // parts
    pieces = neurons // chunk
    length = recorded_ref[0]

    small = [
        pltpu.make_async_copy(delays_hbm, delays_ref, small_sems.at[0]),
        pltpu.make_async_copy(bias_hbm, bias_ref, small_sems.at[1]),
        pltpu.make_async_copy(load_hbm, load_ext.at[pl.ds(0, lats)], small_sems.at[2]),
    ]
    for copy in small:
        copy.start()

    def counts_copy(index):
        rows = pl.ds(pl.multiple_of(index * chunk, chunk), chunk)
        return pltpu.make_async_copy(counts_hbm.at[rows], counts_ref.at[rows], counts_sems.at[index])

    def load_copy(index):
        rows = pl.ds(pl.multiple_of(index * chunk, chunk), chunk)
        return pltpu.make_async_copy(grad_load_ref.at[:, rows], grad_load_hbm.at[:, rows], out_sems.at[index])

    for index in range(pieces):
        counts_copy(index).start()
    row = lax.broadcasted_iota(jnp.int32, (EXTRA, total), 0)
    shifted[lats:, :] = jnp.where(row < 3, 1.0, 0.0).astype(BF16)
    grad_shift[...] = jnp.zeros_like(grad_shift)

    small[0].wait()
    diagonal = lax.broadcasted_iota(jnp.int32, (lats, lats), 0) == lax.broadcasted_iota(jnp.int32, (lats, lats), 1)
    spread = jnp.broadcast_to(delays_ref[...].astype(F32), (lats, lats))
    column = jnp.sum(jnp.where(diagonal, spread, 0.0), axis=1, keepdims=True)
    delay = jnp.broadcast_to(column, (lats, LANES)).astype(jnp.int32)
    tiles = [latents_ref[:, j * LANES : (j + 1) * LANES].astype(F32) for j in range(total // LANES)]
    for j, tile in enumerate(shift_tiles(tiles, delay, True)):
        shifted[0:lats, j * LANES : (j + 1) * LANES] = tile.astype(BF16)

    small[1].wait()
    bias = bias_ref[...]
    high = bias.astype(BF16).astype(F32)
    middle = (bias - high).astype(BF16).astype(F32)
    low = bias - high - middle
    row = lax.broadcasted_iota(jnp.int32, (EXTRA, neurons), 0)
    below = jnp.where(row == 0, high, jnp.where(row == 1, middle, jnp.where(row == 2, low, 0.0)))
    load_ext[lats:, :] = below.astype(BF16)
    small[2].wait()

    bins = lax.broadcasted_iota(jnp.int32, (1, total), 1)

    def visit(index, carry):
        rows = pl.ds(pl.multiple_of(index * chunk, chunk), chunk)
        counts_copy(index).wait()
        load_part = load_ext[:, rows]
        grad_load = jnp.zeros((lats, chunk), F32)
        sums = jnp.zeros((chunk, LANES), F32)
        for begin in range(0, total, step):
            span = slice(begin, begin + step)
            piece = shifted[:, span]
            eta = lax.dot_general(load_part, piece, (((0,), (0,)), ((), ())), preferred_element_type=F32)
            observed = counts_ref[rows, span].astype(F32)
            resid = jnp.where(bins[:, span] < length, jnp.exp(eta) - observed, 0.0)
            resid_low = resid.astype(BF16)
            for j in range(step // LANES):
                sums = sums + resid[:, j * LANES : (j + 1) * LANES]
            grad_load = grad_load + lax.dot_general(
                piece[0:lats], resid_low, (((1,), (1,)), ((), ())), preferred_element_type=F32
            )
            grad_shift[:, span] += jnp.dot(load_part[0:lats], resid_low, preferred_element_type=F32)
        grad_load_ref[:, rows] = grad_load
        load_copy(index).start()
        grad_bias_ref[:, rows] = jnp.sum(sums.T, axis=0, keepdims=True)
        return carry

    lax.fori_loop(0, pieces, visit, 0, unroll=total <= 1024)
    bias_copy = pltpu.make_async_copy(grad_bias_ref, grad_bias_hbm, small_sems.at[0])
    bias_copy.start()

    tiles = [grad_shift[:, j * LANES : (j + 1) * LANES] for j in range(total // LANES)]
    for j, tile in enumerate(shift_tiles(tiles, delay, False)):
        part, at = divmod(j * LANES, width)
        out[part, :, at : at + LANES] = tile
    for index in range(pieces):
        load_copy(index).wait()
    bias_copy.wait()


def per_device(region_count, neuron_count, counts, latents, loadings, bias, delays, recorded):
    neurons, total = counts.shape[1:]
    lats, width = latents.shape
    chunk = 256
    vmem = pl.BlockSpec(memory_space=pltpu.VMEM)
    smem = pl.BlockSpec(memory_space=pltpu.SMEM)
    hbm = pl.BlockSpec(memory_space=pltpu.HBM)

    whole = lax.all_gather(latents, "neuron", axis=1, tiled=True)
    partial, grad_load, grad_bias = pl.pallas_call(
        functools.partial(main_kernel, neuron_count, chunk, 512),
        out_shape=[
            jax.ShapeDtypeStruct((neuron_count, lats, width), F32),
            jax.ShapeDtypeStruct((lats, neurons), F32),
            jax.ShapeDtypeStruct((1, neurons), F32),
        ],
        in_specs=[smem, vmem, hbm, hbm, hbm, hbm],
        out_specs=[vmem, hbm, hbm],
        scratch_shapes=[
            pltpu.VMEM((1, lats), jnp.int32),
            pltpu.VMEM((1, neurons), F32),
            pltpu.VMEM((neurons, total), BF16),
            pltpu.VMEM((lats + EXTRA, total), BF16),
            pltpu.VMEM((lats + EXTRA, neurons), BF16),
            pltpu.VMEM((lats, total), F32),
            pltpu.VMEM((lats, neurons), F32),
            pltpu.VMEM((1, neurons), F32),
            pltpu.SemaphoreType.DMA((3,)),
            pltpu.SemaphoreType.DMA((neurons // chunk,)),
            pltpu.SemaphoreType.DMA((neurons // chunk,)),
        ],
        compiler_params=pltpu.CompilerParams(vmem_limit_bytes=58 * 1024 * 1024),
    )(recorded, whole, delays, bias, loadings[0], counts[0])

    arrived = lax.all_to_all(partial, "neuron", 0, 0)
    block = jnp.sum(arrived, axis=0).reshape(region_count, lats // region_count, width)
    mine = jnp.sum(lax.all_to_all(block, "region", 0, 0), axis=0)
    spread = jnp.broadcast_to(mine[None], block.shape)
    grad_latents = lax.all_to_all(spread, "region", 0, 0).reshape(lats, width)
    return (grad_latents, grad_load[None], grad_bias)


def solution(mesh):
    placed = (
        P("region", "neuron", None),
        P(None, "neuron"),
        P("region", None, "neuron"),
        P("region", "neuron"),
        P("region", None),
        P("region"),
    )
    return jax.shard_map(
        functools.partial(per_device, mesh.shape["region"], mesh.shape["neuron"]),
        mesh=mesh,
        in_specs=placed,
        out_specs=(P(None, "neuron"), P("region", None, "neuron"), P("region", "neuron")),
        check_vma=False,
    )
```

time: 58 us -> 50.3 us (0.87)
  blocking collectives: 0 us -> 39.6 us
  starting transfers between devices: 29.8 us -> 0 us
  waiting for transfers between devices: 11.5 us -> 0 us
  local copies, waits for them, and re-layouts: 6.61 us -> 0.64 us
  Pallas kernels: 7.54 us -> 8.29 us
  other arithmetic: 0.71 us -> 0.03 us
    all_to_all x0 -> x3, blocking collectives: none -> 31.2 us  [the longest x1 12.5 us: per_device(): mine = jnp.sum(lax.all_to_all(block, 'region', 0, 0), axis=0)]
    ppermute x20 -> x0, starting transfers between devices: 29.8 us -> none  [send(): lax.ppermute(value, axis, [(i, (i + k) % count) for i in range(count)])]
    ppermute x20 -> x0, waiting for transfers between devices: 11.5 us -> none  [send(): lax.ppermute(value, axis, [(i, (i + k) % count) for i in range(count)])]
    all_gather x0 -> x1, blocking collectives: none -> 8.41 us  [per_device(): whole = lax.all_gather(latents, 'neuron', axis=1, tiled=True)]
    unnamed x34 -> x1, local copies, waits for them, and re-layouts: 6.61 us -> 0.63 us
    pallas_call x3 -> x1, Pallas kernels: 7.54 us -> 8.29 us  [per_device(): pl.pallas_call(functools.partial(main_kernel, neuron_count, chunk, 512),...]
    add x1 -> x0, other arithmetic: 0.71 us -> none  [per_device(): mine = functools.reduce(jnp.add, arrived)]
  transfers between devices with their start and end apart: 20 -> 0, of which waited for: 9 -> 0; matrix products, arithmetic and copies ran while one was open for 0% -> 0% of each run, Pallas kernels for 0% -> 0%
where the time goes in v2:
time: 50.3 us; the launch traced here: 49.9 us
  blocking collectives  39.6 us (79%)
  Pallas kernels  8.29 us (16%)
  between operations  1.3 us (3%)
  local copies, waits for them, and re-layouts  0.64 us (1%)
    all_to_all x1, blocking collectives, per_device(): mine = jnp.sum(lax.all_to_all(block, 'region', 0, 0), axis=0)  12.5 us
    all_to_all x1, blocking collectives, per_device(): arrived = lax.all_to_all(partial, 'neuron', 0, 0)  9.42 us
    all_to_all x1, blocking collectives, per_device(): grad_latents = lax.all_to_all(spread, 'region', 0, 0).reshape(lats, width)  9.29 us
    all_gather x1, blocking collectives, per_device(): whole = lax.all_gather(latents, 'neuron', axis=1, tiled=True)  8.41 us
    pallas_call x1, Pallas kernels, per_device(): pl.pallas_call(functools.partial(main_kernel, neuron_count, chunk, 512),...  8.29 us

profile of v2, /device:TPU:0, one launch (start us, length us, event | category | flops | bytes accessed | tf_op | source)
XLA Modules:
  0.0 49.9 jit_solution(493618006083001966)
XLA Ops:
  1.3 8.4 %all_gather.3.refs_1_ = bf16[64,1024]{1,0:T(8,128)(2,1)} all-gather(bf16[64,256]{1,0:T(8,128)(2,1)} %param.7), channel_id=1, replica_groups=mesh['region'=8,'neuron'=4] {'neuron'}, dimensions={1}, use_global_device_ids=true | all-gather | bytes 163840 | tf_op jit(solution)/shard_map/all_gather | solution.py:134
  9.7 8.3 %shard_map.85 = (f32[4,64,256]{2,1,0:T(8,128)}, f32[64,1280]{1,0:T(8,128)}, f32[1,1280]{1,0:T(1,128)}) custom-call(s32[1]{0:T(128)S(6)} %copy.10.refs_0_, bf16[64,1024]{1,0:T(8,128)(2,1)} %all_gather.3.refs_1_, s32[1,64]{1,0:T(1,128)} %refs_2_.1, f32[1,1280]{1,0:T(1,128)} %refs_3_.1, bf16[64,1280]{1,0:T(8,128)(2,1)} %bitcast.8, bf16[1280,1024]{1,0:T(8,128)(2,1)} %bitcast.5), custom_call_target="tpu_custom_call" | custom-call | tf_op jit(solution)/shard_map/pallas_call | solution.py:135
  18.0 9.4 %all_to_all.15 = f32[4,64,256]{2,1,0:T(8,128)S(1)} all-to-all(f32[4,64,256]{2,1,0:T(8,128)} %get-tuple-element.6), channel_id=1, replica_groups=mesh['region'=8,'neuron'=4] {'neuron'}, dimensions={0} | all-to-all | bytes 524288 | tf_op jit(solution)/shard_map/all_to_all | solution.py:160
  27.4 12.5 %all_to_all.16 = f32[8,8,256]{2,1,0:T(8,128)S(1)} all-to-all(f32[8,8,256]{2,1,0:T(8,128)S(1)} %bitcast.6), channel_id=1, replica_groups=mesh['region'=8,'neuron'=4] {'region'}, dimensions={0} | all-to-all | bytes 131072 | tf_op jit(solution)/shard_map/all_to_all | solution.py:162
  40.0 9.3 %all_to_all.17 = f32[8,8,256]{2,1,0:T(8,128)S(1)} all-to-all(f32[8,8,256]{2,1,0:T(8,128)S(1)} %broadcast_in_dim.4), channel_id=1, replica_groups=mesh['region'=8,'neuron'=4] {'region'}, dimensions={0} | all-to-all | bytes 131072 | tf_op jit(solution)/shard_map/all_to_all | solution.py:164
  49.3 0.6 %copy.11 = f32[64,256]{1,0:T(8,128)} copy(f32[64,256]{1,0:T(8,128)S(1)} %bitcast.7) | data formatting | bytes 131072
  (3 shorter events, 0.0 us)

commit v3 on v2

--- a/solution.py
+++ b/solution.py
@@ -33,10 +33,14 @@
     return [jnp.where(chosen, o, tile) for o, tile in zip(other, tiles)]
 
 
-def main_kernel(parts, chunk, step, *refs):
-    recorded_ref, latents_ref, delays_hbm, bias_hbm, load_hbm, counts_hbm, out, grad_load_hbm, grad_bias_hbm = refs[:9]
-    delays_ref, bias_ref, counts_ref, shifted, load_ext, grad_shift, grad_load_ref, grad_bias_ref = refs[9:17]
-    small_sems, counts_sems, out_sems = refs[17:]
+def main_kernel(parts, axis, chunk, step, *refs):
+    recorded_ref, delays_hbm, bias_hbm, load_hbm, counts_hbm = refs[:5]
+    held = parts.bit_length()
+    blocks = refs[5 : 5 + held]
+    keep, away, grad_load_hbm, grad_bias_hbm = refs[5 + held : 9 + held]
+    whole, delays_ref, bias_ref, counts_ref, shifted, load_ext, grad_shift, grad_load_ref, grad_bias_ref = refs[9 + held : 18 + held]
+    small_sems, counts_sems, out_sems = refs[18 + held :]
+    me = lax.axis_index(axis)
     lats, total = grad_shift.shape
     neurons = counts_ref.shape[0]
     width = total // parts
@@ -70,7 +74,13 @@
     spread = jnp.broadcast_to(delays_ref[...].astype(F32), (lats, lats))
     column = jnp.sum(jnp.where(diagonal, spread, 0.0), axis=1, keepdims=True)
     delay = jnp.broadcast_to(column, (lats, LANES)).astype(jnp.int32)
-    tiles = [latents_ref[:, j * LANES : (j + 1) * LANES].astype(F32) for j in range(total // LANES)]
+    k = 0
+    for ref in blocks:
+        for j in range(ref.shape[0]):
+            start = pl.multiple_of((me ^ k) * width, width)
+            whole[:, pl.ds(start, width)] = ref[j]
+            k += 1
+    tiles = [whole[:, j * LANES : (j + 1) * LANES].astype(F32) for j in range(total // LANES)]
     for j, tile in enumerate(shift_tiles(tiles, delay, True)):
         shifted[0:lats, j * LANES : (j + 1) * LANES] = tile.astype(BF16)
 
@@ -116,8 +126,11 @@
 
     tiles = [grad_shift[:, j * LANES : (j + 1) * LANES] for j in range(total // LANES)]
     for j, tile in enumerate(shift_tiles(tiles, delay, False)):
-        part, at = divmod(j * LANES, width)
-        out[part, :, at : at + LANES] = tile
+        grad_shift[:, j * LANES : (j + 1) * LANES] = tile
+    for k in range(parts):
+        start = pl.multiple_of((me ^ k) * width, width)
+        target = away if k % 2 else keep
+        target[k // 2] = grad_shift[:, pl.ds(start, width)]
     for index in range(pieces):
         load_copy(index).wait()
     bias_copy.wait()
@@ -131,17 +144,26 @@
     smem = pl.BlockSpec(memory_space=pltpu.SMEM)
     hbm = pl.BlockSpec(memory_space=pltpu.HBM)
 
-    whole = lax.all_gather(latents, "neuron", axis=1, tiled=True)
-    partial, grad_load, grad_bias = pl.pallas_call(
-        functools.partial(main_kernel, neuron_count, chunk, 512),
+    def swap(value, axis, count, bit):
+        return lax.ppermute(value, axis, [(i, i ^ bit) for i in range(count)])
+
+    blocks = [latents[None]]
+    bit = 1
+    while bit < neuron_count:
+        blocks.append(swap(jnp.concatenate(blocks, axis=0), "neuron", neuron_count, bit))
+        bit *= 2
+    keep, away, grad_load, grad_bias = pl.pallas_call(
+        functools.partial(main_kernel, neuron_count, "neuron", chunk, 512),
         out_shape=[
-            jax.ShapeDtypeStruct((neuron_count, lats, width), F32),
+            jax.ShapeDtypeStruct((neuron_count // 2, lats, width), F32),
+            jax.ShapeDtypeStruct((neuron_count // 2, lats, width), F32),
             jax.ShapeDtypeStruct((lats, neurons), F32),
             jax.ShapeDtypeStruct((1, neurons), F32),
         ],
-        in_specs=[smem, vmem, hbm, hbm, hbm, hbm],
-        out_specs=[vmem, hbm, hbm],
+        in_specs=[smem, hbm, hbm, hbm, hbm] + [vmem] * len(blocks),
+        out_specs=[vmem, vmem, hbm, hbm],
         scratch_shapes=[
+            pltpu.VMEM((lats, total), BF16),
             pltpu.VMEM((1, lats), jnp.int32),
             pltpu.VMEM((1, neurons), F32),
             pltpu.VMEM((neurons, total), BF16),
@@ -155,14 +177,19 @@
             pltpu.SemaphoreType.DMA((neurons // chunk,)),
         ],
         compiler_params=pltpu.CompilerParams(vmem_limit_bytes=58 * 1024 * 1024),
-    )(recorded, whole, delays, bias, loadings[0], counts[0])
-
-    arrived = lax.all_to_all(partial, "neuron", 0, 0)
-    block = jnp.sum(arrived, axis=0).reshape(region_count, lats // region_count, width)
-    mine = jnp.sum(lax.all_to_all(block, "region", 0, 0), axis=0)
-    spread = jnp.broadcast_to(mine[None], block.shape)
-    grad_latents = lax.all_to_all(spread, "region", 0, 0).reshape(lats, width)
-    return (grad_latents, grad_load[None], grad_bias)
+    )(recorded, delays, bias, loadings[0], counts[0], *blocks)
+
+    value = keep + swap(away, "neuron", neuron_count, 1)
+    bit = 2
+    while bit < neuron_count:
+        value = value[0::2] + swap(value[1::2], "neuron", neuron_count, bit)
+        bit *= 2
+    value = value[0]
+    bit = 1
+    while bit < region_count:
+        value = value + swap(value, "region", region_count, bit)
+        bit *= 2
+    return (value, grad_load[None], grad_bias)
 
 
 def solution(mesh):

time: 50.3 us -> 39.7 us (0.79)
  blocking collectives: 39.6 us -> 0 us
  waiting for transfers between devices: 0 us -> 13.9 us
  starting transfers between devices: 0 us -> 12.8 us
  other arithmetic: 0.03 us -> 2.37 us
    all_to_all x3 -> x0, blocking collectives: 31.2 us -> none  [the longest x1 12.5 us: per_device(): mine = jnp.sum(lax.all_to_all(block, 'region', 0, 0), axis=0)]
    ppermute x0 -> x7, waiting for transfers between devices: none -> 13.9 us  [swap(): return lax.ppermute(value, axis, [(i, i ^ bit) for i in range(count)])]
    ppermute x0 -> x7, starting transfers between devices: none -> 12.8 us  [swap(): return lax.ppermute(value, axis, [(i, i ^ bit) for i in range(count)])]
    all_gather x1 -> x0, blocking collectives: 8.41 us -> none  [per_device(): whole = lax.all_gather(latents, 'neuron', axis=1, tiled=True)]
    add x0 -> x4, other arithmetic: none -> 1.58 us  [the longest x1 0.92 us: per_device(): value = keep + swap(away, 'neuron', neuron_count, 1)]
    concatenate x0 -> x1, other arithmetic: none -> 0.78 us  [per_device(): jnp.concatenate(blocks, axis=0)]
  transfers between devices with their start and end apart: 0 -> 7, of which waited for: 0 -> 7; matrix products, arithmetic and copies ran while one was open for 0% -> 0% of each run, Pallas kernels for 0% -> 0%
where the time goes in v3:
time: 39.7 us; the launch traced here: 39.4 us
  waiting for transfers between devices  13.9 us (35%)
  starting transfers between devices  12.8 us (32%)
  Pallas kernels  8.3 us (21%)
  other arithmetic  2.37 us (6%)
  between operations  1.33 us (3%)
  local copies, waits for them, and re-layouts  0.64 us (2%)
    ppermute x7, waiting for transfers between devices, swap(): return lax.ppermute(value, axis, [(i, i ^ bit) for i in range(count)])  13.9 us
    ppermute x7, starting transfers between devices, swap(): return lax.ppermute(value, axis, [(i, i ^ bit) for i in range(count)])  12.8 us
    pallas_call x1, Pallas kernels, per_device(): pl.pallas_call(functools.partial(main_kernel, neuron_count, 'neuron', chu...  8.3 us
    add x1, other arithmetic, per_device(): value = keep + swap(away, 'neuron', neuron_count, 1)  0.92 us
  transfers between devices with their start and end apart: 7, of which 7 were waited for; matrix products, arithmetic and copies ran while one was open for 0% of the time, Pallas kernels for 0%

profile of v3, /device:TPU:0, one launch (start us, length us, event | category | flops | bytes accessed | tf_op | source)
XLA Modules:
  0.0 39.4 jit_solution(17917324806124802507)
XLA Ops:
  0.6 0.5 %collective-permute-start = (bf16[1,64,256]{2,1,0:T(8,128)(2,1)}, bf16[1,64,256]{2,1,0:T(8,128)(2,1)S(1)}, u32[]{:S(2)}, u32[]{:S(2)}) collective-permute-start(bf16[1,64,256]{2,1,0:T(8,128)(2,1)} %bitcast.8), channel_id=1, source_target_pairs={{0,1},{1,0},{2,3},{3,2},{4,5},{5,4},{6,7},{7,6},{8,9},{9,8},{10,11... | collective-permute-start | bytes 98312 | tf_op jit(solution)/shard_map/ppermute | solution.py:148
  1.1 1.1 %collective-permute-done.refs_6_ = bf16[1,64,256]{2,1,0:T(8,128)(2,1)S(1)} collective-permute-done((bf16[1,64,256]{2,1,0:T(8,128)(2,1)}, bf16[1,64,256]{2,1,0:T(8,128)(2,1)S(1)}, u32[]{:S(2)}, u32[]{:S(2)}) %collective-permute-start) | collective-permute-done | bytes 32800 | tf_op jit(solution)/shard_map/ppermute | solution.py:148
  2.2 0.0 copy-start
  2.2 0.8 %pad_maximum_fusion = bf16[2,64,256]{2,1,0:T(8,128)(2,1)S(1)} fusion(bf16[1,64,256]{2,1,0:T(8,128)(2,1)S(1)} %collective-permute-done.refs_6_, bf16[1,64,256]{2,1,0:T(8,128)(2,1)} %bitcast.9), kind=kLoop, calls=%fused_computation.2 | loop fusion | flops 32768 | bytes 131072 | tf_op jit(solution)/shard_map/concatenate | solution.py:153
  3.0 2.9 %collective-permute-start.1 = (bf16[2,64,256]{2,1,0:T(8,128)(2,1)S(1)}, bf16[2,64,256]{2,1,0:T(8,128)(2,1)S(1)}, u32[]{:S(2)}, u32[]{:S(2)}) collective-permute-start(bf16[2,64,256]{2,1,0:T(8,128)(2,1)S(1)} %pad_maximum_fusion), channel_id=1, source_target_pairs={{0,2},{1,3},{2,0},{3,1},{4,6},{5,7},{6,4},{7,5},{8,10},{9,11},{10,... | collective-permute-start | bytes 196616 | tf_op jit(solution)/shard_map/ppermute | solution.py:148
  6.5 1.8 %collective-permute-done.1.refs_7_ = bf16[2,64,256]{2,1,0:T(8,128)(2,1)S(1)} collective-permute-done((bf16[2,64,256]{2,1,0:T(8,128)(2,1)S(1)}, bf16[2,64,256]{2,1,0:T(8,128)(2,1)S(1)}, u32[]{:S(2)}, u32[]{:S(2)}) %collective-permute-start.1) | collective-permute-done | bytes 65568 | tf_op jit(solution)/shard_map/ppermute | solution.py:148
  8.3 0.0 copy-start.1
  8.3 0.0 copy-done
  8.3 0.6 %copy-done.1 = bf16[2,64,256]{2,1,0:T(8,128)(2,1)} copy-done((bf16[2,64,256]{2,1,0:T(8,128)(2,1)}, bf16[2,64,256]{2,1,0:T(8,128)(2,1)S(1)}, u32[]{:S(2)}) %copy-start.1) | copy-done | bytes 65560
  8.9 8.3 %shard_map.85 = (f32[2,64,256]{2,1,0:T(8,128)}, f32[2,64,256]{2,1,0:T(8,128)}, f32[64,1280]{1,0:T(8,128)}, f32[1,1280]{1,0:T(1,128)}) custom-call(s32[1]{0:T(128)S(6)} %copy.9.refs_0_, s32[1,64]{1,0:T(1,128)} %refs_1_.1, f32[1,1280]{1,0:T(1,128)} %refs_2_.1, bf16[64,1280]{1,0:T(8,128)(2,1)} %bitcast.7, bf16[1280,1024]{1,0:T(8,128)(2,1)} %bitcast.6, ...), custom_call_target="tpu_custom_call" | custom-call | tf_op jit(solution)/shard_map/pallas_call | solution.py:155
  17.2 0.1 collective-permute-start.2
  17.3 1.5 %collective-permute-done.2 = f32[2,64,256]{2,1,0:T(8,128)S(1)} collective-permute-done((f32[2,64,256]{2,1,0:T(8,128)}, f32[2,64,256]{2,1,0:T(8,128)S(1)}, u32[]{:S(2)}, u32[]{:S(2)}) %collective-permute-start.2) | collective-permute-done | bytes 131104 | tf_op jit(solution)/shard_map/ppermute | solution.py:148
  18.8 0.9 %add.15 = f32[2,64,256]{2,1,0:T(8,128)S(1)} add(f32[2,64,256]{2,1,0:T(8,128)} %get-tuple-element.7, f32[2,64,256]{2,1,0:T(8,128)S(1)} %collective-permute-done.2) | non-fusion elementwise | flops 32768 | bytes 393216 | tf_op jit(solution)/shard_map/add | solution.py:182
  19.8 1.9 %collective-permute-start.3 = (f32[1,64,256]{2,1,0:T(8,128)S(1)}, f32[1,64,256]{2,1,0:T(8,128)S(1)}, u32[]{:S(2)}, u32[]{:S(2)}) collective-permute-start(f32[1,64,256]{2,1,0:T(8,128)S(1)} %slice.11), channel_id=1, source_target_pairs={{0,2},{1,3},{2,0},{3,1},{4,6},{5,7},{6,4},{7,5},{8,10},{9,11},{10,... | collective-permute-start | bytes 196616 | tf_op jit(solution)/shard_map/ppermute | solution.py:148
  21.7 2.4 %collective-permute-done.3 = f32[1,64,256]{2,1,0:T(8,128)S(1)} collective-permute-done((f32[1,64,256]{2,1,0:T(8,128)S(1)}, f32[1,64,256]{2,1,0:T(8,128)S(1)}, u32[]{:S(2)}, u32[]{:S(2)}) %collective-permute-start.3) | collective-permute-done | bytes 65568 | tf_op jit(solution)/shard_map/ppermute | solution.py:148
  24.1 1.9 %collective-permute-start.4 = (f32[64,256]{1,0:T(8,128)S(1)}, f32[64,256]{1,0:T(8,128)S(1)}, u32[]{:S(2)}, u32[]{:S(2)}) collective-permute-start(f32[64,256]{1,0:T(8,128)S(1)} %fusion), channel_id=1, source_target_pairs={{0,4},{4,0},{8,12},{12,8},{16,20},{20,16},{24,28},{28,24},{1,5},{5... | collective-permute-start | bytes 196616 | tf_op jit(solution)/shard_map/ppermute | solution.py:148
  26.0 2.5 %collective-permute-done.4 = f32[64,256]{1,0:T(8,128)S(1)} collective-permute-done((f32[64,256]{1,0:T(8,128)S(1)}, f32[64,256]{1,0:T(8,128)S(1)}, u32[]{:S(2)}, u32[]{:S(2)}) %collective-permute-start.4) | collective-permute-done | bytes 65568 | tf_op jit(solution)/shard_map/ppermute | solution.py:148
  28.5 2.0 %collective-permute-start.5 = (f32[64,256]{1,0:T(8,128)S(1)}, f32[64,256]{1,0:T(8,128)S(1)}, u32[]{:S(2)}, u32[]{:S(2)}) collective-permute-start(f32[64,256]{1,0:T(8,128)S(1)} %add.17), channel_id=1, source_target_pairs={{0,8},{4,12},{8,0},{12,4},{16,24},{20,28},{24,16},{28,20},{1,9},{5... | collective-permute-start | bytes 196616 | tf_op jit(solution)/shard_map/ppermute | solution.py:148
  30.4 2.4 %collective-permute-done.5 = f32[64,256]{1,0:T(8,128)S(1)} collective-permute-done((f32[64,256]{1,0:T(8,128)S(1)}, f32[64,256]{1,0:T(8,128)S(1)}, u32[]{:S(2)}, u32[]{:S(2)}) %collective-permute-start.5) | collective-permute-done | bytes 65568 | tf_op jit(solution)/shard_map/ppermute | solution.py:148
  32.8 3.6 %collective-permute-start.6 = (f32[64,256]{1,0:T(8,128)S(1)}, f32[64,256]{1,0:T(8,128)S(1)}, u32[]{:S(2)}, u32[]{:S(2)}) collective-permute-start(f32[64,256]{1,0:T(8,128)S(1)} %add.18), channel_id=1, source_target_pairs={{0,16},{4,20},{8,24},{12,28},{16,0},{20,4},{24,8},{28,12},{1,17},{... | collective-permute-start | bytes 196616 | tf_op jit(solution)/shard_map/ppermute | solution.py:148
  36.5 2.3 %collective-permute-done.6 = f32[64,256]{1,0:T(8,128)S(1)} collective-permute-done((f32[64,256]{1,0:T(8,128)S(1)}, f32[64,256]{1,0:T(8,128)S(1)}, u32[]{:S(2)}, u32[]{:S(2)}) %collective-permute-start.6) | collective-permute-done | bytes 65568 | tf_op jit(solution)/shard_map/ppermute | solution.py:148
  38.7 0.6 %add.19 = f32[64,256]{1,0:T(8,128)} add(f32[64,256]{1,0:T(8,128)S(1)} %add.18, f32[64,256]{1,0:T(8,128)S(1)} %collective-permute-done.6) | non-fusion elementwise | flops 16384 | bytes 196608 | tf_op jit(solution)/shard_map/add | solution.py:190
  (4 shorter events, 0.0 us)
Async XLA Ops:
  0.6 1.6 %collective-permute-start = (bf16[1,64,256]{2,1,0:T(8,128)(2,1)}, bf16[1,64,256]{2,1,0:T(8,128)(2,1)S(1)}, u32[]{:S(2)}, u32[]{:S(2)}) collective-permute-start(bf16[1,64,256]{2,1,0:T(8,128)(2,1)} %bitcast.8), channel_id=1, source_target_pairs={{0,1},{1,0},{2,3},{3,2},{4,5},{5,4},{6,7},{7,6},{8,9},{9,8},{10,11... | collective-permute-start | bytes 98312 | tf_op jit(solution)/shard_map/ppermute | solution.py:148
  2.2 6.1 %copy-start = (bf16[1,64,256]{2,1,0:T(8,128)(2,1)}, bf16[1,64,256]{2,1,0:T(8,128)(2,1)S(1)}, u32[]{:S(2)}) copy-start(bf16[1,64,256]{2,1,0:T(8,128)(2,1)S(1)} %collective-permute-done.refs_6_) | copy-start | bytes 98308
  3.0 5.3 %collective-permute-start.1 = (bf16[2,64,256]{2,1,0:T(8,128)(2,1)S(1)}, bf16[2,64,256]{2,1,0:T(8,128)(2,1)S(1)}, u32[]{:S(2)}, u32[]{:S(2)}) collective-permute-start(bf16[2,64,256]{2,1,0:T(8,128)(2,1)S(1)} %pad_maximum_fusion), channel_id=1, source_target_pairs={{0,2},{1,3},{2,0},{3,1},{4,6},{5,7},{6,4},{7,5},{8,10},{9,11},{10,... | collective-permute-start | bytes 196616 | tf_op jit(solution)/shard_map/ppermute | solution.py:148
  8.3 0.6 %copy-start.1 = (bf16[2,64,256]{2,1,0:T(8,128)(2,1)}, bf16[2,64,256]{2,1,0:T(8,128)(2,1)S(1)}, u32[]{:S(2)}) copy-start(bf16[2,64,256]{2,1,0:T(8,128)(2,1)S(1)} %collective-permute-done.1.refs_7_) | copy-start | bytes 196612
  17.2 1.6 %collective-permute-start.2 = (f32[2,64,256]{2,1,0:T(8,128)}, f32[2,64,256]{2,1,0:T(8,128)S(1)}, u32[]{:S(2)}, u32[]{:S(2)}) collective-permute-start(f32[2,64,256]{2,1,0:T(8,128)} %get-tuple-element.8), channel_id=1, source_target_pairs={{0,1},{1,0},{2,3},{3,2},{4,5},{5,4},{6,7},{7,6},{8,9},{9,8},{10,11... | collective-permute-start | bytes 393224 | tf_op jit(solution)/shard_map/ppermute | solution.py:148
  19.8 4.3 %collective-permute-start.3 = (f32[1,64,256]{2,1,0:T(8,128)S(1)}, f32[1,64,256]{2,1,0:T(8,128)S(1)}, u32[]{:S(2)}, u32[]{:S(2)}) collective-permute-start(f32[1,64,256]{2,1,0:T(8,128)S(1)} %slice.11), channel_id=1, source_target_pairs={{0,2},{1,3},{2,0},{3,1},{4,6},{5,7},{6,4},{7,5},{8,10},{9,11},{10,... | collective-permute-start | bytes 196616 | tf_op jit(solution)/shard_map/ppermute | solution.py:148
  24.1 4.3 %collective-permute-start.4 = (f32[64,256]{1,0:T(8,128)S(1)}, f32[64,256]{1,0:T(8,128)S(1)}, u32[]{:S(2)}, u32[]{:S(2)}) collective-permute-start(f32[64,256]{1,0:T(8,128)S(1)} %fusion), channel_id=1, source_target_pairs={{0,4},{4,0},{8,12},{12,8},{16,20},{20,16},{24,28},{28,24},{1,5},{5... | collective-permute-start | bytes 196616 | tf_op jit(solution)/shard_map/ppermute | solution.py:148
  28.5 4.3 %collective-permute-start.5 = (f32[64,256]{1,0:T(8,128)S(1)}, f32[64,256]{1,0:T(8,128)S(1)}, u32[]{:S(2)}, u32[]{:S(2)}) collective-permute-start(f32[64,256]{1,0:T(8,128)S(1)} %add.17), channel_id=1, source_target_pairs={{0,8},{4,12},{8,0},{12,4},{16,24},{20,28},{24,16},{28,20},{1,9},{5... | collective-permute-start | bytes 196616 | tf_op jit(solution)/shard_map/ppermute | solution.py:148
  32.8 5.9 %collective-permute-start.6 = (f32[64,256]{1,0:T(8,128)S(1)}, f32[64,256]{1,0:T(8,128)S(1)}, u32[]{:S(2)}, u32[]{:S(2)}) collective-permute-start(f32[64,256]{1,0:T(8,128)S(1)} %add.18), channel_id=1, source_target_pairs={{0,16},{4,20},{8,24},{12,28},{16,0},{20,4},{24,8},{28,12},{1,17},{... | collective-permute-start | bytes 196616 | tf_op jit(solution)/shard_map/ppermute | solution.py:148

commit v4 on v3

--- a/solution.py
+++ b/solution.py
@@ -34,26 +34,18 @@
 
 
 def main_kernel(parts, axis, chunk, step, *refs):
-    recorded_ref, delays_hbm, bias_hbm, load_hbm, counts_hbm = refs[:5]
-    held = parts.bit_length()
-    blocks = refs[5 : 5 + held]
-    keep, away, grad_load_hbm, grad_bias_hbm = refs[5 + held : 9 + held]
-    whole, delays_ref, bias_ref, counts_ref, shifted, load_ext, grad_shift, grad_load_ref, grad_bias_ref = refs[9 + held : 18 + held]
-    small_sems, counts_sems, out_sems = refs[18 + held :]
+    recorded_ref, delay_ref, load_ext, counts_hbm = refs[:4]
+    held = len(refs) - 17
+    blocks = refs[4 : 4 + held]
+    keep, away, grad_load_hbm, grad_bias_hbm = refs[4 + held : 8 + held]
+    whole, counts_ref, shifted, grad_shift, grad_load_ref, grad_bias_ref = refs[8 + held : 14 + held]
+    bias_sem, counts_sems, out_sems = refs[14 + held :]
     me = lax.axis_index(axis)
     lats, total = grad_shift.shape
     neurons = counts_ref.shape[0]
     width = total // parts
     pieces = neurons // chunk
     length = recorded_ref[0]
-
-    small = [
-        pltpu.make_async_copy(delays_hbm, delays_ref, small_sems.at[0]),
-        pltpu.make_async_copy(bias_hbm, bias_ref, small_sems.at[1]),
-        pltpu.make_async_copy(load_hbm, load_ext.at[pl.ds(0, lats)], small_sems.at[2]),
-    ]
-    for copy in small:
-        copy.start()
 
     def counts_copy(index):
         rows = pl.ds(pl.multiple_of(index * chunk, chunk), chunk)
@@ -69,30 +61,16 @@
     shifted[lats:, :] = jnp.where(row < 3, 1.0, 0.0).astype(BF16)
     grad_shift[...] = jnp.zeros_like(grad_shift)
 
-    small[0].wait()
-    diagonal = lax.broadcasted_iota(jnp.int32, (lats, lats), 0) == lax.broadcasted_iota(jnp.int32, (lats, lats), 1)
-    spread = jnp.broadcast_to(delays_ref[...].astype(F32), (lats, lats))
-    column = jnp.sum(jnp.where(diagonal, spread, 0.0), axis=1, keepdims=True)
-    delay = jnp.broadcast_to(column, (lats, LANES)).astype(jnp.int32)
     k = 0
     for ref in blocks:
         for j in range(ref.shape[0]):
             start = pl.multiple_of((me ^ k) * width, width)
             whole[:, pl.ds(start, width)] = ref[j]
             k += 1
+    delay = delay_ref[...]
     tiles = [whole[:, j * LANES : (j + 1) * LANES].astype(F32) for j in range(total // LANES)]
     for j, tile in enumerate(shift_tiles(tiles, delay, True)):
         shifted[0:lats, j * LANES : (j + 1) * LANES] = tile.astype(BF16)
-
-    small[1].wait()
-    bias = bias_ref[...]
-    high = bias.astype(BF16).astype(F32)
-    middle = (bias - high).astype(BF16).astype(F32)
-    low = bias - high - middle
-    row = lax.broadcasted_iota(jnp.int32, (EXTRA, neurons), 0)
-    below = jnp.where(row == 0, high, jnp.where(row == 1, middle, jnp.where(row == 2, low, 0.0)))
-    load_ext[lats:, :] = below.astype(BF16)
-    small[2].wait()
 
     bins = lax.broadcasted_iota(jnp.int32, (1, total), 1)
 
@@ -121,7 +99,7 @@
         return carry
 
     lax.fori_loop(0, pieces, visit, 0, unroll=total <= 1024)
-    bias_copy = pltpu.make_async_copy(grad_bias_ref, grad_bias_hbm, small_sems.at[0])
+    bias_copy = pltpu.make_async_copy(grad_bias_ref, grad_bias_hbm, bias_sem)
     bias_copy.start()
 
     tiles = [grad_shift[:, j * LANES : (j + 1) * LANES] for j in range(total // LANES)]
@@ -147,10 +125,19 @@
     def swap(value, axis, count, bit):
         return lax.ppermute(value, axis, [(i, i ^ bit) for i in range(count)])
 
-    blocks = [latents[None]]
+    high = lax.reduce_precision(bias, 8, 7)
+    middle = lax.reduce_precision(bias - high, 8, 7)
+    low = bias - high - middle
+    below = jnp.concatenate([high, middle, low], axis=0).astype(BF16)
+    load_ext = jnp.pad(jnp.concatenate([loadings[0], below], axis=0), ((0, EXTRA - 3), (0, 0)))
+    delay = jnp.broadcast_to(delays.reshape(lats, 1), (lats, LANES))
+
+    near = latents[None]
+    far = near[:0]
     bit = 1
     while bit < neuron_count:
-        blocks.append(swap(jnp.concatenate(blocks, axis=0), "neuron", neuron_count, bit))
+        near = jnp.concatenate([near, far], axis=0)
+        far = swap(near, "neuron", neuron_count, bit)
         bit *= 2
     keep, away, grad_load, grad_bias = pl.pallas_call(
         functools.partial(main_kernel, neuron_count, "neuron", chunk, 512),
@@ -160,24 +147,21 @@
             jax.ShapeDtypeStruct((lats, neurons), F32),
             jax.ShapeDtypeStruct((1, neurons), F32),
         ],
-        in_specs=[smem, hbm, hbm, hbm, hbm] + [vmem] * len(blocks),
+        in_specs=[smem, vmem, vmem, hbm, vmem, vmem],
         out_specs=[vmem, vmem, hbm, hbm],
         scratch_shapes=[
             pltpu.VMEM((lats, total), BF16),
-            pltpu.VMEM((1, lats), jnp.int32),
-            pltpu.VMEM((1, neurons), F32),
             pltpu.VMEM((neurons, total), BF16),
             pltpu.VMEM((lats + EXTRA, total), BF16),
-            pltpu.VMEM((lats + EXTRA, neurons), BF16),
             pltpu.VMEM((lats, total), F32),
             pltpu.VMEM((lats, neurons), F32),
             pltpu.VMEM((1, neurons), F32),
-            pltpu.SemaphoreType.DMA((3,)),
+            pltpu.SemaphoreType.DMA,
             pltpu.SemaphoreType.DMA((neurons // chunk,)),
             pltpu.SemaphoreType.DMA((neurons // chunk,)),
         ],
-        compiler_params=pltpu.CompilerParams(vmem_limit_bytes=58 * 1024 * 1024),
-    )(recorded, delays, bias, loadings[0], counts[0], *blocks)
+        compiler_params=pltpu.CompilerParams(vmem_limit_bytes=52 * 1024 * 1024),
+    )(recorded, delay, load_ext, counts[0], near, far)
 
     value = keep + swap(away, "neuron", neuron_count, 1)
     bit = 2

time: 39.7 us -> 36.5 us (0.919)
  Pallas kernels: 8.3 us -> 6.18 us
  waiting for transfers between devices: 13.9 us -> 12 us
  other arithmetic: 2.37 us -> 3.1 us
    pallas_call x1, Pallas kernels: 8.3 us -> 6.18 us  [per_device(): pl.pallas_call(functools.partial(main_kernel, neuron_count, 'neuron', chu...]
    ppermute x7, waiting for transfers between devices: 13.9 us -> 12 us  [swap(): return lax.ppermute(value, axis, [(i, i ^ bit) for i in range(count)])]
    concatenate x1 -> x2, other arithmetic: 0.78 us -> 1.71 us  [the longest x1 0.95 us: per_device(): jnp.concatenate([loadings[0], below], axis=0)]
    add x1, other arithmetic: 0.92 us -> 0.02 us  [per_device(): value = keep + swap(away, 'neuron', neuron_count, 1)]
    broadcast_in_dim x0 -> x1, local copies, waits for them, and re-layouts: none -> 0.73 us  [per_device(): delay = jnp.broadcast_to(delays.reshape(lats, 1), (lats, LANES))]
    another operation x0 -> x1, other arithmetic: none -> 0.7 us
    unnamed x4 -> x0, local copies, waits for them, and re-layouts: 0.63 us -> none
  transfers between devices with their start and end apart: 7 -> 7, of which waited for: 7 -> 7; matrix products, arithmetic and copies ran while one was open for 0% -> 5% of each run, Pallas kernels for 0% -> 0%
where the time goes in v4:
time: 36.5 us; the launch traced here: 36.2 us
  starting transfers between devices  12.9 us (35%)
  waiting for transfers between devices  12 us (33%)
  Pallas kernels  6.18 us (17%)
  other arithmetic  3.1 us (8%)
  between operations  1.33 us (4%)
  local copies, waits for them, and re-layouts  0.73 us (2%)
    ppermute x7, starting transfers between devices, swap(): return lax.ppermute(value, axis, [(i, i ^ bit) for i in range(count)])  12.9 us
    ppermute x7, waiting for transfers between devices, swap(): return lax.ppermute(value, axis, [(i, i ^ bit) for i in range(count)])  12 us
    pallas_call x1, Pallas kernels, per_device(): pl.pallas_call(functools.partial(main_kernel, neuron_count, 'neuron', chu...  6.18 us
    concatenate x1, other arithmetic, per_device(): jnp.concatenate([loadings[0], below], axis=0)  0.95 us
    concatenate x1, other arithmetic, per_device(): near = jnp.concatenate([near, far], axis=0)  0.76 us
  transfers between devices with their start and end apart: 7, of which 7 were waited for; matrix products, arithmetic and copies ran while one was open for 5% of the time, Pallas kernels for 0%

profile of v4, /device:TPU:0, one launch (start us, length us, event | category | flops | bytes accessed | tf_op | source)
XLA Modules:
  0.0 36.2 jit_solution(9408216874341037181)
XLA Ops:
  0.6 0.5 %collective-permute-start = (bf16[1,64,256]{2,1,0:T(8,128)(2,1)}, bf16[1,64,256]{2,1,0:T(8,128)(2,1)S(1)}, u32[]{:S(2)}, u32[]{:S(2)}) collective-permute-start(bf16[1,64,256]{2,1,0:T(8,128)(2,1)} %bitcast.9), channel_id=1, source_target_pairs={{0,1},{1,0},{2,3},{3,2},{4,5},{5,4},{6,7},{7,6},{8,9},{9,8},{10,11... | collective-permute-start | bytes 98312 | tf_op jit(solution)/shard_map/ppermute | solution.py:126
  1.1 0.7 %reduce-precision_convert_fusion.1 = (bf16[1,1280]{1,0:T(2,128)(2,1)S(1)}, bf16[1,1280]{1,0:T(2,128)(2,1)S(1)}, bf16[1,1280]{1,0:T(2,128)(2,1)S(1)}) fusion(f32[1,1280]{1,0:T(1,128)} %param.9), kind=kLoop, calls=%fused_computation.14 | loop fusion | flops 8960 | bytes 12800 | tf_op jit(solution)/shard_map/convert
  1.9 0.4 %collective-permute-done = bf16[1,64,256]{2,1,0:T(8,128)(2,1)S(1)} collective-permute-done((bf16[1,64,256]{2,1,0:T(8,128)(2,1)}, bf16[1,64,256]{2,1,0:T(8,128)(2,1)S(1)}, u32[]{:S(2)}, u32[]{:S(2)}) %collective-permute-start) | collective-permute-done | bytes 32800 | tf_op jit(solution)/shard_map/ppermute | solution.py:126
  2.2 0.8 %pad_maximum_fusion.refs_4_ = bf16[2,64,256]{2,1,0:T(8,128)(2,1)S(1)} fusion(bf16[1,64,256]{2,1,0:T(8,128)(2,1)S(1)} %collective-permute-done, bf16[1,64,256]{2,1,0:T(8,128)(2,1)} %bitcast.10), kind=kLoop, calls=%fused_computation.10 | loop fusion | flops 32768 | bytes 131072 | tf_op jit(solution)/shard_map/concatenate | solution.py:139
  3.0 2.9 %collective-permute-start.1 = (bf16[2,64,256]{2,1,0:T(8,128)(2,1)S(1)}, bf16[2,64,256]{2,1,0:T(8,128)(2,1)S(1)}, u32[]{:S(2)}, u32[]{:S(2)}) collective-permute-start(bf16[2,64,256]{2,1,0:T(8,128)(2,1)S(1)} %pad_maximum_fusion.refs_4_), channel_id=1, source_target_pairs={{0,2},{1,3},{2,0},{3,1},{4,6},{5,7},{6,4},{7,5},{8,10},{9,11},{10,... | collective-permute-start | bytes 196616 | tf_op jit(solution)/shard_map/ppermute | solution.py:126
  5.8 0.9 %fusion.6.refs_2_ = bf16[80,1280]{1,0:T(8,128)(2,1)S(1)} fusion(bf16[1,1280]{1,0:T(2,128)(2,1)S(1)} %get-tuple-element.12, bf16[1,1280]{1,0:T(2,128)(2,1)S(1)} %get-tuple-element.13, bf16[1,1280]{1,0:T(2,128)(2,1)S(1)} %get-tuple-element.11, bf16[64,1280]{1,0:T(8,128)(2,1)} %bitcast.8), kind=kLoop, calls=%fused_computation.7 | loop fusion | flops 1331200 | bytes 376320 | tf_op jit(solution)/shard_map/concatenate | solution.py:132
  7.4 0.8 %collective-permute-done.1.refs_5_ = bf16[2,64,256]{2,1,0:T(8,128)(2,1)S(1)} collective-permute-done((bf16[2,64,256]{2,1,0:T(8,128)(2,1)S(1)}, bf16[2,64,256]{2,1,0:T(8,128)(2,1)S(1)}, u32[]{:S(2)}, u32[]{:S(2)}) %collective-permute-start.1) | collective-permute-done | bytes 65568 | tf_op jit(solution)/shard_map/ppermute | solution.py:126
  8.3 0.7 %broadcast_in_dim.14.refs_1_ = s32[64,128]{1,0:T(8,128)S(1)} broadcast(s32[64]{0:T(128)} %bitcast.11), dimensions={0} | broadcast | bytes 33024 | tf_op jit(solution)/shard_map/broadcast_in_dim | solution.py:133
  9.0 6.2 %shard_map.85 = (f32[2,64,256]{2,1,0:T(8,128)S(1)}, f32[2,64,256]{2,1,0:T(8,128)S(1)}, f32[64,1280]{1,0:T(8,128)}, f32[1,1280]{1,0:T(1,128)}) custom-call(s32[1]{0:T(128)S(6)} %copy.9.refs_0_, s32[64,128]{1,0:T(8,128)S(1)} %broadcast_in_dim.14.refs_1_, bf16[80,1280]{1,0:T(8,128)(2,1)S(1)} %fusion.6.refs_2_, bf16[1280,1024]{1,0:T(8,128)(2,1)} %bitcast.7, ...), custom_call_target="tpu_custom_call" | custom-call | tf_op jit(solution)/shard_map/pallas_call | solution.py:142
  15.2 0.1 collective-permute-start.2
  15.3 1.3 %collective-permute-done.2 = f32[2,64,256]{2,1,0:T(8,128)S(1)} collective-permute-done((f32[2,64,256]{2,1,0:T(8,128)S(1)}, f32[2,64,256]{2,1,0:T(8,128)S(1)}, u32[]{:S(2)}, u32[]{:S(2)}) %collective-permute-start.2) | collective-permute-done | bytes 131104 | tf_op jit(solution)/shard_map/ppermute | solution.py:126
  16.6 1.9 %collective-permute-start.3 = (f32[1,64,256]{2,1,0:T(8,128)S(1)}, f32[1,64,256]{2,1,0:T(8,128)S(1)}, u32[]{:S(2)}, u32[]{:S(2)}) collective-permute-start(f32[1,64,256]{2,1,0:T(8,128)S(1)} %slice.11), channel_id=1, source_target_pairs={{0,2},{1,3},{2,0},{3,1},{4,6},{5,7},{6,4},{7,5},{8,10},{9,11},{10,... | collective-permute-start | bytes 196616 | tf_op jit(solution)/shard_map/ppermute | solution.py:126
  18.5 2.4 %collective-permute-done.3 = f32[1,64,256]{2,1,0:T(8,128)S(1)} collective-permute-done((f32[1,64,256]{2,1,0:T(8,128)S(1)}, f32[1,64,256]{2,1,0:T(8,128)S(1)}, u32[]{:S(2)}, u32[]{:S(2)}) %collective-permute-start.3) | collective-permute-done | bytes 65568 | tf_op jit(solution)/shard_map/ppermute | solution.py:126
  21.0 1.9 %collective-permute-start.4 = (f32[64,256]{1,0:T(8,128)S(1)}, f32[64,256]{1,0:T(8,128)S(1)}, u32[]{:S(2)}, u32[]{:S(2)}) collective-permute-start(f32[64,256]{1,0:T(8,128)S(1)} %fusion.7), channel_id=1, source_target_pairs={{0,4},{4,0},{8,12},{12,8},{16,20},{20,16},{24,28},{28,24},{1,5},{5... | collective-permute-start | bytes 196616 | tf_op jit(solution)/shard_map/ppermute | solution.py:126
  22.9 2.4 %collective-permute-done.4 = f32[64,256]{1,0:T(8,128)S(1)} collective-permute-done((f32[64,256]{1,0:T(8,128)S(1)}, f32[64,256]{1,0:T(8,128)S(1)}, u32[]{:S(2)}, u32[]{:S(2)}) %collective-permute-start.4) | collective-permute-done | bytes 65568 | tf_op jit(solution)/shard_map/ppermute | solution.py:126
  25.3 2.0 %collective-permute-start.5 = (f32[64,256]{1,0:T(8,128)S(1)}, f32[64,256]{1,0:T(8,128)S(1)}, u32[]{:S(2)}, u32[]{:S(2)}) collective-permute-start(f32[64,256]{1,0:T(8,128)S(1)} %add.19), channel_id=1, source_target_pairs={{0,8},{4,12},{8,0},{12,4},{16,24},{20,28},{24,16},{28,20},{1,9},{5... | collective-permute-start | bytes 196616 | tf_op jit(solution)/shard_map/ppermute | solution.py:126
  27.3 2.4 %collective-permute-done.5 = f32[64,256]{1,0:T(8,128)S(1)} collective-permute-done((f32[64,256]{1,0:T(8,128)S(1)}, f32[64,256]{1,0:T(8,128)S(1)}, u32[]{:S(2)}, u32[]{:S(2)}) %collective-permute-start.5) | collective-permute-done | bytes 65568 | tf_op jit(solution)/shard_map/ppermute | solution.py:126
  29.7 3.6 %collective-permute-start.6 = (f32[64,256]{1,0:T(8,128)S(1)}, f32[64,256]{1,0:T(8,128)S(1)}, u32[]{:S(2)}, u32[]{:S(2)}) collective-permute-start(f32[64,256]{1,0:T(8,128)S(1)} %add.20), channel_id=1, source_target_pairs={{0,16},{4,20},{8,24},{12,28},{16,0},{20,4},{24,8},{28,12},{1,17},{... | collective-permute-start | bytes 196616 | tf_op jit(solution)/shard_map/ppermute | solution.py:126
  33.3 2.3 %collective-permute-done.6 = f32[64,256]{1,0:T(8,128)S(1)} collective-permute-done((f32[64,256]{1,0:T(8,128)S(1)}, f32[64,256]{1,0:T(8,128)S(1)}, u32[]{:S(2)}, u32[]{:S(2)}) %collective-permute-start.6) | collective-permute-done | bytes 65568 | tf_op jit(solution)/shard_map/ppermute | solution.py:126
  35.6 0.6 %add.21 = f32[64,256]{1,0:T(8,128)} add(f32[64,256]{1,0:T(8,128)S(1)} %add.20, f32[64,256]{1,0:T(8,128)S(1)} %collective-permute-done.6) | non-fusion elementwise | flops 16384 | bytes 196608 | tf_op jit(solution)/shard_map/add | solution.py:174
  (5 shorter events, 0.1 us)
Async XLA Ops:
  0.6 1.6 %collective-permute-start = (bf16[1,64,256]{2,1,0:T(8,128)(2,1)}, bf16[1,64,256]{2,1,0:T(8,128)(2,1)S(1)}, u32[]{:S(2)}, u32[]{:S(2)}) collective-permute-start(bf16[1,64,256]{2,1,0:T(8,128)(2,1)} %bitcast.9), channel_id=1, source_target_pairs={{0,1},{1,0},{2,3},{3,2},{4,5},{5,4},{6,7},{7,6},{8,9},{9,8},{10,11... | collective-permute-start | bytes 98312 | tf_op jit(solution)/shard_map/ppermute | solution.py:126
  3.0 5.3 %collective-permute-start.1 = (bf16[2,64,256]{2,1,0:T(8,128)(2,1)S(1)}, bf16[2,64,256]{2,1,0:T(8,128)(2,1)S(1)}, u32[]{:S(2)}, u32[]{:S(2)}) collective-permute-start(bf16[2,64,256]{2,1,0:T(8,128)(2,1)S(1)} %pad_maximum_fusion.refs_4_), channel_id=1, source_target_pairs={{0,2},{1,3},{2,0},{3,1},{4,6},{5,7},{6,4},{7,5},{8,10},{9,11},{10,... | collective-permute-start | bytes 196616 | tf_op jit(solution)/shard_map/ppermute | solution.py:126
  15.2 1.4 %collective-permute-start.2 = (f32[2,64,256]{2,1,0:T(8,128)S(1)}, f32[2,64,256]{2,1,0:T(8,128)S(1)}, u32[]{:S(2)}, u32[]{:S(2)}) collective-permute-start(f32[2,64,256]{2,1,0:T(8,128)S(1)} %get-tuple-element.8), channel_id=1, source_target_pairs={{0,1},{1,0},{2,3},{3,2},{4,5},{5,4},{6,7},{7,6},{8,9},{9,8},{10,11... | collective-permute-start | bytes 393224 | tf_op jit(solution)/shard_map/ppermute | solution.py:126
  16.6 4.3 %collective-permute-start.3 = (f32[1,64,256]{2,1,0:T(8,128)S(1)}, f32[1,64,256]{2,1,0:T(8,128)S(1)}, u32[]{:S(2)}, u32[]{:S(2)}) collective-permute-start(f32[1,64,256]{2,1,0:T(8,128)S(1)} %slice.11), channel_id=1, source_target_pairs={{0,2},{1,3},{2,0},{3,1},{4,6},{5,7},{6,4},{7,5},{8,10},{9,11},{10,... | collective-permute-start | bytes 196616 | tf_op jit(solution)/shard_map/ppermute | solution.py:126
  21.0 4.3 %collective-permute-start.4 = (f32[64,256]{1,0:T(8,128)S(1)}, f32[64,256]{1,0:T(8,128)S(1)}, u32[]{:S(2)}, u32[]{:S(2)}) collective-permute-start(f32[64,256]{1,0:T(8,128)S(1)} %fusion.7), channel_id=1, source_target_pairs={{0,4},{4,0},{8,12},{12,8},{16,20},{20,16},{24,28},{28,24},{1,5},{5... | collective-permute-start | bytes 196616 | tf_op jit(solution)/shard_map/ppermute | solution.py:126
  25.3 4.3 %collective-permute-start.5 = (f32[64,256]{1,0:T(8,128)S(1)}, f32[64,256]{1,0:T(8,128)S(1)}, u32[]{:S(2)}, u32[]{:S(2)}) collective-permute-start(f32[64,256]{1,0:T(8,128)S(1)} %add.19), channel_id=1, source_target_pairs={{0,8},{4,12},{8,0},{12,4},{16,24},{20,28},{24,16},{28,20},{1,9},{5... | collective-permute-start | bytes 196616 | tf_op jit(solution)/shard_map/ppermute | solution.py:126
  29.7 5.9 %collective-permute-start.6 = (f32[64,256]{1,0:T(8,128)S(1)}, f32[64,256]{1,0:T(8,128)S(1)}, u32[]{:S(2)}, u32[]{:S(2)}) collective-permute-start(f32[64,256]{1,0:T(8,128)S(1)} %add.20), channel_id=1, source_target_pairs={{0,16},{4,20},{8,24},{12,28},{16,0},{20,4},{24,8},{28,12},{1,17},{... | collective-permute-start | bytes 196616 | tf_op jit(solution)/shard_map/ppermute | solution.py:126

commit v5 on v4

--- a/solution.py
+++ b/solution.py
@@ -169,10 +169,8 @@
         value = value[0::2] + swap(value[1::2], "neuron", neuron_count, bit)
         bit *= 2
     value = value[0]
-    bit = 1
-    while bit < region_count:
-        value = value + swap(value, "region", region_count, bit)
-        bit *= 2
+    everyone = lax.all_gather(value.astype(BF16), "region", axis=0)
+    value = jnp.sum(everyone.astype(F32), axis=0)
     return (value, grad_load[None], grad_bias)
 
 

time: 36.5 us -> 53.3 us (1.46)
  blocking collectives: 0 us -> 31.4 us
  starting transfers between devices: 12.9 us -> 5.36 us
  waiting for transfers between devices: 12 us -> 4.93 us
    all_gather x0 -> x1, blocking collectives: none -> 31.4 us  [per_device(): everyone = lax.all_gather(value.astype(BF16), 'region', axis=0)]
    ppermute x7 -> x4, starting transfers between devices: 12.9 us -> 5.36 us  [swap(): return lax.ppermute(value, axis, [(i, i ^ bit) for i in range(count)])]
    ppermute x7 -> x4, waiting for transfers between devices: 12 us -> 4.93 us  [swap(): return lax.ppermute(value, axis, [(i, i ^ bit) for i in range(count)])]
    reduce_sum x0 -> x1, other arithmetic: none -> 0.67 us  [per_device(): value = jnp.sum(everyone.astype(F32), axis=0)]
    add x3 -> x0, other arithmetic: 0.66 us -> none  [per_device(): value = value + swap(value, 'region', region_count, bit)]
  transfers between devices with their start and end apart: 7 -> 4, of which waited for: 7 -> 4; matrix products, arithmetic and copies ran while one was open for 5% -> 3% of each run, Pallas kernels for 0% -> 0%
where the time goes in v5:
time: 53.3 us; the launch traced here: 53 us
  blocking collectives  31.4 us (59%)
  Pallas kernels  6.18 us (12%)
  starting transfers between devices  5.36 us (10%)
  waiting for transfers between devices  4.93 us (9%)
  other arithmetic  3.11 us (6%)
  between operations  1.32 us (2%)
  local copies, waits for them, and re-layouts  0.73 us (1%)
    all_gather x1, blocking collectives, per_device(): everyone = lax.all_gather(value.astype(BF16), 'region', axis=0)  31.4 us
    pallas_call x1, Pallas kernels, per_device(): pl.pallas_call(functools.partial(main_kernel, neuron_count, 'neuron', chu...  6.18 us
    ppermute x4, starting transfers between devices, swap(): return lax.ppermute(value, axis, [(i, i ^ bit) for i in range(count)])  5.36 us
    ppermute x4, waiting for transfers between devices, swap(): return lax.ppermute(value, axis, [(i, i ^ bit) for i in range(count)])  4.93 us
  transfers between devices with their start and end apart: 4, of which 4 were waited for; matrix products, arithmetic and copies ran while one was open for 3% of the time, Pallas kernels for 0%

profile of v5, /device:TPU:0, one launch (start us, length us, event | category | flops | bytes accessed | tf_op | source)
XLA Modules:
  0.0 53.0 jit_solution(12902665519842760395)
XLA Ops:
  0.6 0.5 collective-permute-start
  1.1 0.7 %reduce-precision_convert_fusion.1 = (bf16[1,1280]{1,0:T(2,128)(2,1)S(1)}, bf16[1,1280]{1,0:T(2,128)(2,1)S(1)}, bf16[1,1280]{1,0:T(2,128)(2,1)S(1)}) fusion(f32[1,1280]{1,0:T(1,128)} %param.9), kind=kLoop, calls=%fused_computation.15 | loop fusion | flops 8960 | bytes 12800 | tf_op jit(solution)/shard_map/convert
  1.9 0.4 collective-permute-done
  2.2 0.8 %pad_maximum_fusion.refs_4_ = bf16[2,64,256]{2,1,0:T(8,128)(2,1)S(1)} fusion(bf16[1,64,256]{2,1,0:T(8,128)(2,1)S(1)} %collective-permute-done, bf16[1,64,256]{2,1,0:T(8,128)(2,1)} %bitcast.8), kind=kLoop, calls=%fused_computation.11 | loop fusion | flops 32768 | bytes 131072 | tf_op jit(solution)/shard_map/concatenate | solution.py:139
  3.0 2.9 %collective-permute-start.1 = (bf16[2,64,256]{2,1,0:T(8,128)(2,1)S(1)}, bf16[2,64,256]{2,1,0:T(8,128)(2,1)S(1)}, u32[]{:S(2)}, u32[]{:S(2)}) collective-permute-start(bf16[2,64,256]{2,1,0:T(8,128)(2,1)S(1)} %pad_maximum_fusion.refs_4_), channel_id=1, source_target_pairs={{0,2},{1,3},{2,0},{3,1},{4,6},{5,7},{6,4},{7,5},{8,10},{9,11},{10,... | collective-permute-start | bytes 196616 | tf_op jit(solution)/shard_map/ppermute | solution.py:126
  5.8 0.9 %fusion.6.refs_2_ = bf16[80,1280]{1,0:T(8,128)(2,1)S(1)} fusion(bf16[1,1280]{1,0:T(2,128)(2,1)S(1)} %get-tuple-element.12, bf16[1,1280]{1,0:T(2,128)(2,1)S(1)} %get-tuple-element.13, bf16[1,1280]{1,0:T(2,128)(2,1)S(1)} %get-tuple-element.11, bf16[64,1280]{1,0:T(8,128)(2,1)} %bitcast.6), kind=kLoop, calls=%fused_computation.8 | loop fusion | flops 1331200 | bytes 376320 | tf_op jit(solution)/shard_map/concatenate | solution.py:132
  7.4 0.8 %collective-permute-done.1.refs_5_ = bf16[2,64,256]{2,1,0:T(8,128)(2,1)S(1)} collective-permute-done((bf16[2,64,256]{2,1,0:T(8,128)(2,1)S(1)}, bf16[2,64,256]{2,1,0:T(8,128)(2,1)S(1)}, u32[]{:S(2)}, u32[]{:S(2)}) %collective-permute-start.1) | collective-permute-done | bytes 65568 | tf_op jit(solution)/shard_map/ppermute | solution.py:126
  8.3 0.7 %broadcast_in_dim.14.refs_1_ = s32[64,128]{1,0:T(8,128)S(1)} broadcast(s32[64]{0:T(128)} %bitcast.9), dimensions={0} | broadcast | bytes 33024 | tf_op jit(solution)/shard_map/broadcast_in_dim | solution.py:133
  9.0 6.2 %shard_map.85 = (f32[2,64,256]{2,1,0:T(8,128)S(1)}, f32[2,64,256]{2,1,0:T(8,128)S(1)}, f32[64,1280]{1,0:T(8,128)}, f32[1,1280]{1,0:T(1,128)}) custom-call(s32[1]{0:T(128)S(6)} %copy.9.refs_0_, s32[64,128]{1,0:T(8,128)S(1)} %broadcast_in_dim.14.refs_1_, bf16[80,1280]{1,0:T(8,128)(2,1)S(1)} %fusion.6.refs_2_, bf16[1280,1024]{1,0:T(8,128)(2,1)} %bitcast.5, ...), custom_call_target="tpu_custom_call" | custom-call | tf_op jit(solution)/shard_map/pallas_call | solution.py:142
  15.2 0.1 collective-permute-start.2
  15.3 1.3 %collective-permute-done.2 = f32[2,64,256]{2,1,0:T(8,128)S(1)} collective-permute-done((f32[2,64,256]{2,1,0:T(8,128)S(1)}, f32[2,64,256]{2,1,0:T(8,128)S(1)}, u32[]{:S(2)}, u32[]{:S(2)}) %collective-permute-start.2) | collective-permute-done | bytes 131104 | tf_op jit(solution)/shard_map/ppermute | solution.py:126
  16.6 1.9 %collective-permute-start.3 = (f32[1,64,256]{2,1,0:T(8,128)S(1)}, f32[1,64,256]{2,1,0:T(8,128)S(1)}, u32[]{:S(2)}, u32[]{:S(2)}) collective-permute-start(f32[1,64,256]{2,1,0:T(8,128)S(1)} %slice.11), channel_id=1, source_target_pairs={{0,2},{1,3},{2,0},{3,1},{4,6},{5,7},{6,4},{7,5},{8,10},{9,11},{10,... | collective-permute-start | bytes 196616 | tf_op jit(solution)/shard_map/ppermute | solution.py:126
  18.5 2.4 %collective-permute-done.3 = f32[1,64,256]{2,1,0:T(8,128)S(1)} collective-permute-done((f32[1,64,256]{2,1,0:T(8,128)S(1)}, f32[1,64,256]{2,1,0:T(8,128)S(1)}, u32[]{:S(2)}, u32[]{:S(2)}) %collective-permute-start.3) | collective-permute-done | bytes 65568 | tf_op jit(solution)/shard_map/ppermute | solution.py:126
  21.0 31.4 %all_gather.4 = bf16[8,64,256]{2,1,0:T(8,128)(2,1)S(1)} all-gather(bf16[1,64,256]{2,1,0:T(8,128)(2,1)S(1)} %fusion.7), channel_id=1, replica_groups=mesh['region'=8,'neuron'=4] {'region'}, dimensions={0}, use_global_device_ids=true | all-gather | bytes 294912 | tf_op jit(solution)/shard_map/all_gather | solution.py:172
  52.4 0.7 %convert_reduce_fusion = f32[64,256]{1,0:T(8,128)} fusion(bf16[8,64,256]{2,1,0:T(8,128)(2,1)S(1)} %all_gather.4), kind=kLoop, calls=%fused_computation | loop fusion | flops 245760 | bytes 327680 | tf_op jit(solution)/shard_map/reduce_sum | solution.py:173
  (3 shorter events, 0.0 us)
Async XLA Ops:
  0.6 1.6 %collective-permute-start = (bf16[1,64,256]{2,1,0:T(8,128)(2,1)}, bf16[1,64,256]{2,1,0:T(8,128)(2,1)S(1)}, u32[]{:S(2)}, u32[]{:S(2)}) collective-permute-start(bf16[1,64,256]{2,1,0:T(8,128)(2,1)} %bitcast.7), channel_id=1, source_target_pairs={{0,1},{1,0},{2,3},{3,2},{4,5},{5,4},{6,7},{7,6},{8,9},{9,8},{10,11... | collective-permute-start | bytes 98312 | tf_op jit(solution)/shard_map/ppermute | solution.py:126
  3.0 5.3 %collective-permute-start.1 = (bf16[2,64,256]{2,1,0:T(8,128)(2,1)S(1)}, bf16[2,64,256]{2,1,0:T(8,128)(2,1)S(1)}, u32[]{:S(2)}, u32[]{:S(2)}) collective-permute-start(bf16[2,64,256]{2,1,0:T(8,128)(2,1)S(1)} %pad_maximum_fusion.refs_4_), channel_id=1, source_target_pairs={{0,2},{1,3},{2,0},{3,1},{4,6},{5,7},{6,4},{7,5},{8,10},{9,11},{10,... | collective-permute-start | bytes 196616 | tf_op jit(solution)/shard_map/ppermute | solution.py:126
  15.2 1.4 %collective-permute-start.2 = (f32[2,64,256]{2,1,0:T(8,128)S(1)}, f32[2,64,256]{2,1,0:T(8,128)S(1)}, u32[]{:S(2)}, u32[]{:S(2)}) collective-permute-start(f32[2,64,256]{2,1,0:T(8,128)S(1)} %get-tuple-element.8), channel_id=1, source_target_pairs={{0,1},{1,0},{2,3},{3,2},{4,5},{5,4},{6,7},{7,6},{8,9},{9,8},{10,11... | collective-permute-start | bytes 393224 | tf_op jit(solution)/shard_map/ppermute | solution.py:126
  16.6 4.3 %collective-permute-start.3 = (f32[1,64,256]{2,1,0:T(8,128)S(1)}, f32[1,64,256]{2,1,0:T(8,128)S(1)}, u32[]{:S(2)}, u32[]{:S(2)}) collective-permute-start(f32[1,64,256]{2,1,0:T(8,128)S(1)} %slice.11), channel_id=1, source_target_pairs={{0,2},{1,3},{2,0},{3,1},{4,6},{5,7},{6,4},{7,5},{8,10},{9,11},{10,... | collective-permute-start | bytes 196616 | tf_op jit(solution)/shard_map/ppermute | solution.py:126

commit v6 on v5

--- a/solution.py
+++ b/solution.py
@@ -34,19 +34,15 @@
 
 
 def main_kernel(parts, axis, chunk, step, *refs):
-    recorded_ref, delay_ref, load_ext, counts_hbm = refs[:4]
-    held = len(refs) - 17
-    blocks = refs[4 : 4 + held]
-    keep, away, grad_load_hbm, grad_bias_hbm = refs[4 + held : 8 + held]
-    whole, counts_ref, shifted, grad_shift, grad_load_ref, grad_bias_ref = refs[8 + held : 14 + held]
-    bias_sem, counts_sems, out_sems = refs[14 + held :]
+    meta_ref, load_ext, counts_hbm, near, far = refs[:5]
+    keep, away, grad_load_hbm, grad_bias_hbm = refs[5:9]
+    whole, counts_ref, shifted, grad_shift, grad_load_ref, grad_bias_ref = refs[9:15]
+    bias_sem, counts_sems, out_sems = refs[15:]
     me = lax.axis_index(axis)
     lats, total = grad_shift.shape
     neurons = counts_ref.shape[0]
     width = total // parts
     pieces = neurons // chunk
-    length = recorded_ref[0]
-
     def counts_copy(index):
         rows = pl.ds(pl.multiple_of(index * chunk, chunk), chunk)
         return pltpu.make_async_copy(counts_hbm.at[rows], counts_ref.at[rows], counts_sems.at[index])
@@ -62,12 +58,16 @@
     grad_shift[...] = jnp.zeros_like(grad_shift)
 
     k = 0
-    for ref in blocks:
+    for ref in (near, far):
         for j in range(ref.shape[0]):
             start = pl.multiple_of((me ^ k) * width, width)
             whole[:, pl.ds(start, width)] = ref[j]
             k += 1
-    delay = delay_ref[...]
+    diagonal = lax.broadcasted_iota(jnp.int32, (lats, LANES), 0) == lax.broadcasted_iota(jnp.int32, (lats, LANES), 1)
+    spread = jnp.broadcast_to(meta_ref[...].astype(F32), (lats, LANES))
+    column = jnp.sum(jnp.where(diagonal, spread, 0.0), axis=1, keepdims=True)
+    delay = jnp.broadcast_to(column, (lats, LANES)).astype(jnp.int32)
+    length = meta_ref[:, lats : lats + 1]
     tiles = [whole[:, j * LANES : (j + 1) * LANES].astype(F32) for j in range(total // LANES)]
     for j, tile in enumerate(shift_tiles(tiles, delay, True)):
         shifted[0:lats, j * LANES : (j + 1) * LANES] = tile.astype(BF16)
@@ -119,26 +119,28 @@
     lats, width = latents.shape
     chunk = 256
     vmem = pl.BlockSpec(memory_space=pltpu.VMEM)
-    smem = pl.BlockSpec(memory_space=pltpu.SMEM)
     hbm = pl.BlockSpec(memory_space=pltpu.HBM)
 
     def swap(value, axis, count, bit):
         return lax.ppermute(value, axis, [(i, i ^ bit) for i in range(count)])
+
+    near = latents[None]
+    far = near[:0]
+    bit = 1
+    while bit < neuron_count:
+        near = jnp.concatenate([near, far], axis=0)
+        if bit > 1:
+            near, loadings, delays = lax.optimization_barrier((near, loadings, delays))
+        far = swap(near, "neuron", neuron_count, bit)
+        bit *= 2
 
     high = lax.reduce_precision(bias, 8, 7)
     middle = lax.reduce_precision(bias - high, 8, 7)
     low = bias - high - middle
     below = jnp.concatenate([high, middle, low], axis=0).astype(BF16)
     load_ext = jnp.pad(jnp.concatenate([loadings[0], below], axis=0), ((0, EXTRA - 3), (0, 0)))
-    delay = jnp.broadcast_to(delays.reshape(lats, 1), (lats, LANES))
-
-    near = latents[None]
-    far = near[:0]
-    bit = 1
-    while bit < neuron_count:
-        near = jnp.concatenate([near, far], axis=0)
-        far = swap(near, "neuron", neuron_count, bit)
-        bit *= 2
+    meta = jnp.concatenate([delays.reshape(lats), recorded, jnp.zeros((LANES - lats - 1,), jnp.int32)])[None]
+
     keep, away, grad_load, grad_bias = pl.pallas_call(
         functools.partial(main_kernel, neuron_count, "neuron", chunk, 512),
         out_shape=[
@@ -147,7 +149,7 @@
             jax.ShapeDtypeStruct((lats, neurons), F32),
             jax.ShapeDtypeStruct((1, neurons), F32),
         ],
-        in_specs=[smem, vmem, vmem, hbm, vmem, vmem],
+        in_specs=[vmem, vmem, hbm, vmem, vmem],
         out_specs=[vmem, vmem, hbm, hbm],
         scratch_shapes=[
             pltpu.VMEM((lats, total), BF16),
@@ -161,7 +163,7 @@
             pltpu.SemaphoreType.DMA((neurons // chunk,)),
         ],
         compiler_params=pltpu.CompilerParams(vmem_limit_bytes=52 * 1024 * 1024),
-    )(recorded, delay, load_ext, counts[0], near, far)
+    )(meta, load_ext, counts[0], near, far)
 
     value = keep + swap(away, "neuron", neuron_count, 1)
     bit = 2
@@ -169,8 +171,15 @@
         value = value[0::2] + swap(value[1::2], "neuron", neuron_count, bit)
         bit *= 2
     value = value[0]
-    everyone = lax.all_gather(value.astype(BF16), "region", axis=0)
-    value = jnp.sum(everyone.astype(F32), axis=0)
+    bits = [1 << level for level in range(region_count.bit_length() - 1)]
+    orders = (bits[:1] + bits[:0:-1], bits[1:2] + bits[:1] + bits[2:])
+    for step in range(len(bits)):
+        pairs = [
+            (r * neuron_count + n, (r ^ orders[n % 2][step]) * neuron_count + n)
+            for r in range(region_count)
+            for n in range(neuron_count)
+        ]
+        value = value + lax.ppermute(value, ("region", "neuron"), pairs)
     return (value, grad_load[None], grad_bias)
 
 

time: 53.3 us -> 36.4 us (0.68)
  blocking collectives: 31.4 us -> 0 us
  waiting for transfers between devices: 4.93 us -> 12.5 us
  starting transfers between devices: 5.36 us -> 12.3 us
  other arithmetic: 3.11 us -> 3.84 us
  local copies, waits for them, and re-layouts: 0.73 us -> 0.01 us
    all_gather x1 -> x0, blocking collectives: 31.4 us -> none  [per_device(): everyone = lax.all_gather(value.astype(BF16), 'region', axis=0)]
    ppermute x0 -> x3, waiting for transfers between devices: none -> 7.58 us  [per_device(): value = value + lax.ppermute(value, ('region', 'neuron'), pairs)]
    ppermute x0 -> x3, starting transfers between devices: none -> 7.29 us  [per_device(): value = value + lax.ppermute(value, ('region', 'neuron'), pairs)]
    broadcast_in_dim x0 -> x1, other arithmetic: none -> 0.73 us  [per_device(): jnp.concatenate([delays.reshape(lats), recorded, jnp.zeros((LANES - lats...]
    broadcast_in_dim x1, local copies, waits for them, and re-layouts: 0.73 us -> 0.01 us  [per_device(): jnp.zeros((LANES - lats - 1,), jnp.int32)]
    reduce_sum x1 -> x0, other arithmetic: 0.67 us -> none  [per_device(): value = jnp.sum(everyone.astype(F32), axis=0)]
    add x0 -> x3, other arithmetic: none -> 0.66 us  [per_device(): value = value + lax.ppermute(value, ('region', 'neuron'), pairs)]
  transfers between devices with their start and end apart: 4 -> 7, of which waited for: 4 -> 6; matrix products, arithmetic and copies ran while one was open for 3% -> 7% of each run, Pallas kernels for 0% -> 0%
where the time goes in v6:
time: 36.4 us; the launch traced here: 36.1 us
  waiting for transfers between devices  12.5 us (34%)
  starting transfers between devices  12.3 us (34%)
  Pallas kernels  6.19 us (17%)
  other arithmetic  3.84 us (11%)
  between operations  1.34 us (4%)
    ppermute x3, waiting for transfers between devices, per_device(): value = value + lax.ppermute(value, ('region', 'neuron'), pairs)  7.58 us
    ppermute x3, starting transfers between devices, per_device(): value = value + lax.ppermute(value, ('region', 'neuron'), pairs)  7.29 us
    pallas_call x1, Pallas kernels, per_device(): pl.pallas_call(functools.partial(main_kernel, neuron_count, 'neuron', chu...  6.19 us
    ppermute x4, starting transfers between devices, swap(): return lax.ppermute(value, axis, [(i, i ^ bit) for i in range(count)])  4.96 us
    ppermute x4, waiting for transfers between devices, swap(): return lax.ppermute(value, axis, [(i, i ^ bit) for i in range(count)])  4.88 us
    concatenate x1, other arithmetic, per_device(): jnp.concatenate([loadings[0], below], axis=0)  0.95 us
    concatenate x1, other arithmetic, per_device(): near = jnp.concatenate([near, far], axis=0)  0.77 us
    broadcast_in_dim x1, other arithmetic, per_device(): jnp.concatenate([delays.reshape(lats), recorded, jnp.zeros((LANES - lats...  0.73 us
  transfers between devices with their start and end apart: 7, of which 6 were waited for; matrix products, arithmetic and copies ran while one was open for 7% of the time, Pallas kernels for 0%

profile of v6, /device:TPU:0, one launch (start us, length us, event | category | flops | bytes accessed | tf_op | source)
XLA Modules:
  0.0 36.1 jit_solution(4860553898685878455)
XLA Ops:
  0.6 0.5 %collective-permute-start = (bf16[1,64,256]{2,1,0:T(8,128)(2,1)}, bf16[1,64,256]{2,1,0:T(8,128)(2,1)S(1)}, u32[]{:S(2)}, u32[]{:S(2)}) collective-permute-start(bf16[1,64,256]{2,1,0:T(8,128)(2,1)} %bitcast.11), channel_id=1, source_target_pairs={{0,1},{1,0},{2,3},{3,2},{4,5},{5,4},{6,7},{7,6},{8,9},{9,8},{10,11... | collective-permute-start | bytes 98312 | tf_op jit(solution)/shard_map/ppermute | solution.py:125
  1.1 0.7 %reduce-precision_convert_fusion.1 = (bf16[1,1280]{1,0:T(2,128)(2,1)S(1)}, bf16[1,1280]{1,0:T(2,128)(2,1)S(1)}, bf16[1,1280]{1,0:T(2,128)(2,1)S(1)}) fusion(f32[1,1280]{1,0:T(1,128)} %param.9), kind=kLoop, calls=%fused_computation.14 | loop fusion | flops 8960 | bytes 12800 | tf_op jit(solution)/shard_map/convert
  2.5 0.0 collective-permute-done
  2.5 0.8 %pad_maximum_fusion.refs_3_ = bf16[2,64,256]{2,1,0:T(8,128)(2,1)S(1)} fusion(bf16[1,64,256]{2,1,0:T(8,128)(2,1)S(1)} %collective-permute-done, bf16[1,64,256]{2,1,0:T(8,128)(2,1)} %bitcast.12), kind=kLoop, calls=%fused_computation.10 | loop fusion | flops 32768 | bytes 131072 | tf_op jit(solution)/shard_map/concatenate | solution.py:131
  3.3 2.6 %collective-permute-start.1 = (bf16[2,64,256]{2,1,0:T(8,128)(2,1)S(1)}, bf16[2,64,256]{2,1,0:T(8,128)(2,1)S(1)}, u32[]{:S(2)}, u32[]{:S(2)}) collective-permute-start(bf16[2,64,256]{2,1,0:T(8,128)(2,1)S(1)} %pad_maximum_fusion.refs_3_), channel_id=1, source_target_pairs={{0,2},{1,3},{2,0},{3,1},{4,6},{5,7},{6,4},{7,5},{8,10},{9,11},{10,... | collective-permute-start | bytes 196616 | tf_op jit(solution)/shard_map/ppermute | solution.py:125
  5.8 0.9 %fusion.6.refs_1_ = bf16[80,1280]{1,0:T(8,128)(2,1)S(1)} fusion(bf16[1,1280]{1,0:T(2,128)(2,1)S(1)} %get-tuple-element.18, bf16[1,1280]{1,0:T(2,128)(2,1)S(1)} %get-tuple-element.19, bf16[1,1280]{1,0:T(2,128)(2,1)S(1)} %get-tuple-element.17, bf16[64,1280]{1,0:T(8,128)(2,1)} %bitcast.10), kind=kLoop, calls=%fused_computation.7 | loop fusion | flops 1331200 | bytes 376320 | tf_op jit(solution)/shard_map/concatenate | solution.py:141
  6.8 0.7 %add_bitcast_fusion.refs_0_ = s32[1,128]{1,0:T(1,128)S(1)} fusion(s32[63]{0:T(128)S(1)} %broadcast_in_dim.13, s32[1]{0:T(128)S(6)} %copy.9, s32[64]{0:T(128)} %bitcast.13), kind=kLoop, calls=%fused_computation.16 | loop fusion | flops 256 | bytes 1024 | tf_op jit(solution)/shard_map/broadcast_in_dim | solution.py:142
  7.5 1.0 %collective-permute-done.1.refs_4_ = bf16[2,64,256]{2,1,0:T(8,128)(2,1)S(1)} collective-permute-done((bf16[2,64,256]{2,1,0:T(8,128)(2,1)S(1)}, bf16[2,64,256]{2,1,0:T(8,128)(2,1)S(1)}, u32[]{:S(2)}, u32[]{:S(2)}) %collective-permute-start.1) | collective-permute-done | bytes 65568 | tf_op jit(solution)/shard_map/ppermute | solution.py:125
  8.6 6.2 %shard_map.85 = (f32[2,64,256]{2,1,0:T(8,128)S(1)}, f32[2,64,256]{2,1,0:T(8,128)S(1)}, f32[64,1280]{1,0:T(8,128)}, f32[1,1280]{1,0:T(1,128)}) custom-call(s32[1,128]{1,0:T(1,128)S(1)} %add_bitcast_fusion.refs_0_, bf16[80,1280]{1,0:T(8,128)(2,1)S(1)} %fusion.6.refs_1_, bf16[1280,1024]{1,0:T(8,128)(2,1)} %bitcast.9, ...), custom_call_target="tpu_custom_call" | custom-call | tf_op jit(solution)/shard_map/pallas_call | solution.py:144
  14.8 0.1 collective-permute-start.2
  14.8 1.3 %collective-permute-done.2 = f32[2,64,256]{2,1,0:T(8,128)S(1)} collective-permute-done((f32[2,64,256]{2,1,0:T(8,128)S(1)}, f32[2,64,256]{2,1,0:T(8,128)S(1)}, u32[]{:S(2)}, u32[]{:S(2)}) %collective-permute-start.2) | collective-permute-done | bytes 131104 | tf_op jit(solution)/shard_map/ppermute | solution.py:125
  16.2 1.8 %collective-permute-start.3 = (f32[1,64,256]{2,1,0:T(8,128)S(1)}, f32[1,64,256]{2,1,0:T(8,128)S(1)}, u32[]{:S(2)}, u32[]{:S(2)}) collective-permute-start(f32[1,64,256]{2,1,0:T(8,128)S(1)} %slice.11), channel_id=1, source_target_pairs={{0,2},{1,3},{2,0},{3,1},{4,6},{5,7},{6,4},{7,5},{8,10},{9,11},{10,... | collective-permute-start | bytes 196616 | tf_op jit(solution)/shard_map/ppermute | solution.py:125
  18.0 2.5 %collective-permute-done.3 = f32[1,64,256]{2,1,0:T(8,128)S(1)} collective-permute-done((f32[1,64,256]{2,1,0:T(8,128)S(1)}, f32[1,64,256]{2,1,0:T(8,128)S(1)}, u32[]{:S(2)}, u32[]{:S(2)}) %collective-permute-start.3) | collective-permute-done | bytes 65568 | tf_op jit(solution)/shard_map/ppermute | solution.py:125
  20.5 1.8 %collective-permute-start.4 = (f32[64,256]{1,0:T(8,128)S(1)}, f32[64,256]{1,0:T(8,128)S(1)}, u32[]{:S(2)}, u32[]{:S(2)}) collective-permute-start(f32[64,256]{1,0:T(8,128)S(1)} %fusion.7), channel_id=1, source_target_pairs={{0,4},{1,9},{2,6},{3,11},{4,0},{5,13},{6,2},{7,15},{8,12},{9,1},{1... | collective-permute-start | bytes 196616 | tf_op jit(solution)/shard_map/ppermute | solution.py:182
  22.3 2.5 %collective-permute-done.4 = f32[64,256]{1,0:T(8,128)S(1)} collective-permute-done((f32[64,256]{1,0:T(8,128)S(1)}, f32[64,256]{1,0:T(8,128)S(1)}, u32[]{:S(2)}, u32[]{:S(2)}) %collective-permute-start.4) | collective-permute-done | bytes 65568 | tf_op jit(solution)/shard_map/ppermute | solution.py:182
  24.9 2.9 %collective-permute-start.5 = (f32[64,256]{1,0:T(8,128)S(1)}, f32[64,256]{1,0:T(8,128)S(1)}, u32[]{:S(2)}, u32[]{:S(2)}) collective-permute-start(f32[64,256]{1,0:T(8,128)S(1)} %add.19), channel_id=1, source_target_pairs={{0,16},{1,5},{2,18},{3,7},{4,20},{5,1},{6,22},{7,3},{8,24},{9,13},... | collective-permute-start | bytes 196616 | tf_op jit(solution)/shard_map/ppermute | solution.py:182
  27.8 2.8 %collective-permute-done.5 = f32[64,256]{1,0:T(8,128)S(1)} collective-permute-done((f32[64,256]{1,0:T(8,128)S(1)}, f32[64,256]{1,0:T(8,128)S(1)}, u32[]{:S(2)}, u32[]{:S(2)}) %collective-permute-start.5) | collective-permute-done | bytes 65568 | tf_op jit(solution)/shard_map/ppermute | solution.py:182
  30.6 2.6 %collective-permute-start.6 = (f32[64,256]{1,0:T(8,128)S(1)}, f32[64,256]{1,0:T(8,128)S(1)}, u32[]{:S(2)}, u32[]{:S(2)}) collective-permute-start(f32[64,256]{1,0:T(8,128)S(1)} %add.20), channel_id=1, source_target_pairs={{0,8},{1,17},{2,10},{3,19},{4,12},{5,21},{6,14},{7,23},{8,0},{9,25... | collective-permute-start | bytes 196616 | tf_op jit(solution)/shard_map/ppermute | solution.py:182
  33.2 2.2 %collective-permute-done.6 = f32[64,256]{1,0:T(8,128)S(1)} collective-permute-done((f32[64,256]{1,0:T(8,128)S(1)}, f32[64,256]{1,0:T(8,128)S(1)}, u32[]{:S(2)}, u32[]{:S(2)}) %collective-permute-start.6) | collective-permute-done | bytes 65568 | tf_op jit(solution)/shard_map/ppermute | solution.py:182
  35.5 0.6 %add.21 = f32[64,256]{1,0:T(8,128)} add(f32[64,256]{1,0:T(8,128)S(1)} %add.20, f32[64,256]{1,0:T(8,128)S(1)} %collective-permute-done.6) | non-fusion elementwise | flops 16384 | bytes 196608 | tf_op jit(solution)/shard_map/add | solution.py:182
  (6 shorter events, 0.1 us)
Async XLA Ops:
  0.6 1.9 %collective-permute-start = (bf16[1,64,256]{2,1,0:T(8,128)(2,1)}, bf16[1,64,256]{2,1,0:T(8,128)(2,1)S(1)}, u32[]{:S(2)}, u32[]{:S(2)}) collective-permute-start(bf16[1,64,256]{2,1,0:T(8,128)(2,1)} %bitcast.11), channel_id=1, source_target_pairs={{0,1},{1,0},{2,3},{3,2},{4,5},{5,4},{6,7},{7,6},{8,9},{9,8},{10,11... | collective-permute-start | bytes 98312 | tf_op jit(solution)/shard_map/ppermute | solution.py:125
  3.3 5.3 %collective-permute-start.1 = (bf16[2,64,256]{2,1,0:T(8,128)(2,1)S(1)}, bf16[2,64,256]{2,1,0:T(8,128)(2,1)S(1)}, u32[]{:S(2)}, u32[]{:S(2)}) collective-permute-start(bf16[2,64,256]{2,1,0:T(8,128)(2,1)S(1)} %pad_maximum_fusion.refs_3_), channel_id=1, source_target_pairs={{0,2},{1,3},{2,0},{3,1},{4,6},{5,7},{6,4},{7,5},{8,10},{9,11},{10,... | collective-permute-start | bytes 196616 | tf_op jit(solution)/shard_map/ppermute | solution.py:125
  14.8 1.4 %collective-permute-start.2 = (f32[2,64,256]{2,1,0:T(8,128)S(1)}, f32[2,64,256]{2,1,0:T(8,128)S(1)}, u32[]{:S(2)}, u32[]{:S(2)}) collective-permute-start(f32[2,64,256]{2,1,0:T(8,128)S(1)} %get-tuple-element.14), channel_id=1, source_target_pairs={{0,1},{1,0},{2,3},{3,2},{4,5},{5,4},{6,7},{7,6},{8,9},{9,8},{10,11... | collective-permute-start | bytes 393224 | tf_op jit(solution)/shard_map/ppermute | solution.py:125
  16.2 4.3 %collective-permute-start.3 = (f32[1,64,256]{2,1,0:T(8,128)S(1)}, f32[1,64,256]{2,1,0:T(8,128)S(1)}, u32[]{:S(2)}, u32[]{:S(2)}) collective-permute-start(f32[1,64,256]{2,1,0:T(8,128)S(1)} %slice.11), channel_id=1, source_target_pairs={{0,2},{1,3},{2,0},{3,1},{4,6},{5,7},{6,4},{7,5},{8,10},{9,11},{10,... | collective-permute-start | bytes 196616 | tf_op jit(solution)/shard_map/ppermute | solution.py:125
  20.5 4.3 %collective-permute-start.4 = (f32[64,256]{1,0:T(8,128)S(1)}, f32[64,256]{1,0:T(8,128)S(1)}, u32[]{:S(2)}, u32[]{:S(2)}) collective-permute-start(f32[64,256]{1,0:T(8,128)S(1)} %fusion.7), channel_id=1, source_target_pairs={{0,4},{1,9},{2,6},{3,11},{4,0},{5,13},{6,2},{7,15},{8,12},{9,1},{1... | collective-permute-start | bytes 196616 | tf_op jit(solution)/shard_map/ppermute | solution.py:182
  24.9 5.7 %collective-permute-start.5 = (f32[64,256]{1,0:T(8,128)S(1)}, f32[64,256]{1,0:T(8,128)S(1)}, u32[]{:S(2)}, u32[]{:S(2)}) collective-permute-start(f32[64,256]{1,0:T(8,128)S(1)} %add.19), channel_id=1, source_target_pairs={{0,16},{1,5},{2,18},{3,7},{4,20},{5,1},{6,22},{7,3},{8,24},{9,13},... | collective-permute-start | bytes 196616 | tf_op jit(solution)/shard_map/ppermute | solution.py:182
  30.6 4.9 %collective-permute-start.6 = (f32[64,256]{1,0:T(8,128)S(1)}, f32[64,256]{1,0:T(8,128)S(1)}, u32[]{:S(2)}, u32[]{:S(2)}) collective-permute-start(f32[64,256]{1,0:T(8,128)S(1)} %add.20), channel_id=1, source_target_pairs={{0,8},{1,17},{2,10},{3,19},{4,12},{5,21},{6,14},{7,23},{8,0},{9,25... | collective-permute-start | bytes 196616 | tf_op jit(solution)/shard_map/ppermute | solution.py:182

commit v7 on v6

--- a/solution.py
+++ b/solution.py
@@ -44,15 +44,14 @@
     width = total // parts
     pieces = neurons // chunk
     def counts_copy(index):
-        rows = pl.ds(pl.multiple_of(index * chunk, chunk), chunk)
+        rows = pl.ds(index * chunk, chunk)
         return pltpu.make_async_copy(counts_hbm.at[rows], counts_ref.at[rows], counts_sems.at[index])
 
     def load_copy(index):
-        rows = pl.ds(pl.multiple_of(index * chunk, chunk), chunk)
+        rows = pl.ds(index * chunk, chunk)
         return pltpu.make_async_copy(grad_load_ref.at[:, rows], grad_load_hbm.at[:, rows], out_sems.at[index])
 
-    for index in range(pieces):
-        counts_copy(index).start()
+    counts_copy(0).start()
     row = lax.broadcasted_iota(jnp.int32, (EXTRA, total), 0)
     shifted[lats:, :] = jnp.where(row < 3, 1.0, 0.0).astype(BF16)
     grad_shift[...] = jnp.zeros_like(grad_shift)
@@ -73,10 +72,13 @@
         shifted[0:lats, j * LANES : (j + 1) * LANES] = tile.astype(BF16)
 
     bins = lax.broadcasted_iota(jnp.int32, (1, total), 1)
-
-    def visit(index, carry):
-        rows = pl.ds(pl.multiple_of(index * chunk, chunk), chunk)
+    for index in range(pieces):
+        rows = slice(index * chunk, (index + 1) * chunk)
+        if index == 0 and pieces > 1:
+            counts_copy(1).start()
         counts_copy(index).wait()
+        if index + 2 < pieces:
+            counts_copy(index + 2).start()
         load_part = load_ext[:, rows]
         grad_load = jnp.zeros((lats, chunk), F32)
         sums = jnp.zeros((chunk, LANES), F32)
@@ -96,9 +98,7 @@
         grad_load_ref[:, rows] = grad_load
         load_copy(index).start()
         grad_bias_ref[:, rows] = jnp.sum(sums.T, axis=0, keepdims=True)
-        return carry
 
-    lax.fori_loop(0, pieces, visit, 0, unroll=total <= 1024)
     bias_copy = pltpu.make_async_copy(grad_bias_ref, grad_bias_hbm, bias_sem)
     bias_copy.start()
 
@@ -171,15 +171,10 @@
         value = value[0::2] + swap(value[1::2], "neuron", neuron_count, bit)
         bit *= 2
     value = value[0]
-    bits = [1 << level for level in range(region_count.bit_length() - 1)]
-    orders = (bits[:1] + bits[:0:-1], bits[1:2] + bits[:1] + bits[2:])
-    for step in range(len(bits)):
-        pairs = [
-            (r * neuron_count + n, (r ^ orders[n % 2][step]) * neuron_count + n)
-            for r in range(region_count)
-            for n in range(neuron_count)
-        ]
-        value = value + lax.ppermute(value, ("region", "neuron"), pairs)
+    bit = 1
+    while bit < region_count:
+        value = value + swap(value, "region", region_count, bit)
+        bit *= 2
     return (value, grad_load[None], grad_bias)
 
 

time: 36.4 us -> 36 us (0.989)
  waiting for transfers between devices: 12.5 us -> 12.1 us
    ppermute x3 -> x0, waiting for transfers between devices: 7.58 us -> none  [per_device(): value = value + lax.ppermute(value, ('region', 'neuron'), pairs)]
    ppermute x3 -> x0, starting transfers between devices: 7.29 us -> none  [per_device(): value = value + lax.ppermute(value, ('region', 'neuron'), pairs)]
    ppermute x4 -> x7, waiting for transfers between devices: 4.88 us -> 12.1 us  [swap(): return lax.ppermute(value, axis, [(i, i ^ bit) for i in range(count)])]
    ppermute x4 -> x7, starting transfers between devices: 4.96 us -> 12.2 us  [swap(): return lax.ppermute(value, axis, [(i, i ^ bit) for i in range(count)])]
where the time goes in v7:
time: 36 us; the launch traced here: 35.7 us
  starting transfers between devices  12.2 us (34%)
  waiting for transfers between devices  12.1 us (34%)
  Pallas kernels  6.19 us (17%)
  other arithmetic  3.84 us (11%)
  between operations  1.34 us (4%)
    ppermute x7, starting transfers between devices, swap(): return lax.ppermute(value, axis, [(i, i ^ bit) for i in range(count)])  12.2 us
    ppermute x7, waiting for transfers between devices, swap(): return lax.ppermute(value, axis, [(i, i ^ bit) for i in range(count)])  12.1 us
    pallas_call x1, Pallas kernels, per_device(): pl.pallas_call(functools.partial(main_kernel, neuron_count, 'neuron', chu...  6.19 us
    concatenate x1, other arithmetic, per_device(): jnp.concatenate([loadings[0], below], axis=0)  0.95 us
    concatenate x1, other arithmetic, per_device(): near = jnp.concatenate([near, far], axis=0)  0.77 us
    broadcast_in_dim x1, other arithmetic, per_device(): jnp.concatenate([delays.reshape(lats), recorded, jnp.zeros((LANES - lats...  0.73 us
  transfers between devices with their start and end apart: 7, of which 6 were waited for; matrix products, arithmetic and copies ran while one was open for 7% of the time, Pallas kernels for 0%

profile of v7, /device:TPU:0, one launch (start us, length us, event | category | flops | bytes accessed | tf_op | source)
XLA Modules:
  0.0 35.7 jit_solution(10908259667081518479)
XLA Ops:
  0.6 0.5 %collective-permute-start = (bf16[1,64,256]{2,1,0:T(8,128)(2,1)}, bf16[1,64,256]{2,1,0:T(8,128)(2,1)S(1)}, u32[]{:S(2)}, u32[]{:S(2)}) collective-permute-start(bf16[1,64,256]{2,1,0:T(8,128)(2,1)} %bitcast.11), channel_id=1, source_target_pairs={{0,1},{1,0},{2,3},{3,2},{4,5},{5,4},{6,7},{7,6},{8,9},{9,8},{10,11... | collective-permute-start | bytes 98312 | tf_op jit(solution)/shard_map/ppermute | solution.py:125
  1.1 0.7 %reduce-precision_convert_fusion.1 = (bf16[1,1280]{1,0:T(2,128)(2,1)S(1)}, bf16[1,1280]{1,0:T(2,128)(2,1)S(1)}, bf16[1,1280]{1,0:T(2,128)(2,1)S(1)}) fusion(f32[1,1280]{1,0:T(1,128)} %param.9), kind=kLoop, calls=%fused_computation.14 | loop fusion | flops 8960 | bytes 12800 | tf_op jit(solution)/shard_map/convert
  2.5 0.0 collective-permute-done
  2.5 0.8 %pad_maximum_fusion.refs_3_ = bf16[2,64,256]{2,1,0:T(8,128)(2,1)S(1)} fusion(bf16[1,64,256]{2,1,0:T(8,128)(2,1)S(1)} %collective-permute-done, bf16[1,64,256]{2,1,0:T(8,128)(2,1)} %bitcast.12), kind=kLoop, calls=%fused_computation.10 | loop fusion | flops 32768 | bytes 131072 | tf_op jit(solution)/shard_map/concatenate | solution.py:131
  3.3 2.6 %collective-permute-start.1 = (bf16[2,64,256]{2,1,0:T(8,128)(2,1)S(1)}, bf16[2,64,256]{2,1,0:T(8,128)(2,1)S(1)}, u32[]{:S(2)}, u32[]{:S(2)}) collective-permute-start(bf16[2,64,256]{2,1,0:T(8,128)(2,1)S(1)} %pad_maximum_fusion.refs_3_), channel_id=1, source_target_pairs={{0,2},{1,3},{2,0},{3,1},{4,6},{5,7},{6,4},{7,5},{8,10},{9,11},{10,... | collective-permute-start | bytes 196616 | tf_op jit(solution)/shard_map/ppermute | solution.py:125
  5.8 0.9 %fusion.6.refs_1_ = bf16[80,1280]{1,0:T(8,128)(2,1)S(1)} fusion(bf16[1,1280]{1,0:T(2,128)(2,1)S(1)} %get-tuple-element.18, bf16[1,1280]{1,0:T(2,128)(2,1)S(1)} %get-tuple-element.19, bf16[1,1280]{1,0:T(2,128)(2,1)S(1)} %get-tuple-element.17, bf16[64,1280]{1,0:T(8,128)(2,1)} %bitcast.10), kind=kLoop, calls=%fused_computation.7 | loop fusion | flops 1331200 | bytes 376320 | tf_op jit(solution)/shard_map/concatenate | solution.py:141
  6.8 0.7 %add_bitcast_fusion.refs_0_ = s32[1,128]{1,0:T(1,128)S(1)} fusion(s32[63]{0:T(128)S(1)} %broadcast_in_dim.13, s32[1]{0:T(128)S(6)} %copy.9, s32[64]{0:T(128)} %bitcast.13), kind=kLoop, calls=%fused_computation.16 | loop fusion | flops 256 | bytes 1024 | tf_op jit(solution)/shard_map/broadcast_in_dim | solution.py:142
  7.5 1.0 %collective-permute-done.1.refs_4_ = bf16[2,64,256]{2,1,0:T(8,128)(2,1)S(1)} collective-permute-done((bf16[2,64,256]{2,1,0:T(8,128)(2,1)S(1)}, bf16[2,64,256]{2,1,0:T(8,128)(2,1)S(1)}, u32[]{:S(2)}, u32[]{:S(2)}) %collective-permute-start.1) | collective-permute-done | bytes 65568 | tf_op jit(solution)/shard_map/ppermute | solution.py:125
  8.6 6.2 %shard_map.85 = (f32[2,64,256]{2,1,0:T(8,128)S(1)}, f32[2,64,256]{2,1,0:T(8,128)S(1)}, f32[64,1280]{1,0:T(8,128)}, f32[1,1280]{1,0:T(1,128)}) custom-call(s32[1,128]{1,0:T(1,128)S(1)} %add_bitcast_fusion.refs_0_, bf16[80,1280]{1,0:T(8,128)(2,1)S(1)} %fusion.6.refs_1_, bf16[1280,1024]{1,0:T(8,128)(2,1)} %bitcast.9, ...), custom_call_target="tpu_custom_call" | custom-call | tf_op jit(solution)/shard_map/pallas_call | solution.py:144
  14.8 0.1 collective-permute-start.2
  14.8 1.3 %collective-permute-done.2 = f32[2,64,256]{2,1,0:T(8,128)S(1)} collective-permute-done((f32[2,64,256]{2,1,0:T(8,128)S(1)}, f32[2,64,256]{2,1,0:T(8,128)S(1)}, u32[]{:S(2)}, u32[]{:S(2)}) %collective-permute-start.2) | collective-permute-done | bytes 131104 | tf_op jit(solution)/shard_map/ppermute | solution.py:125
  16.2 1.8 %collective-permute-start.3 = (f32[1,64,256]{2,1,0:T(8,128)S(1)}, f32[1,64,256]{2,1,0:T(8,128)S(1)}, u32[]{:S(2)}, u32[]{:S(2)}) collective-permute-start(f32[1,64,256]{2,1,0:T(8,128)S(1)} %slice.11), channel_id=1, source_target_pairs={{0,2},{1,3},{2,0},{3,1},{4,6},{5,7},{6,4},{7,5},{8,10},{9,11},{10,... | collective-permute-start | bytes 196616 | tf_op jit(solution)/shard_map/ppermute | solution.py:125
  18.0 2.5 %collective-permute-done.3 = f32[1,64,256]{2,1,0:T(8,128)S(1)} collective-permute-done((f32[1,64,256]{2,1,0:T(8,128)S(1)}, f32[1,64,256]{2,1,0:T(8,128)S(1)}, u32[]{:S(2)}, u32[]{:S(2)}) %collective-permute-start.3) | collective-permute-done | bytes 65568 | tf_op jit(solution)/shard_map/ppermute | solution.py:125
  20.6 1.8 %collective-permute-start.4 = (f32[64,256]{1,0:T(8,128)S(1)}, f32[64,256]{1,0:T(8,128)S(1)}, u32[]{:S(2)}, u32[]{:S(2)}) collective-permute-start(f32[64,256]{1,0:T(8,128)S(1)} %fusion.7), channel_id=1, source_target_pairs={{0,4},{4,0},{8,12},{12,8},{16,20},{20,16},{24,28},{28,24},{1,5},{5... | collective-permute-start | bytes 196616 | tf_op jit(solution)/shard_map/ppermute | solution.py:125
  22.3 2.5 %collective-permute-done.4 = f32[64,256]{1,0:T(8,128)S(1)} collective-permute-done((f32[64,256]{1,0:T(8,128)S(1)}, f32[64,256]{1,0:T(8,128)S(1)}, u32[]{:S(2)}, u32[]{:S(2)}) %collective-permute-start.4) | collective-permute-done | bytes 65568 | tf_op jit(solution)/shard_map/ppermute | solution.py:125
  24.9 1.9 %collective-permute-start.5 = (f32[64,256]{1,0:T(8,128)S(1)}, f32[64,256]{1,0:T(8,128)S(1)}, u32[]{:S(2)}, u32[]{:S(2)}) collective-permute-start(f32[64,256]{1,0:T(8,128)S(1)} %add.19), channel_id=1, source_target_pairs={{0,8},{4,12},{8,0},{12,4},{16,24},{20,28},{24,16},{28,20},{1,9},{5... | collective-permute-start | bytes 196616 | tf_op jit(solution)/shard_map/ppermute | solution.py:125
  26.8 2.5 %collective-permute-done.5 = f32[64,256]{1,0:T(8,128)S(1)} collective-permute-done((f32[64,256]{1,0:T(8,128)S(1)}, f32[64,256]{1,0:T(8,128)S(1)}, u32[]{:S(2)}, u32[]{:S(2)}) %collective-permute-start.5) | collective-permute-done | bytes 65568 | tf_op jit(solution)/shard_map/ppermute | solution.py:125
  29.2 3.5 %collective-permute-start.6 = (f32[64,256]{1,0:T(8,128)S(1)}, f32[64,256]{1,0:T(8,128)S(1)}, u32[]{:S(2)}, u32[]{:S(2)}) collective-permute-start(f32[64,256]{1,0:T(8,128)S(1)} %add.20), channel_id=1, source_target_pairs={{0,16},{4,20},{8,24},{12,28},{16,0},{20,4},{24,8},{28,12},{1,17},{... | collective-permute-start | bytes 196616 | tf_op jit(solution)/shard_map/ppermute | solution.py:125
  32.8 2.3 %collective-permute-done.6 = f32[64,256]{1,0:T(8,128)S(1)} collective-permute-done((f32[64,256]{1,0:T(8,128)S(1)}, f32[64,256]{1,0:T(8,128)S(1)}, u32[]{:S(2)}, u32[]{:S(2)}) %collective-permute-start.6) | collective-permute-done | bytes 65568 | tf_op jit(solution)/shard_map/ppermute | solution.py:125
  35.0 0.6 %add.21 = f32[64,256]{1,0:T(8,128)} add(f32[64,256]{1,0:T(8,128)S(1)} %add.20, f32[64,256]{1,0:T(8,128)S(1)} %collective-permute-done.6) | non-fusion elementwise | flops 16384 | bytes 196608 | tf_op jit(solution)/shard_map/add | solution.py:176
  (6 shorter events, 0.1 us)
Async XLA Ops:
  0.6 1.9 %collective-permute-start = (bf16[1,64,256]{2,1,0:T(8,128)(2,1)}, bf16[1,64,256]{2,1,0:T(8,128)(2,1)S(1)}, u32[]{:S(2)}, u32[]{:S(2)}) collective-permute-start(bf16[1,64,256]{2,1,0:T(8,128)(2,1)} %bitcast.11), channel_id=1, source_target_pairs={{0,1},{1,0},{2,3},{3,2},{4,5},{5,4},{6,7},{7,6},{8,9},{9,8},{10,11... | collective-permute-start | bytes 98312 | tf_op jit(solution)/shard_map/ppermute | solution.py:125
  3.3 5.3 %collective-permute-start.1 = (bf16[2,64,256]{2,1,0:T(8,128)(2,1)S(1)}, bf16[2,64,256]{2,1,0:T(8,128)(2,1)S(1)}, u32[]{:S(2)}, u32[]{:S(2)}) collective-permute-start(bf16[2,64,256]{2,1,0:T(8,128)(2,1)S(1)} %pad_maximum_fusion.refs_3_), channel_id=1, source_target_pairs={{0,2},{1,3},{2,0},{3,1},{4,6},{5,7},{6,4},{7,5},{8,10},{9,11},{10,... | collective-permute-start | bytes 196616 | tf_op jit(solution)/shard_map/ppermute | solution.py:125
  14.8 1.4 %collective-permute-start.2 = (f32[2,64,256]{2,1,0:T(8,128)S(1)}, f32[2,64,256]{2,1,0:T(8,128)S(1)}, u32[]{:S(2)}, u32[]{:S(2)}) collective-permute-start(f32[2,64,256]{2,1,0:T(8,128)S(1)} %get-tuple-element.14), channel_id=1, source_target_pairs={{0,1},{1,0},{2,3},{3,2},{4,5},{5,4},{6,7},{7,6},{8,9},{9,8},{10,11... | collective-permute-start | bytes 393224 | tf_op jit(solution)/shard_map/ppermute | solution.py:125
  16.2 4.3 %collective-permute-start.3 = (f32[1,64,256]{2,1,0:T(8,128)S(1)}, f32[1,64,256]{2,1,0:T(8,128)S(1)}, u32[]{:S(2)}, u32[]{:S(2)}) collective-permute-start(f32[1,64,256]{2,1,0:T(8,128)S(1)} %slice.11), channel_id=1, source_target_pairs={{0,2},{1,3},{2,0},{3,1},{4,6},{5,7},{6,4},{7,5},{8,10},{9,11},{10,... | collective-permute-start | bytes 196616 | tf_op jit(solution)/shard_map/ppermute | solution.py:125
  20.6 4.3 %collective-permute-start.4 = (f32[64,256]{1,0:T(8,128)S(1)}, f32[64,256]{1,0:T(8,128)S(1)}, u32[]{:S(2)}, u32[]{:S(2)}) collective-permute-start(f32[64,256]{1,0:T(8,128)S(1)} %fusion.7), channel_id=1, source_target_pairs={{0,4},{4,0},{8,12},{12,8},{16,20},{20,16},{24,28},{28,24},{1,5},{5... | collective-permute-start | bytes 196616 | tf_op jit(solution)/shard_map/ppermute | solution.py:125
  24.9 4.3 %collective-permute-start.5 = (f32[64,256]{1,0:T(8,128)S(1)}, f32[64,256]{1,0:T(8,128)S(1)}, u32[]{:S(2)}, u32[]{:S(2)}) collective-permute-start(f32[64,256]{1,0:T(8,128)S(1)} %add.19), channel_id=1, source_target_pairs={{0,8},{4,12},{8,0},{12,4},{16,24},{20,28},{24,16},{28,20},{1,9},{5... | collective-permute-start | bytes 196616 | tf_op jit(solution)/shard_map/ppermute | solution.py:125
  29.2 5.8 %collective-permute-start.6 = (f32[64,256]{1,0:T(8,128)S(1)}, f32[64,256]{1,0:T(8,128)S(1)}, u32[]{:S(2)}, u32[]{:S(2)}) collective-permute-start(f32[64,256]{1,0:T(8,128)S(1)} %add.20), channel_id=1, source_target_pairs={{0,16},{4,20},{8,24},{12,28},{16,0},{20,4},{24,8},{28,12},{1,17},{... | collective-permute-start | bytes 196616 | tf_op jit(solution)/shard_map/ppermute | solution.py:125

commit v8 on v7

v8 whole, which is shorter than its diff:
```python
import functools

import jax
import jax.numpy as jnp
from jax import lax
from jax.experimental import pallas as pl
from jax.experimental.pallas import tpu as pltpu
from jax.sharding import PartitionSpec as P

LANES = 128
EXTRA = 16
F32 = jnp.float32
BF16 = jnp.bfloat16


def shift_tiles(tiles, delay, forward):
    lane = lax.broadcasted_iota(jnp.int32, delay.shape, 1)
    nothing = jnp.zeros_like(tiles[0])
    for level in range(7):
        amount = 1 << level
        chosen = (delay & amount) != 0
        if forward:
            turned = [pltpu.roll(tile, amount, 1) for tile in tiles]
            before = [nothing] + turned[:-1]
            moved = [jnp.where(lane < amount, b, t) for b, t in zip(before, turned)]
        else:
            turned = [pltpu.roll(tile, LANES - amount, 1) for tile in tiles]
            after = turned[1:] + [nothing]
            moved = [jnp.where(lane < LANES - amount, t, a) for t, a in zip(turned, after)]
        tiles = [jnp.where(chosen, m, tile) for m, tile in zip(moved, tiles)]
    chosen = delay >= LANES
    other = [nothing] + tiles[:-1] if forward else tiles[1:] + [nothing]
    return [jnp.where(chosen, o, tile) for o, tile in zip(other, tiles)]


def expected(load_part, piece):
    eta = lax.dot_general(load_part, piece, (((0,), (0,)), ((), ())), preferred_element_type=F32)
    return jnp.exp(eta)


def shift_kernel(parts, axis, chunk, step, early, *refs):
    meta_ref, load_ext, counts_hbm, near, far, keep, away, shifted = refs[:8]
    whole, counts_ref, held, grad_shift, counts_sem = refs[8:]
    me = lax.axis_index(axis)
    lats, total = grad_shift.shape
    neurons = counts_ref.shape[0]
    width = total // parts
    counts_copy = pltpu.make_async_copy(counts_hbm, counts_ref, counts_sem)
    counts_copy.start()

    k = 0
    for ref in (near, far):
        for j in range(ref.shape[0]):
            start = pl.multiple_of((me ^ k) * width, width)
            whole[:, pl.ds(start, width)] = ref[j]
            k += 1
    diagonal = lax.broadcasted_iota(jnp.int32, (lats, LANES), 0) == lax.broadcasted_iota(jnp.int32, (lats, LANES), 1)
    spread = jnp.broadcast_to(meta_ref[...].astype(F32), (lats, LANES))
    column = jnp.sum(jnp.where(diagonal, spread, 0.0), axis=1, keepdims=True)
    delay = jnp.broadcast_to(column, (lats, LANES)).astype(jnp.int32)
    length = meta_ref[:, lats : lats + 1]
    tiles = [whole[:, j * LANES : (j + 1) * LANES].astype(F32) for j in range(total // LANES)]
    for j, tile in enumerate(shift_tiles(tiles, delay, True)):
        shifted[0:lats, j * LANES : (j + 1) * LANES] = tile.astype(BF16)
    row = lax.broadcasted_iota(jnp.int32, (EXTRA, total), 0)
    shifted[lats:, :] = jnp.where(row < 3, 1.0, 0.0).astype(BF16)

    bins = lax.broadcasted_iota(jnp.int32, (1, total), 1)
    blocks = [
        (slice(first, first + chunk), slice(begin, begin + step))
        for first in range(0, neurons, chunk)
        for begin in range(0, total, step)
    ]
    for rows, span in blocks:
        if rows.start < early:
            held[rows, span] = expected(load_ext[:, rows], shifted[:, span])
    counts_copy.wait()
    for rows, span in blocks:
        rate = held[rows, span] if rows.start < early else expected(load_ext[:, rows], shifted[:, span])
        resid = jnp.where(bins[:, span] < length, rate - counts_ref[rows, span].astype(F32), 0.0)
        part = jnp.dot(load_ext[0:lats, rows], resid.astype(BF16), preferred_element_type=F32)
        grad_shift[:, span] = part if rows.start == 0 else grad_shift[:, span] + part

    tiles = [grad_shift[:, j * LANES : (j + 1) * LANES] for j in range(total // LANES)]
    for j, tile in enumerate(shift_tiles(tiles, delay, False)):
        grad_shift[:, j * LANES : (j + 1) * LANES] = tile
    for k in range(parts):
        start = pl.multiple_of((me ^ k) * width, width)
        target = away if k % 2 else keep
        target[k // 2] = grad_shift[:, pl.ds(start, width)]


def load_kernel(lats, first, chunk, step, *refs):
    meta_ref, load_ext, shifted, counts_hbm = refs[:4]
    load_hbm, bias_hbm, counts_ref, held, load_ref, bias_ref, sems = refs[-7:]
    count, total = counts_ref.shape
    place = pl.ds(first, count)
    counts_copy = pltpu.make_async_copy(counts_hbm.at[place], counts_ref, sems.at[0])
    counts_copy.start()
    length = meta_ref[:, lats : lats + 1]
    bins = lax.broadcasted_iota(jnp.int32, (1, total), 1)
    blocks = [(begin, at) for begin in range(0, count, chunk) for at in range(0, total, step)]
    for begin, at in blocks:
        rows, span = slice(begin, begin + chunk), slice(at, at + step)
        held[rows, span] = expected(load_ext[:, first + begin : first + begin + chunk], shifted[:, span])
    counts_copy.wait()
    for begin, at in blocks:
        rows, span = slice(begin, begin + chunk), slice(at, at + step)
        resid = jnp.where(bins[:, span] < length, held[rows, span] - counts_ref[rows, span].astype(F32), 0.0)
        sums = resid[:, 0:LANES]
        for j in range(1, step // LANES):
            sums = sums + resid[:, j * LANES : (j + 1) * LANES]
        line = jnp.sum(sums.T, axis=0, keepdims=True)
        part = lax.dot_general(
            shifted[0:lats, span], resid.astype(BF16), (((1,), (1,)), ((), ())), preferred_element_type=F32
        )
        load_ref[:, rows] = part if at == 0 else load_ref[:, rows] + part
        bias_ref[:, rows] = line if at == 0 else bias_ref[:, rows] + line
    outward = [
        pltpu.make_async_copy(load_ref, load_hbm.at[:, place], sems.at[1]),
        pltpu.make_async_copy(bias_ref, bias_hbm.at[:, place], sems.at[2]),
    ]
    for copy in outward:
        copy.start()
    for copy in outward:
        copy.wait()


def per_device(region_count, neuron_count, counts, latents, loadings, bias, delays, recorded):
    neurons, total = counts.shape[1:]
    lats, width = latents.shape
    chunk, step = 256, 512
    vmem = pl.BlockSpec(memory_space=pltpu.VMEM)
    hbm = pl.BlockSpec(memory_space=pltpu.HBM)
    params = pltpu.CompilerParams(vmem_limit_bytes=52 * 1024 * 1024)

    def swap(value, axis, count, bit):
        return lax.ppermute(value, axis, [(i, i ^ bit) for i in range(count)])

    near = latents[None]
    far = near[:0]
    bit = 1
    while bit < neuron_count:
        near = jnp.concatenate([near, far], axis=0)
        if bit > 1:
            near, loadings, delays = lax.optimization_barrier((near, loadings, delays))
        far = swap(near, "neuron", neuron_count, bit)
        bit *= 2

    high = lax.reduce_precision(bias, 8, 7)
    middle = lax.reduce_precision(bias - high, 8, 7)
    low = bias - high - middle
    below = jnp.concatenate([high, middle, low], axis=0).astype(BF16)
    load_ext = jnp.pad(jnp.concatenate([loadings[0], below], axis=0), ((0, EXTRA - 3), (0, 0)))
    meta = jnp.concatenate([delays.reshape(lats), recorded, jnp.zeros((LANES - lats - 1,), jnp.int32)])[None]

    early = 3 * chunk
    keep, away, shifted = pl.pallas_call(
        functools.partial(shift_kernel, neuron_count, "neuron", chunk, step, early),
        out_shape=[
            jax.ShapeDtypeStruct((neuron_count // 2, lats, width), F32),
            jax.ShapeDtypeStruct((neuron_count // 2, lats, width), F32),
            jax.ShapeDtypeStruct((lats + EXTRA, total), BF16),
        ],
        in_specs=[vmem, vmem, hbm, vmem, vmem],
        out_specs=[vmem, vmem, vmem],
        scratch_shapes=[
            pltpu.VMEM((lats, total), BF16),
            pltpu.VMEM((neurons, total), BF16),
            pltpu.VMEM((early, total), F32),
            pltpu.VMEM((lats, total), F32),
            pltpu.SemaphoreType.DMA,
        ],
        compiler_params=params,
    )(meta, load_ext, counts[0], near, far)

    shares = [(0, 2 * chunk), (2 * chunk, 2 * chunk), (4 * chunk, neurons - 4 * chunk)]
    made = []

    def make(before):
        first, count = shares.pop(0)
        before, start_load = lax.optimization_barrier((before, load_ext))
        out = pl.pallas_call(
            functools.partial(load_kernel, lats, first, chunk, step),
            out_shape=[jax.ShapeDtypeStruct((lats, neurons), F32), jax.ShapeDtypeStruct((1, neurons), F32)],
            in_specs=[vmem, vmem, vmem, hbm] + [hbm] * len(made),
            out_specs=[hbm, hbm],
            scratch_shapes=[
                pltpu.VMEM((count, total), BF16),
                pltpu.VMEM((count, total), F32),
                pltpu.VMEM((lats, count), F32),
                pltpu.VMEM((1, count), F32),
                pltpu.SemaphoreType.DMA((3,)),
            ],
            input_output_aliases={4 + i: i for i in range(len(made))},
            compiler_params=params,
            cost_estimate=pl.CostEstimate(
                flops=4 * lats * count * total, bytes_accessed=2 * count * total, transcendentals=count * total
            ),
        )(meta, start_load, shifted, counts[0], *made)
        return before, out

    value = keep + swap(away, "neuron", neuron_count, 1)
    bit = 2
    while bit < neuron_count:
        if shares:
            value, made = make(value)
        arrived = swap(value[1::2], "neuron", neuron_count, bit)
        arrived, made = lax.optimization_barrier((arrived, made))
        value = value[0::2] + arrived
        bit *= 2
    value = value[0]
    bit = 1
    while bit < region_count:
        if shares:
            value, made = make(value)
        arrived = swap(value, "region", region_count, bit)
        arrived, made = lax.optimization_barrier((arrived, made))
        value = value + arrived
        bit *= 2
    grad_load, grad_bias = made
    return (value, grad_load[None], grad_bias)


def solution(mesh):
    placed = (
        P("region", "neuron", None),
        P(None, "neuron"),
        P("region", None, "neuron"),
        P("region", "neuron"),
        P("region", None),
        P("region"),
    )
    return jax.shard_map(
        functools.partial(per_device, mesh.shape["region"], mesh.shape["neuron"]),
        mesh=mesh,
        in_specs=placed,
        out_specs=(P(None, "neuron"), P("region", None, "neuron"), P("region", "neuron")),
        check_vma=False,
    )
```

time: 36 us -> 33.1 us (0.919)
  waiting for transfers between devices: 12.1 us -> 5.11 us
  Pallas kernels: 6.19 us -> 10.8 us
  starting transfers between devices: 12.2 us -> 11.5 us
    ppermute x7, waiting for transfers between devices: 12.1 us -> 5.11 us  [swap(): return lax.ppermute(value, axis, [(i, i ^ bit) for i in range(count)])]
    pallas_call x1 -> x4, Pallas kernels: 6.19 us -> 10.8 us  [the longest x3 7.12 us: make(): pl.pallas_call(functools.partial(load_kernel, lats, first, chunk, step),...]
    ppermute x7, starting transfers between devices: 12.2 us -> 11.5 us  [swap(): return lax.ppermute(value, axis, [(i, i ^ bit) for i in range(count)])]
  transfers between devices with their start and end apart: 7 -> 7, of which waited for: 6 -> 5; matrix products, arithmetic and copies ran while one was open for 7% -> 7% of each run, Pallas kernels for 0% -> 22%
where the time goes in v8:
time: 33.1 us; the launch traced here: 32.6 us
  starting transfers between devices  11.5 us (35%)
  Pallas kernels  10.8 us (33%)
  waiting for transfers between devices  5.11 us (15%)
  other arithmetic  3.84 us (12%)
  between operations  1.37 us (4%)
    ppermute x7, starting transfers between devices, swap(): return lax.ppermute(value, axis, [(i, i ^ bit) for i in range(count)])  11.5 us
    pallas_call x3, Pallas kernels, make(): pl.pallas_call(functools.partial(load_kernel, lats, first, chunk, step),...  7.12 us
    ppermute x7, waiting for transfers between devices, swap(): return lax.ppermute(value, axis, [(i, i ^ bit) for i in range(count)])  5.11 us
    pallas_call x1, Pallas kernels, per_device(): pl.pallas_call(functools.partial(shift_kernel, neuron_count, 'neuron', ch...  3.71 us
    concatenate x1, other arithmetic, per_device(): jnp.concatenate([loadings[0], below], axis=0)  0.95 us
    concatenate x1, other arithmetic, per_device(): near = jnp.concatenate([near, far], axis=0)  0.77 us
    broadcast_in_dim x1, other arithmetic, per_device(): jnp.concatenate([delays.reshape(lats), recorded, jnp.zeros((LANES - lats...  0.73 us
    another operation x1, other arithmetic  0.7 us
  transfers between devices with their start and end apart: 7, of which 5 were waited for; matrix products, arithmetic and copies ran while one was open for 7% of the time, Pallas kernels for 22%

profile of v8, /device:TPU:0, one launch (start us, length us, event | category | flops | bytes accessed | tf_op | source)
XLA Modules:
  0.0 32.6 jit_solution(12868205078792428402)
XLA Ops:
  0.6 0.5 %collective-permute-start = (bf16[1,64,256]{2,1,0:T(8,128)(2,1)}, bf16[1,64,256]{2,1,0:T(8,128)(2,1)S(1)}, u32[]{:S(2)}, u32[]{:S(2)}) collective-permute-start(bf16[1,64,256]{2,1,0:T(8,128)(2,1)} %bitcast.15), channel_id=1, source_target_pairs={{0,1},{1,0},{2,3},{3,2},{4,5},{5,4},{6,7},{7,6},{8,9},{9,8},{10,11... | collective-permute-start | bytes 98312 | tf_op jit(solution)/shard_map/ppermute | solution.py:138
  1.1 0.7 %reduce-precision_convert_fusion.1 = (bf16[1,1280]{1,0:T(2,128)(2,1)S(1)}, bf16[1,1280]{1,0:T(2,128)(2,1)S(1)}, bf16[1,1280]{1,0:T(2,128)(2,1)S(1)}) fusion(f32[1,1280]{1,0:T(1,128)} %param.9), kind=kLoop, calls=%fused_computation.13 | loop fusion | flops 8960 | bytes 12800 | tf_op jit(solution)/shard_map/convert
  2.5 0.0 collective-permute-done
  2.5 0.8 %pad_maximum_fusion.refs_3_ = bf16[2,64,256]{2,1,0:T(8,128)(2,1)S(1)} fusion(bf16[1,64,256]{2,1,0:T(8,128)(2,1)S(1)} %collective-permute-done, bf16[1,64,256]{2,1,0:T(8,128)(2,1)} %bitcast.16), kind=kLoop, calls=%fused_computation.8 | loop fusion | flops 32768 | bytes 131072 | tf_op jit(solution)/shard_map/concatenate | solution.py:144
  3.3 2.6 %collective-permute-start.1 = (bf16[2,64,256]{2,1,0:T(8,128)(2,1)S(1)}, bf16[2,64,256]{2,1,0:T(8,128)(2,1)S(1)}, u32[]{:S(2)}, u32[]{:S(2)}) collective-permute-start(bf16[2,64,256]{2,1,0:T(8,128)(2,1)S(1)} %pad_maximum_fusion.refs_3_), channel_id=1, source_target_pairs={{0,2},{1,3},{2,0},{3,1},{4,6},{5,7},{6,4},{7,5},{8,10},{9,11},{10,... | collective-permute-start | bytes 196616 | tf_op jit(solution)/shard_map/ppermute | solution.py:138
  5.8 0.9 %fusion.6.refs_1_ = bf16[80,1280]{1,0:T(8,128)(2,1)S(1)} fusion(bf16[1,1280]{1,0:T(2,128)(2,1)S(1)} %get-tuple-element.64, bf16[1,1280]{1,0:T(2,128)(2,1)S(1)} %get-tuple-element.65, bf16[1,1280]{1,0:T(2,128)(2,1)S(1)} %get-tuple-element.63, bf16[64,1280]{1,0:T(8,128)(2,1)} %bitcast.14), kind=kLoop, calls=%fused_computation.7 | loop fusion | flops 1331200 | bytes 376320 | tf_op jit(solution)/shard_map/concatenate | solution.py:154
  6.8 0.7 %add_bitcast_fusion.1.refs_0_ = s32[1,128]{1,0:T(1,128)S(1)} fusion(s32[63]{0:T(128)S(1)} %broadcast_in_dim.13, s32[1]{0:T(128)S(6)} %copy.17, s32[64]{0:T(128)} %bitcast.17), kind=kLoop, calls=%fused_computation.15 | loop fusion | flops 256 | bytes 1024 | tf_op jit(solution)/shard_map/broadcast_in_dim | solution.py:155
  7.5 1.0 %collective-permute-done.1.refs_4_ = bf16[2,64,256]{2,1,0:T(8,128)(2,1)S(1)} collective-permute-done((bf16[2,64,256]{2,1,0:T(8,128)(2,1)S(1)}, bf16[2,64,256]{2,1,0:T(8,128)(2,1)S(1)}, u32[]{:S(2)}, u32[]{:S(2)}) %collective-permute-start.1) | collective-permute-done | bytes 65568 | tf_op jit(solution)/shard_map/ppermute | solution.py:138
  8.6 3.7 %shard_map.85 = (f32[2,64,256]{2,1,0:T(8,128)S(1)}, f32[2,64,256]{2,1,0:T(8,128)S(1)}, bf16[80,1024]{1,0:T(8,128)(2,1)S(1)}) custom-call(s32[1,128]{1,0:T(1,128)S(1)} %add_bitcast_fusion.1.refs_0_, bf16[80,1280]{1,0:T(8,128)(2,1)S(1)} %fusion.6.refs_1_, bf16[1280,1024]{1,0:T(8,128)(2,1)} %bitcast.9, bf16[2,64,256]{2,1,0:T(8,128)(2,1)S(1)} %pad_maximum_fusion.refs_3_, ...), custom_call_target="tpu_custom_call" | custom-call | tf_op jit(solution)/shard_map/pallas_call | solution.py:158
  12.3 0.1 collective-permute-start.2
  12.4 1.3 %collective-permute-done.2 = f32[2,64,256]{2,1,0:T(8,128)S(1)} collective-permute-done((f32[2,64,256]{2,1,0:T(8,128)S(1)}, f32[2,64,256]{2,1,0:T(8,128)S(1)}, u32[]{:S(2)}, u32[]{:S(2)}) %collective-permute-start.2) | collective-permute-done | bytes 131104 | tf_op jit(solution)/shard_map/ppermute | solution.py:138
  13.7 1.8 %collective-permute-start.3 = (f32[1,64,256]{2,1,0:T(8,128)S(1)}, f32[1,64,256]{2,1,0:T(8,128)S(1)}, u32[]{:S(2)}, u32[]{:S(2)}) collective-permute-start(f32[1,64,256]{2,1,0:T(8,128)S(1)} %slice.9), channel_id=1, source_target_pairs={{0,2},{1,3},{2,0},{3,1},{4,6},{5,7},{6,4},{7,5},{8,10},{9,11},{10,... | collective-permute-start | bytes 196616 | tf_op jit(solution)/shard_map/ppermute | solution.py:138
  15.5 2.5 %shard_map.86 = (f32[64,1280]{1,0:T(8,128)}, f32[1,1280]{1,0:T(1,128)}) custom-call(s32[1,128]{1,0:T(1,128)S(1)} %add_bitcast_fusion.1.refs_0_, bf16[80,1280]{1,0:T(8,128)(2,1)S(1)} %fusion.6.refs_1_, bf16[80,1024]{1,0:T(8,128)(2,1)S(1)} %get-tuple-element.40.refs_2_, bf16[1280,1024]{1,0:T(8,128)(2,1)} %bitcast.10), custom_call_target="tpu_custom_call" | custom-call | flops 134217728 | bytes 1048576 | tf_op jit(solution)/shard_map/pallas_call | solution.py:183
  18.0 0.0 collective-permute-done.3
  18.1 1.8 %collective-permute-start.4 = (f32[64,256]{1,0:T(8,128)S(1)}, f32[64,256]{1,0:T(8,128)S(1)}, u32[]{:S(2)}, u32[]{:S(2)}) collective-permute-start(f32[64,256]{1,0:T(8,128)S(1)} %add_bitcast_fusion), channel_id=1, source_target_pairs={{0,4},{4,0},{8,12},{12,8},{16,20},{20,16},{24,28},{28,24},{1,5},{5... | collective-permute-start | bytes 196616 | tf_op jit(solution)/shard_map/ppermute | solution.py:138
  19.8 2.5 %shard_map.87 = (f32[64,1280]{1,0:T(8,128)}, f32[1,1280]{1,0:T(1,128)}) custom-call(s32[1,128]{1,0:T(1,128)S(1)} %add_bitcast_fusion.1.refs_0_, bf16[80,1280]{1,0:T(8,128)(2,1)S(1)} %fusion.6.refs_1_, bf16[80,1024]{1,0:T(8,128)(2,1)S(1)} %get-tuple-element.40.refs_2_, bf16[1280,1024]{1,0:T(8,128)(2,1)} %bitcast.11, ...), custom_call_target="tpu_custom_call", output_to_operand_aliasing={{0}: (4, {}), {1}: (5, {})} | custom-call | flops 134217728 | bytes 1048576 | tf_op jit(solution)/shard_map/pallas_call | solution.py:183
  22.4 0.1 collective-permute-done.4
  22.4 1.9 %collective-permute-start.5 = (f32[64,256]{1,0:T(8,128)S(1)}, f32[64,256]{1,0:T(8,128)S(1)}, u32[]{:S(2)}, u32[]{:S(2)}) collective-permute-start(f32[64,256]{1,0:T(8,128)S(1)} %add.19), channel_id=1, source_target_pairs={{0,8},{4,12},{8,0},{12,4},{16,24},{20,28},{24,16},{28,20},{1,9},{5... | collective-permute-start | bytes 196616 | tf_op jit(solution)/shard_map/ppermute | solution.py:138
  24.3 2.1 %shard_map.88 = (f32[64,1280]{1,0:T(8,128)}, f32[1,1280]{1,0:T(1,128)}) custom-call(s32[1,128]{1,0:T(1,128)S(1)} %add_bitcast_fusion.1.refs_0_, bf16[80,1280]{1,0:T(8,128)(2,1)S(1)} %fusion.6.refs_1_, bf16[80,1024]{1,0:T(8,128)(2,1)S(1)} %get-tuple-element.40.refs_2_, bf16[1280,1024]{1,0:T(8,128)(2,1)} %bitcast.12, ...), custom_call_target="tpu_custom_call", output_to_operand_aliasing={{0}: (4, {}), {1}: (5, {})} | custom-call | flops 67108864 | bytes 524288 | tf_op jit(solution)/shard_map/pallas_call | solution.py:183
  26.4 0.3 %collective-permute-done.5 = f32[64,256]{1,0:T(8,128)S(1)} collective-permute-done((f32[64,256]{1,0:T(8,128)S(1)}, f32[64,256]{1,0:T(8,128)S(1)}, u32[]{:S(2)}, u32[]{:S(2)}) %collective-permute-start.5) | collective-permute-done | bytes 65568 | tf_op jit(solution)/shard_map/ppermute | solution.py:138
  26.8 2.9 %collective-permute-start.6 = (f32[64,256]{1,0:T(8,128)S(1)}, f32[64,256]{1,0:T(8,128)S(1)}, u32[]{:S(2)}, u32[]{:S(2)}) collective-permute-start(f32[64,256]{1,0:T(8,128)S(1)} %add.20), channel_id=1, source_target_pairs={{0,16},{4,20},{8,24},{12,28},{16,0},{20,4},{24,8},{28,12},{1,17},{... | collective-permute-start | bytes 196616 | tf_op jit(solution)/shard_map/ppermute | solution.py:138
  29.6 2.4 %collective-permute-done.6 = f32[64,256]{1,0:T(8,128)S(1)} collective-permute-done((f32[64,256]{1,0:T(8,128)S(1)}, f32[64,256]{1,0:T(8,128)S(1)}, u32[]{:S(2)}, u32[]{:S(2)}) %collective-permute-start.6) | collective-permute-done | bytes 65568 | tf_op jit(solution)/shard_map/ppermute | solution.py:138
  32.0 0.6 %add.21 = f32[64,256]{1,0:T(8,128)} add(f32[64,256]{1,0:T(8,128)S(1)} %add.20, f32[64,256]{1,0:T(8,128)S(1)} %collective-permute-done.6) | non-fusion elementwise | flops 16384 | bytes 196608 | tf_op jit(solution)/shard_map/add | solution.py:219
  (6 shorter events, 0.1 us)
Async XLA Ops:
  0.6 1.9 %collective-permute-start = (bf16[1,64,256]{2,1,0:T(8,128)(2,1)}, bf16[1,64,256]{2,1,0:T(8,128)(2,1)S(1)}, u32[]{:S(2)}, u32[]{:S(2)}) collective-permute-start(bf16[1,64,256]{2,1,0:T(8,128)(2,1)} %bitcast.15), channel_id=1, source_target_pairs={{0,1},{1,0},{2,3},{3,2},{4,5},{5,4},{6,7},{7,6},{8,9},{9,8},{10,11... | collective-permute-start | bytes 98312 | tf_op jit(solution)/shard_map/ppermute | solution.py:138
  3.3 5.3 %collective-permute-start.1 = (bf16[2,64,256]{2,1,0:T(8,128)(2,1)S(1)}, bf16[2,64,256]{2,1,0:T(8,128)(2,1)S(1)}, u32[]{:S(2)}, u32[]{:S(2)}) collective-permute-start(bf16[2,64,256]{2,1,0:T(8,128)(2,1)S(1)} %pad_maximum_fusion.refs_3_), channel_id=1, source_target_pairs={{0,2},{1,3},{2,0},{3,1},{4,6},{5,7},{6,4},{7,5},{8,10},{9,11},{10,... | collective-permute-start | bytes 196616 | tf_op jit(solution)/shard_map/ppermute | solution.py:138
  12.3 1.4 %collective-permute-start.2 = (f32[2,64,256]{2,1,0:T(8,128)S(1)}, f32[2,64,256]{2,1,0:T(8,128)S(1)}, u32[]{:S(2)}, u32[]{:S(2)}) collective-permute-start(f32[2,64,256]{2,1,0:T(8,128)S(1)} %get-tuple-element.37), channel_id=1, source_target_pairs={{0,1},{1,0},{2,3},{3,2},{4,5},{5,4},{6,7},{7,6},{8,9},{9,8},{10,11... | collective-permute-start | bytes 393224 | tf_op jit(solution)/shard_map/ppermute | solution.py:138
  13.7 4.3 %collective-permute-start.3 = (f32[1,64,256]{2,1,0:T(8,128)S(1)}, f32[1,64,256]{2,1,0:T(8,128)S(1)}, u32[]{:S(2)}, u32[]{:S(2)}) collective-permute-start(f32[1,64,256]{2,1,0:T(8,128)S(1)} %slice.9), channel_id=1, source_target_pairs={{0,2},{1,3},{2,0},{3,1},{4,6},{5,7},{6,4},{7,5},{8,10},{9,11},{10,... | collective-permute-start | bytes 196616 | tf_op jit(solution)/shard_map/ppermute | solution.py:138
  18.1 4.3 %collective-permute-start.4 = (f32[64,256]{1,0:T(8,128)S(1)}, f32[64,256]{1,0:T(8,128)S(1)}, u32[]{:S(2)}, u32[]{:S(2)}) collective-permute-start(f32[64,256]{1,0:T(8,128)S(1)} %add_bitcast_fusion), channel_id=1, source_target_pairs={{0,4},{4,0},{8,12},{12,8},{16,20},{20,16},{24,28},{28,24},{1,5},{5... | collective-permute-start | bytes 196616 | tf_op jit(solution)/shard_map/ppermute | solution.py:138
  22.4 4.3 %collective-permute-start.5 = (f32[64,256]{1,0:T(8,128)S(1)}, f32[64,256]{1,0:T(8,128)S(1)}, u32[]{:S(2)}, u32[]{:S(2)}) collective-permute-start(f32[64,256]{1,0:T(8,128)S(1)} %add.19), channel_id=1, source_target_pairs={{0,8},{4,12},{8,0},{12,4},{16,24},{20,28},{24,16},{28,20},{1,9},{5... | collective-permute-start | bytes 196616 | tf_op jit(solution)/shard_map/ppermute | solution.py:138
  26.8 5.2 %collective-permute-start.6 = (f32[64,256]{1,0:T(8,128)S(1)}, f32[64,256]{1,0:T(8,128)S(1)}, u32[]{:S(2)}, u32[]{:S(2)}) collective-permute-start(f32[64,256]{1,0:T(8,128)S(1)} %add.20), channel_id=1, source_target_pairs={{0,16},{4,20},{8,24},{12,28},{16,0},{20,4},{24,8},{28,12},{1,17},{... | collective-permute-start | bytes 196616 | tf_op jit(solution)/shard_map/ppermute | solution.py:138

commit v9 on v8

--- a/solution.py
+++ b/solution.py
@@ -39,8 +39,10 @@
 
 
 def shift_kernel(parts, axis, chunk, step, early, *refs):
-    meta_ref, load_ext, counts_hbm, near, far, keep, away, shifted = refs[:8]
-    whole, counts_ref, held, grad_shift, counts_sem = refs[8:]
+    meta_ref, pack_ref, counts_hbm = refs[:3]
+    arrived = refs[3 : 2 + parts]
+    outs = refs[2 + parts : 2 + 2 * parts]
+    load_ext, shifted, whole, counts_ref, held, grad_shift, counts_sem = refs[2 + 2 * parts :]
     me = lax.axis_index(axis)
     lats, total = grad_shift.shape
     neurons = counts_ref.shape[0]
@@ -48,22 +50,28 @@
     counts_copy = pltpu.make_async_copy(counts_hbm, counts_ref, counts_sem)
     counts_copy.start()
 
-    k = 0
-    for ref in (near, far):
-        for j in range(ref.shape[0]):
-            start = pl.multiple_of((me ^ k) * width, width)
-            whole[:, pl.ds(start, width)] = ref[j]
-            k += 1
+    for k in range(parts):
+        start = pl.multiple_of((me ^ k) * width, width)
+        whole[:, pl.ds(start, width)] = arrived[k - 1][...] if k else pack_ref[:, neurons:]
     diagonal = lax.broadcasted_iota(jnp.int32, (lats, LANES), 0) == lax.broadcasted_iota(jnp.int32, (lats, LANES), 1)
-    spread = jnp.broadcast_to(meta_ref[...].astype(F32), (lats, LANES))
+    spread = jnp.broadcast_to(meta_ref[1:2, 0:LANES], (lats, LANES))
     column = jnp.sum(jnp.where(diagonal, spread, 0.0), axis=1, keepdims=True)
     delay = jnp.broadcast_to(column, (lats, LANES)).astype(jnp.int32)
-    length = meta_ref[:, lats : lats + 1]
+    length = meta_ref[2:3, 0:1].astype(jnp.int32)
     tiles = [whole[:, j * LANES : (j + 1) * LANES].astype(F32) for j in range(total // LANES)]
     for j, tile in enumerate(shift_tiles(tiles, delay, True)):
         shifted[0:lats, j * LANES : (j + 1) * LANES] = tile.astype(BF16)
     row = lax.broadcasted_iota(jnp.int32, (EXTRA, total), 0)
     shifted[lats:, :] = jnp.where(row < 3, 1.0, 0.0).astype(BF16)
+
+    load_ext[0:lats, :] = pack_ref[:, 0:neurons]
+    bias = meta_ref[0:1, :]
+    high = bias.astype(BF16).astype(F32)
+    middle = (bias - high).astype(BF16).astype(F32)
+    low = bias - high - middle
+    row = lax.broadcasted_iota(jnp.int32, (EXTRA, neurons), 0)
+    below = jnp.where(row == 0, high, jnp.where(row == 1, middle, jnp.where(row == 2, low, 0.0)))
+    load_ext[lats:, :] = below.astype(BF16)
 
     bins = lax.broadcasted_iota(jnp.int32, (1, total), 1)
     blocks = [
@@ -86,8 +94,7 @@
         grad_shift[:, j * LANES : (j + 1) * LANES] = tile
     for k in range(parts):
         start = pl.multiple_of((me ^ k) * width, width)
-        target = away if k % 2 else keep
-        target[k // 2] = grad_shift[:, pl.ds(start, width)]
+        outs[k][...] = grad_shift[:, pl.ds(start, width)]
 
 
 def load_kernel(lats, first, chunk, step, *refs):
@@ -97,7 +104,7 @@
     place = pl.ds(first, count)
     counts_copy = pltpu.make_async_copy(counts_hbm.at[place], counts_ref, sems.at[0])
     counts_copy.start()
-    length = meta_ref[:, lats : lats + 1]
+    length = meta_ref[2:3, 0:1].astype(jnp.int32)
     bins = lax.broadcasted_iota(jnp.int32, (1, total), 1)
     blocks = [(begin, at) for begin in range(0, count, chunk) for at in range(0, total, step)]
     for begin, at in blocks:
@@ -134,36 +141,23 @@
     hbm = pl.BlockSpec(memory_space=pltpu.HBM)
     params = pltpu.CompilerParams(vmem_limit_bytes=52 * 1024 * 1024)
 
-    def swap(value, axis, count, bit):
-        return lax.ppermute(value, axis, [(i, i ^ bit) for i in range(count)])
-
-    near = latents[None]
-    far = near[:0]
-    bit = 1
-    while bit < neuron_count:
-        near = jnp.concatenate([near, far], axis=0)
-        if bit > 1:
-            near, loadings, delays = lax.optimization_barrier((near, loadings, delays))
-        far = swap(near, "neuron", neuron_count, bit)
-        bit *= 2
-
-    high = lax.reduce_precision(bias, 8, 7)
-    middle = lax.reduce_precision(bias - high, 8, 7)
-    low = bias - high - middle
-    below = jnp.concatenate([high, middle, low], axis=0).astype(BF16)
-    load_ext = jnp.pad(jnp.concatenate([loadings[0], below], axis=0), ((0, EXTRA - 3), (0, 0)))
-    meta = jnp.concatenate([delays.reshape(lats), recorded, jnp.zeros((LANES - lats - 1,), jnp.int32)])[None]
+    def swap(value, axis, count, mask):
+        return lax.ppermute(value, axis, [(i, i ^ mask) for i in range(count)])
+
+    arrived = [swap(latents, "neuron", neuron_count, k) for k in range(1, neuron_count)]
+    pack = jnp.concatenate([loadings[0], latents], axis=1)
+    row = lax.broadcasted_iota(jnp.int32, (8, neurons), 0)
+    lines = jnp.pad(delays, ((1, 6), (0, neurons - lats)))
+    lines = jnp.where(row == 2, jnp.broadcast_to(recorded[:, None], lines.shape), lines)
+    meta = jnp.pad(bias, ((0, 7), (0, 0))) + lines.astype(F32)
 
     early = 3 * chunk
-    keep, away, shifted = pl.pallas_call(
+    *outs, load_ext, shifted = pl.pallas_call(
         functools.partial(shift_kernel, neuron_count, "neuron", chunk, step, early),
-        out_shape=[
-            jax.ShapeDtypeStruct((neuron_count // 2, lats, width), F32),
-            jax.ShapeDtypeStruct((neuron_count // 2, lats, width), F32),
-            jax.ShapeDtypeStruct((lats + EXTRA, total), BF16),
-        ],
-        in_specs=[vmem, vmem, hbm, vmem, vmem],
-        out_specs=[vmem, vmem, vmem],
+        out_shape=[jax.ShapeDtypeStruct((lats, width), F32)] * neuron_count
+        + [jax.ShapeDtypeStruct((lats + EXTRA, neurons), BF16), jax.ShapeDtypeStruct((lats + EXTRA, total), BF16)],
+        in_specs=[vmem, vmem, hbm] + [vmem] * (neuron_count - 1),
+        out_specs=[vmem] * (neuron_count + 2),
         scratch_shapes=[
             pltpu.VMEM((lats, total), BF16),
             pltpu.VMEM((neurons, total), BF16),
@@ -172,7 +166,7 @@
             pltpu.SemaphoreType.DMA,
         ],
         compiler_params=params,
-    )(meta, load_ext, counts[0], near, far)
+    )(meta, pack, counts[0], *arrived)
 
     shares = [(0, 2 * chunk), (2 * chunk, 2 * chunk), (4 * chunk, neurons - 4 * chunk)]
     made = []
@@ -200,24 +194,21 @@
         )(meta, start_load, shifted, counts[0], *made)
         return before, out
 
-    value = keep + swap(away, "neuron", neuron_count, 1)
-    bit = 2
-    while bit < neuron_count:
+    outs, made = make(outs)
+    arrived = [swap(outs[k], "neuron", neuron_count, k) for k in range(1, neuron_count)]
+    arrived, made = lax.optimization_barrier((arrived, made))
+    value = functools.reduce(jnp.add, [outs[0]] + arrived)
+    mask = 1
+    while mask < region_count:
+        masks = [mask, 2 * mask, 3 * mask] if 2 * mask < region_count else [mask]
         if shares:
             value, made = make(value)
-        arrived = swap(value[1::2], "neuron", neuron_count, bit)
+        arrived = [swap(value, "region", region_count, k) for k in masks]
         arrived, made = lax.optimization_barrier((arrived, made))
-        value = value[0::2] + arrived
-        bit *= 2
-    value = value[0]
-    bit = 1
-    while bit < region_count:
-        if shares:
-            value, made = make(value)
-        arrived = swap(value, "region", region_count, bit)
-        arrived, made = lax.optimization_barrier((arrived, made))
-        value = value + arrived
-        bit *= 2
+        value = value + arrived[0]
+        if len(masks) == 3:
+            value = value + (arrived[1] + arrived[2])
+        mask *= 1 + len(masks)
     grad_load, grad_bias = made
     return (value, grad_load[None], grad_bias)
 

time: 33.1 us -> 30.7 us (0.927)
  other arithmetic: 3.84 us -> 2.42 us
  waiting for transfers between devices: 5.11 us -> 4.42 us
    add x4, other arithmetic: 0.68 us -> 1.46 us  [the longest x1 0.78 us: per_device(): meta = jnp.pad(bias, ((0, 7), (0, 0))) + lines.astype(F32)]
    concatenate x2 -> x1, other arithmetic: 1.72 us -> 0.95 us  [per_device(): pack = jnp.concatenate([loadings[0], latents], axis=1)]
    broadcast_in_dim x1 -> x0, other arithmetic: 0.73 us -> none  [per_device(): jnp.concatenate([delays.reshape(lats), recorded, jnp.zeros((LANES - lats...]
    another operation x1 -> x0, other arithmetic: 0.7 us -> none
    ppermute x7 -> x10, waiting for transfers between devices: 5.11 us -> 4.42 us  [swap(): return lax.ppermute(value, axis, [(i, i ^ mask) for i in range(count)])]
    ppermute x7 -> x10, starting transfers between devices: 11.5 us -> 11.3 us  [swap(): return lax.ppermute(value, axis, [(i, i ^ mask) for i in range(count)])]
  transfers between devices with their start and end apart: 7 -> 10, of which waited for: 5 -> 6; matrix products, arithmetic and copies ran while one was open for 7% -> 6% of each run, Pallas kernels for 22% -> 23%
where the time goes in v9:
time: 30.7 us; the launch traced here: 30.4 us
  starting transfers between devices  11.3 us (37%)
  Pallas kernels  10.8 us (35%)
  waiting for transfers between devices  4.42 us (14%)
  other arithmetic  2.42 us (8%)
  between operations  1.36 us (4%)
    ppermute x10, starting transfers between devices, swap(): return lax.ppermute(value, axis, [(i, i ^ mask) for i in range(count)])  11.3 us
    pallas_call x3, Pallas kernels, make(): pl.pallas_call(functools.partial(load_kernel, lats, first, chunk, step),...  7.1 us
    ppermute x10, waiting for transfers between devices, swap(): return lax.ppermute(value, axis, [(i, i ^ mask) for i in range(count)])  4.42 us
    pallas_call x1, Pallas kernels, per_device(): pl.pallas_call(functools.partial(shift_kernel, neuron_count, 'neuron', ch...  3.72 us
    concatenate x1, other arithmetic, per_device(): pack = jnp.concatenate([loadings[0], latents], axis=1)  0.95 us
    add x1, other arithmetic, per_device(): meta = jnp.pad(bias, ((0, 7), (0, 0))) + lines.astype(F32)  0.78 us
    add x1, other arithmetic, per_device(): value = value + arrived[0]  0.64 us
  transfers between devices with their start and end apart: 10, of which 6 were waited for; matrix products, arithmetic and copies ran while one was open for 6% of the time, Pallas kernels for 23%

profile of v9, /device:TPU:0, one launch (start us, length us, event | category | flops | bytes accessed | tf_op | source)
XLA Modules:
  0.0 30.4 jit_solution(2548726364735081828)
XLA Ops:
  0.6 0.5 %collective-permute-start = (bf16[64,256]{1,0:T(8,128)(2,1)}, bf16[64,256]{1,0:T(8,128)(2,1)S(1)}, u32[]{:S(2)}, u32[]{:S(2)}) collective-permute-start(bf16[64,256]{1,0:T(8,128)(2,1)} %param.7), channel_id=1, source_target_pairs={{0,1},{1,0},{2,3},{3,2},{4,5},{5,4},{6,7},{7,6},{8,9},{9,8},{10,11... | collective-permute-start | bytes 98312 | tf_op jit(solution)/shard_map/ppermute | solution.py:145
  1.1 2.6 %collective-permute-start.2 = (bf16[64,256]{1,0:T(8,128)(2,1)}, bf16[64,256]{1,0:T(8,128)(2,1)S(1)}, u32[]{:S(2)}, u32[]{:S(2)}) collective-permute-start(bf16[64,256]{1,0:T(8,128)(2,1)} %param.7), channel_id=1, source_target_pairs={{0,3},{1,2},{2,1},{3,0},{4,7},{5,6},{6,5},{7,4},{8,11},{9,10},{10,... | collective-permute-start | bytes 98312 | tf_op jit(solution)/shard_map/ppermute | solution.py:145
  3.8 0.0 collective-permute-start.1
  4.5 0.8 %convert_add_fusion.refs_0_ = f32[8,1280]{1,0:T(8,128)S(1)} fusion(s32[1,64]{1,0:T(1,128)} %param.10, f32[1,1280]{1,0:T(1,128)} %param.9, s32[]{:T(128)} %bitcast.4, pred[8]{0:T(512)(128)(4,1)S(1)} %iota_compare_fusion), kind=kLoop, calls=%fused_computation.3 | loop fusion | flops 30720 | bytes 46348 | tf_op jit(solution)/shard_map/add | solution.py:152
  5.3 0.9 %pad_maximum_fusion.refs_1_ = bf16[64,1536]{1,0:T(8,128)(2,1)S(1)} fusion(bf16[64,256]{1,0:T(8,128)(2,1)} %param.7, bf16[64,1280]{1,0:T(8,128)(2,1)} %bitcast.10), kind=kLoop, calls=%fused_computation | loop fusion | flops 393216 | bytes 393216 | tf_op jit(solution)/shard_map/concatenate | solution.py:148
  6.2 0.0 collective-permute-done.refs_3_
  6.2 0.0 collective-permute-done.2.refs_5_
  6.3 1.7 %collective-permute-done.1.refs_4_ = bf16[64,256]{1,0:T(8,128)(2,1)S(1)} collective-permute-done((bf16[64,256]{1,0:T(8,128)(2,1)}, bf16[64,256]{1,0:T(8,128)(2,1)S(1)}, u32[]{:S(2)}, u32[]{:S(2)}) %collective-permute-start.1) | collective-permute-done | bytes 32800 | tf_op jit(solution)/shard_map/ppermute | solution.py:145
  7.9 3.7 %shard_map.85 = (f32[64,256]{1,0:T(8,128)S(1)}, f32[64,256]{1,0:T(8,128)S(1)}, f32[64,256]{1,0:T(8,128)S(1)}, f32[64,256]{1,0:T(8,128)S(1)}, bf16[80,1280]{1,0:T(8,128)(2,1)S(1)}, /*index=5*/bf16[80,1024]{1,0:T(8,128)(2,1)S(1)}) custom-call(f32[8,1280]{1,0:T(8,128)S(1)} %convert_add_fusion.refs_0_, bf16[64,1536]{1,0:T(8,128)(2,1)S(1)} %pad_maximum_fusion.refs_1_, ...), custom_call_target="tpu_custom_call" | custom-call | tf_op jit(solution)/shard_map/pallas_call | solution.py:155
  11.6 0.1 collective-permute-start.3
  11.7 0.5 %collective-permute-start.4 = (f32[64,256]{1,0:T(8,128)S(1)}, f32[64,256]{1,0:T(8,128)S(1)}, u32[]{:S(2)}, u32[]{:S(2)}) collective-permute-start(f32[64,256]{1,0:T(8,128)S(1)} %get-tuple-element.44), channel_id=1, source_target_pairs={{0,2},{1,3},{2,0},{3,1},{4,6},{5,7},{6,4},{7,5},{8,10},{9,11},{10,... | collective-permute-start | bytes 196616 | tf_op jit(solution)/shard_map/ppermute | solution.py:145
  12.2 1.4 %collective-permute-start.5 = (f32[64,256]{1,0:T(8,128)S(1)}, f32[64,256]{1,0:T(8,128)S(1)}, u32[]{:S(2)}, u32[]{:S(2)}) collective-permute-start(f32[64,256]{1,0:T(8,128)S(1)} %get-tuple-element.45), channel_id=1, source_target_pairs={{0,3},{1,2},{2,1},{3,0},{4,7},{5,6},{6,5},{7,4},{8,11},{9,10},{10,... | collective-permute-start | bytes 196616 | tf_op jit(solution)/shard_map/ppermute | solution.py:145
  13.6 2.5 %shard_map.86 = (f32[64,1280]{1,0:T(8,128)}, f32[1,1280]{1,0:T(1,128)}) custom-call(f32[8,1280]{1,0:T(8,128)S(1)} %convert_add_fusion.refs_0_, bf16[80,1280]{1,0:T(8,128)(2,1)S(1)} %get-tuple-element.63.refs_1_, bf16[80,1024]{1,0:T(8,128)(2,1)S(1)} %get-tuple-element.47.refs_2_, bf16[1280,1024]{1,0:T(8,128)(2,1)} %bitcast.6), custom_call_target="tpu_custom_call" | custom-call | flops 134217728 | bytes 1048576 | tf_op jit(solution)/shard_map/pallas_call | solution.py:177
  16.1 0.0 collective-permute-done.3
  16.1 0.6 %collective-permute-done.4 = f32[64,256]{1,0:T(8,128)S(1)} collective-permute-done((f32[64,256]{1,0:T(8,128)S(1)}, f32[64,256]{1,0:T(8,128)S(1)}, u32[]{:S(2)}, u32[]{:S(2)}) %collective-permute-start.4) | collective-permute-done | bytes 65568 | tf_op jit(solution)/shard_map/ppermute | solution.py:145
  16.7 0.5 %collective-permute-done.5 = f32[64,256]{1,0:T(8,128)S(1)} collective-permute-done((f32[64,256]{1,0:T(8,128)S(1)}, f32[64,256]{1,0:T(8,128)S(1)}, u32[]{:S(2)}, u32[]{:S(2)}) %collective-permute-start.5) | collective-permute-done | bytes 65568 | tf_op jit(solution)/shard_map/ppermute | solution.py:145
  17.2 2.6 %collective-permute-start.8 = (f32[64,256]{1,0:T(8,128)S(1)}, f32[64,256]{1,0:T(8,128)S(1)}, u32[]{:S(2)}, u32[]{:S(2)}) collective-permute-start(f32[64,256]{1,0:T(8,128)S(1)} %add_add_fusion.1), channel_id=1, source_target_pairs={{0,12},{4,8},{8,4},{12,0},{16,28},{20,24},{24,20},{28,16},{1,13},{... | collective-permute-start | bytes 196616 | tf_op jit(solution)/shard_map/ppermute | solution.py:145
  19.8 0.4 %collective-permute-start.7 = (f32[64,256]{1,0:T(8,128)S(1)}, f32[64,256]{1,0:T(8,128)S(1)}, u32[]{:S(2)}, u32[]{:S(2)}) collective-permute-start(f32[64,256]{1,0:T(8,128)S(1)} %add_add_fusion.1), channel_id=1, source_target_pairs={{0,8},{4,12},{8,0},{12,4},{16,24},{20,28},{24,16},{28,20},{1,9},{5... | collective-permute-start | bytes 196616 | tf_op jit(solution)/shard_map/ppermute | solution.py:145
  20.2 0.5 %collective-permute-start.6 = (f32[64,256]{1,0:T(8,128)S(1)}, f32[64,256]{1,0:T(8,128)S(1)}, u32[]{:S(2)}, u32[]{:S(2)}) collective-permute-start(f32[64,256]{1,0:T(8,128)S(1)} %add_add_fusion.1), channel_id=1, source_target_pairs={{0,4},{4,0},{8,12},{12,8},{16,20},{20,16},{24,28},{28,24},{1,5},{5... | collective-permute-start | bytes 196616 | tf_op jit(solution)/shard_map/ppermute | solution.py:145
  20.8 2.5 %shard_map.87 = (f32[64,1280]{1,0:T(8,128)}, f32[1,1280]{1,0:T(1,128)}) custom-call(f32[8,1280]{1,0:T(8,128)S(1)} %convert_add_fusion.refs_0_, bf16[80,1280]{1,0:T(8,128)(2,1)S(1)} %get-tuple-element.63.refs_1_, bf16[80,1024]{1,0:T(8,128)(2,1)S(1)} %get-tuple-element.47.refs_2_, ...), custom_call_target="tpu_custom_call", output_to_operand_aliasing={{0}: (4, {}), {1}: (5, {})} | custom-call | flops 134217728 | bytes 1048576 | tf_op jit(solution)/shard_map/pallas_call | solution.py:177
  23.2 0.0 collective-permute-done.8
  23.3 0.8 %collective-permute-done.7 = f32[64,256]{1,0:T(8,128)S(1)} collective-permute-done((f32[64,256]{1,0:T(8,128)S(1)}, f32[64,256]{1,0:T(8,128)S(1)}, u32[]{:S(2)}, u32[]{:S(2)}) %collective-permute-start.7) | collective-permute-done | bytes 65568 | tf_op jit(solution)/shard_map/ppermute | solution.py:145
  24.0 0.4 %collective-permute-done.6 = f32[64,256]{1,0:T(8,128)S(1)} collective-permute-done((f32[64,256]{1,0:T(8,128)S(1)}, f32[64,256]{1,0:T(8,128)S(1)}, u32[]{:S(2)}, u32[]{:S(2)}) %collective-permute-start.6) | collective-permute-done | bytes 65568 | tf_op jit(solution)/shard_map/ppermute | solution.py:145
  24.5 2.7 %collective-permute-start.9 = (f32[64,256]{1,0:T(8,128)S(1)}, f32[64,256]{1,0:T(8,128)S(1)}, u32[]{:S(2)}, u32[]{:S(2)}) collective-permute-start(f32[64,256]{1,0:T(8,128)S(1)} %add_add_fusion), channel_id=1, source_target_pairs={{0,16},{4,20},{8,24},{12,28},{16,0},{20,4},{24,8},{28,12},{1,17},{... | collective-permute-start | bytes 196616 | tf_op jit(solution)/shard_map/ppermute | solution.py:145
  27.2 2.1 %shard_map.88 = (f32[64,1280]{1,0:T(8,128)}, f32[1,1280]{1,0:T(1,128)}) custom-call(f32[8,1280]{1,0:T(8,128)S(1)} %convert_add_fusion.refs_0_, bf16[80,1280]{1,0:T(8,128)(2,1)S(1)} %get-tuple-element.63.refs_1_, bf16[80,1024]{1,0:T(8,128)(2,1)S(1)} %get-tuple-element.47.refs_2_, ...), custom_call_target="tpu_custom_call", output_to_operand_aliasing={{0}: (4, {}), {1}: (5, {})} | custom-call | flops 67108864 | bytes 524288 | tf_op jit(solution)/shard_map/pallas_call | solution.py:177
  29.3 0.4 %collective-permute-done.9 = f32[64,256]{1,0:T(8,128)S(1)} collective-permute-done((f32[64,256]{1,0:T(8,128)S(1)}, f32[64,256]{1,0:T(8,128)S(1)}, u32[]{:S(2)}, u32[]{:S(2)}) %collective-permute-start.9) | collective-permute-done | bytes 65568 | tf_op jit(solution)/shard_map/ppermute | solution.py:145
  29.7 0.6 %add.35 = f32[64,256]{1,0:T(8,128)} add(f32[64,256]{1,0:T(8,128)S(1)} %add_add_fusion, f32[64,256]{1,0:T(8,128)S(1)} %collective-permute-done.9) | non-fusion elementwise | flops 16384 | bytes 196608 | tf_op jit(solution)/shard_map/add | solution.py:208
  (3 shorter events, 0.0 us)
Async XLA Ops:
  0.6 5.6 %collective-permute-start = (bf16[64,256]{1,0:T(8,128)(2,1)}, bf16[64,256]{1,0:T(8,128)(2,1)S(1)}, u32[]{:S(2)}, u32[]{:S(2)}) collective-permute-start(bf16[64,256]{1,0:T(8,128)(2,1)} %param.7), channel_id=1, source_target_pairs={{0,1},{1,0},{2,3},{3,2},{4,5},{5,4},{6,7},{7,6},{8,9},{9,8},{10,11... | collective-permute-start | bytes 98312 | tf_op jit(solution)/shard_map/ppermute | solution.py:145
  1.1 5.1 %collective-permute-start.2 = (bf16[64,256]{1,0:T(8,128)(2,1)}, bf16[64,256]{1,0:T(8,128)(2,1)S(1)}, u32[]{:S(2)}, u32[]{:S(2)}) collective-permute-start(bf16[64,256]{1,0:T(8,128)(2,1)} %param.7), channel_id=1, source_target_pairs={{0,3},{1,2},{2,1},{3,0},{4,7},{5,6},{6,5},{7,4},{8,11},{9,10},{10,... | collective-permute-start | bytes 98312 | tf_op jit(solution)/shard_map/ppermute | solution.py:145
  3.8 4.1 %collective-permute-start.1 = (bf16[64,256]{1,0:T(8,128)(2,1)}, bf16[64,256]{1,0:T(8,128)(2,1)S(1)}, u32[]{:S(2)}, u32[]{:S(2)}) collective-permute-start(bf16[64,256]{1,0:T(8,128)(2,1)} %param.7), channel_id=1, source_target_pairs={{0,2},{1,3},{2,0},{3,1},{4,6},{5,7},{6,4},{7,5},{8,10},{9,11},{10,... | collective-permute-start | bytes 98312 | tf_op jit(solution)/shard_map/ppermute | solution.py:145
  11.6 4.4 %collective-permute-start.3 = (f32[64,256]{1,0:T(8,128)S(1)}, f32[64,256]{1,0:T(8,128)S(1)}, u32[]{:S(2)}, u32[]{:S(2)}) collective-permute-start(f32[64,256]{1,0:T(8,128)S(1)} %get-tuple-element.43), channel_id=1, source_target_pairs={{0,1},{1,0},{2,3},{3,2},{4,5},{5,4},{6,7},{7,6},{8,9},{9,8},{10,11... | collective-permute-start | bytes 196616 | tf_op jit(solution)/shard_map/ppermute | solution.py:145
  11.7 5.0 %collective-permute-start.4 = (f32[64,256]{1,0:T(8,128)S(1)}, f32[64,256]{1,0:T(8,128)S(1)}, u32[]{:S(2)}, u32[]{:S(2)}) collective-permute-start(f32[64,256]{1,0:T(8,128)S(1)} %get-tuple-element.44), channel_id=1, source_target_pairs={{0,2},{1,3},{2,0},{3,1},{4,6},{5,7},{6,4},{7,5},{8,10},{9,11},{10,... | collective-permute-start | bytes 196616 | tf_op jit(solution)/shard_map/ppermute | solution.py:145
  12.2 5.0 %collective-permute-start.5 = (f32[64,256]{1,0:T(8,128)S(1)}, f32[64,256]{1,0:T(8,128)S(1)}, u32[]{:S(2)}, u32[]{:S(2)}) collective-permute-start(f32[64,256]{1,0:T(8,128)S(1)} %get-tuple-element.45), channel_id=1, source_target_pairs={{0,3},{1,2},{2,1},{3,0},{4,7},{5,6},{6,5},{7,4},{8,11},{9,10},{10,... | collective-permute-start | bytes 196616 | tf_op jit(solution)/shard_map/ppermute | solution.py:145
  17.2 6.1 %collective-permute-start.8 = (f32[64,256]{1,0:T(8,128)S(1)}, f32[64,256]{1,0:T(8,128)S(1)}, u32[]{:S(2)}, u32[]{:S(2)}) collective-permute-start(f32[64,256]{1,0:T(8,128)S(1)} %add_add_fusion.1), channel_id=1, source_target_pairs={{0,12},{4,8},{8,4},{12,0},{16,28},{20,24},{24,20},{28,16},{1,13},{... | collective-permute-start | bytes 196616 | tf_op jit(solution)/shard_map/ppermute | solution.py:145
  19.8 4.3 %collective-permute-start.7 = (f32[64,256]{1,0:T(8,128)S(1)}, f32[64,256]{1,0:T(8,128)S(1)}, u32[]{:S(2)}, u32[]{:S(2)}) collective-permute-start(f32[64,256]{1,0:T(8,128)S(1)} %add_add_fusion.1), channel_id=1, source_target_pairs={{0,8},{4,12},{8,0},{12,4},{16,24},{20,28},{24,16},{28,20},{1,9},{5... | collective-permute-start | bytes 196616 | tf_op jit(solution)/shard_map/ppermute | solution.py:145
  20.2 4.3 %collective-permute-start.6 = (f32[64,256]{1,0:T(8,128)S(1)}, f32[64,256]{1,0:T(8,128)S(1)}, u32[]{:S(2)}, u32[]{:S(2)}) collective-permute-start(f32[64,256]{1,0:T(8,128)S(1)} %add_add_fusion.1), channel_id=1, source_target_pairs={{0,4},{4,0},{8,12},{12,8},{16,20},{20,16},{24,28},{28,24},{1,5},{5... | collective-permute-start | bytes 196616 | tf_op jit(solution)/shard_map/ppermute | solution.py:145
  24.5 5.2 %collective-permute-start.9 = (f32[64,256]{1,0:T(8,128)S(1)}, f32[64,256]{1,0:T(8,128)S(1)}, u32[]{:S(2)}, u32[]{:S(2)}) collective-permute-start(f32[64,256]{1,0:T(8,128)S(1)} %add_add_fusion), channel_id=1, source_target_pairs={{0,16},{4,20},{8,24},{12,28},{16,0},{20,4},{24,8},{28,12},{1,17},{... | collective-permute-start | bytes 196616 | tf_op jit(solution)/shard_map/ppermute | solution.py:145

commit v10 on v9

--- a/solution.py
+++ b/solution.py
@@ -94,7 +94,7 @@
         grad_shift[:, j * LANES : (j + 1) * LANES] = tile
     for k in range(parts):
         start = pl.multiple_of((me ^ k) * width, width)
-        outs[k][...] = grad_shift[:, pl.ds(start, width)]
+        outs[k][...] = grad_shift[:, pl.ds(start, width)].astype(outs[k].dtype)
 
 
 def load_kernel(lats, first, chunk, step, *refs):
@@ -154,7 +154,7 @@
     early = 3 * chunk
     *outs, load_ext, shifted = pl.pallas_call(
         functools.partial(shift_kernel, neuron_count, "neuron", chunk, step, early),
-        out_shape=[jax.ShapeDtypeStruct((lats, width), F32)] * neuron_count
+        out_shape=[jax.ShapeDtypeStruct((lats, width), BF16 if k else F32) for k in range(neuron_count)]
         + [jax.ShapeDtypeStruct((lats + EXTRA, neurons), BF16), jax.ShapeDtypeStruct((lats + EXTRA, total), BF16)],
         in_specs=[vmem, vmem, hbm] + [vmem] * (neuron_count - 1),
         out_specs=[vmem] * (neuron_count + 2),
@@ -197,16 +197,21 @@
     outs, made = make(outs)
     arrived = [swap(outs[k], "neuron", neuron_count, k) for k in range(1, neuron_count)]
     arrived, made = lax.optimization_barrier((arrived, made))
-    value = functools.reduce(jnp.add, [outs[0]] + arrived)
+    value = functools.reduce(jnp.add, [outs[0]] + [block.astype(F32) for block in arrived])
     mask = 1
     while mask < region_count:
         masks = [mask, 2 * mask, 3 * mask] if 2 * mask < region_count else [mask]
+        several = len(masks) > 1
+        if several:
+            value = lax.reduce_precision(value, 8, 7)
+        sent = value.astype(BF16) if several else value
         if shares:
-            value, made = make(value)
-        arrived = [swap(value, "region", region_count, k) for k in masks]
+            (value, sent), made = make((value, sent))
+        arrived = [swap(sent, "region", region_count, k) for k in masks]
         arrived, made = lax.optimization_barrier((arrived, made))
+        arrived = [block.astype(F32) for block in arrived]
         value = value + arrived[0]
-        if len(masks) == 3:
+        if several:
             value = value + (arrived[1] + arrived[2])
         mask *= 1 + len(masks)
     grad_load, grad_bias = made

time: 30.7 us -> 29.3 us (0.954)
  waiting for transfers between devices: 4.42 us -> 2.99 us
    ppermute x10, waiting for transfers between devices: 4.42 us -> 2.99 us  [swap(): return lax.ppermute(value, axis, [(i, i ^ mask) for i in range(count)])]
  transfers between devices with their start and end apart: 10 -> 10, of which waited for: 6 -> 4; matrix products, arithmetic and copies ran while one was open for 6% -> 6% of each run, Pallas kernels for 23% -> 24%
where the time goes in v10:
time: 29.3 us; the launch traced here: 29 us
  starting transfers between devices  11.3 us (39%)
  Pallas kernels  10.8 us (37%)
  waiting for transfers between devices  2.99 us (10%)
  other arithmetic  2.42 us (8%)
  between operations  1.39 us (5%)
    ppermute x10, starting transfers between devices, swap(): return lax.ppermute(value, axis, [(i, i ^ mask) for i in range(count)])  11.3 us
    pallas_call x3, Pallas kernels, make(): pl.pallas_call(functools.partial(load_kernel, lats, first, chunk, step),...  7.1 us
    pallas_call x1, Pallas kernels, per_device(): pl.pallas_call(functools.partial(shift_kernel, neuron_count, 'neuron', ch...  3.72 us
    ppermute x10, waiting for transfers between devices, swap(): return lax.ppermute(value, axis, [(i, i ^ mask) for i in range(count)])  2.99 us
    concatenate x1, other arithmetic, per_device(): pack = jnp.concatenate([loadings[0], latents], axis=1)  0.95 us
    add x1, other arithmetic, per_device(): meta = jnp.pad(bias, ((0, 7), (0, 0))) + lines.astype(F32)  0.78 us
    add x1, other arithmetic, per_device(): value = value + arrived[0]  0.64 us
  transfers between devices with their start and end apart: 10, of which 4 were waited for; matrix products, arithmetic and copies ran while one was open for 6% of the time, Pallas kernels for 24%

profile of v10, /device:TPU:0, one launch (start us, length us, event | category | flops | bytes accessed | tf_op | source)
XLA Modules:
  0.0 29.0 jit_solution(2241676652238169390)
XLA Ops:
  0.6 0.5 %collective-permute-start = (bf16[64,256]{1,0:T(8,128)(2,1)}, bf16[64,256]{1,0:T(8,128)(2,1)S(1)}, u32[]{:S(2)}, u32[]{:S(2)}) collective-permute-start(bf16[64,256]{1,0:T(8,128)(2,1)} %param.7), channel_id=1, source_target_pairs={{0,1},{1,0},{2,3},{3,2},{4,5},{5,4},{6,7},{7,6},{8,9},{9,8},{10,11... | collective-permute-start | bytes 98312 | tf_op jit(solution)/shard_map/ppermute | solution.py:145
  1.1 2.6 %collective-permute-start.2 = (bf16[64,256]{1,0:T(8,128)(2,1)}, bf16[64,256]{1,0:T(8,128)(2,1)S(1)}, u32[]{:S(2)}, u32[]{:S(2)}) collective-permute-start(bf16[64,256]{1,0:T(8,128)(2,1)} %param.7), channel_id=1, source_target_pairs={{0,3},{1,2},{2,1},{3,0},{4,7},{5,6},{6,5},{7,4},{8,11},{9,10},{10,... | collective-permute-start | bytes 98312 | tf_op jit(solution)/shard_map/ppermute | solution.py:145
  3.8 0.0 collective-permute-start.1
  4.5 0.8 %convert_add_fusion.refs_0_ = f32[8,1280]{1,0:T(8,128)S(1)} fusion(s32[1,64]{1,0:T(1,128)} %param.10, f32[1,1280]{1,0:T(1,128)} %param.9, s32[]{:T(128)} %bitcast.4, pred[8]{0:T(512)(128)(4,1)S(1)} %iota_compare_fusion), kind=kLoop, calls=%fused_computation.3 | loop fusion | flops 30720 | bytes 46348 | tf_op jit(solution)/shard_map/add | solution.py:152
  5.3 0.9 %pad_maximum_fusion.refs_1_ = bf16[64,1536]{1,0:T(8,128)(2,1)S(1)} fusion(bf16[64,256]{1,0:T(8,128)(2,1)} %param.7, bf16[64,1280]{1,0:T(8,128)(2,1)} %bitcast.10), kind=kLoop, calls=%fused_computation | loop fusion | flops 393216 | bytes 393216 | tf_op jit(solution)/shard_map/concatenate | solution.py:148
  6.2 0.0 collective-permute-done.refs_3_
  6.2 0.0 collective-permute-done.2.refs_5_
  6.3 1.7 %collective-permute-done.1.refs_4_ = bf16[64,256]{1,0:T(8,128)(2,1)S(1)} collective-permute-done((bf16[64,256]{1,0:T(8,128)(2,1)}, bf16[64,256]{1,0:T(8,128)(2,1)S(1)}, u32[]{:S(2)}, u32[]{:S(2)}) %collective-permute-start.1) | collective-permute-done | bytes 32800 | tf_op jit(solution)/shard_map/ppermute | solution.py:145
  7.9 3.7 %shard_map.85 = (f32[64,256]{1,0:T(8,128)S(1)}, bf16[64,256]{1,0:T(8,128)(2,1)S(1)}, bf16[64,256]{1,0:T(8,128)(2,1)S(1)}, bf16[64,256]{1,0:T(8,128)(2,1)S(1)}, b...) custom-call(f32[8,1280]{1,0:T(8,128)S(1)} %convert_add_fusion.refs_0_, ...), custom_call_target="tpu_custom_call" | custom-call | tf_op jit(solution)/shard_map/pallas_call | solution.py:155
  11.6 0.1 collective-permute-start.3
  11.7 0.5 %collective-permute-start.4 = (bf16[64,256]{1,0:T(8,128)(2,1)S(1)}, bf16[64,256]{1,0:T(8,128)(2,1)S(1)}, u32[]{:S(2)}, u32[]{:S(2)}) collective-permute-start(bf16[64,256]{1,0:T(8,128)(2,1)S(1)} %get-tuple-element.46), channel_id=1, source_target_pairs={{0,2},{1,3},{2,0},{3,1},{4,6},{5,7},{6,4},{7,5},{8,10},{9,11},{10,... | collective-permute-start | bytes 98312 | tf_op jit(solution)/shard_map/ppermute | solution.py:145
  12.2 1.4 %collective-permute-start.5 = (bf16[64,256]{1,0:T(8,128)(2,1)S(1)}, bf16[64,256]{1,0:T(8,128)(2,1)S(1)}, u32[]{:S(2)}, u32[]{:S(2)}) collective-permute-start(bf16[64,256]{1,0:T(8,128)(2,1)S(1)} %get-tuple-element.47), channel_id=1, source_target_pairs={{0,3},{1,2},{2,1},{3,0},{4,7},{5,6},{6,5},{7,4},{8,11},{9,10},{10,... | collective-permute-start | bytes 98312 | tf_op jit(solution)/shard_map/ppermute | solution.py:145
  13.6 2.5 %shard_map.86 = (f32[64,1280]{1,0:T(8,128)}, f32[1,1280]{1,0:T(1,128)}) custom-call(f32[8,1280]{1,0:T(8,128)S(1)} %convert_add_fusion.refs_0_, bf16[80,1280]{1,0:T(8,128)(2,1)S(1)} %get-tuple-element.67.refs_1_, bf16[80,1024]{1,0:T(8,128)(2,1)S(1)} %get-tuple-element.49.refs_2_, bf16[1280,1024]{1,0:T(8,128)(2,1)} %bitcast.6), custom_call_target="tpu_custom_call" | custom-call | flops 134217728 | bytes 1048576 | tf_op jit(solution)/shard_map/pallas_call | solution.py:177
  16.1 0.0 collective-permute-done.3
  16.1 0.0 collective-permute-done.4
  16.1 0.0 collective-permute-done.5
  16.1 2.6 %collective-permute-start.8 = (bf16[64,256]{1,0:T(8,128)(2,1)S(1)}, bf16[64,256]{1,0:T(8,128)(2,1)S(1)}, u32[]{:S(2)}, u32[]{:S(2)}) collective-permute-start(bf16[64,256]{1,0:T(8,128)(2,1)S(1)} %get-tuple-element.56), channel_id=1, source_target_pairs={{0,12},{4,8},{8,4},{12,0},{16,28},{20,24},{24,20},{28,16},{1,13},{... | collective-permute-start | bytes 98312 | tf_op jit(solution)/shard_map/ppermute | solution.py:145
  18.7 0.4 %collective-permute-start.7 = (bf16[64,256]{1,0:T(8,128)(2,1)S(1)}, bf16[64,256]{1,0:T(8,128)(2,1)S(1)}, u32[]{:S(2)}, u32[]{:S(2)}) collective-permute-start(bf16[64,256]{1,0:T(8,128)(2,1)S(1)} %get-tuple-element.56), channel_id=1, source_target_pairs={{0,8},{4,12},{8,0},{12,4},{16,24},{20,28},{24,16},{28,20},{1,9},{5... | collective-permute-start | bytes 98312 | tf_op jit(solution)/shard_map/ppermute | solution.py:145
  19.2 0.5 %collective-permute-start.6 = (bf16[64,256]{1,0:T(8,128)(2,1)S(1)}, bf16[64,256]{1,0:T(8,128)(2,1)S(1)}, u32[]{:S(2)}, u32[]{:S(2)}) collective-permute-start(bf16[64,256]{1,0:T(8,128)(2,1)S(1)} %get-tuple-element.56), channel_id=1, source_target_pairs={{0,4},{4,0},{8,12},{12,8},{16,20},{20,16},{24,28},{28,24},{1,5},{5... | collective-permute-start | bytes 98312 | tf_op jit(solution)/shard_map/ppermute | solution.py:145
  19.7 2.5 %shard_map.87 = (f32[64,1280]{1,0:T(8,128)}, f32[1,1280]{1,0:T(1,128)}) custom-call(f32[8,1280]{1,0:T(8,128)S(1)} %convert_add_fusion.refs_0_, bf16[80,1280]{1,0:T(8,128)(2,1)S(1)} %get-tuple-element.67.refs_1_, bf16[80,1024]{1,0:T(8,128)(2,1)S(1)} %get-tuple-element.49.refs_2_, ...), custom_call_target="tpu_custom_call", output_to_operand_aliasing={{0}: (4, {}), {1}: (5, {})} | custom-call | flops 134217728 | bytes 1048576 | tf_op jit(solution)/shard_map/pallas_call | solution.py:177
  22.2 0.0 collective-permute-done.8
  22.2 0.4 %collective-permute-done.7 = bf16[64,256]{1,0:T(8,128)(2,1)S(1)} collective-permute-done((bf16[64,256]{1,0:T(8,128)(2,1)S(1)}, bf16[64,256]{1,0:T(8,128)(2,1)S(1)}, u32[]{:S(2)}, u32[]{:S(2)}) %collective-permute-start.7) | collective-permute-done | bytes 32800 | tf_op jit(solution)/shard_map/ppermute | solution.py:145
  22.6 0.4 %collective-permute-done.6 = bf16[64,256]{1,0:T(8,128)(2,1)S(1)} collective-permute-done((bf16[64,256]{1,0:T(8,128)(2,1)S(1)}, bf16[64,256]{1,0:T(8,128)(2,1)S(1)}, u32[]{:S(2)}, u32[]{:S(2)}) %collective-permute-start.6) | collective-permute-done | bytes 32800 | tf_op jit(solution)/shard_map/ppermute | solution.py:145
  23.1 2.7 %collective-permute-start.9 = (f32[64,256]{1,0:T(8,128)S(1)}, f32[64,256]{1,0:T(8,128)S(1)}, u32[]{:S(2)}, u32[]{:S(2)}) collective-permute-start(f32[64,256]{1,0:T(8,128)S(1)} %add_add_fusion), channel_id=1, source_target_pairs={{0,16},{4,20},{8,24},{12,28},{16,0},{20,4},{24,8},{28,12},{1,17},{... | collective-permute-start | bytes 196616 | tf_op jit(solution)/shard_map/ppermute | solution.py:145
  25.8 2.1 %shard_map.88 = (f32[64,1280]{1,0:T(8,128)}, f32[1,1280]{1,0:T(1,128)}) custom-call(f32[8,1280]{1,0:T(8,128)S(1)} %convert_add_fusion.refs_0_, bf16[80,1280]{1,0:T(8,128)(2,1)S(1)} %get-tuple-element.67.refs_1_, bf16[80,1024]{1,0:T(8,128)(2,1)S(1)} %get-tuple-element.49.refs_2_, ...), custom_call_target="tpu_custom_call", output_to_operand_aliasing={{0}: (4, {}), {1}: (5, {})} | custom-call | flops 67108864 | bytes 524288 | tf_op jit(solution)/shard_map/pallas_call | solution.py:177
  27.9 0.4 %collective-permute-done.9 = f32[64,256]{1,0:T(8,128)S(1)} collective-permute-done((f32[64,256]{1,0:T(8,128)S(1)}, f32[64,256]{1,0:T(8,128)S(1)}, u32[]{:S(2)}, u32[]{:S(2)}) %collective-permute-start.9) | collective-permute-done | bytes 65568 | tf_op jit(solution)/shard_map/ppermute | solution.py:145
  28.3 0.6 %add.35 = f32[64,256]{1,0:T(8,128)} add(f32[64,256]{1,0:T(8,128)S(1)} %add_add_fusion, f32[64,256]{1,0:T(8,128)S(1)} %collective-permute-done.9) | non-fusion elementwise | flops 16384 | bytes 196608 | tf_op jit(solution)/shard_map/add | solution.py:213
  (3 shorter events, 0.0 us)
Async XLA Ops:
  0.6 5.6 %collective-permute-start = (bf16[64,256]{1,0:T(8,128)(2,1)}, bf16[64,256]{1,0:T(8,128)(2,1)S(1)}, u32[]{:S(2)}, u32[]{:S(2)}) collective-permute-start(bf16[64,256]{1,0:T(8,128)(2,1)} %param.7), channel_id=1, source_target_pairs={{0,1},{1,0},{2,3},{3,2},{4,5},{5,4},{6,7},{7,6},{8,9},{9,8},{10,11... | collective-permute-start | bytes 98312 | tf_op jit(solution)/shard_map/ppermute | solution.py:145
  1.1 5.1 %collective-permute-start.2 = (bf16[64,256]{1,0:T(8,128)(2,1)}, bf16[64,256]{1,0:T(8,128)(2,1)S(1)}, u32[]{:S(2)}, u32[]{:S(2)}) collective-permute-start(bf16[64,256]{1,0:T(8,128)(2,1)} %param.7), channel_id=1, source_target_pairs={{0,3},{1,2},{2,1},{3,0},{4,7},{5,6},{6,5},{7,4},{8,11},{9,10},{10,... | collective-permute-start | bytes 98312 | tf_op jit(solution)/shard_map/ppermute | solution.py:145
  3.8 4.1 %collective-permute-start.1 = (bf16[64,256]{1,0:T(8,128)(2,1)}, bf16[64,256]{1,0:T(8,128)(2,1)S(1)}, u32[]{:S(2)}, u32[]{:S(2)}) collective-permute-start(bf16[64,256]{1,0:T(8,128)(2,1)} %param.7), channel_id=1, source_target_pairs={{0,2},{1,3},{2,0},{3,1},{4,6},{5,7},{6,4},{7,5},{8,10},{9,11},{10,... | collective-permute-start | bytes 98312 | tf_op jit(solution)/shard_map/ppermute | solution.py:145
  11.6 4.4 %collective-permute-start.3 = (bf16[64,256]{1,0:T(8,128)(2,1)S(1)}, bf16[64,256]{1,0:T(8,128)(2,1)S(1)}, u32[]{:S(2)}, u32[]{:S(2)}) collective-permute-start(bf16[64,256]{1,0:T(8,128)(2,1)S(1)} %get-tuple-element.45), channel_id=1, source_target_pairs={{0,1},{1,0},{2,3},{3,2},{4,5},{5,4},{6,7},{7,6},{8,9},{9,8},{10,11... | collective-permute-start | bytes 98312 | tf_op jit(solution)/shard_map/ppermute | solution.py:145
  11.7 4.4 %collective-permute-start.4 = (bf16[64,256]{1,0:T(8,128)(2,1)S(1)}, bf16[64,256]{1,0:T(8,128)(2,1)S(1)}, u32[]{:S(2)}, u32[]{:S(2)}) collective-permute-start(bf16[64,256]{1,0:T(8,128)(2,1)S(1)} %get-tuple-element.46), channel_id=1, source_target_pairs={{0,2},{1,3},{2,0},{3,1},{4,6},{5,7},{6,4},{7,5},{8,10},{9,11},{10,... | collective-permute-start | bytes 98312 | tf_op jit(solution)/shard_map/ppermute | solution.py:145
  12.2 3.9 %collective-permute-start.5 = (bf16[64,256]{1,0:T(8,128)(2,1)S(1)}, bf16[64,256]{1,0:T(8,128)(2,1)S(1)}, u32[]{:S(2)}, u32[]{:S(2)}) collective-permute-start(bf16[64,256]{1,0:T(8,128)(2,1)S(1)} %get-tuple-element.47), channel_id=1, source_target_pairs={{0,3},{1,2},{2,1},{3,0},{4,7},{5,6},{6,5},{7,4},{8,11},{9,10},{10,... | collective-permute-start | bytes 98312 | tf_op jit(solution)/shard_map/ppermute | solution.py:145
  16.1 6.1 %collective-permute-start.8 = (bf16[64,256]{1,0:T(8,128)(2,1)S(1)}, bf16[64,256]{1,0:T(8,128)(2,1)S(1)}, u32[]{:S(2)}, u32[]{:S(2)}) collective-permute-start(bf16[64,256]{1,0:T(8,128)(2,1)S(1)} %get-tuple-element.56), channel_id=1, source_target_pairs={{0,12},{4,8},{8,4},{12,0},{16,28},{20,24},{24,20},{28,16},{1,13},{... | collective-permute-start | bytes 98312 | tf_op jit(solution)/shard_map/ppermute | solution.py:145
  18.7 3.9 %collective-permute-start.7 = (bf16[64,256]{1,0:T(8,128)(2,1)S(1)}, bf16[64,256]{1,0:T(8,128)(2,1)S(1)}, u32[]{:S(2)}, u32[]{:S(2)}) collective-permute-start(bf16[64,256]{1,0:T(8,128)(2,1)S(1)} %get-tuple-element.56), channel_id=1, source_target_pairs={{0,8},{4,12},{8,0},{12,4},{16,24},{20,28},{24,16},{28,20},{1,9},{5... | collective-permute-start | bytes 98312 | tf_op jit(solution)/shard_map/ppermute | solution.py:145
  19.2 3.9 %collective-permute-start.6 = (bf16[64,256]{1,0:T(8,128)(2,1)S(1)}, bf16[64,256]{1,0:T(8,128)(2,1)S(1)}, u32[]{:S(2)}, u32[]{:S(2)}) collective-permute-start(bf16[64,256]{1,0:T(8,128)(2,1)S(1)} %get-tuple-element.56), channel_id=1, source_target_pairs={{0,4},{4,0},{8,12},{12,8},{16,20},{20,16},{24,28},{28,24},{1,5},{5... | collective-permute-start | bytes 98312 | tf_op jit(solution)/shard_map/ppermute | solution.py:145
  23.1 5.2 %collective-permute-start.9 = (f32[64,256]{1,0:T(8,128)S(1)}, f32[64,256]{1,0:T(8,128)S(1)}, u32[]{:S(2)}, u32[]{:S(2)}) collective-permute-start(f32[64,256]{1,0:T(8,128)S(1)} %add_add_fusion), channel_id=1, source_target_pairs={{0,16},{4,20},{8,24},{12,28},{16,0},{20,4},{24,8},{28,12},{1,17},{... | collective-permute-start | bytes 196616 | tf_op jit(solution)/shard_map/ppermute | solution.py:145

commit v11 on v10

--- a/solution.py
+++ b/solution.py
@@ -15,22 +15,13 @@
 
 def shift_tiles(tiles, delay, forward):
     lane = lax.broadcasted_iota(jnp.int32, delay.shape, 1)
-    nothing = jnp.zeros_like(tiles[0])
-    for level in range(7):
-        amount = 1 << level
-        chosen = (delay & amount) != 0
-        if forward:
-            turned = [pltpu.roll(tile, amount, 1) for tile in tiles]
-            before = [nothing] + turned[:-1]
-            moved = [jnp.where(lane < amount, b, t) for b, t in zip(before, turned)]
-        else:
-            turned = [pltpu.roll(tile, LANES - amount, 1) for tile in tiles]
-            after = turned[1:] + [nothing]
-            moved = [jnp.where(lane < LANES - amount, t, a) for t, a in zip(turned, after)]
-        tiles = [jnp.where(chosen, m, tile) for m, tile in zip(moved, tiles)]
-    chosen = delay >= LANES
-    other = [nothing] + tiles[:-1] if forward else tiles[1:] + [nothing]
-    return [jnp.where(chosen, o, tile) for o, tile in zip(other, tiles)]
+    source = lane - delay if forward else lane + delay
+    inside = source >= 0 if forward else source < LANES
+    source = source & (LANES - 1)
+    turned = [jnp.take_along_axis(tile, source, axis=1, mode="promise_in_bounds") for tile in tiles]
+    nothing = [jnp.zeros_like(tiles[0])]
+    others = nothing + turned[:-1] if forward else turned[1:] + nothing
+    return [jnp.where(inside, tile, other) for tile, other in zip(turned, others)]
 
 
 def expected(load_part, piece):
@@ -73,7 +64,6 @@
     below = jnp.where(row == 0, high, jnp.where(row == 1, middle, jnp.where(row == 2, low, 0.0)))
     load_ext[lats:, :] = below.astype(BF16)
 
-    bins = lax.broadcasted_iota(jnp.int32, (1, total), 1)
     blocks = [
         (slice(first, first + chunk), slice(begin, begin + step))
         for first in range(0, neurons, chunk)
@@ -85,11 +75,15 @@
     counts_copy.wait()
     for rows, span in blocks:
         rate = held[rows, span] if rows.start < early else expected(load_ext[:, rows], shifted[:, span])
-        resid = jnp.where(bins[:, span] < length, rate - counts_ref[rows, span].astype(F32), 0.0)
+        resid = rate - counts_ref[rows, span].astype(F32)
         part = jnp.dot(load_ext[0:lats, rows], resid.astype(BF16), preferred_element_type=F32)
         grad_shift[:, span] = part if rows.start == 0 else grad_shift[:, span] + part
 
-    tiles = [grad_shift[:, j * LANES : (j + 1) * LANES] for j in range(total // LANES)]
+    bins = lax.broadcasted_iota(jnp.int32, (1, total), 1)
+    tiles = []
+    for j in range(total // LANES):
+        span = slice(j * LANES, (j + 1) * LANES)
+        tiles.append(jnp.where(bins[:, span] < length, grad_shift[:, span], 0.0))
     for j, tile in enumerate(shift_tiles(tiles, delay, False)):
         grad_shift[:, j * LANES : (j + 1) * LANES] = tile
     for k in range(parts):
@@ -106,29 +100,31 @@
     counts_copy.start()
     length = meta_ref[2:3, 0:1].astype(jnp.int32)
     bins = lax.broadcasted_iota(jnp.int32, (1, total), 1)
-    blocks = [(begin, at) for begin in range(0, count, chunk) for at in range(0, total, step)]
-    for begin, at in blocks:
-        rows, span = slice(begin, begin + chunk), slice(at, at + step)
-        held[rows, span] = expected(load_ext[:, first + begin : first + begin + chunk], shifted[:, span])
+    blocks = [(slice(begin, begin + chunk), range(0, total, step)) for begin in range(0, count, chunk)]
+    for rows, starts in blocks:
+        for at in starts:
+            load_part = load_ext[:, first + rows.start : first + rows.stop]
+            held[rows, at : at + step] = expected(load_part, shifted[:, at : at + step])
     counts_copy.wait()
-    for begin, at in blocks:
-        rows, span = slice(begin, begin + chunk), slice(at, at + step)
-        resid = jnp.where(bins[:, span] < length, held[rows, span] - counts_ref[rows, span].astype(F32), 0.0)
-        sums = resid[:, 0:LANES]
-        for j in range(1, step // LANES):
-            sums = sums + resid[:, j * LANES : (j + 1) * LANES]
-        line = jnp.sum(sums.T, axis=0, keepdims=True)
-        part = lax.dot_general(
-            shifted[0:lats, span], resid.astype(BF16), (((1,), (1,)), ((), ())), preferred_element_type=F32
-        )
-        load_ref[:, rows] = part if at == 0 else load_ref[:, rows] + part
-        bias_ref[:, rows] = line if at == 0 else bias_ref[:, rows] + line
-    outward = [
-        pltpu.make_async_copy(load_ref, load_hbm.at[:, place], sems.at[1]),
-        pltpu.make_async_copy(bias_ref, bias_hbm.at[:, place], sems.at[2]),
-    ]
-    for copy in outward:
-        copy.start()
+    outward = []
+    for index, (rows, starts) in enumerate(blocks):
+        sums = jnp.zeros((chunk, LANES), F32)
+        grad = jnp.zeros((chunk, lats), F32)
+        for at in starts:
+            span = slice(at, at + step)
+            resid = jnp.where(bins[:, span] < length, held[rows, span] - counts_ref[rows, span].astype(F32), 0.0)
+            for j in range(step // LANES):
+                sums = sums + resid[:, j * LANES : (j + 1) * LANES]
+            grad = grad + lax.dot_general(
+                resid.astype(BF16), shifted[0:lats, span], (((1,), (1,)), ((), ())), preferred_element_type=F32
+            )
+        load_ref[:, rows] = grad.T
+        bias_ref[:, rows] = jnp.sum(sums.T, axis=0, keepdims=True)
+        place = pl.ds(first + rows.start, chunk)
+        outward.append(pltpu.make_async_copy(load_ref.at[:, rows], load_hbm.at[:, place], sems.at[2 * index + 1]))
+        outward.append(pltpu.make_async_copy(bias_ref.at[:, rows], bias_hbm.at[:, place], sems.at[2 * index + 2]))
+        for copy in outward[-2:]:
+            copy.start()
     for copy in outward:
         copy.wait()
 
@@ -144,17 +140,22 @@
     def swap(value, axis, count, mask):
         return lax.ppermute(value, axis, [(i, i ^ mask) for i in range(count)])
 
-    arrived = [swap(latents, "neuron", neuron_count, k) for k in range(1, neuron_count)]
+    held = {0: latents}
+    masks = [1 << level for level in range(1, neuron_count.bit_length() - 1)] + [1]
+    for mask in masks:
+        for k, block in list(held.items()):
+            held[k ^ mask] = swap(block, "neuron", neuron_count, mask)
+    arrived = [held[k] for k in range(1, neuron_count)]
     pack = jnp.concatenate([loadings[0], latents], axis=1)
     row = lax.broadcasted_iota(jnp.int32, (8, neurons), 0)
     lines = jnp.pad(delays, ((1, 6), (0, neurons - lats)))
     lines = jnp.where(row == 2, jnp.broadcast_to(recorded[:, None], lines.shape), lines)
     meta = jnp.pad(bias, ((0, 7), (0, 0))) + lines.astype(F32)
 
-    early = 3 * chunk
+    early = 4 * chunk
     *outs, load_ext, shifted = pl.pallas_call(
         functools.partial(shift_kernel, neuron_count, "neuron", chunk, step, early),
-        out_shape=[jax.ShapeDtypeStruct((lats, width), BF16 if k else F32) for k in range(neuron_count)]
+        out_shape=[jax.ShapeDtypeStruct((lats, width), BF16 if k > 1 else F32) for k in range(neuron_count)]
         + [jax.ShapeDtypeStruct((lats + EXTRA, neurons), BF16), jax.ShapeDtypeStruct((lats + EXTRA, total), BF16)],
         in_specs=[vmem, vmem, hbm] + [vmem] * (neuron_count - 1),
         out_specs=[vmem] * (neuron_count + 2),
@@ -184,7 +185,7 @@
                 pltpu.VMEM((count, total), F32),
                 pltpu.VMEM((lats, count), F32),
                 pltpu.VMEM((1, count), F32),
-                pltpu.SemaphoreType.DMA((3,)),
+                pltpu.SemaphoreType.DMA((1 + 2 * (count // chunk),)),
             ],
             input_output_aliases={4 + i: i for i in range(len(made))},
             compiler_params=params,

time: 29.3 us -> 29 us (0.990)
  Pallas kernels: 10.8 us -> 10.2 us
  starting transfers between devices: 11.3 us -> 11.6 us
    pallas_call x1, Pallas kernels: 3.72 us -> 2.92 us  [per_device(): pl.pallas_call(functools.partial(shift_kernel, neuron_count, 'neuron', ch...]
  transfers between devices with their start and end apart: 10 -> 10, of which waited for: 4 -> 6; matrix products, arithmetic and copies ran while one was open for 6% -> 6% of each run, Pallas kernels for 24% -> 25%
where the time goes in v11:
time: 29 us; the launch traced here: 28.7 us
  starting transfers between devices  11.6 us (40%)
  Pallas kernels  10.2 us (35%)
  waiting for transfers between devices  3.12 us (11%)
  other arithmetic  2.42 us (8%)
  between operations  1.36 us (5%)
    ppermute x10, starting transfers between devices, swap(): return lax.ppermute(value, axis, [(i, i ^ mask) for i in range(count)])  11.6 us
    pallas_call x3, Pallas kernels, make(): pl.pallas_call(functools.partial(load_kernel, lats, first, chunk, step),...  7.25 us
    ppermute x10, waiting for transfers between devices, swap(): return lax.ppermute(value, axis, [(i, i ^ mask) for i in range(count)])  3.12 us
    pallas_call x1, Pallas kernels, per_device(): pl.pallas_call(functools.partial(shift_kernel, neuron_count, 'neuron', ch...  2.92 us
    concatenate x1, other arithmetic, per_device(): pack = jnp.concatenate([loadings[0], latents], axis=1)  0.95 us
    add x1, other arithmetic, per_device(): meta = jnp.pad(bias, ((0, 7), (0, 0))) + lines.astype(F32)  0.78 us
    add x1, other arithmetic, per_device(): value = value + arrived[0]  0.64 us
  transfers between devices with their start and end apart: 10, of which 6 were waited for; matrix products, arithmetic and copies ran while one was open for 6% of the time, Pallas kernels for 25%

profile of v11, /device:TPU:0, one launch (start us, length us, event | category | flops | bytes accessed | tf_op | source)
XLA Modules:
  0.0 28.7 jit_solution(8367005655407628369)
XLA Ops:
  0.6 3.0 %collective-permute-start.1 = (bf16[64,256]{1,0:T(8,128)(2,1)}, bf16[64,256]{1,0:T(8,128)(2,1)S(1)}, u32[]{:S(2)}, u32[]{:S(2)}) collective-permute-start(bf16[64,256]{1,0:T(8,128)(2,1)} %param.7), channel_id=1, source_target_pairs={{0,2},{1,3},{2,0},{3,1},{4,6},{5,7},{6,4},{7,5},{8,10},{9,11},{10,... | collective-permute-start | bytes 98312 | tf_op jit(solution)/shard_map/ppermute | solution.py:141
  3.7 0.0 collective-permute-start
  4.3 0.8 %convert_add_fusion.refs_0_ = f32[8,1280]{1,0:T(8,128)S(1)} fusion(s32[1,64]{1,0:T(1,128)} %param.10, f32[1,1280]{1,0:T(1,128)} %param.9, s32[]{:T(128)} %bitcast.4, pred[8]{0:T(512)(128)(4,1)S(1)} %iota_compare_fusion), kind=kLoop, calls=%fused_computation.3 | loop fusion | flops 30720 | bytes 46348 | tf_op jit(solution)/shard_map/add | solution.py:153
  5.1 0.7 %collective-permute-done.1.refs_4_ = bf16[64,256]{1,0:T(8,128)(2,1)S(1)} collective-permute-done((bf16[64,256]{1,0:T(8,128)(2,1)}, bf16[64,256]{1,0:T(8,128)(2,1)S(1)}, u32[]{:S(2)}, u32[]{:S(2)}) %collective-permute-start.1) | collective-permute-done | bytes 32800 | tf_op jit(solution)/shard_map/ppermute | solution.py:141
  5.8 0.0 collective-permute-start.2
  5.8 1.0 %pad_maximum_fusion.refs_1_ = bf16[64,1536]{1,0:T(8,128)(2,1)S(1)} fusion(bf16[64,256]{1,0:T(8,128)(2,1)} %param.7, bf16[64,1280]{1,0:T(8,128)(2,1)} %bitcast.10), kind=kLoop, calls=%fused_computation | loop fusion | flops 393216 | bytes 393216 | tf_op jit(solution)/shard_map/concatenate | solution.py:149
  6.7 0.0 collective-permute-done.refs_3_
  6.7 0.2 collective-permute-done.2.refs_5_
  7.0 2.9 %shard_map.85 = (f32[64,256]{1,0:T(8,128)S(1)}, f32[64,256]{1,0:T(8,128)S(1)}, bf16[64,256]{1,0:T(8,128)(2,1)S(1)}, bf16[64,256]{1,0:T(8,128)(2,1)S(1)}, bf16[80...) custom-call(f32[8,1280]{1,0:T(8,128)S(1)} %convert_add_fusion.refs_0_, bf16[64,1536]{1,0:T(8,128)(2,1)S(1)} %pad_maximum_fusion.refs_1_, ...), custom_call_target="tpu_custom_call" | custom-call | tf_op jit(solution)/shard_map/pallas_call | solution.py:156
  9.9 0.3 %collective-permute-start.3 = (f32[64,256]{1,0:T(8,128)S(1)}, f32[64,256]{1,0:T(8,128)S(1)}, u32[]{:S(2)}, u32[]{:S(2)}) collective-permute-start(f32[64,256]{1,0:T(8,128)S(1)} %get-tuple-element.45), channel_id=1, source_target_pairs={{0,1},{1,0},{2,3},{3,2},{4,5},{5,4},{6,7},{7,6},{8,9},{9,8},{10,11... | collective-permute-start | bytes 196616 | tf_op jit(solution)/shard_map/ppermute | solution.py:141
  10.3 2.0 %collective-permute-start.4 = (bf16[64,256]{1,0:T(8,128)(2,1)S(1)}, bf16[64,256]{1,0:T(8,128)(2,1)S(1)}, u32[]{:S(2)}, u32[]{:S(2)}) collective-permute-start(bf16[64,256]{1,0:T(8,128)(2,1)S(1)} %get-tuple-element.46), channel_id=1, source_target_pairs={{0,2},{1,3},{2,0},{3,1},{4,6},{5,7},{6,4},{7,5},{8,10},{9,11},{10,... | collective-permute-start | bytes 98312 | tf_op jit(solution)/shard_map/ppermute | solution.py:141
  12.3 0.0 collective-permute-start.5
  12.3 2.5 %shard_map.86 = (f32[64,1280]{1,0:T(8,128)}, f32[1,1280]{1,0:T(1,128)}) custom-call(f32[8,1280]{1,0:T(8,128)S(1)} %convert_add_fusion.refs_0_, bf16[80,1280]{1,0:T(8,128)(2,1)S(1)} %get-tuple-element.67.refs_1_, bf16[80,1024]{1,0:T(8,128)(2,1)S(1)} %get-tuple-element.49.refs_2_, bf16[1280,1024]{1,0:T(8,128)(2,1)} %bitcast.6), custom_call_target="tpu_custom_call" | custom-call | flops 134217728 | bytes 1048576 | tf_op jit(solution)/shard_map/pallas_call | solution.py:178
  14.8 0.0 collective-permute-done.4
  14.8 1.0 %collective-permute-done.5 = bf16[64,256]{1,0:T(8,128)(2,1)S(1)} collective-permute-done((bf16[64,256]{1,0:T(8,128)(2,1)S(1)}, bf16[64,256]{1,0:T(8,128)(2,1)S(1)}, u32[]{:S(2)}, u32[]{:S(2)}) %collective-permute-start.5) | collective-permute-done | bytes 32800 | tf_op jit(solution)/shard_map/ppermute | solution.py:141
  15.8 0.0 collective-permute-done.3
  15.9 2.6 %collective-permute-start.8 = (bf16[64,256]{1,0:T(8,128)(2,1)S(1)}, bf16[64,256]{1,0:T(8,128)(2,1)S(1)}, u32[]{:S(2)}, u32[]{:S(2)}) collective-permute-start(bf16[64,256]{1,0:T(8,128)(2,1)S(1)} %get-tuple-element.56), channel_id=1, source_target_pairs={{0,12},{4,8},{8,4},{12,0},{16,28},{20,24},{24,20},{28,16},{1,13},{... | collective-permute-start | bytes 98312 | tf_op jit(solution)/shard_map/ppermute | solution.py:141
  18.4 0.4 %collective-permute-start.7 = (bf16[64,256]{1,0:T(8,128)(2,1)S(1)}, bf16[64,256]{1,0:T(8,128)(2,1)S(1)}, u32[]{:S(2)}, u32[]{:S(2)}) collective-permute-start(bf16[64,256]{1,0:T(8,128)(2,1)S(1)} %get-tuple-element.56), channel_id=1, source_target_pairs={{0,8},{4,12},{8,0},{12,4},{16,24},{20,28},{24,16},{28,20},{1,9},{5... | collective-permute-start | bytes 98312 | tf_op jit(solution)/shard_map/ppermute | solution.py:141
  18.9 0.5 %collective-permute-start.6 = (bf16[64,256]{1,0:T(8,128)(2,1)S(1)}, bf16[64,256]{1,0:T(8,128)(2,1)S(1)}, u32[]{:S(2)}, u32[]{:S(2)}) collective-permute-start(bf16[64,256]{1,0:T(8,128)(2,1)S(1)} %get-tuple-element.56), channel_id=1, source_target_pairs={{0,4},{4,0},{8,12},{12,8},{16,20},{20,16},{24,28},{28,24},{1,5},{5... | collective-permute-start | bytes 98312 | tf_op jit(solution)/shard_map/ppermute | solution.py:141
  19.4 2.5 %shard_map.87 = (f32[64,1280]{1,0:T(8,128)}, f32[1,1280]{1,0:T(1,128)}) custom-call(f32[8,1280]{1,0:T(8,128)S(1)} %convert_add_fusion.refs_0_, bf16[80,1280]{1,0:T(8,128)(2,1)S(1)} %get-tuple-element.67.refs_1_, bf16[80,1024]{1,0:T(8,128)(2,1)S(1)} %get-tuple-element.49.refs_2_, ...), custom_call_target="tpu_custom_call", output_to_operand_aliasing={{0}: (4, {}), {1}: (5, {})} | custom-call | flops 134217728 | bytes 1048576 | tf_op jit(solution)/shard_map/pallas_call | solution.py:178
  22.0 0.0 collective-permute-done.8
  22.0 0.4 %collective-permute-done.7 = bf16[64,256]{1,0:T(8,128)(2,1)S(1)} collective-permute-done((bf16[64,256]{1,0:T(8,128)(2,1)S(1)}, bf16[64,256]{1,0:T(8,128)(2,1)S(1)}, u32[]{:S(2)}, u32[]{:S(2)}) %collective-permute-start.7) | collective-permute-done | bytes 32800 | tf_op jit(solution)/shard_map/ppermute | solution.py:141
  22.3 0.4 %collective-permute-done.6 = bf16[64,256]{1,0:T(8,128)(2,1)S(1)} collective-permute-done((bf16[64,256]{1,0:T(8,128)(2,1)S(1)}, bf16[64,256]{1,0:T(8,128)(2,1)S(1)}, u32[]{:S(2)}, u32[]{:S(2)}) %collective-permute-start.6) | collective-permute-done | bytes 32800 | tf_op jit(solution)/shard_map/ppermute | solution.py:141
  22.8 2.7 %collective-permute-start.9 = (f32[64,256]{1,0:T(8,128)S(1)}, f32[64,256]{1,0:T(8,128)S(1)}, u32[]{:S(2)}, u32[]{:S(2)}) collective-permute-start(f32[64,256]{1,0:T(8,128)S(1)} %add_add_fusion), channel_id=1, source_target_pairs={{0,16},{4,20},{8,24},{12,28},{16,0},{20,4},{24,8},{28,12},{1,17},{... | collective-permute-start | bytes 196616 | tf_op jit(solution)/shard_map/ppermute | solution.py:141
  25.5 2.2 %shard_map.88 = (f32[64,1280]{1,0:T(8,128)}, f32[1,1280]{1,0:T(1,128)}) custom-call(f32[8,1280]{1,0:T(8,128)S(1)} %convert_add_fusion.refs_0_, bf16[80,1280]{1,0:T(8,128)(2,1)S(1)} %get-tuple-element.67.refs_1_, bf16[80,1024]{1,0:T(8,128)(2,1)S(1)} %get-tuple-element.49.refs_2_, ...), custom_call_target="tpu_custom_call", output_to_operand_aliasing={{0}: (4, {}), {1}: (5, {})} | custom-call | flops 67108864 | bytes 524288 | tf_op jit(solution)/shard_map/pallas_call | solution.py:178
  27.6 0.4 %collective-permute-done.9 = f32[64,256]{1,0:T(8,128)S(1)} collective-permute-done((f32[64,256]{1,0:T(8,128)S(1)}, f32[64,256]{1,0:T(8,128)S(1)}, u32[]{:S(2)}, u32[]{:S(2)}) %collective-permute-start.9) | collective-permute-done | bytes 65568 | tf_op jit(solution)/shard_map/ppermute | solution.py:141
  28.0 0.6 %add.35 = f32[64,256]{1,0:T(8,128)} add(f32[64,256]{1,0:T(8,128)S(1)} %add_add_fusion, f32[64,256]{1,0:T(8,128)S(1)} %collective-permute-done.9) | non-fusion elementwise | flops 16384 | bytes 196608 | tf_op jit(solution)/shard_map/add | solution.py:214
  (3 shorter events, 0.0 us)
Async XLA Ops:
  0.6 5.1 %collective-permute-start.1 = (bf16[64,256]{1,0:T(8,128)(2,1)}, bf16[64,256]{1,0:T(8,128)(2,1)S(1)}, u32[]{:S(2)}, u32[]{:S(2)}) collective-permute-start(bf16[64,256]{1,0:T(8,128)(2,1)} %param.7), channel_id=1, source_target_pairs={{0,2},{1,3},{2,0},{3,1},{4,6},{5,7},{6,4},{7,5},{8,10},{9,11},{10,... | collective-permute-start | bytes 98312 | tf_op jit(solution)/shard_map/ppermute | solution.py:141
  3.7 3.1 %collective-permute-start = (bf16[64,256]{1,0:T(8,128)(2,1)}, bf16[64,256]{1,0:T(8,128)(2,1)S(1)}, u32[]{:S(2)}, u32[]{:S(2)}) collective-permute-start(bf16[64,256]{1,0:T(8,128)(2,1)} %param.7), channel_id=1, source_target_pairs={{0,1},{1,0},{2,3},{3,2},{4,5},{5,4},{6,7},{7,6},{8,9},{9,8},{10,11... | collective-permute-start | bytes 98312 | tf_op jit(solution)/shard_map/ppermute | solution.py:141
  5.8 1.2 %collective-permute-start.2 = (bf16[64,256]{1,0:T(8,128)(2,1)S(1)}, bf16[64,256]{1,0:T(8,128)(2,1)S(1)}, u32[]{:S(2)}, u32[]{:S(2)}) collective-permute-start(bf16[64,256]{1,0:T(8,128)(2,1)S(1)} %collective-permute-done.1.refs_4_), channel_id=1, source_target_pairs={{0,1},{1,0},{2,3},{3,2},{4,5},{5,4},{6,7},{7,6},{8,9},{9,8},{10,11... | collective-permute-start | bytes 98312 | tf_op jit(solution)/shard_map/ppermute | solution.py:141
  9.9 5.9 %collective-permute-start.3 = (f32[64,256]{1,0:T(8,128)S(1)}, f32[64,256]{1,0:T(8,128)S(1)}, u32[]{:S(2)}, u32[]{:S(2)}) collective-permute-start(f32[64,256]{1,0:T(8,128)S(1)} %get-tuple-element.45), channel_id=1, source_target_pairs={{0,1},{1,0},{2,3},{3,2},{4,5},{5,4},{6,7},{7,6},{8,9},{9,8},{10,11... | collective-permute-start | bytes 196616 | tf_op jit(solution)/shard_map/ppermute | solution.py:141
  10.3 4.6 %collective-permute-start.4 = (bf16[64,256]{1,0:T(8,128)(2,1)S(1)}, bf16[64,256]{1,0:T(8,128)(2,1)S(1)}, u32[]{:S(2)}, u32[]{:S(2)}) collective-permute-start(bf16[64,256]{1,0:T(8,128)(2,1)S(1)} %get-tuple-element.46), channel_id=1, source_target_pairs={{0,2},{1,3},{2,0},{3,1},{4,6},{5,7},{6,4},{7,5},{8,10},{9,11},{10,... | collective-permute-start | bytes 98312 | tf_op jit(solution)/shard_map/ppermute | solution.py:141
  12.3 3.6 %collective-permute-start.5 = (bf16[64,256]{1,0:T(8,128)(2,1)S(1)}, bf16[64,256]{1,0:T(8,128)(2,1)S(1)}, u32[]{:S(2)}, u32[]{:S(2)}) collective-permute-start(bf16[64,256]{1,0:T(8,128)(2,1)S(1)} %get-tuple-element.47), channel_id=1, source_target_pairs={{0,3},{1,2},{2,1},{3,0},{4,7},{5,6},{6,5},{7,4},{8,11},{9,10},{10,... | collective-permute-start | bytes 98312 | tf_op jit(solution)/shard_map/ppermute | solution.py:141
  15.9 6.1 %collective-permute-start.8 = (bf16[64,256]{1,0:T(8,128)(2,1)S(1)}, bf16[64,256]{1,0:T(8,128)(2,1)S(1)}, u32[]{:S(2)}, u32[]{:S(2)}) collective-permute-start(bf16[64,256]{1,0:T(8,128)(2,1)S(1)} %get-tuple-element.56), channel_id=1, source_target_pairs={{0,12},{4,8},{8,4},{12,0},{16,28},{20,24},{24,20},{28,16},{1,13},{... | collective-permute-start | bytes 98312 | tf_op jit(solution)/shard_map/ppermute | solution.py:141
  18.4 3.9 %collective-permute-start.7 = (bf16[64,256]{1,0:T(8,128)(2,1)S(1)}, bf16[64,256]{1,0:T(8,128)(2,1)S(1)}, u32[]{:S(2)}, u32[]{:S(2)}) collective-permute-start(bf16[64,256]{1,0:T(8,128)(2,1)S(1)} %get-tuple-element.56), channel_id=1, source_target_pairs={{0,8},{4,12},{8,0},{12,4},{16,24},{20,28},{24,16},{28,20},{1,9},{5... | collective-permute-start | bytes 98312 | tf_op jit(solution)/shard_map/ppermute | solution.py:141
  18.9 3.9 %collective-permute-start.6 = (bf16[64,256]{1,0:T(8,128)(2,1)S(1)}, bf16[64,256]{1,0:T(8,128)(2,1)S(1)}, u32[]{:S(2)}, u32[]{:S(2)}) collective-permute-start(bf16[64,256]{1,0:T(8,128)(2,1)S(1)} %get-tuple-element.56), channel_id=1, source_target_pairs={{0,4},{4,0},{8,12},{12,8},{16,20},{20,16},{24,28},{28,24},{1,5},{5... | collective-permute-start | bytes 98312 | tf_op jit(solution)/shard_map/ppermute | solution.py:141
  22.8 5.2 %collective-permute-start.9 = (f32[64,256]{1,0:T(8,128)S(1)}, f32[64,256]{1,0:T(8,128)S(1)}, u32[]{:S(2)}, u32[]{:S(2)}) collective-permute-start(f32[64,256]{1,0:T(8,128)S(1)} %add_add_fusion), channel_id=1, source_target_pairs={{0,16},{4,20},{8,24},{12,28},{16,0},{20,4},{24,8},{28,12},{1,17},{... | collective-permute-start | bytes 196616 | tf_op jit(solution)/shard_map/ppermute | solution.py:141

commit v12 on v11

--- a/solution.py
+++ b/solution.py
@@ -29,21 +29,24 @@
     return jnp.exp(eta)
 
 
-def shift_kernel(parts, axis, chunk, step, early, *refs):
+def shift_kernel(parts, order, axis, chunk, step, *refs):
     meta_ref, pack_ref, counts_hbm = refs[:3]
     arrived = refs[3 : 2 + parts]
     outs = refs[2 + parts : 2 + 2 * parts]
-    load_ext, shifted, whole, counts_ref, held, grad_shift, counts_sem = refs[2 + 2 * parts :]
+    load_ext, shifted, whole, counts_ref, held, grad_shift, counts_sems = refs[2 + 2 * parts :]
     me = lax.axis_index(axis)
     lats, total = grad_shift.shape
     neurons = counts_ref.shape[0]
     width = total // parts
-    counts_copy = pltpu.make_async_copy(counts_hbm, counts_ref, counts_sem)
-    counts_copy.start()
+    cut = (neurons // chunk + 1) // 2 * chunk
+    copies = []
+    for index, place in enumerate([pl.ds(0, cut), pl.ds(cut, neurons - cut)]):
+        copies.append(pltpu.make_async_copy(counts_hbm.at[place], counts_ref.at[place], counts_sems.at[index]))
+        copies[-1].start()
 
     for k in range(parts):
         start = pl.multiple_of((me ^ k) * width, width)
-        whole[:, pl.ds(start, width)] = arrived[k - 1][...] if k else pack_ref[:, neurons:]
+        whole[:, pl.ds(start, width)] = arrived[order.index(k)][...] if k else pack_ref[:, neurons:]
     diagonal = lax.broadcasted_iota(jnp.int32, (lats, LANES), 0) == lax.broadcasted_iota(jnp.int32, (lats, LANES), 1)
     spread = jnp.broadcast_to(meta_ref[1:2, 0:LANES], (lats, LANES))
     column = jnp.sum(jnp.where(diagonal, spread, 0.0), axis=1, keepdims=True)
@@ -70,12 +73,12 @@
         for begin in range(0, total, step)
     ]
     for rows, span in blocks:
-        if rows.start < early:
-            held[rows, span] = expected(load_ext[:, rows], shifted[:, span])
-    counts_copy.wait()
+        held[rows, span] = expected(load_ext[:, rows], shifted[:, span])
+    copies[0].wait()
     for rows, span in blocks:
-        rate = held[rows, span] if rows.start < early else expected(load_ext[:, rows], shifted[:, span])
-        resid = rate - counts_ref[rows, span].astype(F32)
+        if rows.start == cut and span.start == 0:
+            copies[1].wait()
+        resid = held[rows, span] - counts_ref[rows, span].astype(F32)
         part = jnp.dot(load_ext[0:lats, rows], resid.astype(BF16), preferred_element_type=F32)
         grad_shift[:, span] = part if rows.start == 0 else grad_shift[:, span] + part
 
@@ -140,21 +143,16 @@
     def swap(value, axis, count, mask):
         return lax.ppermute(value, axis, [(i, i ^ mask) for i in range(count)])
 
-    held = {0: latents}
-    masks = [1 << level for level in range(1, neuron_count.bit_length() - 1)] + [1]
-    for mask in masks:
-        for k, block in list(held.items()):
-            held[k ^ mask] = swap(block, "neuron", neuron_count, mask)
-    arrived = [held[k] for k in range(1, neuron_count)]
+    order = sorted(range(1, neuron_count), key=lambda k: (k != 2, k))
+    arrived = [swap(latents, "neuron", neuron_count, k) for k in order]
     pack = jnp.concatenate([loadings[0], latents], axis=1)
     row = lax.broadcasted_iota(jnp.int32, (8, neurons), 0)
     lines = jnp.pad(delays, ((1, 6), (0, neurons - lats)))
     lines = jnp.where(row == 2, jnp.broadcast_to(recorded[:, None], lines.shape), lines)
     meta = jnp.pad(bias, ((0, 7), (0, 0))) + lines.astype(F32)
 
-    early = 4 * chunk
     *outs, load_ext, shifted = pl.pallas_call(
-        functools.partial(shift_kernel, neuron_count, "neuron", chunk, step, early),
+        functools.partial(shift_kernel, neuron_count, order, "neuron", chunk, step),
         out_shape=[jax.ShapeDtypeStruct((lats, width), BF16 if k > 1 else F32) for k in range(neuron_count)]
         + [jax.ShapeDtypeStruct((lats + EXTRA, neurons), BF16), jax.ShapeDtypeStruct((lats + EXTRA, total), BF16)],
         in_specs=[vmem, vmem, hbm] + [vmem] * (neuron_count - 1),
@@ -162,9 +160,9 @@
         scratch_shapes=[
             pltpu.VMEM((lats, total), BF16),
             pltpu.VMEM((neurons, total), BF16),
-            pltpu.VMEM((early, total), F32),
+            pltpu.VMEM((neurons, total), F32),
             pltpu.VMEM((lats, total), F32),
-            pltpu.SemaphoreType.DMA,
+            pltpu.SemaphoreType.DMA((2,)),
         ],
         compiler_params=params,
     )(meta, pack, counts[0], *arrived)
@@ -196,7 +194,7 @@
         return before, out
 
     outs, made = make(outs)
-    arrived = [swap(outs[k], "neuron", neuron_count, k) for k in range(1, neuron_count)]
+    arrived = [swap(outs[k], "neuron", neuron_count, k) for k in [*range(2, neuron_count), 1]]
     arrived, made = lax.optimization_barrier((arrived, made))
     value = functools.reduce(jnp.add, [outs[0]] + [block.astype(F32) for block in arrived])
     mask = 1

time: 29 us -> 28.1 us (0.969)
  waiting for transfers between devices: 3.12 us -> 2.26 us
    ppermute x10, waiting for transfers between devices: 3.12 us -> 2.26 us  [swap(): return lax.ppermute(value, axis, [(i, i ^ mask) for i in range(count)])]
  transfers between devices with their start and end apart: 10 -> 10, of which waited for: 6 -> 4; matrix products, arithmetic and copies ran while one was open for 6% -> 6% of each run, Pallas kernels for 25% -> 26%
where the time goes in v12:
time: 28.1 us; the launch traced here: 27.8 us
  starting transfers between devices  11.4 us (41%)
  Pallas kernels  10.4 us (37%)
  other arithmetic  2.42 us (9%)
  waiting for transfers between devices  2.26 us (8%)
  between operations  1.38 us (5%)
    ppermute x10, starting transfers between devices, swap(): return lax.ppermute(value, axis, [(i, i ^ mask) for i in range(count)])  11.4 us
    pallas_call x3, Pallas kernels, make(): pl.pallas_call(functools.partial(load_kernel, lats, first, chunk, step),...  7.25 us
    pallas_call x1, Pallas kernels, per_device(): pl.pallas_call(functools.partial(shift_kernel, neuron_count, order, 'neur...  3.1 us
    ppermute x10, waiting for transfers between devices, swap(): return lax.ppermute(value, axis, [(i, i ^ mask) for i in range(count)])  2.26 us
    concatenate x1, other arithmetic, per_device(): pack = jnp.concatenate([loadings[0], latents], axis=1)  0.95 us
    add x1, other arithmetic, per_device(): meta = jnp.pad(bias, ((0, 7), (0, 0))) + lines.astype(F32)  0.78 us
    add x1, other arithmetic, per_device(): value = value + arrived[0]  0.64 us
  transfers between devices with their start and end apart: 10, of which 4 were waited for; matrix products, arithmetic and copies ran while one was open for 6% of the time, Pallas kernels for 26%

profile of v12, /device:TPU:0, one launch (start us, length us, event | category | flops | bytes accessed | tf_op | source)
XLA Modules:
  0.0 27.8 jit_solution(5620409448317811613)
XLA Ops:
  0.6 3.0 %collective-permute-start = (bf16[64,256]{1,0:T(8,128)(2,1)}, bf16[64,256]{1,0:T(8,128)(2,1)S(1)}, u32[]{:S(2)}, u32[]{:S(2)}) collective-permute-start(bf16[64,256]{1,0:T(8,128)(2,1)} %param.7), channel_id=1, source_target_pairs={{0,2},{1,3},{2,0},{3,1},{4,6},{5,7},{6,4},{7,5},{8,10},{9,11},{10,... | collective-permute-start | bytes 98312 | tf_op jit(solution)/shard_map/ppermute | solution.py:144
  3.7 0.0 collective-permute-start.2
  3.7 0.2 collective-permute-start.1
  4.5 0.8 %convert_add_fusion.refs_0_ = f32[8,1280]{1,0:T(8,128)S(1)} fusion(s32[1,64]{1,0:T(1,128)} %param.10, f32[1,1280]{1,0:T(1,128)} %param.9, s32[]{:T(128)} %bitcast.4, pred[8]{0:T(512)(128)(4,1)S(1)} %iota_compare_fusion), kind=kLoop, calls=%fused_computation.3 | loop fusion | flops 30720 | bytes 46348 | tf_op jit(solution)/shard_map/add | solution.py:152
  5.3 0.9 %pad_maximum_fusion.refs_1_ = bf16[64,1536]{1,0:T(8,128)(2,1)S(1)} fusion(bf16[64,256]{1,0:T(8,128)(2,1)} %param.7, bf16[64,1280]{1,0:T(8,128)(2,1)} %bitcast.10), kind=kLoop, calls=%fused_computation | loop fusion | flops 393216 | bytes 393216 | tf_op jit(solution)/shard_map/concatenate | solution.py:148
  6.3 0.0 collective-permute-done.refs_3_
  6.3 1.0 %collective-permute-done.2.refs_5_ = bf16[64,256]{1,0:T(8,128)(2,1)S(1)} collective-permute-done((bf16[64,256]{1,0:T(8,128)(2,1)}, bf16[64,256]{1,0:T(8,128)(2,1)S(1)}, u32[]{:S(2)}, u32[]{:S(2)}) %collective-permute-start.2) | collective-permute-done | bytes 32800 | tf_op jit(solution)/shard_map/ppermute | solution.py:144
  7.3 0.0 collective-permute-done.1.refs_4_
  7.3 3.1 %shard_map.85 = (f32[64,256]{1,0:T(8,128)S(1)}, f32[64,256]{1,0:T(8,128)S(1)}, bf16[64,256]{1,0:T(8,128)(2,1)S(1)}, bf16[64,256]{1,0:T(8,128)(2,1)S(1)}, bf16[80...) custom-call(f32[8,1280]{1,0:T(8,128)S(1)} %convert_add_fusion.refs_0_, bf16[64,1536]{1,0:T(8,128)(2,1)S(1)} %pad_maximum_fusion.refs_1_, ...), custom_call_target="tpu_custom_call" | custom-call | tf_op jit(solution)/shard_map/pallas_call | solution.py:154
  10.4 0.1 collective-permute-start.5
  10.5 1.0 %collective-permute-start.3 = (bf16[64,256]{1,0:T(8,128)(2,1)S(1)}, bf16[64,256]{1,0:T(8,128)(2,1)S(1)}, u32[]{:S(2)}, u32[]{:S(2)}) collective-permute-start(bf16[64,256]{1,0:T(8,128)(2,1)S(1)} %get-tuple-element.45), channel_id=1, source_target_pairs={{0,2},{1,3},{2,0},{3,1},{4,6},{5,7},{6,4},{7,5},{8,10},{9,11},{10,... | collective-permute-start | bytes 98312 | tf_op jit(solution)/shard_map/ppermute | solution.py:144
  11.5 0.9 %collective-permute-start.4 = (bf16[64,256]{1,0:T(8,128)(2,1)S(1)}, bf16[64,256]{1,0:T(8,128)(2,1)S(1)}, u32[]{:S(2)}, u32[]{:S(2)}) collective-permute-start(bf16[64,256]{1,0:T(8,128)(2,1)S(1)} %get-tuple-element.46), channel_id=1, source_target_pairs={{0,3},{1,2},{2,1},{3,0},{4,7},{5,6},{6,5},{7,4},{8,11},{9,10},{10,... | collective-permute-start | bytes 98312 | tf_op jit(solution)/shard_map/ppermute | solution.py:144
  12.4 2.5 %shard_map.86 = (f32[64,1280]{1,0:T(8,128)}, f32[1,1280]{1,0:T(1,128)}) custom-call(f32[8,1280]{1,0:T(8,128)S(1)} %convert_add_fusion.refs_0_, bf16[80,1280]{1,0:T(8,128)(2,1)S(1)} %get-tuple-element.67.refs_1_, bf16[80,1024]{1,0:T(8,128)(2,1)S(1)} %get-tuple-element.49.refs_2_, bf16[1280,1024]{1,0:T(8,128)(2,1)} %bitcast.6), custom_call_target="tpu_custom_call" | custom-call | flops 134217728 | bytes 1048576 | tf_op jit(solution)/shard_map/pallas_call | solution.py:176
  14.9 0.0 collective-permute-done.3
  14.9 0.0 collective-permute-done.4
  14.9 0.0 collective-permute-done.5
  15.0 2.6 %collective-permute-start.8 = (bf16[64,256]{1,0:T(8,128)(2,1)S(1)}, bf16[64,256]{1,0:T(8,128)(2,1)S(1)}, u32[]{:S(2)}, u32[]{:S(2)}) collective-permute-start(bf16[64,256]{1,0:T(8,128)(2,1)S(1)} %get-tuple-element.56), channel_id=1, source_target_pairs={{0,12},{4,8},{8,4},{12,0},{16,28},{20,24},{24,20},{28,16},{1,13},{... | collective-permute-start | bytes 98312 | tf_op jit(solution)/shard_map/ppermute | solution.py:144
  17.5 0.4 %collective-permute-start.7 = (bf16[64,256]{1,0:T(8,128)(2,1)S(1)}, bf16[64,256]{1,0:T(8,128)(2,1)S(1)}, u32[]{:S(2)}, u32[]{:S(2)}) collective-permute-start(bf16[64,256]{1,0:T(8,128)(2,1)S(1)} %get-tuple-element.56), channel_id=1, source_target_pairs={{0,8},{4,12},{8,0},{12,4},{16,24},{20,28},{24,16},{28,20},{1,9},{5... | collective-permute-start | bytes 98312 | tf_op jit(solution)/shard_map/ppermute | solution.py:144
  18.0 0.5 %collective-permute-start.6 = (bf16[64,256]{1,0:T(8,128)(2,1)S(1)}, bf16[64,256]{1,0:T(8,128)(2,1)S(1)}, u32[]{:S(2)}, u32[]{:S(2)}) collective-permute-start(bf16[64,256]{1,0:T(8,128)(2,1)S(1)} %get-tuple-element.56), channel_id=1, source_target_pairs={{0,4},{4,0},{8,12},{12,8},{16,20},{20,16},{24,28},{28,24},{1,5},{5... | collective-permute-start | bytes 98312 | tf_op jit(solution)/shard_map/ppermute | solution.py:144
  18.5 2.5 %shard_map.87 = (f32[64,1280]{1,0:T(8,128)}, f32[1,1280]{1,0:T(1,128)}) custom-call(f32[8,1280]{1,0:T(8,128)S(1)} %convert_add_fusion.refs_0_, bf16[80,1280]{1,0:T(8,128)(2,1)S(1)} %get-tuple-element.67.refs_1_, bf16[80,1024]{1,0:T(8,128)(2,1)S(1)} %get-tuple-element.49.refs_2_, ...), custom_call_target="tpu_custom_call", output_to_operand_aliasing={{0}: (4, {}), {1}: (5, {})} | custom-call | flops 134217728 | bytes 1048576 | tf_op jit(solution)/shard_map/pallas_call | solution.py:176
  21.1 0.0 collective-permute-done.8
  21.1 0.4 %collective-permute-done.7 = bf16[64,256]{1,0:T(8,128)(2,1)S(1)} collective-permute-done((bf16[64,256]{1,0:T(8,128)(2,1)S(1)}, bf16[64,256]{1,0:T(8,128)(2,1)S(1)}, u32[]{:S(2)}, u32[]{:S(2)}) %collective-permute-start.7) | collective-permute-done | bytes 32800 | tf_op jit(solution)/shard_map/ppermute | solution.py:144
  21.4 0.4 %collective-permute-done.6 = bf16[64,256]{1,0:T(8,128)(2,1)S(1)} collective-permute-done((bf16[64,256]{1,0:T(8,128)(2,1)S(1)}, bf16[64,256]{1,0:T(8,128)(2,1)S(1)}, u32[]{:S(2)}, u32[]{:S(2)}) %collective-permute-start.6) | collective-permute-done | bytes 32800 | tf_op jit(solution)/shard_map/ppermute | solution.py:144
  21.9 2.7 %collective-permute-start.9 = (f32[64,256]{1,0:T(8,128)S(1)}, f32[64,256]{1,0:T(8,128)S(1)}, u32[]{:S(2)}, u32[]{:S(2)}) collective-permute-start(f32[64,256]{1,0:T(8,128)S(1)} %add_add_fusion), channel_id=1, source_target_pairs={{0,16},{4,20},{8,24},{12,28},{16,0},{20,4},{24,8},{28,12},{1,17},{... | collective-permute-start | bytes 196616 | tf_op jit(solution)/shard_map/ppermute | solution.py:144
  24.6 2.2 %shard_map.88 = (f32[64,1280]{1,0:T(8,128)}, f32[1,1280]{1,0:T(1,128)}) custom-call(f32[8,1280]{1,0:T(8,128)S(1)} %convert_add_fusion.refs_0_, bf16[80,1280]{1,0:T(8,128)(2,1)S(1)} %get-tuple-element.67.refs_1_, bf16[80,1024]{1,0:T(8,128)(2,1)S(1)} %get-tuple-element.49.refs_2_, ...), custom_call_target="tpu_custom_call", output_to_operand_aliasing={{0}: (4, {}), {1}: (5, {})} | custom-call | flops 67108864 | bytes 524288 | tf_op jit(solution)/shard_map/pallas_call | solution.py:176
  26.8 0.4 %collective-permute-done.9 = f32[64,256]{1,0:T(8,128)S(1)} collective-permute-done((f32[64,256]{1,0:T(8,128)S(1)}, f32[64,256]{1,0:T(8,128)S(1)}, u32[]{:S(2)}, u32[]{:S(2)}) %collective-permute-start.9) | collective-permute-done | bytes 65568 | tf_op jit(solution)/shard_map/ppermute | solution.py:144
  27.1 0.6 %add.35 = f32[64,256]{1,0:T(8,128)} add(f32[64,256]{1,0:T(8,128)S(1)} %add_add_fusion, f32[64,256]{1,0:T(8,128)S(1)} %collective-permute-done.9) | non-fusion elementwise | flops 16384 | bytes 196608 | tf_op jit(solution)/shard_map/add | solution.py:212
  (3 shorter events, 0.0 us)
Async XLA Ops:
  0.6 5.6 %collective-permute-start = (bf16[64,256]{1,0:T(8,128)(2,1)}, bf16[64,256]{1,0:T(8,128)(2,1)S(1)}, u32[]{:S(2)}, u32[]{:S(2)}) collective-permute-start(bf16[64,256]{1,0:T(8,128)(2,1)} %param.7), channel_id=1, source_target_pairs={{0,2},{1,3},{2,0},{3,1},{4,6},{5,7},{6,4},{7,5},{8,10},{9,11},{10,... | collective-permute-start | bytes 98312 | tf_op jit(solution)/shard_map/ppermute | solution.py:144
  3.7 3.6 %collective-permute-start.2 = (bf16[64,256]{1,0:T(8,128)(2,1)}, bf16[64,256]{1,0:T(8,128)(2,1)S(1)}, u32[]{:S(2)}, u32[]{:S(2)}) collective-permute-start(bf16[64,256]{1,0:T(8,128)(2,1)} %param.7), channel_id=1, source_target_pairs={{0,3},{1,2},{2,1},{3,0},{4,7},{5,6},{6,5},{7,4},{8,11},{9,10},{10,... | collective-permute-start | bytes 98312 | tf_op jit(solution)/shard_map/ppermute | solution.py:144
  3.7 3.6 %collective-permute-start.1 = (bf16[64,256]{1,0:T(8,128)(2,1)}, bf16[64,256]{1,0:T(8,128)(2,1)S(1)}, u32[]{:S(2)}, u32[]{:S(2)}) collective-permute-start(bf16[64,256]{1,0:T(8,128)(2,1)} %param.7), channel_id=1, source_target_pairs={{0,1},{1,0},{2,3},{3,2},{4,5},{5,4},{6,7},{7,6},{8,9},{9,8},{10,11... | collective-permute-start | bytes 98312 | tf_op jit(solution)/shard_map/ppermute | solution.py:144
  10.4 4.5 %collective-permute-start.5 = (f32[64,256]{1,0:T(8,128)S(1)}, f32[64,256]{1,0:T(8,128)S(1)}, u32[]{:S(2)}, u32[]{:S(2)}) collective-permute-start(f32[64,256]{1,0:T(8,128)S(1)} %get-tuple-element.47), channel_id=1, source_target_pairs={{0,1},{1,0},{2,3},{3,2},{4,5},{5,4},{6,7},{7,6},{8,9},{9,8},{10,11... | collective-permute-start | bytes 196616 | tf_op jit(solution)/shard_map/ppermute | solution.py:144
  10.5 4.4 %collective-permute-start.3 = (bf16[64,256]{1,0:T(8,128)(2,1)S(1)}, bf16[64,256]{1,0:T(8,128)(2,1)S(1)}, u32[]{:S(2)}, u32[]{:S(2)}) collective-permute-start(bf16[64,256]{1,0:T(8,128)(2,1)S(1)} %get-tuple-element.45), channel_id=1, source_target_pairs={{0,2},{1,3},{2,0},{3,1},{4,6},{5,7},{6,4},{7,5},{8,10},{9,11},{10,... | collective-permute-start | bytes 98312 | tf_op jit(solution)/shard_map/ppermute | solution.py:144
  11.5 3.4 %collective-permute-start.4 = (bf16[64,256]{1,0:T(8,128)(2,1)S(1)}, bf16[64,256]{1,0:T(8,128)(2,1)S(1)}, u32[]{:S(2)}, u32[]{:S(2)}) collective-permute-start(bf16[64,256]{1,0:T(8,128)(2,1)S(1)} %get-tuple-element.46), channel_id=1, source_target_pairs={{0,3},{1,2},{2,1},{3,0},{4,7},{5,6},{6,5},{7,4},{8,11},{9,10},{10,... | collective-permute-start | bytes 98312 | tf_op jit(solution)/shard_map/ppermute | solution.py:144
  15.0 6.1 %collective-permute-start.8 = (bf16[64,256]{1,0:T(8,128)(2,1)S(1)}, bf16[64,256]{1,0:T(8,128)(2,1)S(1)}, u32[]{:S(2)}, u32[]{:S(2)}) collective-permute-start(bf16[64,256]{1,0:T(8,128)(2,1)S(1)} %get-tuple-element.56), channel_id=1, source_target_pairs={{0,12},{4,8},{8,4},{12,0},{16,28},{20,24},{24,20},{28,16},{1,13},{... | collective-permute-start | bytes 98312 | tf_op jit(solution)/shard_map/ppermute | solution.py:144
  17.5 3.9 %collective-permute-start.7 = (bf16[64,256]{1,0:T(8,128)(2,1)S(1)}, bf16[64,256]{1,0:T(8,128)(2,1)S(1)}, u32[]{:S(2)}, u32[]{:S(2)}) collective-permute-start(bf16[64,256]{1,0:T(8,128)(2,1)S(1)} %get-tuple-element.56), channel_id=1, source_target_pairs={{0,8},{4,12},{8,0},{12,4},{16,24},{20,28},{24,16},{28,20},{1,9},{5... | collective-permute-start | bytes 98312 | tf_op jit(solution)/shard_map/ppermute | solution.py:144
  18.0 3.9 %collective-permute-start.6 = (bf16[64,256]{1,0:T(8,128)(2,1)S(1)}, bf16[64,256]{1,0:T(8,128)(2,1)S(1)}, u32[]{:S(2)}, u32[]{:S(2)}) collective-permute-start(bf16[64,256]{1,0:T(8,128)(2,1)S(1)} %get-tuple-element.56), channel_id=1, source_target_pairs={{0,4},{4,0},{8,12},{12,8},{16,20},{20,16},{24,28},{28,24},{1,5},{5... | collective-permute-start | bytes 98312 | tf_op jit(solution)/shard_map/ppermute | solution.py:144
  21.9 5.2 %collective-permute-start.9 = (f32[64,256]{1,0:T(8,128)S(1)}, f32[64,256]{1,0:T(8,128)S(1)}, u32[]{:S(2)}, u32[]{:S(2)}) collective-permute-start(f32[64,256]{1,0:T(8,128)S(1)} %add_add_fusion), channel_id=1, source_target_pairs={{0,16},{4,20},{8,24},{12,28},{16,0},{20,4},{24,8},{28,12},{1,17},{... | collective-permute-start | bytes 196616 | tf_op jit(solution)/shard_map/ppermute | solution.py:144

commit v13 on v11

--- a/solution.py
+++ b/solution.py
@@ -29,13 +29,14 @@
     return jnp.exp(eta)
 
 
-def shift_kernel(parts, axis, chunk, step, early, *refs):
-    meta_ref, pack_ref, counts_hbm = refs[:3]
-    arrived = refs[3 : 2 + parts]
-    outs = refs[2 + parts : 2 + 2 * parts]
-    load_ext, shifted, whole, counts_ref, held, grad_shift, counts_sem = refs[2 + 2 * parts :]
+def shift_kernel(parts, order, axis, chunk, step, *refs):
+    pack_ref, counts_hbm = refs[:2]
+    arrived = refs[2 : 1 + parts]
+    outs = refs[1 + parts : 1 + 2 * parts]
+    load_ext, shifted, whole, counts_ref, held, grad_shift, counts_sem = refs[1 + 2 * parts :]
     me = lax.axis_index(axis)
     lats, total = grad_shift.shape
+    early = held.shape[0]
     neurons = counts_ref.shape[0]
     width = total // parts
     counts_copy = pltpu.make_async_copy(counts_hbm, counts_ref, counts_sem)
@@ -43,20 +44,20 @@
 
     for k in range(parts):
         start = pl.multiple_of((me ^ k) * width, width)
-        whole[:, pl.ds(start, width)] = arrived[k - 1][...] if k else pack_ref[:, neurons:]
+        whole[:, pl.ds(start, width)] = arrived[order.index(k)][...] if k else pack_ref[0:lats, neurons:].astype(BF16)
     diagonal = lax.broadcasted_iota(jnp.int32, (lats, LANES), 0) == lax.broadcasted_iota(jnp.int32, (lats, LANES), 1)
-    spread = jnp.broadcast_to(meta_ref[1:2, 0:LANES], (lats, LANES))
+    spread = jnp.broadcast_to(pack_ref[lats + 1 : lats + 2, 0:LANES], (lats, LANES))
     column = jnp.sum(jnp.where(diagonal, spread, 0.0), axis=1, keepdims=True)
     delay = jnp.broadcast_to(column, (lats, LANES)).astype(jnp.int32)
-    length = meta_ref[2:3, 0:1].astype(jnp.int32)
+    length = pack_ref[lats + 2 : lats + 3, 0:1].astype(jnp.int32)
     tiles = [whole[:, j * LANES : (j + 1) * LANES].astype(F32) for j in range(total // LANES)]
     for j, tile in enumerate(shift_tiles(tiles, delay, True)):
         shifted[0:lats, j * LANES : (j + 1) * LANES] = tile.astype(BF16)
     row = lax.broadcasted_iota(jnp.int32, (EXTRA, total), 0)
     shifted[lats:, :] = jnp.where(row < 3, 1.0, 0.0).astype(BF16)
 
-    load_ext[0:lats, :] = pack_ref[:, 0:neurons]
-    bias = meta_ref[0:1, :]
+    load_ext[0:lats, :] = pack_ref[0:lats, 0:neurons].astype(BF16)
+    bias = pack_ref[lats : lats + 1, 0:neurons]
     high = bias.astype(BF16).astype(F32)
     middle = (bias - high).astype(BF16).astype(F32)
     low = bias - high - middle
@@ -92,13 +93,13 @@
 
 
 def load_kernel(lats, first, chunk, step, *refs):
-    meta_ref, load_ext, shifted, counts_hbm = refs[:4]
+    pack_ref, load_ext, shifted, counts_hbm = refs[:4]
     load_hbm, bias_hbm, counts_ref, held, load_ref, bias_ref, sems = refs[-7:]
     count, total = counts_ref.shape
     place = pl.ds(first, count)
     counts_copy = pltpu.make_async_copy(counts_hbm.at[place], counts_ref, sems.at[0])
     counts_copy.start()
-    length = meta_ref[2:3, 0:1].astype(jnp.int32)
+    length = pack_ref[lats + 2 : lats + 3, 0:1].astype(jnp.int32)
     bins = lax.broadcasted_iota(jnp.int32, (1, total), 1)
     blocks = [(slice(begin, begin + chunk), range(0, total, step)) for begin in range(0, count, chunk)]
     for rows, starts in blocks:
@@ -140,34 +141,30 @@
     def swap(value, axis, count, mask):
         return lax.ppermute(value, axis, [(i, i ^ mask) for i in range(count)])
 
-    held = {0: latents}
-    masks = [1 << level for level in range(1, neuron_count.bit_length() - 1)] + [1]
-    for mask in masks:
-        for k, block in list(held.items()):
-            held[k ^ mask] = swap(block, "neuron", neuron_count, mask)
-    arrived = [held[k] for k in range(1, neuron_count)]
-    pack = jnp.concatenate([loadings[0], latents], axis=1)
-    row = lax.broadcasted_iota(jnp.int32, (8, neurons), 0)
-    lines = jnp.pad(delays, ((1, 6), (0, neurons - lats)))
-    lines = jnp.where(row == 2, jnp.broadcast_to(recorded[:, None], lines.shape), lines)
-    meta = jnp.pad(bias, ((0, 7), (0, 0))) + lines.astype(F32)
-
-    early = 4 * chunk
+    order = sorted(range(1, neuron_count), key=lambda k: (k != 2, k))
+    arrived = [swap(latents, "neuron", neuron_count, k) for k in order]
+    row = lax.broadcasted_iota(jnp.int32, (lats + 8, neurons + width), 0)
+    lines = jnp.pad(delays, ((lats + 1, 6), (0, neurons + width - lats)))
+    lines = jnp.where(row == lats + 2, jnp.broadcast_to(recorded[:, None], lines.shape), lines)
+    pack = jnp.pad(bias, ((lats, 7), (0, width))) + lines.astype(F32)
+    pack = pack + jnp.pad(loadings[0], ((0, 8), (0, width))).astype(F32)
+    pack = pack + jnp.pad(latents, ((0, 8), (neurons, 0))).astype(F32)
+
     *outs, load_ext, shifted = pl.pallas_call(
-        functools.partial(shift_kernel, neuron_count, "neuron", chunk, step, early),
+        functools.partial(shift_kernel, neuron_count, order, "neuron", chunk, step),
         out_shape=[jax.ShapeDtypeStruct((lats, width), BF16 if k > 1 else F32) for k in range(neuron_count)]
         + [jax.ShapeDtypeStruct((lats + EXTRA, neurons), BF16), jax.ShapeDtypeStruct((lats + EXTRA, total), BF16)],
-        in_specs=[vmem, vmem, hbm] + [vmem] * (neuron_count - 1),
+        in_specs=[vmem, hbm] + [vmem] * (neuron_count - 1),
         out_specs=[vmem] * (neuron_count + 2),
         scratch_shapes=[
             pltpu.VMEM((lats, total), BF16),
             pltpu.VMEM((neurons, total), BF16),
-            pltpu.VMEM((early, total), F32),
+            pltpu.VMEM((4 * chunk, total), F32),
             pltpu.VMEM((lats, total), F32),
             pltpu.SemaphoreType.DMA,
         ],
         compiler_params=params,
-    )(meta, pack, counts[0], *arrived)
+    )(pack, counts[0], *arrived)
 
     shares = [(0, 2 * chunk), (2 * chunk, 2 * chunk), (4 * chunk, neurons - 4 * chunk)]
     made = []
@@ -192,11 +189,11 @@
             cost_estimate=pl.CostEstimate(
                 flops=4 * lats * count * total, bytes_accessed=2 * count * total, transcendentals=count * total
             ),
-        )(meta, start_load, shifted, counts[0], *made)
+        )(pack, start_load, shifted, counts[0], *made)
         return before, out
 
     outs, made = make(outs)
-    arrived = [swap(outs[k], "neuron", neuron_count, k) for k in range(1, neuron_count)]
+    arrived = [swap(outs[k], "neuron", neuron_count, k) for k in [*range(2, neuron_count), 1]]
     arrived, made = lax.optimization_barrier((arrived, made))
     value = functools.reduce(jnp.add, [outs[0]] + [block.astype(F32) for block in arrived])
     mask = 1

time: 29 us -> 28 us (0.966)
  other arithmetic: 2.42 us -> 1.76 us
    concatenate x1 -> x0, other arithmetic: 0.95 us -> none  [per_device(): pack = jnp.concatenate([loadings[0], latents], axis=1)]
    add x1, other arithmetic: 0.78 us -> 1.07 us  [per_device(): pack = pack + jnp.pad(latents, ((0, 8), (neurons, 0))).astype(F32)]
  transfers between devices with their start and end apart: 10 -> 10, of which waited for: 6 -> 5; matrix products, arithmetic and copies ran while one was open for 6% -> 4% of each run, Pallas kernels for 25% -> 26%
where the time goes in v13:
time: 28 us; the launch traced here: 27.6 us
  starting transfers between devices  11.4 us (41%)
  Pallas kernels  10.1 us (36%)
  waiting for transfers between devices  3 us (11%)
  other arithmetic  1.76 us (6%)
  between operations  1.37 us (5%)
    ppermute x10, starting transfers between devices, swap(): return lax.ppermute(value, axis, [(i, i ^ mask) for i in range(count)])  11.4 us
    pallas_call x3, Pallas kernels, make(): pl.pallas_call(functools.partial(load_kernel, lats, first, chunk, step),...  7.23 us
    ppermute x10, waiting for transfers between devices, swap(): return lax.ppermute(value, axis, [(i, i ^ mask) for i in range(count)])  3 us
    pallas_call x1, Pallas kernels, per_device(): pl.pallas_call(functools.partial(shift_kernel, neuron_count, order, 'neur...  2.91 us
    add x1, other arithmetic, per_device(): pack = pack + jnp.pad(latents, ((0, 8), (neurons, 0))).astype(F32)  1.07 us
    add x1, other arithmetic, per_device(): value = value + arrived[0]  0.64 us
  transfers between devices with their start and end apart: 10, of which 5 were waited for; matrix products, arithmetic and copies ran while one was open for 4% of the time, Pallas kernels for 26%

profile of v13, /device:TPU:0, one launch (start us, length us, event | category | flops | bytes accessed | tf_op | source)
XLA Modules:
  0.0 27.6 jit_solution(1804941956942870157)
XLA Ops:
  0.6 3.0 %collective-permute-start = (bf16[64,256]{1,0:T(8,128)(2,1)}, bf16[64,256]{1,0:T(8,128)(2,1)S(1)}, u32[]{:S(2)}, u32[]{:S(2)}) collective-permute-start(bf16[64,256]{1,0:T(8,128)(2,1)} %param.7), channel_id=1, source_target_pairs={{0,2},{1,3},{2,0},{3,1},{4,6},{5,7},{6,4},{7,5},{8,10},{9,11},{10,... | collective-permute-start | bytes 98312 | tf_op jit(solution)/shard_map/ppermute | solution.py:142
  3.7 0.0 collective-permute-start.2
  3.7 0.2 collective-permute-start.1
  4.5 1.1 %convert_add_fusion.refs_0_ = f32[72,1536]{1,0:T(8,128)S(1)} fusion(s32[1,64]{1,0:T(1,128)} %param.10, f32[1,1280]{1,0:T(1,128)} %param.9, bf16[64,256]{1,0:T(8,128)(2,1)} %param.7, bf16[64,1280]{1,0:T(8,128)(2,1)} %bitcast.10, s32[]{:T(128)} %bitcast.4, pred[72]{0:T(512)(128)(4,1)S(1)} %iota_compare_fusion), kind=kLoop, calls=%fused_computation | loop fusion | flops 774144 | bytes 644428 | tf_op jit(solution)/shard_map/add | solution.py:151
  5.6 0.2 collective-permute-done.refs_2_
  5.8 1.5 %collective-permute-done.2.refs_4_ = bf16[64,256]{1,0:T(8,128)(2,1)S(1)} collective-permute-done((bf16[64,256]{1,0:T(8,128)(2,1)}, bf16[64,256]{1,0:T(8,128)(2,1)S(1)}, u32[]{:S(2)}, u32[]{:S(2)}) %collective-permute-start.2) | collective-permute-done | bytes 32800 | tf_op jit(solution)/shard_map/ppermute | solution.py:142
  7.3 0.0 collective-permute-done.1.refs_3_
  7.3 2.9 %shard_map.85 = (f32[64,256]{1,0:T(8,128)S(1)}, f32[64,256]{1,0:T(8,128)S(1)}, bf16[64,256]{1,0:T(8,128)(2,1)S(1)}, bf16[64,256]{1,0:T(8,128)(2,1)S(1)}, bf16[80...) custom-call(f32[72,1536]{1,0:T(8,128)S(1)} %convert_add_fusion.refs_0_, bf16[1280,1024]{1,0:T(8,128)(2,1)} %bitcast.5, ...), custom_call_target="tpu_custom_call" | custom-call | tf_op jit(solution)/shard_map/pallas_call | solution.py:153
  10.2 0.1 collective-permute-start.5
  10.3 0.7 %collective-permute-start.3 = (bf16[64,256]{1,0:T(8,128)(2,1)S(1)}, bf16[64,256]{1,0:T(8,128)(2,1)S(1)}, u32[]{:S(2)}, u32[]{:S(2)}) collective-permute-start(bf16[64,256]{1,0:T(8,128)(2,1)S(1)} %get-tuple-element.45), channel_id=1, source_target_pairs={{0,2},{1,3},{2,0},{3,1},{4,6},{5,7},{6,4},{7,5},{8,10},{9,11},{10,... | collective-permute-start | bytes 98312 | tf_op jit(solution)/shard_map/ppermute | solution.py:142
  11.0 1.2 %collective-permute-start.4 = (bf16[64,256]{1,0:T(8,128)(2,1)S(1)}, bf16[64,256]{1,0:T(8,128)(2,1)S(1)}, u32[]{:S(2)}, u32[]{:S(2)}) collective-permute-start(bf16[64,256]{1,0:T(8,128)(2,1)S(1)} %get-tuple-element.46), channel_id=1, source_target_pairs={{0,3},{1,2},{2,1},{3,0},{4,7},{5,6},{6,5},{7,4},{8,11},{9,10},{10,... | collective-permute-start | bytes 98312 | tf_op jit(solution)/shard_map/ppermute | solution.py:142
  12.2 2.5 %shard_map.86 = (f32[64,1280]{1,0:T(8,128)}, f32[1,1280]{1,0:T(1,128)}) custom-call(f32[72,1536]{1,0:T(8,128)S(1)} %convert_add_fusion.refs_0_, bf16[80,1280]{1,0:T(8,128)(2,1)S(1)} %get-tuple-element.67.refs_1_, bf16[80,1024]{1,0:T(8,128)(2,1)S(1)} %get-tuple-element.49.refs_2_, bf16[1280,1024]{1,0:T(8,128)(2,1)} %bitcast.6), custom_call_target="tpu_custom_call" | custom-call | flops 134217728 | bytes 1048576 | tf_op jit(solution)/shard_map/pallas_call | solution.py:175
  14.7 0.0 collective-permute-done.3
  14.7 0.0 collective-permute-done.4
  14.7 0.0 collective-permute-done.5
  14.8 2.6 %collective-permute-start.8 = (bf16[64,256]{1,0:T(8,128)(2,1)S(1)}, bf16[64,256]{1,0:T(8,128)(2,1)S(1)}, u32[]{:S(2)}, u32[]{:S(2)}) collective-permute-start(bf16[64,256]{1,0:T(8,128)(2,1)S(1)} %get-tuple-element.56), channel_id=1, source_target_pairs={{0,12},{4,8},{8,4},{12,0},{16,28},{20,24},{24,20},{28,16},{1,13},{... | collective-permute-start | bytes 98312 | tf_op jit(solution)/shard_map/ppermute | solution.py:142
  17.4 0.4 %collective-permute-start.7 = (bf16[64,256]{1,0:T(8,128)(2,1)S(1)}, bf16[64,256]{1,0:T(8,128)(2,1)S(1)}, u32[]{:S(2)}, u32[]{:S(2)}) collective-permute-start(bf16[64,256]{1,0:T(8,128)(2,1)S(1)} %get-tuple-element.56), channel_id=1, source_target_pairs={{0,8},{4,12},{8,0},{12,4},{16,24},{20,28},{24,16},{28,20},{1,9},{5... | collective-permute-start | bytes 98312 | tf_op jit(solution)/shard_map/ppermute | solution.py:142
  17.8 0.5 %collective-permute-start.6 = (bf16[64,256]{1,0:T(8,128)(2,1)S(1)}, bf16[64,256]{1,0:T(8,128)(2,1)S(1)}, u32[]{:S(2)}, u32[]{:S(2)}) collective-permute-start(bf16[64,256]{1,0:T(8,128)(2,1)S(1)} %get-tuple-element.56), channel_id=1, source_target_pairs={{0,4},{4,0},{8,12},{12,8},{16,20},{20,16},{24,28},{28,24},{1,5},{5... | collective-permute-start | bytes 98312 | tf_op jit(solution)/shard_map/ppermute | solution.py:142
  18.3 2.5 %shard_map.87 = (f32[64,1280]{1,0:T(8,128)}, f32[1,1280]{1,0:T(1,128)}) custom-call(f32[72,1536]{1,0:T(8,128)S(1)} %convert_add_fusion.refs_0_, bf16[80,1280]{1,0:T(8,128)(2,1)S(1)} %get-tuple-element.67.refs_1_, bf16[80,1024]{1,0:T(8,128)(2,1)S(1)} %get-tuple-element.49.refs_2_, ...), custom_call_target="tpu_custom_call", output_to_operand_aliasing={{0}: (4, {}), {1}: (5, {})} | custom-call | flops 134217728 | bytes 1048576 | tf_op jit(solution)/shard_map/pallas_call | solution.py:175
  20.9 0.0 collective-permute-done.8
  20.9 0.4 %collective-permute-done.7 = bf16[64,256]{1,0:T(8,128)(2,1)S(1)} collective-permute-done((bf16[64,256]{1,0:T(8,128)(2,1)S(1)}, bf16[64,256]{1,0:T(8,128)(2,1)S(1)}, u32[]{:S(2)}, u32[]{:S(2)}) %collective-permute-start.7) | collective-permute-done | bytes 32800 | tf_op jit(solution)/shard_map/ppermute | solution.py:142
  21.3 0.4 %collective-permute-done.6 = bf16[64,256]{1,0:T(8,128)(2,1)S(1)} collective-permute-done((bf16[64,256]{1,0:T(8,128)(2,1)S(1)}, bf16[64,256]{1,0:T(8,128)(2,1)S(1)}, u32[]{:S(2)}, u32[]{:S(2)}) %collective-permute-start.6) | collective-permute-done | bytes 32800 | tf_op jit(solution)/shard_map/ppermute | solution.py:142
  21.8 2.7 %collective-permute-start.9 = (f32[64,256]{1,0:T(8,128)S(1)}, f32[64,256]{1,0:T(8,128)S(1)}, u32[]{:S(2)}, u32[]{:S(2)}) collective-permute-start(f32[64,256]{1,0:T(8,128)S(1)} %add_add_fusion), channel_id=1, source_target_pairs={{0,16},{4,20},{8,24},{12,28},{16,0},{20,4},{24,8},{28,12},{1,17},{... | collective-permute-start | bytes 196616 | tf_op jit(solution)/shard_map/ppermute | solution.py:142
  24.4 2.2 %shard_map.88 = (f32[64,1280]{1,0:T(8,128)}, f32[1,1280]{1,0:T(1,128)}) custom-call(f32[72,1536]{1,0:T(8,128)S(1)} %convert_add_fusion.refs_0_, bf16[80,1280]{1,0:T(8,128)(2,1)S(1)} %get-tuple-element.67.refs_1_, bf16[80,1024]{1,0:T(8,128)(2,1)S(1)} %get-tuple-element.49.refs_2_, ...), custom_call_target="tpu_custom_call", output_to_operand_aliasing={{0}: (4, {}), {1}: (5, {})} | custom-call | flops 67108864 | bytes 524288 | tf_op jit(solution)/shard_map/pallas_call | solution.py:175
  26.6 0.4 %collective-permute-done.9 = f32[64,256]{1,0:T(8,128)S(1)} collective-permute-done((f32[64,256]{1,0:T(8,128)S(1)}, f32[64,256]{1,0:T(8,128)S(1)}, u32[]{:S(2)}, u32[]{:S(2)}) %collective-permute-start.9) | collective-permute-done | bytes 65568 | tf_op jit(solution)/shard_map/ppermute | solution.py:142
  27.0 0.6 %add.47 = f32[64,256]{1,0:T(8,128)} add(f32[64,256]{1,0:T(8,128)S(1)} %add_add_fusion, f32[64,256]{1,0:T(8,128)S(1)} %collective-permute-done.9) | non-fusion elementwise | flops 16384 | bytes 196608 | tf_op jit(solution)/shard_map/add | solution.py:211
  (3 shorter events, 0.0 us)
Async XLA Ops:
  0.6 5.1 %collective-permute-start = (bf16[64,256]{1,0:T(8,128)(2,1)}, bf16[64,256]{1,0:T(8,128)(2,1)S(1)}, u32[]{:S(2)}, u32[]{:S(2)}) collective-permute-start(bf16[64,256]{1,0:T(8,128)(2,1)} %param.7), channel_id=1, source_target_pairs={{0,2},{1,3},{2,0},{3,1},{4,6},{5,7},{6,4},{7,5},{8,10},{9,11},{10,... | collective-permute-start | bytes 98312 | tf_op jit(solution)/shard_map/ppermute | solution.py:142
  3.7 3.6 %collective-permute-start.2 = (bf16[64,256]{1,0:T(8,128)(2,1)}, bf16[64,256]{1,0:T(8,128)(2,1)S(1)}, u32[]{:S(2)}, u32[]{:S(2)}) collective-permute-start(bf16[64,256]{1,0:T(8,128)(2,1)} %param.7), channel_id=1, source_target_pairs={{0,3},{1,2},{2,1},{3,0},{4,7},{5,6},{6,5},{7,4},{8,11},{9,10},{10,... | collective-permute-start | bytes 98312 | tf_op jit(solution)/shard_map/ppermute | solution.py:142
  3.7 3.6 %collective-permute-start.1 = (bf16[64,256]{1,0:T(8,128)(2,1)}, bf16[64,256]{1,0:T(8,128)(2,1)S(1)}, u32[]{:S(2)}, u32[]{:S(2)}) collective-permute-start(bf16[64,256]{1,0:T(8,128)(2,1)} %param.7), channel_id=1, source_target_pairs={{0,1},{1,0},{2,3},{3,2},{4,5},{5,4},{6,7},{7,6},{8,9},{9,8},{10,11... | collective-permute-start | bytes 98312 | tf_op jit(solution)/shard_map/ppermute | solution.py:142
  10.2 4.5 %collective-permute-start.5 = (f32[64,256]{1,0:T(8,128)S(1)}, f32[64,256]{1,0:T(8,128)S(1)}, u32[]{:S(2)}, u32[]{:S(2)}) collective-permute-start(f32[64,256]{1,0:T(8,128)S(1)} %get-tuple-element.47), channel_id=1, source_target_pairs={{0,1},{1,0},{2,3},{3,2},{4,5},{5,4},{6,7},{7,6},{8,9},{9,8},{10,11... | collective-permute-start | bytes 196616 | tf_op jit(solution)/shard_map/ppermute | solution.py:142
  10.3 4.4 %collective-permute-start.3 = (bf16[64,256]{1,0:T(8,128)(2,1)S(1)}, bf16[64,256]{1,0:T(8,128)(2,1)S(1)}, u32[]{:S(2)}, u32[]{:S(2)}) collective-permute-start(bf16[64,256]{1,0:T(8,128)(2,1)S(1)} %get-tuple-element.45), channel_id=1, source_target_pairs={{0,2},{1,3},{2,0},{3,1},{4,6},{5,7},{6,4},{7,5},{8,10},{9,11},{10,... | collective-permute-start | bytes 98312 | tf_op jit(solution)/shard_map/ppermute | solution.py:142
  11.0 3.8 %collective-permute-start.4 = (bf16[64,256]{1,0:T(8,128)(2,1)S(1)}, bf16[64,256]{1,0:T(8,128)(2,1)S(1)}, u32[]{:S(2)}, u32[]{:S(2)}) collective-permute-start(bf16[64,256]{1,0:T(8,128)(2,1)S(1)} %get-tuple-element.46), channel_id=1, source_target_pairs={{0,3},{1,2},{2,1},{3,0},{4,7},{5,6},{6,5},{7,4},{8,11},{9,10},{10,... | collective-permute-start | bytes 98312 | tf_op jit(solution)/shard_map/ppermute | solution.py:142
  14.8 6.1 %collective-permute-start.8 = (bf16[64,256]{1,0:T(8,128)(2,1)S(1)}, bf16[64,256]{1,0:T(8,128)(2,1)S(1)}, u32[]{:S(2)}, u32[]{:S(2)}) collective-permute-start(bf16[64,256]{1,0:T(8,128)(2,1)S(1)} %get-tuple-element.56), channel_id=1, source_target_pairs={{0,12},{4,8},{8,4},{12,0},{16,28},{20,24},{24,20},{28,16},{1,13},{... | collective-permute-start | bytes 98312 | tf_op jit(solution)/shard_map/ppermute | solution.py:142
  17.4 3.9 %collective-permute-start.7 = (bf16[64,256]{1,0:T(8,128)(2,1)S(1)}, bf16[64,256]{1,0:T(8,128)(2,1)S(1)}, u32[]{:S(2)}, u32[]{:S(2)}) collective-permute-start(bf16[64,256]{1,0:T(8,128)(2,1)S(1)} %get-tuple-element.56), channel_id=1, source_target_pairs={{0,8},{4,12},{8,0},{12,4},{16,24},{20,28},{24,16},{28,20},{1,9},{5... | collective-permute-start | bytes 98312 | tf_op jit(solution)/shard_map/ppermute | solution.py:142
  17.8 3.9 %collective-permute-start.6 = (bf16[64,256]{1,0:T(8,128)(2,1)S(1)}, bf16[64,256]{1,0:T(8,128)(2,1)S(1)}, u32[]{:S(2)}, u32[]{:S(2)}) collective-permute-start(bf16[64,256]{1,0:T(8,128)(2,1)S(1)} %get-tuple-element.56), channel_id=1, source_target_pairs={{0,4},{4,0},{8,12},{12,8},{16,20},{20,16},{24,28},{28,24},{1,5},{5... | collective-permute-start | bytes 98312 | tf_op jit(solution)/shard_map/ppermute | solution.py:142
  21.8 5.2 %collective-permute-start.9 = (f32[64,256]{1,0:T(8,128)S(1)}, f32[64,256]{1,0:T(8,128)S(1)}, u32[]{:S(2)}, u32[]{:S(2)}) collective-permute-start(f32[64,256]{1,0:T(8,128)S(1)} %add_add_fusion), channel_id=1, source_target_pairs={{0,16},{4,20},{8,24},{12,28},{16,0},{20,4},{24,8},{28,12},{1,17},{... | collective-permute-start | bytes 196616 | tf_op jit(solution)/shard_map/ppermute | solution.py:142

commit v14 on v13

--- a/solution.py
+++ b/solution.py
@@ -166,7 +166,7 @@
         compiler_params=params,
     )(pack, counts[0], *arrived)
 
-    shares = [(0, 2 * chunk), (2 * chunk, 2 * chunk), (4 * chunk, neurons - 4 * chunk)]
+    shares = [(0, 2 * chunk), (2 * chunk, neurons - 2 * chunk)]
     made = []
 
     def make(before):
@@ -198,20 +198,19 @@
     value = functools.reduce(jnp.add, [outs[0]] + [block.astype(F32) for block in arrived])
     mask = 1
     while mask < region_count:
-        masks = [mask, 2 * mask, 3 * mask] if 2 * mask < region_count else [mask]
-        several = len(masks) > 1
-        if several:
+        group = min(8, region_count // mask)
+        if group > 2:
             value = lax.reduce_precision(value, 8, 7)
-        sent = value.astype(BF16) if several else value
+        sent = value.astype(BF16) if group > 2 else value
         if shares:
             (value, sent), made = make((value, sent))
-        arrived = [swap(sent, "region", region_count, k) for k in masks]
+        arrived = [swap(sent, "region", region_count, k * mask) for k in range(1, group)]
         arrived, made = lax.optimization_barrier((arrived, made))
-        arrived = [block.astype(F32) for block in arrived]
-        value = value + arrived[0]
-        if several:
-            value = value + (arrived[1] + arrived[2])
-        mask *= 1 + len(masks)
+        terms = [value] + [block.astype(F32) for block in arrived]
+        while len(terms) > 1:
+            terms = [terms[i] + terms[i + 1] for i in range(0, len(terms), 2)]
+        value = terms[0]
+        mask *= group
     grad_load, grad_bias = made
     return (value, grad_load[None], grad_bias)
 

time: 28 us -> 30.5 us (1.089)
  starting transfers between devices: 11.4 us -> 16.4 us
  waiting for transfers between devices: 3 us -> 1.73 us
  Pallas kernels: 10.1 us -> 8.98 us
    ppermute x10 -> x13, starting transfers between devices: 11.4 us -> 16.4 us  [swap(): return lax.ppermute(value, axis, [(i, i ^ mask) for i in range(count)])]
    ppermute x10 -> x13, waiting for transfers between devices: 3 us -> 1.73 us  [swap(): return lax.ppermute(value, axis, [(i, i ^ mask) for i in range(count)])]
    pallas_call x3 -> x2, Pallas kernels: 7.23 us -> 6.07 us  [make(): pl.pallas_call(functools.partial(load_kernel, lats, first, chunk, step),...]
    add x2 -> x1, other arithmetic: 0.65 us -> 0.67 us  [per_device(): terms = [terms[i] + terms[i + 1] for i in range(0, len(terms), 2)]]
  transfers between devices with their start and end apart: 10 -> 13, of which waited for: 5 -> 2; matrix products, arithmetic and copies ran while one was open for 4% -> 4% of each run, Pallas kernels for 26% -> 20%
where the time goes in v14:
time: 30.5 us; the launch traced here: 30.2 us
  starting transfers between devices  16.4 us (54%)
  Pallas kernels  8.98 us (29%)
  other arithmetic  1.77 us (6%)
  waiting for transfers between devices  1.73 us (6%)
  between operations  1.39 us (5%)
    ppermute x13, starting transfers between devices, swap(): return lax.ppermute(value, axis, [(i, i ^ mask) for i in range(count)])  16.4 us
    pallas_call x2, Pallas kernels, make(): pl.pallas_call(functools.partial(load_kernel, lats, first, chunk, step),...  6.07 us
    pallas_call x1, Pallas kernels, per_device(): pl.pallas_call(functools.partial(shift_kernel, neuron_count, order, 'neur...  2.91 us
    ppermute x13, waiting for transfers between devices, swap(): return lax.ppermute(value, axis, [(i, i ^ mask) for i in range(count)])  1.73 us
    add x1, other arithmetic, per_device(): pack = pack + jnp.pad(latents, ((0, 8), (neurons, 0))).astype(F32)  1.07 us
    add x1, other arithmetic, per_device(): terms = [terms[i] + terms[i + 1] for i in range(0, len(terms), 2)]  0.67 us
  transfers between devices with their start and end apart: 13, of which 2 were waited for; matrix products, arithmetic and copies ran while one was open for 4% of the time, Pallas kernels for 20%

profile of v14, /device:TPU:0, one launch (start us, length us, event | category | flops | bytes accessed | tf_op | source)
XLA Modules:
  0.0 30.2 jit_solution(6012250295243434658)
XLA Ops:
  0.6 3.0 %collective-permute-start = (bf16[64,256]{1,0:T(8,128)(2,1)}, bf16[64,256]{1,0:T(8,128)(2,1)S(1)}, u32[]{:S(2)}, u32[]{:S(2)}) collective-permute-start(bf16[64,256]{1,0:T(8,128)(2,1)} %param.7), channel_id=1, source_target_pairs={{0,2},{1,3},{2,0},{3,1},{4,6},{5,7},{6,4},{7,5},{8,10},{9,11},{10,... | collective-permute-start | bytes 98312 | tf_op jit(solution)/shard_map/ppermute | solution.py:142
  3.7 0.0 collective-permute-start.2
  3.7 0.2 collective-permute-start.1
  4.5 1.1 %convert_add_fusion.refs_0_ = f32[72,1536]{1,0:T(8,128)S(1)} fusion(s32[1,64]{1,0:T(1,128)} %param.10, f32[1,1280]{1,0:T(1,128)} %param.9, bf16[64,256]{1,0:T(8,128)(2,1)} %param.7, bf16[64,1280]{1,0:T(8,128)(2,1)} %bitcast.9, s32[]{:T(128)} %bitcast.4, pred[72]{0:T(512)(128)(4,1)S(1)} %iota_compare_fusion), kind=kLoop, calls=%fused_computation | loop fusion | flops 774144 | bytes 644428 | tf_op jit(solution)/shard_map/add | solution.py:151
  5.6 0.2 collective-permute-done.refs_2_
  5.8 1.5 %collective-permute-done.2.refs_4_ = bf16[64,256]{1,0:T(8,128)(2,1)S(1)} collective-permute-done((bf16[64,256]{1,0:T(8,128)(2,1)}, bf16[64,256]{1,0:T(8,128)(2,1)S(1)}, u32[]{:S(2)}, u32[]{:S(2)}) %collective-permute-start.2) | collective-permute-done | bytes 32800 | tf_op jit(solution)/shard_map/ppermute | solution.py:142
  7.3 0.0 collective-permute-done.1.refs_3_
  7.3 2.9 %shard_map.85 = (f32[64,256]{1,0:T(8,128)S(1)}, f32[64,256]{1,0:T(8,128)S(1)}, bf16[64,256]{1,0:T(8,128)(2,1)S(1)}, bf16[64,256]{1,0:T(8,128)(2,1)S(1)}, bf16[80...) custom-call(f32[72,1536]{1,0:T(8,128)S(1)} %convert_add_fusion.refs_0_, bf16[1280,1024]{1,0:T(8,128)(2,1)} %bitcast.5, ...), custom_call_target="tpu_custom_call" | custom-call | tf_op jit(solution)/shard_map/pallas_call | solution.py:153
  10.2 0.1 collective-permute-start.5
  10.3 0.7 %collective-permute-start.3 = (bf16[64,256]{1,0:T(8,128)(2,1)S(1)}, bf16[64,256]{1,0:T(8,128)(2,1)S(1)}, u32[]{:S(2)}, u32[]{:S(2)}) collective-permute-start(bf16[64,256]{1,0:T(8,128)(2,1)S(1)} %get-tuple-element.41), channel_id=1, source_target_pairs={{0,2},{1,3},{2,0},{3,1},{4,6},{5,7},{6,4},{7,5},{8,10},{9,11},{10,... | collective-permute-start | bytes 98312 | tf_op jit(solution)/shard_map/ppermute | solution.py:142
  11.0 1.2 %collective-permute-start.4 = (bf16[64,256]{1,0:T(8,128)(2,1)S(1)}, bf16[64,256]{1,0:T(8,128)(2,1)S(1)}, u32[]{:S(2)}, u32[]{:S(2)}) collective-permute-start(bf16[64,256]{1,0:T(8,128)(2,1)S(1)} %get-tuple-element.42), channel_id=1, source_target_pairs={{0,3},{1,2},{2,1},{3,0},{4,7},{5,6},{6,5},{7,4},{8,11},{9,10},{10,... | collective-permute-start | bytes 98312 | tf_op jit(solution)/shard_map/ppermute | solution.py:142
  12.2 2.5 %shard_map.86 = (f32[64,1280]{1,0:T(8,128)}, f32[1,1280]{1,0:T(1,128)}) custom-call(f32[72,1536]{1,0:T(8,128)S(1)} %convert_add_fusion.refs_0_, bf16[80,1280]{1,0:T(8,128)(2,1)S(1)} %get-tuple-element.53.refs_1_, bf16[80,1024]{1,0:T(8,128)(2,1)S(1)} %get-tuple-element.45.refs_2_, bf16[1280,1024]{1,0:T(8,128)(2,1)} %bitcast.6), custom_call_target="tpu_custom_call" | custom-call | flops 134217728 | bytes 1048576 | tf_op jit(solution)/shard_map/pallas_call | solution.py:175
  14.7 0.0 collective-permute-done.3
  14.7 0.0 collective-permute-done.4
  14.7 0.0 collective-permute-done.5
  14.8 4.7 %collective-permute-start.12 = (bf16[64,256]{1,0:T(8,128)(2,1)S(1)}, bf16[64,256]{1,0:T(8,128)(2,1)S(1)}, u32[]{:S(2)}, u32[]{:S(2)}) collective-permute-start(bf16[64,256]{1,0:T(8,128)(2,1)S(1)} %get-tuple-element.52), channel_id=1, source_target_pairs={{0,28},{4,24},{8,20},{12,16},{16,12},{20,8},{24,4},{28,0},{1,29},{... | collective-permute-start | bytes 98312 | tf_op jit(solution)/shard_map/ppermute | solution.py:142
  19.4 0.2 collective-permute-start.11
  19.6 0.8 %collective-permute-start.10 = (bf16[64,256]{1,0:T(8,128)(2,1)S(1)}, bf16[64,256]{1,0:T(8,128)(2,1)S(1)}, u32[]{:S(2)}, u32[]{:S(2)}) collective-permute-start(bf16[64,256]{1,0:T(8,128)(2,1)S(1)} %get-tuple-element.52), channel_id=1, source_target_pairs={{0,20},{4,16},{8,28},{12,24},{16,4},{20,0},{24,12},{28,8},{1,21},{... | collective-permute-start | bytes 98312 | tf_op jit(solution)/shard_map/ppermute | solution.py:142
  20.4 2.1 %collective-permute-start.9 = (bf16[64,256]{1,0:T(8,128)(2,1)S(1)}, bf16[64,256]{1,0:T(8,128)(2,1)S(1)}, u32[]{:S(2)}, u32[]{:S(2)}) collective-permute-start(bf16[64,256]{1,0:T(8,128)(2,1)S(1)} %get-tuple-element.52), channel_id=1, source_target_pairs={{0,16},{4,20},{8,24},{12,28},{16,0},{20,4},{24,8},{28,12},{1,17},{... | collective-permute-start | bytes 98312 | tf_op jit(solution)/shard_map/ppermute | solution.py:142
  22.5 2.2 %collective-permute-start.8 = (bf16[64,256]{1,0:T(8,128)(2,1)S(1)}, bf16[64,256]{1,0:T(8,128)(2,1)S(1)}, u32[]{:S(2)}, u32[]{:S(2)}) collective-permute-start(bf16[64,256]{1,0:T(8,128)(2,1)S(1)} %get-tuple-element.52), channel_id=1, source_target_pairs={{0,12},{4,8},{8,4},{12,0},{16,28},{20,24},{24,20},{28,16},{1,13},{... | collective-permute-start | bytes 98312 | tf_op jit(solution)/shard_map/ppermute | solution.py:142
  24.7 0.0 collective-permute-done.12
  24.7 0.8 %collective-permute-start.7 = (bf16[64,256]{1,0:T(8,128)(2,1)S(1)}, bf16[64,256]{1,0:T(8,128)(2,1)S(1)}, u32[]{:S(2)}, u32[]{:S(2)}) collective-permute-start(bf16[64,256]{1,0:T(8,128)(2,1)S(1)} %get-tuple-element.52), channel_id=1, source_target_pairs={{0,8},{4,12},{8,0},{12,4},{16,24},{20,28},{24,16},{28,20},{1,9},{5... | collective-permute-start | bytes 98312 | tf_op jit(solution)/shard_map/ppermute | solution.py:142
  25.5 0.0 collective-permute-done.11
  25.5 0.5 %collective-permute-start.6 = (bf16[64,256]{1,0:T(8,128)(2,1)S(1)}, bf16[64,256]{1,0:T(8,128)(2,1)S(1)}, u32[]{:S(2)}, u32[]{:S(2)}) collective-permute-start(bf16[64,256]{1,0:T(8,128)(2,1)S(1)} %get-tuple-element.52), channel_id=1, source_target_pairs={{0,4},{4,0},{8,12},{12,8},{16,20},{20,16},{24,28},{28,24},{1,5},{5... | collective-permute-start | bytes 98312 | tf_op jit(solution)/shard_map/ppermute | solution.py:142
  26.0 3.5 %shard_map.87 = (f32[64,1280]{1,0:T(8,128)}, f32[1,1280]{1,0:T(1,128)}) custom-call(f32[72,1536]{1,0:T(8,128)S(1)} %convert_add_fusion.refs_0_, bf16[80,1280]{1,0:T(8,128)(2,1)S(1)} %get-tuple-element.53.refs_1_, bf16[80,1024]{1,0:T(8,128)(2,1)S(1)} %get-tuple-element.45.refs_2_, ...), custom_call_target="tpu_custom_call", output_to_operand_aliasing={{0}: (4, {}), {1}: (5, {})} | custom-call | flops 201326592 | bytes 1572864 | tf_op jit(solution)/shard_map/pallas_call | solution.py:175
  29.5 0.0 collective-permute-done.10
  29.5 0.0 collective-permute-done.9
  29.5 0.0 collective-permute-done.8
  29.5 0.0 collective-permute-done.7
  29.6 0.0 collective-permute-done.6
  29.6 0.7 %add_add_fusion = f32[64,256]{1,0:T(8,128)} fusion(bf16[64,256]{1,0:T(8,128)(2,1)S(1)} %collective-permute-done.12, bf16[64,256]{1,0:T(8,128)(2,1)S(1)} %collective-permute-done.11, bf16[64,256]{1,0:T(8,128)(2,1)S(1)} %collective-permute-done.10, bf16[64,256]{1,0:T(8,128)(2,1)S(1)} %collective-permute-done.9, bf16[64,256]{1,0:T(8,128)(2,1)S(1)} %collective-permute-done.8, ...), kind=kLoop, calls=%fused_computation.1 | loop fusion | flops 229376 | bytes 360448 | tf_op jit(solution)/shard_map/add | solution.py:211
  (2 shorter events, 0.0 us)
Async XLA Ops:
  0.6 5.1 %collective-permute-start = (bf16[64,256]{1,0:T(8,128)(2,1)}, bf16[64,256]{1,0:T(8,128)(2,1)S(1)}, u32[]{:S(2)}, u32[]{:S(2)}) collective-permute-start(bf16[64,256]{1,0:T(8,128)(2,1)} %param.7), channel_id=1, source_target_pairs={{0,2},{1,3},{2,0},{3,1},{4,6},{5,7},{6,4},{7,5},{8,10},{9,11},{10,... | collective-permute-start | bytes 98312 | tf_op jit(solution)/shard_map/ppermute | solution.py:142
  3.7 3.6 %collective-permute-start.2 = (bf16[64,256]{1,0:T(8,128)(2,1)}, bf16[64,256]{1,0:T(8,128)(2,1)S(1)}, u32[]{:S(2)}, u32[]{:S(2)}) collective-permute-start(bf16[64,256]{1,0:T(8,128)(2,1)} %param.7), channel_id=1, source_target_pairs={{0,3},{1,2},{2,1},{3,0},{4,7},{5,6},{6,5},{7,4},{8,11},{9,10},{10,... | collective-permute-start | bytes 98312 | tf_op jit(solution)/shard_map/ppermute | solution.py:142
  3.7 3.6 %collective-permute-start.1 = (bf16[64,256]{1,0:T(8,128)(2,1)}, bf16[64,256]{1,0:T(8,128)(2,1)S(1)}, u32[]{:S(2)}, u32[]{:S(2)}) collective-permute-start(bf16[64,256]{1,0:T(8,128)(2,1)} %param.7), channel_id=1, source_target_pairs={{0,1},{1,0},{2,3},{3,2},{4,5},{5,4},{6,7},{7,6},{8,9},{9,8},{10,11... | collective-permute-start | bytes 98312 | tf_op jit(solution)/shard_map/ppermute | solution.py:142
  10.2 4.5 %collective-permute-start.5 = (f32[64,256]{1,0:T(8,128)S(1)}, f32[64,256]{1,0:T(8,128)S(1)}, u32[]{:S(2)}, u32[]{:S(2)}) collective-permute-start(f32[64,256]{1,0:T(8,128)S(1)} %get-tuple-element.43), channel_id=1, source_target_pairs={{0,1},{1,0},{2,3},{3,2},{4,5},{5,4},{6,7},{7,6},{8,9},{9,8},{10,11... | collective-permute-start | bytes 196616 | tf_op jit(solution)/shard_map/ppermute | solution.py:142
  10.3 4.4 %collective-permute-start.3 = (bf16[64,256]{1,0:T(8,128)(2,1)S(1)}, bf16[64,256]{1,0:T(8,128)(2,1)S(1)}, u32[]{:S(2)}, u32[]{:S(2)}) collective-permute-start(bf16[64,256]{1,0:T(8,128)(2,1)S(1)} %get-tuple-element.41), channel_id=1, source_target_pairs={{0,2},{1,3},{2,0},{3,1},{4,6},{5,7},{6,4},{7,5},{8,10},{9,11},{10,... | collective-permute-start | bytes 98312 | tf_op jit(solution)/shard_map/ppermute | solution.py:142
  11.0 3.8 %collective-permute-start.4 = (bf16[64,256]{1,0:T(8,128)(2,1)S(1)}, bf16[64,256]{1,0:T(8,128)(2,1)S(1)}, u32[]{:S(2)}, u32[]{:S(2)}) collective-permute-start(bf16[64,256]{1,0:T(8,128)(2,1)S(1)} %get-tuple-element.42), channel_id=1, source_target_pairs={{0,3},{1,2},{2,1},{3,0},{4,7},{5,6},{6,5},{7,4},{8,11},{9,10},{10,... | collective-permute-start | bytes 98312 | tf_op jit(solution)/shard_map/ppermute | solution.py:142
  14.8 10.0 %collective-permute-start.12 = (bf16[64,256]{1,0:T(8,128)(2,1)S(1)}, bf16[64,256]{1,0:T(8,128)(2,1)S(1)}, u32[]{:S(2)}, u32[]{:S(2)}) collective-permute-start(bf16[64,256]{1,0:T(8,128)(2,1)S(1)} %get-tuple-element.52), channel_id=1, source_target_pairs={{0,28},{4,24},{8,20},{12,16},{16,12},{20,8},{24,4},{28,0},{1,29},{... | collective-permute-start | bytes 98312 | tf_op jit(solution)/shard_map/ppermute | solution.py:142
  19.4 6.1 %collective-permute-start.11 = (bf16[64,256]{1,0:T(8,128)(2,1)S(1)}, bf16[64,256]{1,0:T(8,128)(2,1)S(1)}, u32[]{:S(2)}, u32[]{:S(2)}) collective-permute-start(bf16[64,256]{1,0:T(8,128)(2,1)S(1)} %get-tuple-element.52), channel_id=1, source_target_pairs={{0,24},{4,28},{8,16},{12,20},{16,8},{20,12},{24,0},{28,4},{1,25},{... | collective-permute-start | bytes 98312 | tf_op jit(solution)/shard_map/ppermute | solution.py:142
  19.6 9.9 %collective-permute-start.10 = (bf16[64,256]{1,0:T(8,128)(2,1)S(1)}, bf16[64,256]{1,0:T(8,128)(2,1)S(1)}, u32[]{:S(2)}, u32[]{:S(2)}) collective-permute-start(bf16[64,256]{1,0:T(8,128)(2,1)S(1)} %get-tuple-element.52), channel_id=1, source_target_pairs={{0,20},{4,16},{8,28},{12,24},{16,4},{20,0},{24,12},{28,8},{1,21},{... | collective-permute-start | bytes 98312 | tf_op jit(solution)/shard_map/ppermute | solution.py:142
  20.4 9.1 %collective-permute-start.9 = (bf16[64,256]{1,0:T(8,128)(2,1)S(1)}, bf16[64,256]{1,0:T(8,128)(2,1)S(1)}, u32[]{:S(2)}, u32[]{:S(2)}) collective-permute-start(bf16[64,256]{1,0:T(8,128)(2,1)S(1)} %get-tuple-element.52), channel_id=1, source_target_pairs={{0,16},{4,20},{8,24},{12,28},{16,0},{20,4},{24,8},{28,12},{1,17},{... | collective-permute-start | bytes 98312 | tf_op jit(solution)/shard_map/ppermute | solution.py:142
  22.5 7.1 %collective-permute-start.8 = (bf16[64,256]{1,0:T(8,128)(2,1)S(1)}, bf16[64,256]{1,0:T(8,128)(2,1)S(1)}, u32[]{:S(2)}, u32[]{:S(2)}) collective-permute-start(bf16[64,256]{1,0:T(8,128)(2,1)S(1)} %get-tuple-element.52), channel_id=1, source_target_pairs={{0,12},{4,8},{8,4},{12,0},{16,28},{20,24},{24,20},{28,16},{1,13},{... | collective-permute-start | bytes 98312 | tf_op jit(solution)/shard_map/ppermute | solution.py:142
  24.7 4.8 %collective-permute-start.7 = (bf16[64,256]{1,0:T(8,128)(2,1)S(1)}, bf16[64,256]{1,0:T(8,128)(2,1)S(1)}, u32[]{:S(2)}, u32[]{:S(2)}) collective-permute-start(bf16[64,256]{1,0:T(8,128)(2,1)S(1)} %get-tuple-element.52), channel_id=1, source_target_pairs={{0,8},{4,12},{8,0},{12,4},{16,24},{20,28},{24,16},{28,20},{1,9},{5... | collective-permute-start | bytes 98312 | tf_op jit(solution)/shard_map/ppermute | solution.py:142
  25.5 4.1 %collective-permute-start.6 = (bf16[64,256]{1,0:T(8,128)(2,1)S(1)}, bf16[64,256]{1,0:T(8,128)(2,1)S(1)}, u32[]{:S(2)}, u32[]{:S(2)}) collective-permute-start(bf16[64,256]{1,0:T(8,128)(2,1)S(1)} %get-tuple-element.52), channel_id=1, source_target_pairs={{0,4},{4,0},{8,12},{12,8},{16,20},{20,16},{24,28},{28,24},{1,5},{5... | collective-permute-start | bytes 98312 | tf_op jit(solution)/shard_map/ppermute | solution.py:142

commit v15 on v13

--- a/solution.py
+++ b/solution.py
@@ -130,6 +130,18 @@
         copy.wait()
 
 
+def encode(value):
+    top = jnp.maximum(jnp.max(jnp.abs(value), axis=0, keepdims=True), 2.0**-100)
+    power = jnp.ceil(jnp.log2(top)) - 14.0
+    rows = jnp.broadcast_to(power, (8, value.shape[1]))
+    return jnp.concatenate([value * jnp.exp2(-power), rows], axis=0).astype(jnp.float16)
+
+
+def decode(code):
+    power = code[-8:-7].astype(F32)
+    return code[:-8].astype(F32) * jnp.exp2(power)
+
+
 def per_device(region_count, neuron_count, counts, latents, loadings, bias, delays, recorded):
     neurons, total = counts.shape[1:]
     lats, width = latents.shape
@@ -199,18 +211,14 @@
     mask = 1
     while mask < region_count:
         masks = [mask, 2 * mask, 3 * mask] if 2 * mask < region_count else [mask]
-        several = len(masks) > 1
-        if several:
-            value = lax.reduce_precision(value, 8, 7)
-        sent = value.astype(BF16) if several else value
+        code = lax.optimization_barrier(encode(value))
         if shares:
-            (value, sent), made = make((value, sent))
-        arrived = [swap(sent, "region", region_count, k) for k in masks]
+            code, made = make(code)
+        arrived = [swap(code, "region", region_count, k) for k in masks]
         arrived, made = lax.optimization_barrier((arrived, made))
-        arrived = [block.astype(F32) for block in arrived]
-        value = value + arrived[0]
-        if several:
-            value = value + (arrived[1] + arrived[2])
+        value = decode(code) + decode(arrived[0])
+        if len(masks) == 3:
+            value = value + (decode(arrived[1]) + decode(arrived[2]))
         mask *= 1 + len(masks)
     grad_load, grad_bias = made
     return (value, grad_load[None], grad_bias)

time: 28 us -> 28 us (level)
  waiting for transfers between devices: 3 us -> 2.71 us
    ppermute x10, waiting for transfers between devices: 3 us -> 2.71 us  [swap(): return lax.ppermute(value, axis, [(i, i ^ mask) for i in range(count)])]
    add x2 -> x1, other arithmetic: 0.65 us -> 0.65 us  [per_device(): value = decode(code) + decode(arrived[0])]
where the time goes in v15:
time: 28 us; the launch traced here: 27.7 us
  starting transfers between devices  11.4 us (41%)
  Pallas kernels  10.2 us (36%)
  waiting for transfers between devices  2.71 us (10%)
  other arithmetic  1.99 us (7%)
  between operations  1.41 us (5%)
    ppermute x10, starting transfers between devices, swap(): return lax.ppermute(value, axis, [(i, i ^ mask) for i in range(count)])  11.4 us
    pallas_call x3, Pallas kernels, make(): pl.pallas_call(functools.partial(load_kernel, lats, first, chunk, step),...  7.25 us
    pallas_call x1, Pallas kernels, per_device(): pl.pallas_call(functools.partial(shift_kernel, neuron_count, order, 'neur...  2.91 us
    ppermute x10, waiting for transfers between devices, swap(): return lax.ppermute(value, axis, [(i, i ^ mask) for i in range(count)])  2.71 us
    add x1, other arithmetic, per_device(): pack = pack + jnp.pad(latents, ((0, 8), (neurons, 0))).astype(F32)  1.07 us
    add x1, other arithmetic, per_device(): value = decode(code) + decode(arrived[0])  0.65 us
  transfers between devices with their start and end apart: 10, of which 5 were waited for; matrix products, arithmetic and copies ran while one was open for 4% of the time, Pallas kernels for 26%

profile of v15, /device:TPU:0, one launch (start us, length us, event | category | flops | bytes accessed | tf_op | source)
XLA Modules:
  0.0 27.7 jit_solution(9284683375167635889)
XLA Ops:
  0.6 3.0 %collective-permute-start = (bf16[64,256]{1,0:T(8,128)(2,1)}, bf16[64,256]{1,0:T(8,128)(2,1)S(1)}, u32[]{:S(2)}, u32[]{:S(2)}) collective-permute-start(bf16[64,256]{1,0:T(8,128)(2,1)} %param.7), channel_id=1, source_target_pairs={{0,2},{1,3},{2,0},{3,1},{4,6},{5,7},{6,4},{7,5},{8,10},{9,11},{10,... | collective-permute-start | bytes 98312 | tf_op jit(solution)/shard_map/ppermute | solution.py:154
  3.7 0.0 collective-permute-start.2
  3.7 0.2 collective-permute-start.1
  4.5 1.1 %convert_add_fusion.refs_0_ = f32[72,1536]{1,0:T(8,128)S(1)} fusion(s32[1,64]{1,0:T(1,128)} %param.10, f32[1,1280]{1,0:T(1,128)} %param.9, bf16[64,256]{1,0:T(8,128)(2,1)} %param.7, bf16[64,1280]{1,0:T(8,128)(2,1)} %bitcast.16, s32[]{:T(128)} %bitcast.10, pred[72]{0:T(512)(128)(4,1)S(1)} %iota_compare_fusion), kind=kLoop, calls=%fused_computation | loop fusion | flops 774144 | bytes 644428 | tf_op jit(solution)/shard_map/add | solution.py:163
  5.6 0.2 collective-permute-done.refs_2_
  5.8 1.5 %collective-permute-done.2.refs_4_ = bf16[64,256]{1,0:T(8,128)(2,1)S(1)} collective-permute-done((bf16[64,256]{1,0:T(8,128)(2,1)}, bf16[64,256]{1,0:T(8,128)(2,1)S(1)}, u32[]{:S(2)}, u32[]{:S(2)}) %collective-permute-start.2) | collective-permute-done | bytes 32800 | tf_op jit(solution)/shard_map/ppermute | solution.py:154
  7.3 0.0 collective-permute-done.1.refs_3_
  7.3 2.9 %shard_map.85 = (f32[64,256]{1,0:T(8,128)S(1)}, f32[64,256]{1,0:T(8,128)S(1)}, bf16[64,256]{1,0:T(8,128)(2,1)S(1)}, bf16[64,256]{1,0:T(8,128)(2,1)S(1)}, bf16[80...) custom-call(f32[72,1536]{1,0:T(8,128)S(1)} %convert_add_fusion.refs_0_, bf16[1280,1024]{1,0:T(8,128)(2,1)} %bitcast.11, ...), custom_call_target="tpu_custom_call" | custom-call | tf_op jit(solution)/shard_map/pallas_call | solution.py:165
  10.2 0.1 collective-permute-start.5
  10.3 0.7 %collective-permute-start.3 = (bf16[64,256]{1,0:T(8,128)(2,1)S(1)}, bf16[64,256]{1,0:T(8,128)(2,1)S(1)}, u32[]{:S(2)}, u32[]{:S(2)}) collective-permute-start(bf16[64,256]{1,0:T(8,128)(2,1)S(1)} %get-tuple-element.43), channel_id=1, source_target_pairs={{0,2},{1,3},{2,0},{3,1},{4,6},{5,7},{6,4},{7,5},{8,10},{9,11},{10,... | collective-permute-start | bytes 98312 | tf_op jit(solution)/shard_map/ppermute | solution.py:154
  11.0 1.2 %collective-permute-start.4 = (bf16[64,256]{1,0:T(8,128)(2,1)S(1)}, bf16[64,256]{1,0:T(8,128)(2,1)S(1)}, u32[]{:S(2)}, u32[]{:S(2)}) collective-permute-start(bf16[64,256]{1,0:T(8,128)(2,1)S(1)} %get-tuple-element.44), channel_id=1, source_target_pairs={{0,3},{1,2},{2,1},{3,0},{4,7},{5,6},{6,5},{7,4},{8,11},{9,10},{10,... | collective-permute-start | bytes 98312 | tf_op jit(solution)/shard_map/ppermute | solution.py:154
  12.2 2.5 %shard_map.86 = (f32[64,1280]{1,0:T(8,128)}, f32[1,1280]{1,0:T(1,128)}) custom-call(f32[72,1536]{1,0:T(8,128)S(1)} %convert_add_fusion.refs_0_, bf16[80,1280]{1,0:T(8,128)(2,1)S(1)} %get-tuple-element.63.refs_1_, bf16[80,1024]{1,0:T(8,128)(2,1)S(1)} %get-tuple-element.47.refs_2_, bf16[1280,1024]{1,0:T(8,128)(2,1)} %bitcast.12), custom_call_target="tpu_custom_call" | custom-call | flops 134217728 | bytes 1048576 | tf_op jit(solution)/shard_map/pallas_call | solution.py:187
  14.7 0.0 collective-permute-done.3
  14.7 0.0 collective-permute-done.4
  14.7 0.0 collective-permute-done.5
  14.9 2.6 %collective-permute-start.8 = (f16[72,256]{1,0:T(8,128)(2,1)S(1)}, f16[72,256]{1,0:T(8,128)(2,1)S(1)}, u32[]{:S(2)}, u32[]{:S(2)}) collective-permute-start(f16[72,256]{1,0:T(8,128)(2,1)S(1)} %pad_maximum_fusion), channel_id=1, source_target_pairs={{0,12},{4,8},{8,4},{12,0},{16,28},{20,24},{24,20},{28,16},{1,13},{... | collective-permute-start | bytes 110600 | tf_op jit(solution)/shard_map/ppermute | solution.py:154
  17.5 0.4 %collective-permute-start.7 = (f16[72,256]{1,0:T(8,128)(2,1)S(1)}, f16[72,256]{1,0:T(8,128)(2,1)S(1)}, u32[]{:S(2)}, u32[]{:S(2)}) collective-permute-start(f16[72,256]{1,0:T(8,128)(2,1)S(1)} %pad_maximum_fusion), channel_id=1, source_target_pairs={{0,8},{4,12},{8,0},{12,4},{16,24},{20,28},{24,16},{28,20},{1,9},{5... | collective-permute-start | bytes 110600 | tf_op jit(solution)/shard_map/ppermute | solution.py:154
  17.9 0.5 %collective-permute-start.6 = (f16[72,256]{1,0:T(8,128)(2,1)S(1)}, f16[72,256]{1,0:T(8,128)(2,1)S(1)}, u32[]{:S(2)}, u32[]{:S(2)}) collective-permute-start(f16[72,256]{1,0:T(8,128)(2,1)S(1)} %pad_maximum_fusion), channel_id=1, source_target_pairs={{0,4},{4,0},{8,12},{12,8},{16,20},{20,16},{24,28},{28,24},{1,5},{5... | collective-permute-start | bytes 110600 | tf_op jit(solution)/shard_map/ppermute | solution.py:154
  18.4 2.5 %shard_map.87 = (f32[64,1280]{1,0:T(8,128)}, f32[1,1280]{1,0:T(1,128)}) custom-call(f32[72,1536]{1,0:T(8,128)S(1)} %convert_add_fusion.refs_0_, bf16[80,1280]{1,0:T(8,128)(2,1)S(1)} %get-tuple-element.63.refs_1_, bf16[80,1024]{1,0:T(8,128)(2,1)S(1)} %get-tuple-element.47.refs_2_, ...), custom_call_target="tpu_custom_call", output_to_operand_aliasing={{0}: (4, {}), {1}: (5, {})} | custom-call | flops 134217728 | bytes 1048576 | tf_op jit(solution)/shard_map/pallas_call | solution.py:187
  21.0 0.0 collective-permute-done.8
  21.0 0.5 %collective-permute-done.7 = f16[72,256]{1,0:T(8,128)(2,1)S(1)} collective-permute-done((f16[72,256]{1,0:T(8,128)(2,1)S(1)}, f16[72,256]{1,0:T(8,128)(2,1)S(1)}, u32[]{:S(2)}, u32[]{:S(2)}) %collective-permute-start.7) | collective-permute-done | bytes 36896 | tf_op jit(solution)/shard_map/ppermute | solution.py:154
  21.5 0.4 %collective-permute-done.6 = f16[72,256]{1,0:T(8,128)(2,1)S(1)} collective-permute-done((f16[72,256]{1,0:T(8,128)(2,1)S(1)}, f16[72,256]{1,0:T(8,128)(2,1)S(1)}, u32[]{:S(2)}, u32[]{:S(2)}) %collective-permute-start.6) | collective-permute-done | bytes 36896 | tf_op jit(solution)/shard_map/ppermute | solution.py:154
  22.1 2.7 %collective-permute-start.9 = (f16[72,256]{1,0:T(8,128)(2,1)S(1)}, f16[72,256]{1,0:T(8,128)(2,1)S(1)}, u32[]{:S(2)}, u32[]{:S(2)}) collective-permute-start(f16[72,256]{1,0:T(8,128)(2,1)S(1)} %pad_maximum_fusion.1), channel_id=1, source_target_pairs={{0,16},{4,20},{8,24},{12,28},{16,0},{20,4},{24,8},{28,12},{1,17},{... | collective-permute-start | bytes 110600 | tf_op jit(solution)/shard_map/ppermute | solution.py:154
  24.7 2.2 %shard_map.88 = (f32[64,1280]{1,0:T(8,128)}, f32[1,1280]{1,0:T(1,128)}) custom-call(f32[72,1536]{1,0:T(8,128)S(1)} %convert_add_fusion.refs_0_, bf16[80,1280]{1,0:T(8,128)(2,1)S(1)} %get-tuple-element.63.refs_1_, bf16[80,1024]{1,0:T(8,128)(2,1)S(1)} %get-tuple-element.47.refs_2_, ...), custom_call_target="tpu_custom_call", output_to_operand_aliasing={{0}: (4, {}), {1}: (5, {})} | custom-call | flops 67108864 | bytes 524288 | tf_op jit(solution)/shard_map/pallas_call | solution.py:187
  26.9 0.1 collective-permute-done.9
  27.0 0.7 %multiply_add_fusion = f32[64,256]{1,0:T(8,128)} fusion(f32[256]{0:T(256)S(1)} %bitcast.26, f16[72,256]{1,0:T(8,128)(2,1)S(1)} %collective-permute-done.9, f32[256]{0:T(256)S(1)} %bitcast.25, f16[72,256]{1,0:T(8,128)(2,1)S(1)} %pad_maximum_fusion.1), kind=kLoop, calls=%fused_computation.1 | loop fusion | flops 81920 | bytes 133120 | tf_op jit(solution)/shard_map/add | solution.py:219
  (16 shorter events, 0.3 us)
Async XLA Ops:
  0.6 5.1 %collective-permute-start = (bf16[64,256]{1,0:T(8,128)(2,1)}, bf16[64,256]{1,0:T(8,128)(2,1)S(1)}, u32[]{:S(2)}, u32[]{:S(2)}) collective-permute-start(bf16[64,256]{1,0:T(8,128)(2,1)} %param.7), channel_id=1, source_target_pairs={{0,2},{1,3},{2,0},{3,1},{4,6},{5,7},{6,4},{7,5},{8,10},{9,11},{10,... | collective-permute-start | bytes 98312 | tf_op jit(solution)/shard_map/ppermute | solution.py:154
  3.7 3.6 %collective-permute-start.2 = (bf16[64,256]{1,0:T(8,128)(2,1)}, bf16[64,256]{1,0:T(8,128)(2,1)S(1)}, u32[]{:S(2)}, u32[]{:S(2)}) collective-permute-start(bf16[64,256]{1,0:T(8,128)(2,1)} %param.7), channel_id=1, source_target_pairs={{0,3},{1,2},{2,1},{3,0},{4,7},{5,6},{6,5},{7,4},{8,11},{9,10},{10,... | collective-permute-start | bytes 98312 | tf_op jit(solution)/shard_map/ppermute | solution.py:154
  3.7 3.6 %collective-permute-start.1 = (bf16[64,256]{1,0:T(8,128)(2,1)}, bf16[64,256]{1,0:T(8,128)(2,1)S(1)}, u32[]{:S(2)}, u32[]{:S(2)}) collective-permute-start(bf16[64,256]{1,0:T(8,128)(2,1)} %param.7), channel_id=1, source_target_pairs={{0,1},{1,0},{2,3},{3,2},{4,5},{5,4},{6,7},{7,6},{8,9},{9,8},{10,11... | collective-permute-start | bytes 98312 | tf_op jit(solution)/shard_map/ppermute | solution.py:154
  10.2 4.5 %collective-permute-start.5 = (f32[64,256]{1,0:T(8,128)S(1)}, f32[64,256]{1,0:T(8,128)S(1)}, u32[]{:S(2)}, u32[]{:S(2)}) collective-permute-start(f32[64,256]{1,0:T(8,128)S(1)} %get-tuple-element.45), channel_id=1, source_target_pairs={{0,1},{1,0},{2,3},{3,2},{4,5},{5,4},{6,7},{7,6},{8,9},{9,8},{10,11... | collective-permute-start | bytes 196616 | tf_op jit(solution)/shard_map/ppermute | solution.py:154
  10.3 4.4 %collective-permute-start.3 = (bf16[64,256]{1,0:T(8,128)(2,1)S(1)}, bf16[64,256]{1,0:T(8,128)(2,1)S(1)}, u32[]{:S(2)}, u32[]{:S(2)}) collective-permute-start(bf16[64,256]{1,0:T(8,128)(2,1)S(1)} %get-tuple-element.43), channel_id=1, source_target_pairs={{0,2},{1,3},{2,0},{3,1},{4,6},{5,7},{6,4},{7,5},{8,10},{9,11},{10,... | collective-permute-start | bytes 98312 | tf_op jit(solution)/shard_map/ppermute | solution.py:154
  11.0 3.8 %collective-permute-start.4 = (bf16[64,256]{1,0:T(8,128)(2,1)S(1)}, bf16[64,256]{1,0:T(8,128)(2,1)S(1)}, u32[]{:S(2)}, u32[]{:S(2)}) collective-permute-start(bf16[64,256]{1,0:T(8,128)(2,1)S(1)} %get-tuple-element.44), channel_id=1, source_target_pairs={{0,3},{1,2},{2,1},{3,0},{4,7},{5,6},{6,5},{7,4},{8,11},{9,10},{10,... | collective-permute-start | bytes 98312 | tf_op jit(solution)/shard_map/ppermute | solution.py:154
  14.9 6.1 %collective-permute-start.8 = (f16[72,256]{1,0:T(8,128)(2,1)S(1)}, f16[72,256]{1,0:T(8,128)(2,1)S(1)}, u32[]{:S(2)}, u32[]{:S(2)}) collective-permute-start(f16[72,256]{1,0:T(8,128)(2,1)S(1)} %pad_maximum_fusion), channel_id=1, source_target_pairs={{0,12},{4,8},{8,4},{12,0},{16,28},{20,24},{24,20},{28,16},{1,13},{... | collective-permute-start | bytes 110600 | tf_op jit(solution)/shard_map/ppermute | solution.py:154
  17.5 4.0 %collective-permute-start.7 = (f16[72,256]{1,0:T(8,128)(2,1)S(1)}, f16[72,256]{1,0:T(8,128)(2,1)S(1)}, u32[]{:S(2)}, u32[]{:S(2)}) collective-permute-start(f16[72,256]{1,0:T(8,128)(2,1)S(1)} %pad_maximum_fusion), channel_id=1, source_target_pairs={{0,8},{4,12},{8,0},{12,4},{16,24},{20,28},{24,16},{28,20},{1,9},{5... | collective-permute-start | bytes 110600 | tf_op jit(solution)/shard_map/ppermute | solution.py:154
  17.9 4.0 %collective-permute-start.6 = (f16[72,256]{1,0:T(8,128)(2,1)S(1)}, f16[72,256]{1,0:T(8,128)(2,1)S(1)}, u32[]{:S(2)}, u32[]{:S(2)}) collective-permute-start(f16[72,256]{1,0:T(8,128)(2,1)S(1)} %pad_maximum_fusion), channel_id=1, source_target_pairs={{0,4},{4,0},{8,12},{12,8},{16,20},{20,16},{24,28},{28,24},{1,5},{5... | collective-permute-start | bytes 110600 | tf_op jit(solution)/shard_map/ppermute | solution.py:154
  22.1 4.9 %collective-permute-start.9 = (f16[72,256]{1,0:T(8,128)(2,1)S(1)}, f16[72,256]{1,0:T(8,128)(2,1)S(1)}, u32[]{:S(2)}, u32[]{:S(2)}) collective-permute-start(f16[72,256]{1,0:T(8,128)(2,1)S(1)} %pad_maximum_fusion.1), channel_id=1, source_target_pairs={{0,16},{4,20},{8,24},{12,28},{16,0},{20,4},{24,8},{28,12},{1,17},{... | collective-permute-start | bytes 110600 | tf_op jit(solution)/shard_map/ppermute | solution.py:154

commit v16 on v15

--- a/solution.py
+++ b/solution.py
@@ -33,7 +33,7 @@
     pack_ref, counts_hbm = refs[:2]
     arrived = refs[2 : 1 + parts]
     outs = refs[1 + parts : 1 + 2 * parts]
-    load_ext, shifted, whole, counts_ref, held, grad_shift, counts_sem = refs[1 + 2 * parts :]
+    load_ext, shifted, whole, counts_ref, held, resid_low, grad_shift, counts_sem = refs[1 + 2 * parts :]
     me = lax.axis_index(axis)
     lats, total = grad_shift.shape
     early = held.shape[0]
@@ -76,9 +76,10 @@
     counts_copy.wait()
     for rows, span in blocks:
         rate = held[rows, span] if rows.start < early else expected(load_ext[:, rows], shifted[:, span])
-        resid = rate - counts_ref[rows, span].astype(F32)
-        part = jnp.dot(load_ext[0:lats, rows], resid.astype(BF16), preferred_element_type=F32)
-        grad_shift[:, span] = part if rows.start == 0 else grad_shift[:, span] + part
+        resid_low[rows, span] = (rate - counts_ref[rows, span].astype(F32)).astype(BF16)
+    for begin in range(0, total, step):
+        span = slice(begin, begin + step)
+        grad_shift[:, span] = jnp.dot(load_ext[0:lats, :], resid_low[:, span], preferred_element_type=F32)
 
     bins = lax.broadcasted_iota(jnp.int32, (1, total), 1)
     tiles = []
@@ -172,13 +173,14 @@
             pltpu.VMEM((lats, total), BF16),
             pltpu.VMEM((neurons, total), BF16),
             pltpu.VMEM((4 * chunk, total), F32),
+            pltpu.VMEM((neurons, total), BF16),
             pltpu.VMEM((lats, total), F32),
             pltpu.SemaphoreType.DMA,
         ],
         compiler_params=params,
     )(pack, counts[0], *arrived)
 
-    shares = [(0, 2 * chunk), (2 * chunk, 2 * chunk), (4 * chunk, neurons - 4 * chunk)]
+    shares = [(0, 2 * chunk), (2 * chunk, neurons - 2 * chunk)]
     made = []
 
     def make(before):

time: 28 us -> 27.8 us (level)
  Pallas kernels: 10.2 us -> 8.82 us
  waiting for transfers between devices: 2.71 us -> 3.92 us
    ppermute x10, waiting for transfers between devices: 2.71 us -> 3.92 us  [swap(): return lax.ppermute(value, axis, [(i, i ^ mask) for i in range(count)])]
    pallas_call x3 -> x2, Pallas kernels: 7.25 us -> 6.07 us  [make(): pl.pallas_call(functools.partial(load_kernel, lats, first, chunk, step),...]
  transfers between devices with their start and end apart: 10 -> 10, of which waited for: 5 -> 3; matrix products, arithmetic and copies ran while one was open for 4% -> 4% of each run, Pallas kernels for 26% -> 22%
where the time goes in v16:
time: 27.8 us; the launch traced here: 27.6 us
  starting transfers between devices  11.4 us (41%)
  Pallas kernels  8.82 us (32%)
  waiting for transfers between devices  3.92 us (14%)
  other arithmetic  1.99 us (7%)
  between operations  1.42 us (5%)
    ppermute x10, starting transfers between devices, swap(): return lax.ppermute(value, axis, [(i, i ^ mask) for i in range(count)])  11.4 us
    pallas_call x2, Pallas kernels, make(): pl.pallas_call(functools.partial(load_kernel, lats, first, chunk, step),...  6.07 us
    ppermute x10, waiting for transfers between devices, swap(): return lax.ppermute(value, axis, [(i, i ^ mask) for i in range(count)])  3.92 us
    pallas_call x1, Pallas kernels, per_device(): pl.pallas_call(functools.partial(shift_kernel, neuron_count, order, 'neur...  2.75 us
    add x1, other arithmetic, per_device(): pack = pack + jnp.pad(latents, ((0, 8), (neurons, 0))).astype(F32)  1.07 us
    add x1, other arithmetic, per_device(): value = decode(code) + decode(arrived[0])  0.65 us
  transfers between devices with their start and end apart: 10, of which 3 were waited for; matrix products, arithmetic and copies ran while one was open for 4% of the time, Pallas kernels for 22%

profile of v16, /device:TPU:0, one launch (start us, length us, event | category | flops | bytes accessed | tf_op | source)
XLA Modules:
  0.0 27.6 jit_solution(4084090651986211163)
XLA Ops:
  0.6 3.0 %collective-permute-start = (bf16[64,256]{1,0:T(8,128)(2,1)}, bf16[64,256]{1,0:T(8,128)(2,1)S(1)}, u32[]{:S(2)}, u32[]{:S(2)}) collective-permute-start(bf16[64,256]{1,0:T(8,128)(2,1)} %param.7), channel_id=1, source_target_pairs={{0,2},{1,3},{2,0},{3,1},{4,6},{5,7},{6,4},{7,5},{8,10},{9,11},{10,... | collective-permute-start | bytes 98312 | tf_op jit(solution)/shard_map/ppermute | solution.py:155
  3.7 0.0 collective-permute-start.2
  3.7 0.2 collective-permute-start.1
  4.5 1.1 %convert_add_fusion.refs_0_ = f32[72,1536]{1,0:T(8,128)S(1)} fusion(s32[1,64]{1,0:T(1,128)} %param.10, f32[1,1280]{1,0:T(1,128)} %param.9, bf16[64,256]{1,0:T(8,128)(2,1)} %param.7, bf16[64,1280]{1,0:T(8,128)(2,1)} %bitcast.15, s32[]{:T(128)} %bitcast.10, pred[72]{0:T(512)(128)(4,1)S(1)} %iota_compare_fusion), kind=kLoop, calls=%fused_computation | loop fusion | flops 774144 | bytes 644428 | tf_op jit(solution)/shard_map/add | solution.py:164
  5.6 0.2 collective-permute-done.refs_2_
  5.8 1.5 %collective-permute-done.2.refs_4_ = bf16[64,256]{1,0:T(8,128)(2,1)S(1)} collective-permute-done((bf16[64,256]{1,0:T(8,128)(2,1)}, bf16[64,256]{1,0:T(8,128)(2,1)S(1)}, u32[]{:S(2)}, u32[]{:S(2)}) %collective-permute-start.2) | collective-permute-done | bytes 32800 | tf_op jit(solution)/shard_map/ppermute | solution.py:155
  7.3 0.0 collective-permute-done.1.refs_3_
  7.3 2.8 %shard_map.85 = (f32[64,256]{1,0:T(8,128)S(1)}, f32[64,256]{1,0:T(8,128)S(1)}, bf16[64,256]{1,0:T(8,128)(2,1)S(1)}, bf16[64,256]{1,0:T(8,128)(2,1)S(1)}, bf16[80...) custom-call(f32[72,1536]{1,0:T(8,128)S(1)} %convert_add_fusion.refs_0_, bf16[1280,1024]{1,0:T(8,128)(2,1)} %bitcast.11, ...), custom_call_target="tpu_custom_call" | custom-call | tf_op jit(solution)/shard_map/pallas_call | solution.py:166
  10.1 0.1 collective-permute-start.5
  10.1 0.6 %collective-permute-start.3 = (bf16[64,256]{1,0:T(8,128)(2,1)S(1)}, bf16[64,256]{1,0:T(8,128)(2,1)S(1)}, u32[]{:S(2)}, u32[]{:S(2)}) collective-permute-start(bf16[64,256]{1,0:T(8,128)(2,1)S(1)} %get-tuple-element.39), channel_id=1, source_target_pairs={{0,2},{1,3},{2,0},{3,1},{4,6},{5,7},{6,4},{7,5},{8,10},{9,11},{10,... | collective-permute-start | bytes 98312 | tf_op jit(solution)/shard_map/ppermute | solution.py:155
  10.8 1.2 %collective-permute-start.4 = (bf16[64,256]{1,0:T(8,128)(2,1)S(1)}, bf16[64,256]{1,0:T(8,128)(2,1)S(1)}, u32[]{:S(2)}, u32[]{:S(2)}) collective-permute-start(bf16[64,256]{1,0:T(8,128)(2,1)S(1)} %get-tuple-element.40), channel_id=1, source_target_pairs={{0,3},{1,2},{2,1},{3,0},{4,7},{5,6},{6,5},{7,4},{8,11},{9,10},{10,... | collective-permute-start | bytes 98312 | tf_op jit(solution)/shard_map/ppermute | solution.py:155
  12.0 2.5 %shard_map.86 = (f32[64,1280]{1,0:T(8,128)}, f32[1,1280]{1,0:T(1,128)}) custom-call(f32[72,1536]{1,0:T(8,128)S(1)} %convert_add_fusion.refs_0_, bf16[80,1280]{1,0:T(8,128)(2,1)S(1)} %get-tuple-element.50.refs_1_, bf16[80,1024]{1,0:T(8,128)(2,1)S(1)} %get-tuple-element.43.refs_2_, bf16[1280,1024]{1,0:T(8,128)(2,1)} %bitcast.12), custom_call_target="tpu_custom_call" | custom-call | flops 134217728 | bytes 1048576 | tf_op jit(solution)/shard_map/pallas_call | solution.py:189
  14.5 0.0 collective-permute-done.3
  14.5 0.0 collective-permute-done.4
  14.6 0.0 collective-permute-done.5
  14.7 2.6 %collective-permute-start.8 = (f16[72,256]{1,0:T(8,128)(2,1)S(1)}, f16[72,256]{1,0:T(8,128)(2,1)S(1)}, u32[]{:S(2)}, u32[]{:S(2)}) collective-permute-start(f16[72,256]{1,0:T(8,128)(2,1)S(1)} %pad_maximum_fusion), channel_id=1, source_target_pairs={{0,12},{4,8},{8,4},{12,0},{16,28},{20,24},{24,20},{28,16},{1,13},{... | collective-permute-start | bytes 110600 | tf_op jit(solution)/shard_map/ppermute | solution.py:155
  17.3 0.4 %collective-permute-start.7 = (f16[72,256]{1,0:T(8,128)(2,1)S(1)}, f16[72,256]{1,0:T(8,128)(2,1)S(1)}, u32[]{:S(2)}, u32[]{:S(2)}) collective-permute-start(f16[72,256]{1,0:T(8,128)(2,1)S(1)} %pad_maximum_fusion), channel_id=1, source_target_pairs={{0,8},{4,12},{8,0},{12,4},{16,24},{20,28},{24,16},{28,20},{1,9},{5... | collective-permute-start | bytes 110600 | tf_op jit(solution)/shard_map/ppermute | solution.py:155
  17.8 0.5 %collective-permute-start.6 = (f16[72,256]{1,0:T(8,128)(2,1)S(1)}, f16[72,256]{1,0:T(8,128)(2,1)S(1)}, u32[]{:S(2)}, u32[]{:S(2)}) collective-permute-start(f16[72,256]{1,0:T(8,128)(2,1)S(1)} %pad_maximum_fusion), channel_id=1, source_target_pairs={{0,4},{4,0},{8,12},{12,8},{16,20},{20,16},{24,28},{28,24},{1,5},{5... | collective-permute-start | bytes 110600 | tf_op jit(solution)/shard_map/ppermute | solution.py:155
  18.3 3.5 %shard_map.87 = (f32[64,1280]{1,0:T(8,128)}, f32[1,1280]{1,0:T(1,128)}) custom-call(f32[72,1536]{1,0:T(8,128)S(1)} %convert_add_fusion.refs_0_, bf16[80,1280]{1,0:T(8,128)(2,1)S(1)} %get-tuple-element.50.refs_1_, bf16[80,1024]{1,0:T(8,128)(2,1)S(1)} %get-tuple-element.43.refs_2_, ...), custom_call_target="tpu_custom_call", output_to_operand_aliasing={{0}: (4, {}), {1}: (5, {})} | custom-call | flops 201326592 | bytes 1572864 | tf_op jit(solution)/shard_map/pallas_call | solution.py:189
  21.8 0.0 collective-permute-done.8
  21.8 0.0 collective-permute-done.7
  21.8 0.0 collective-permute-done.6
  22.0 2.7 %collective-permute-start.9 = (f16[72,256]{1,0:T(8,128)(2,1)S(1)}, f16[72,256]{1,0:T(8,128)(2,1)S(1)}, u32[]{:S(2)}, u32[]{:S(2)}) collective-permute-start(f16[72,256]{1,0:T(8,128)(2,1)S(1)} %pad_maximum_fusion.1), channel_id=1, source_target_pairs={{0,16},{4,20},{8,24},{12,28},{16,0},{20,4},{24,8},{28,12},{1,17},{... | collective-permute-start | bytes 110600 | tf_op jit(solution)/shard_map/ppermute | solution.py:155
  24.7 2.2 %collective-permute-done.9 = f16[72,256]{1,0:T(8,128)(2,1)S(1)} collective-permute-done((f16[72,256]{1,0:T(8,128)(2,1)S(1)}, f16[72,256]{1,0:T(8,128)(2,1)S(1)}, u32[]{:S(2)}, u32[]{:S(2)}) %collective-permute-start.9) | collective-permute-done | bytes 36896 | tf_op jit(solution)/shard_map/ppermute | solution.py:155
  26.9 0.7 %multiply_add_fusion = f32[64,256]{1,0:T(8,128)} fusion(f16[72,256]{1,0:T(8,128)(2,1)S(1)} %pad_maximum_fusion.1, f32[256]{0:T(256)S(1)} %bitcast.25, f16[72,256]{1,0:T(8,128)(2,1)S(1)} %collective-permute-done.9, f32[256]{0:T(256)S(1)} %bitcast.24), kind=kLoop, calls=%fused_computation.1 | loop fusion | flops 81920 | bytes 133120 | tf_op jit(solution)/shard_map/add | solution.py:221
  (16 shorter events, 0.3 us)
Async XLA Ops:
  0.6 5.1 %collective-permute-start = (bf16[64,256]{1,0:T(8,128)(2,1)}, bf16[64,256]{1,0:T(8,128)(2,1)S(1)}, u32[]{:S(2)}, u32[]{:S(2)}) collective-permute-start(bf16[64,256]{1,0:T(8,128)(2,1)} %param.7), channel_id=1, source_target_pairs={{0,2},{1,3},{2,0},{3,1},{4,6},{5,7},{6,4},{7,5},{8,10},{9,11},{10,... | collective-permute-start | bytes 98312 | tf_op jit(solution)/shard_map/ppermute | solution.py:155
  3.7 3.6 %collective-permute-start.2 = (bf16[64,256]{1,0:T(8,128)(2,1)}, bf16[64,256]{1,0:T(8,128)(2,1)S(1)}, u32[]{:S(2)}, u32[]{:S(2)}) collective-permute-start(bf16[64,256]{1,0:T(8,128)(2,1)} %param.7), channel_id=1, source_target_pairs={{0,3},{1,2},{2,1},{3,0},{4,7},{5,6},{6,5},{7,4},{8,11},{9,10},{10,... | collective-permute-start | bytes 98312 | tf_op jit(solution)/shard_map/ppermute | solution.py:155
  3.7 3.6 %collective-permute-start.1 = (bf16[64,256]{1,0:T(8,128)(2,1)}, bf16[64,256]{1,0:T(8,128)(2,1)S(1)}, u32[]{:S(2)}, u32[]{:S(2)}) collective-permute-start(bf16[64,256]{1,0:T(8,128)(2,1)} %param.7), channel_id=1, source_target_pairs={{0,1},{1,0},{2,3},{3,2},{4,5},{5,4},{6,7},{7,6},{8,9},{9,8},{10,11... | collective-permute-start | bytes 98312 | tf_op jit(solution)/shard_map/ppermute | solution.py:155
  10.1 4.5 %collective-permute-start.5 = (f32[64,256]{1,0:T(8,128)S(1)}, f32[64,256]{1,0:T(8,128)S(1)}, u32[]{:S(2)}, u32[]{:S(2)}) collective-permute-start(f32[64,256]{1,0:T(8,128)S(1)} %get-tuple-element.41), channel_id=1, source_target_pairs={{0,1},{1,0},{2,3},{3,2},{4,5},{5,4},{6,7},{7,6},{8,9},{9,8},{10,11... | collective-permute-start | bytes 196616 | tf_op jit(solution)/shard_map/ppermute | solution.py:155
  10.1 4.4 %collective-permute-start.3 = (bf16[64,256]{1,0:T(8,128)(2,1)S(1)}, bf16[64,256]{1,0:T(8,128)(2,1)S(1)}, u32[]{:S(2)}, u32[]{:S(2)}) collective-permute-start(bf16[64,256]{1,0:T(8,128)(2,1)S(1)} %get-tuple-element.39), channel_id=1, source_target_pairs={{0,2},{1,3},{2,0},{3,1},{4,6},{5,7},{6,4},{7,5},{8,10},{9,11},{10,... | collective-permute-start | bytes 98312 | tf_op jit(solution)/shard_map/ppermute | solution.py:155
  10.8 3.8 %collective-permute-start.4 = (bf16[64,256]{1,0:T(8,128)(2,1)S(1)}, bf16[64,256]{1,0:T(8,128)(2,1)S(1)}, u32[]{:S(2)}, u32[]{:S(2)}) collective-permute-start(bf16[64,256]{1,0:T(8,128)(2,1)S(1)} %get-tuple-element.40), channel_id=1, source_target_pairs={{0,3},{1,2},{2,1},{3,0},{4,7},{5,6},{6,5},{7,4},{8,11},{9,10},{10,... | collective-permute-start | bytes 98312 | tf_op jit(solution)/shard_map/ppermute | solution.py:155
  14.7 7.1 %collective-permute-start.8 = (f16[72,256]{1,0:T(8,128)(2,1)S(1)}, f16[72,256]{1,0:T(8,128)(2,1)S(1)}, u32[]{:S(2)}, u32[]{:S(2)}) collective-permute-start(f16[72,256]{1,0:T(8,128)(2,1)S(1)} %pad_maximum_fusion), channel_id=1, source_target_pairs={{0,12},{4,8},{8,4},{12,0},{16,28},{20,24},{24,20},{28,16},{1,13},{... | collective-permute-start | bytes 110600 | tf_op jit(solution)/shard_map/ppermute | solution.py:155
  17.3 4.5 %collective-permute-start.7 = (f16[72,256]{1,0:T(8,128)(2,1)S(1)}, f16[72,256]{1,0:T(8,128)(2,1)S(1)}, u32[]{:S(2)}, u32[]{:S(2)}) collective-permute-start(f16[72,256]{1,0:T(8,128)(2,1)S(1)} %pad_maximum_fusion), channel_id=1, source_target_pairs={{0,8},{4,12},{8,0},{12,4},{16,24},{20,28},{24,16},{28,20},{1,9},{5... | collective-permute-start | bytes 110600 | tf_op jit(solution)/shard_map/ppermute | solution.py:155
  17.8 4.1 %collective-permute-start.6 = (f16[72,256]{1,0:T(8,128)(2,1)S(1)}, f16[72,256]{1,0:T(8,128)(2,1)S(1)}, u32[]{:S(2)}, u32[]{:S(2)}) collective-permute-start(f16[72,256]{1,0:T(8,128)(2,1)S(1)} %pad_maximum_fusion), channel_id=1, source_target_pairs={{0,4},{4,0},{8,12},{12,8},{16,20},{20,16},{24,28},{28,24},{1,5},{5... | collective-permute-start | bytes 110600 | tf_op jit(solution)/shard_map/ppermute | solution.py:155
  22.0 4.9 %collective-permute-start.9 = (f16[72,256]{1,0:T(8,128)(2,1)S(1)}, f16[72,256]{1,0:T(8,128)(2,1)S(1)}, u32[]{:S(2)}, u32[]{:S(2)}) collective-permute-start(f16[72,256]{1,0:T(8,128)(2,1)S(1)} %pad_maximum_fusion.1), channel_id=1, source_target_pairs={{0,16},{4,20},{8,24},{12,28},{16,0},{20,4},{24,8},{28,12},{1,17},{... | collective-permute-start | bytes 110600 | tf_op jit(solution)/shard_map/ppermute | solution.py:155

commit v17 on v16

--- a/solution.py
+++ b/solution.py
@@ -25,15 +25,14 @@
 
 
 def expected(load_part, piece):
-    eta = lax.dot_general(load_part, piece, (((0,), (0,)), ((), ())), preferred_element_type=F32)
-    return jnp.exp(eta)
+    return jnp.exp(jnp.dot(load_part, piece, preferred_element_type=F32))
 
 
 def shift_kernel(parts, order, axis, chunk, step, *refs):
     pack_ref, counts_hbm = refs[:2]
     arrived = refs[2 : 1 + parts]
     outs = refs[1 + parts : 1 + 2 * parts]
-    load_ext, shifted, whole, counts_ref, held, resid_low, grad_shift, counts_sem = refs[1 + 2 * parts :]
+    turned, shifted, whole, counts_ref, held, resid_low, load_ext, grad_shift, counts_sem = refs[1 + 2 * parts :]
     me = lax.axis_index(axis)
     lats, total = grad_shift.shape
     early = held.shape[0]
@@ -64,6 +63,7 @@
     row = lax.broadcasted_iota(jnp.int32, (EXTRA, neurons), 0)
     below = jnp.where(row == 0, high, jnp.where(row == 1, middle, jnp.where(row == 2, low, 0.0)))
     load_ext[lats:, :] = below.astype(BF16)
+    turned[...] = load_ext[...].astype(F32).T.astype(BF16)
 
     blocks = [
         (slice(first, first + chunk), slice(begin, begin + step))
@@ -72,10 +72,10 @@
     ]
     for rows, span in blocks:
         if rows.start < early:
-            held[rows, span] = expected(load_ext[:, rows], shifted[:, span])
+            held[rows, span] = expected(turned[rows, :], shifted[:, span])
     counts_copy.wait()
     for rows, span in blocks:
-        rate = held[rows, span] if rows.start < early else expected(load_ext[:, rows], shifted[:, span])
+        rate = held[rows, span] if rows.start < early else expected(turned[rows, :], shifted[:, span])
         resid_low[rows, span] = (rate - counts_ref[rows, span].astype(F32)).astype(BF16)
     for begin in range(0, total, step):
         span = slice(begin, begin + step)
@@ -94,7 +94,7 @@
 
 
 def load_kernel(lats, first, chunk, step, *refs):
-    pack_ref, load_ext, shifted, counts_hbm = refs[:4]
+    pack_ref, turned, shifted, counts_hbm = refs[:4]
     load_hbm, bias_hbm, counts_ref, held, load_ref, bias_ref, sems = refs[-7:]
     count, total = counts_ref.shape
     place = pl.ds(first, count)
@@ -105,8 +105,9 @@
     blocks = [(slice(begin, begin + chunk), range(0, total, step)) for begin in range(0, count, chunk)]
     for rows, starts in blocks:
         for at in starts:
-            load_part = load_ext[:, first + rows.start : first + rows.stop]
+            load_part = turned[first + rows.start : first + rows.stop, :]
             held[rows, at : at + step] = expected(load_part, shifted[:, at : at + step])
+    columns = shifted[0:lats, :].astype(F32).T.astype(BF16)
     counts_copy.wait()
     outward = []
     for index, (rows, starts) in enumerate(blocks):
@@ -117,9 +118,7 @@
             resid = jnp.where(bins[:, span] < length, held[rows, span] - counts_ref[rows, span].astype(F32), 0.0)
             for j in range(step // LANES):
                 sums = sums + resid[:, j * LANES : (j + 1) * LANES]
-            grad = grad + lax.dot_general(
-                resid.astype(BF16), shifted[0:lats, span], (((1,), (1,)), ((), ())), preferred_element_type=F32
-            )
+            grad = grad + jnp.dot(resid.astype(BF16), columns[span], preferred_element_type=F32)
         load_ref[:, rows] = grad.T
         bias_ref[:, rows] = jnp.sum(sums.T, axis=0, keepdims=True)
         place = pl.ds(first + rows.start, chunk)
@@ -163,10 +162,10 @@
     pack = pack + jnp.pad(loadings[0], ((0, 8), (0, width))).astype(F32)
     pack = pack + jnp.pad(latents, ((0, 8), (neurons, 0))).astype(F32)
 
-    *outs, load_ext, shifted = pl.pallas_call(
+    *outs, turned, shifted = pl.pallas_call(
         functools.partial(shift_kernel, neuron_count, order, "neuron", chunk, step),
         out_shape=[jax.ShapeDtypeStruct((lats, width), BF16 if k > 1 else F32) for k in range(neuron_count)]
-        + [jax.ShapeDtypeStruct((lats + EXTRA, neurons), BF16), jax.ShapeDtypeStruct((lats + EXTRA, total), BF16)],
+        + [jax.ShapeDtypeStruct((neurons, lats + EXTRA), BF16), jax.ShapeDtypeStruct((lats + EXTRA, total), BF16)],
         in_specs=[vmem, hbm] + [vmem] * (neuron_count - 1),
         out_specs=[vmem] * (neuron_count + 2),
         scratch_shapes=[
@@ -174,6 +173,7 @@
             pltpu.VMEM((neurons, total), BF16),
             pltpu.VMEM((4 * chunk, total), F32),
             pltpu.VMEM((neurons, total), BF16),
+            pltpu.VMEM((lats + EXTRA, neurons), BF16),
             pltpu.VMEM((lats, total), F32),
             pltpu.SemaphoreType.DMA,
         ],
@@ -185,7 +185,7 @@
 
     def make(before):
         first, count = shares.pop(0)
-        before, start_load = lax.optimization_barrier((before, load_ext))
+        before, start_load = lax.optimization_barrier((before, turned))
         out = pl.pallas_call(
             functools.partial(load_kernel, lats, first, chunk, step),
             out_shape=[jax.ShapeDtypeStruct((lats, neurons), F32), jax.ShapeDtypeStruct((1, neurons), F32)],

time: 27.8 us -> 28 us (level)
  transfers between devices with their start and end apart: 10 -> 10, of which waited for: 3 -> 3; matrix products, arithmetic and copies ran while one was open for 4% -> 4% of each run, Pallas kernels for 22% -> 23%
where the time goes in v17:
time: 28 us; the launch traced here: 27.7 us
  starting transfers between devices  11.4 us (41%)
  Pallas kernels  8.94 us (32%)
  waiting for transfers between devices  3.98 us (14%)
  other arithmetic  1.99 us (7%)
  between operations  1.43 us (5%)
    ppermute x10, starting transfers between devices, swap(): return lax.ppermute(value, axis, [(i, i ^ mask) for i in range(count)])  11.4 us
    pallas_call x2, Pallas kernels, make(): pl.pallas_call(functools.partial(load_kernel, lats, first, chunk, step),...  6.25 us
    ppermute x10, waiting for transfers between devices, swap(): return lax.ppermute(value, axis, [(i, i ^ mask) for i in range(count)])  3.98 us
    pallas_call x1, Pallas kernels, per_device(): pl.pallas_call(functools.partial(shift_kernel, neuron_count, order, 'neur...  2.69 us
    add x1, other arithmetic, per_device(): pack = pack + jnp.pad(latents, ((0, 8), (neurons, 0))).astype(F32)  1.07 us
    add x1, other arithmetic, per_device(): value = decode(code) + decode(arrived[0])  0.65 us
  transfers between devices with their start and end apart: 10, of which 3 were waited for; matrix products, arithmetic and copies ran while one was open for 4% of the time, Pallas kernels for 23%

profile of v17, /device:TPU:0, one launch (start us, length us, event | category | flops | bytes accessed | tf_op | source)
XLA Modules:
  0.0 27.7 jit_solution(11449922875614649598)
XLA Ops:
  0.6 3.0 %collective-permute-start = (bf16[64,256]{1,0:T(8,128)(2,1)}, bf16[64,256]{1,0:T(8,128)(2,1)S(1)}, u32[]{:S(2)}, u32[]{:S(2)}) collective-permute-start(bf16[64,256]{1,0:T(8,128)(2,1)} %param.7), channel_id=1, source_target_pairs={{0,2},{1,3},{2,0},{3,1},{4,6},{5,7},{6,4},{7,5},{8,10},{9,11},{10,... | collective-permute-start | bytes 98312 | tf_op jit(solution)/shard_map/ppermute | solution.py:154
  3.7 0.0 collective-permute-start.2
  3.7 0.2 collective-permute-start.1
  4.5 1.1 %convert_add_fusion.refs_0_ = f32[72,1536]{1,0:T(8,128)S(1)} fusion(s32[1,64]{1,0:T(1,128)} %param.10, f32[1,1280]{1,0:T(1,128)} %param.9, bf16[64,256]{1,0:T(8,128)(2,1)} %param.7, bf16[64,1280]{1,0:T(8,128)(2,1)} %bitcast.15, s32[]{:T(128)} %bitcast.10, pred[72]{0:T(512)(128)(4,1)S(1)} %iota_compare_fusion), kind=kLoop, calls=%fused_computation | loop fusion | flops 774144 | bytes 644428 | tf_op jit(solution)/shard_map/add | solution.py:163
  5.6 0.2 collective-permute-done.refs_2_
  5.8 1.5 %collective-permute-done.2.refs_4_ = bf16[64,256]{1,0:T(8,128)(2,1)S(1)} collective-permute-done((bf16[64,256]{1,0:T(8,128)(2,1)}, bf16[64,256]{1,0:T(8,128)(2,1)S(1)}, u32[]{:S(2)}, u32[]{:S(2)}) %collective-permute-start.2) | collective-permute-done | bytes 32800 | tf_op jit(solution)/shard_map/ppermute | solution.py:154
  7.3 0.0 collective-permute-done.1.refs_3_
  7.3 2.7 %shard_map.85 = (f32[64,256]{1,0:T(8,128)S(1)}, f32[64,256]{1,0:T(8,128)S(1)}, bf16[64,256]{1,0:T(8,128)(2,1)S(1)}, bf16[64,256]{1,0:T(8,128)(2,1)S(1)}, bf16[12...) custom-call(f32[72,1536]{1,0:T(8,128)S(1)} %convert_add_fusion.refs_0_, bf16[1280,1024]{1,0:T(8,128)(2,1)} %bitcast.11, ...), custom_call_target="tpu_custom_call" | custom-call | tf_op jit(solution)/shard_map/pallas_call | solution.py:165
  10.0 0.1 collective-permute-start.5
  10.1 0.7 %collective-permute-start.3 = (bf16[64,256]{1,0:T(8,128)(2,1)S(1)}, bf16[64,256]{1,0:T(8,128)(2,1)S(1)}, u32[]{:S(2)}, u32[]{:S(2)}) collective-permute-start(bf16[64,256]{1,0:T(8,128)(2,1)S(1)} %get-tuple-element.39), channel_id=1, source_target_pairs={{0,2},{1,3},{2,0},{3,1},{4,6},{5,7},{6,4},{7,5},{8,10},{9,11},{10,... | collective-permute-start | bytes 98312 | tf_op jit(solution)/shard_map/ppermute | solution.py:154
  10.7 1.2 %collective-permute-start.4 = (bf16[64,256]{1,0:T(8,128)(2,1)S(1)}, bf16[64,256]{1,0:T(8,128)(2,1)S(1)}, u32[]{:S(2)}, u32[]{:S(2)}) collective-permute-start(bf16[64,256]{1,0:T(8,128)(2,1)S(1)} %get-tuple-element.40), channel_id=1, source_target_pairs={{0,3},{1,2},{2,1},{3,0},{4,7},{5,6},{6,5},{7,4},{8,11},{9,10},{10,... | collective-permute-start | bytes 98312 | tf_op jit(solution)/shard_map/ppermute | solution.py:154
  11.9 2.8 %shard_map.86 = (f32[64,1280]{1,0:T(8,128)}, f32[1,1280]{1,0:T(1,128)}) custom-call(f32[72,1536]{1,0:T(8,128)S(1)} %convert_add_fusion.refs_0_, bf16[1280,80]{1,0:T(8,128)(2,1)S(1)} %get-tuple-element.50.refs_1_, bf16[80,1024]{1,0:T(8,128)(2,1)S(1)} %get-tuple-element.43.refs_2_, bf16[1280,1024]{1,0:T(8,128)(2,1)} %bitcast.12), custom_call_target="tpu_custom_call" | custom-call | flops 134217728 | bytes 1048576 | tf_op jit(solution)/shard_map/pallas_call | solution.py:189
  14.8 0.0 collective-permute-done.3
  14.8 0.0 collective-permute-done.4
  14.8 0.0 collective-permute-done.5
  14.9 2.6 %collective-permute-start.8 = (f16[72,256]{1,0:T(8,128)(2,1)S(1)}, f16[72,256]{1,0:T(8,128)(2,1)S(1)}, u32[]{:S(2)}, u32[]{:S(2)}) collective-permute-start(f16[72,256]{1,0:T(8,128)(2,1)S(1)} %pad_maximum_fusion), channel_id=1, source_target_pairs={{0,12},{4,8},{8,4},{12,0},{16,28},{20,24},{24,20},{28,16},{1,13},{... | collective-permute-start | bytes 110600 | tf_op jit(solution)/shard_map/ppermute | solution.py:154
  17.5 0.4 %collective-permute-start.7 = (f16[72,256]{1,0:T(8,128)(2,1)S(1)}, f16[72,256]{1,0:T(8,128)(2,1)S(1)}, u32[]{:S(2)}, u32[]{:S(2)}) collective-permute-start(f16[72,256]{1,0:T(8,128)(2,1)S(1)} %pad_maximum_fusion), channel_id=1, source_target_pairs={{0,8},{4,12},{8,0},{12,4},{16,24},{20,28},{24,16},{28,20},{1,9},{5... | collective-permute-start | bytes 110600 | tf_op jit(solution)/shard_map/ppermute | solution.py:154
  17.9 0.5 %collective-permute-start.6 = (f16[72,256]{1,0:T(8,128)(2,1)S(1)}, f16[72,256]{1,0:T(8,128)(2,1)S(1)}, u32[]{:S(2)}, u32[]{:S(2)}) collective-permute-start(f16[72,256]{1,0:T(8,128)(2,1)S(1)} %pad_maximum_fusion), channel_id=1, source_target_pairs={{0,4},{4,0},{8,12},{12,8},{16,20},{20,16},{24,28},{28,24},{1,5},{5... | collective-permute-start | bytes 110600 | tf_op jit(solution)/shard_map/ppermute | solution.py:154
  18.5 3.4 %shard_map.87 = (f32[64,1280]{1,0:T(8,128)}, f32[1,1280]{1,0:T(1,128)}) custom-call(f32[72,1536]{1,0:T(8,128)S(1)} %convert_add_fusion.refs_0_, bf16[1280,80]{1,0:T(8,128)(2,1)S(1)} %get-tuple-element.50.refs_1_, bf16[80,1024]{1,0:T(8,128)(2,1)S(1)} %get-tuple-element.43.refs_2_, ...), custom_call_target="tpu_custom_call", output_to_operand_aliasing={{0}: (4, {}), {1}: (5, {})} | custom-call | flops 201326592 | bytes 1572864 | tf_op jit(solution)/shard_map/pallas_call | solution.py:189
  21.9 0.0 collective-permute-done.8
  21.9 0.0 collective-permute-done.7
  21.9 0.0 collective-permute-done.6
  22.0 0.1 abs_reduce_fusion
  22.1 2.7 %collective-permute-start.9 = (f16[72,256]{1,0:T(8,128)(2,1)S(1)}, f16[72,256]{1,0:T(8,128)(2,1)S(1)}, u32[]{:S(2)}, u32[]{:S(2)}) collective-permute-start(f16[72,256]{1,0:T(8,128)(2,1)S(1)} %pad_maximum_fusion.1), channel_id=1, source_target_pairs={{0,16},{4,20},{8,24},{12,28},{16,0},{20,4},{24,8},{28,12},{1,17},{... | collective-permute-start | bytes 110600 | tf_op jit(solution)/shard_map/ppermute | solution.py:154
  24.8 2.3 %collective-permute-done.9 = f16[72,256]{1,0:T(8,128)(2,1)S(1)} collective-permute-done((f16[72,256]{1,0:T(8,128)(2,1)S(1)}, f16[72,256]{1,0:T(8,128)(2,1)S(1)}, u32[]{:S(2)}, u32[]{:S(2)}) %collective-permute-start.9) | collective-permute-done | bytes 36896 | tf_op jit(solution)/shard_map/ppermute | solution.py:154
  27.1 0.7 %multiply_add_fusion = f32[64,256]{1,0:T(8,128)} fusion(f16[72,256]{1,0:T(8,128)(2,1)S(1)} %pad_maximum_fusion.1, f32[256]{0:T(256)S(1)} %bitcast.25, f16[72,256]{1,0:T(8,128)(2,1)S(1)} %collective-permute-done.9, f32[256]{0:T(256)S(1)} %bitcast.24), kind=kLoop, calls=%fused_computation.1 | loop fusion | flops 81920 | bytes 133120 | tf_op jit(solution)/shard_map/add | solution.py:221
  (15 shorter events, 0.2 us)
Async XLA Ops:
  0.6 5.1 %collective-permute-start = (bf16[64,256]{1,0:T(8,128)(2,1)}, bf16[64,256]{1,0:T(8,128)(2,1)S(1)}, u32[]{:S(2)}, u32[]{:S(2)}) collective-permute-start(bf16[64,256]{1,0:T(8,128)(2,1)} %param.7), channel_id=1, source_target_pairs={{0,2},{1,3},{2,0},{3,1},{4,6},{5,7},{6,4},{7,5},{8,10},{9,11},{10,... | collective-permute-start | bytes 98312 | tf_op jit(solution)/shard_map/ppermute | solution.py:154
  3.7 3.6 %collective-permute-start.2 = (bf16[64,256]{1,0:T(8,128)(2,1)}, bf16[64,256]{1,0:T(8,128)(2,1)S(1)}, u32[]{:S(2)}, u32[]{:S(2)}) collective-permute-start(bf16[64,256]{1,0:T(8,128)(2,1)} %param.7), channel_id=1, source_target_pairs={{0,3},{1,2},{2,1},{3,0},{4,7},{5,6},{6,5},{7,4},{8,11},{9,10},{10,... | collective-permute-start | bytes 98312 | tf_op jit(solution)/shard_map/ppermute | solution.py:154
  3.7 3.6 %collective-permute-start.1 = (bf16[64,256]{1,0:T(8,128)(2,1)}, bf16[64,256]{1,0:T(8,128)(2,1)S(1)}, u32[]{:S(2)}, u32[]{:S(2)}) collective-permute-start(bf16[64,256]{1,0:T(8,128)(2,1)} %param.7), channel_id=1, source_target_pairs={{0,1},{1,0},{2,3},{3,2},{4,5},{5,4},{6,7},{7,6},{8,9},{9,8},{10,11... | collective-permute-start | bytes 98312 | tf_op jit(solution)/shard_map/ppermute | solution.py:154
  10.0 4.8 %collective-permute-start.5 = (f32[64,256]{1,0:T(8,128)S(1)}, f32[64,256]{1,0:T(8,128)S(1)}, u32[]{:S(2)}, u32[]{:S(2)}) collective-permute-start(f32[64,256]{1,0:T(8,128)S(1)} %get-tuple-element.41), channel_id=1, source_target_pairs={{0,1},{1,0},{2,3},{3,2},{4,5},{5,4},{6,7},{7,6},{8,9},{9,8},{10,11... | collective-permute-start | bytes 196616 | tf_op jit(solution)/shard_map/ppermute | solution.py:154
  10.1 4.7 %collective-permute-start.3 = (bf16[64,256]{1,0:T(8,128)(2,1)S(1)}, bf16[64,256]{1,0:T(8,128)(2,1)S(1)}, u32[]{:S(2)}, u32[]{:S(2)}) collective-permute-start(bf16[64,256]{1,0:T(8,128)(2,1)S(1)} %get-tuple-element.39), channel_id=1, source_target_pairs={{0,2},{1,3},{2,0},{3,1},{4,6},{5,7},{6,4},{7,5},{8,10},{9,11},{10,... | collective-permute-start | bytes 98312 | tf_op jit(solution)/shard_map/ppermute | solution.py:154
  10.7 4.0 %collective-permute-start.4 = (bf16[64,256]{1,0:T(8,128)(2,1)S(1)}, bf16[64,256]{1,0:T(8,128)(2,1)S(1)}, u32[]{:S(2)}, u32[]{:S(2)}) collective-permute-start(bf16[64,256]{1,0:T(8,128)(2,1)S(1)} %get-tuple-element.40), channel_id=1, source_target_pairs={{0,3},{1,2},{2,1},{3,0},{4,7},{5,6},{6,5},{7,4},{8,11},{9,10},{10,... | collective-permute-start | bytes 98312 | tf_op jit(solution)/shard_map/ppermute | solution.py:154
  14.9 7.0 %collective-permute-start.8 = (f16[72,256]{1,0:T(8,128)(2,1)S(1)}, f16[72,256]{1,0:T(8,128)(2,1)S(1)}, u32[]{:S(2)}, u32[]{:S(2)}) collective-permute-start(f16[72,256]{1,0:T(8,128)(2,1)S(1)} %pad_maximum_fusion), channel_id=1, source_target_pairs={{0,12},{4,8},{8,4},{12,0},{16,28},{20,24},{24,20},{28,16},{1,13},{... | collective-permute-start | bytes 110600 | tf_op jit(solution)/shard_map/ppermute | solution.py:154
  17.5 4.5 %collective-permute-start.7 = (f16[72,256]{1,0:T(8,128)(2,1)S(1)}, f16[72,256]{1,0:T(8,128)(2,1)S(1)}, u32[]{:S(2)}, u32[]{:S(2)}) collective-permute-start(f16[72,256]{1,0:T(8,128)(2,1)S(1)} %pad_maximum_fusion), channel_id=1, source_target_pairs={{0,8},{4,12},{8,0},{12,4},{16,24},{20,28},{24,16},{28,20},{1,9},{5... | collective-permute-start | bytes 110600 | tf_op jit(solution)/shard_map/ppermute | solution.py:154
  17.9 4.0 %collective-permute-start.6 = (f16[72,256]{1,0:T(8,128)(2,1)S(1)}, f16[72,256]{1,0:T(8,128)(2,1)S(1)}, u32[]{:S(2)}, u32[]{:S(2)}) collective-permute-start(f16[72,256]{1,0:T(8,128)(2,1)S(1)} %pad_maximum_fusion), channel_id=1, source_target_pairs={{0,4},{4,0},{8,12},{12,8},{16,20},{20,16},{24,28},{28,24},{1,5},{5... | collective-permute-start | bytes 110600 | tf_op jit(solution)/shard_map/ppermute | solution.py:154
  22.1 4.9 %collective-permute-start.9 = (f16[72,256]{1,0:T(8,128)(2,1)S(1)}, f16[72,256]{1,0:T(8,128)(2,1)S(1)}, u32[]{:S(2)}, u32[]{:S(2)}) collective-permute-start(f16[72,256]{1,0:T(8,128)(2,1)S(1)} %pad_maximum_fusion.1), channel_id=1, source_target_pairs={{0,16},{4,20},{8,24},{12,28},{16,0},{20,4},{24,8},{28,12},{1,17},{... | collective-permute-start | bytes 110600 | tf_op jit(solution)/shard_map/ppermute | solution.py:154

commit v18 on v17

--- a/solution.py
+++ b/solution.py
@@ -28,18 +28,26 @@
     return jnp.exp(jnp.dot(load_part, piece, preferred_element_type=F32))
 
 
+def fetch(counts_hbm, counts_ref, first, chunk, sems):
+    copies = []
+    for index in range(counts_ref.shape[0] // chunk):
+        source = counts_hbm.at[pl.ds(first + index * chunk, chunk)]
+        copies.append(pltpu.make_async_copy(source, counts_ref.at[pl.ds(index * chunk, chunk)], sems.at[index]))
+        copies[-1].start()
+    return copies
+
+
 def shift_kernel(parts, order, axis, chunk, step, *refs):
     pack_ref, counts_hbm = refs[:2]
     arrived = refs[2 : 1 + parts]
     outs = refs[1 + parts : 1 + 2 * parts]
-    turned, shifted, whole, counts_ref, held, resid_low, load_ext, grad_shift, counts_sem = refs[1 + 2 * parts :]
+    turned, shifted, whole, counts_ref, held, resid_low, load_ext, grad_shift, counts_sems = refs[1 + 2 * parts :]
     me = lax.axis_index(axis)
     lats, total = grad_shift.shape
     early = held.shape[0]
     neurons = counts_ref.shape[0]
     width = total // parts
-    counts_copy = pltpu.make_async_copy(counts_hbm, counts_ref, counts_sem)
-    counts_copy.start()
+    copies = fetch(counts_hbm, counts_ref, 0, chunk, counts_sems)
 
     for k in range(parts):
         start = pl.multiple_of((me ^ k) * width, width)
@@ -73,7 +81,8 @@
     for rows, span in blocks:
         if rows.start < early:
             held[rows, span] = expected(turned[rows, :], shifted[:, span])
-    counts_copy.wait()
+    for copy in copies:
+        copy.wait()
     for rows, span in blocks:
         rate = held[rows, span] if rows.start < early else expected(turned[rows, :], shifted[:, span])
         resid_low[rows, span] = (rate - counts_ref[rows, span].astype(F32)).astype(BF16)
@@ -95,11 +104,9 @@
 
 def load_kernel(lats, first, chunk, step, *refs):
     pack_ref, turned, shifted, counts_hbm = refs[:4]
-    load_hbm, bias_hbm, counts_ref, held, load_ref, bias_ref, sems = refs[-7:]
+    load_hbm, bias_hbm, counts_ref, held, load_ref, bias_ref, counts_sems, sems = refs[-8:]
     count, total = counts_ref.shape
-    place = pl.ds(first, count)
-    counts_copy = pltpu.make_async_copy(counts_hbm.at[place], counts_ref, sems.at[0])
-    counts_copy.start()
+    copies = fetch(counts_hbm, counts_ref, first, chunk, counts_sems)
     length = pack_ref[lats + 2 : lats + 3, 0:1].astype(jnp.int32)
     bins = lax.broadcasted_iota(jnp.int32, (1, total), 1)
     blocks = [(slice(begin, begin + chunk), range(0, total, step)) for begin in range(0, count, chunk)]
@@ -107,8 +114,8 @@
         for at in starts:
             load_part = turned[first + rows.start : first + rows.stop, :]
             held[rows, at : at + step] = expected(load_part, shifted[:, at : at + step])
-    columns = shifted[0:lats, :].astype(F32).T.astype(BF16)
-    counts_copy.wait()
+    for copy in copies:
+        copy.wait()
     outward = []
     for index, (rows, starts) in enumerate(blocks):
         sums = jnp.zeros((chunk, LANES), F32)
@@ -118,12 +125,14 @@
             resid = jnp.where(bins[:, span] < length, held[rows, span] - counts_ref[rows, span].astype(F32), 0.0)
             for j in range(step // LANES):
                 sums = sums + resid[:, j * LANES : (j + 1) * LANES]
-            grad = grad + jnp.dot(resid.astype(BF16), columns[span], preferred_element_type=F32)
+            grad = grad + lax.dot_general(
+                resid.astype(BF16), shifted[0:lats, span], (((1,), (1,)), ((), ())), preferred_element_type=F32
+            )
         load_ref[:, rows] = grad.T
         bias_ref[:, rows] = jnp.sum(sums.T, axis=0, keepdims=True)
         place = pl.ds(first + rows.start, chunk)
-        outward.append(pltpu.make_async_copy(load_ref.at[:, rows], load_hbm.at[:, place], sems.at[2 * index + 1]))
-        outward.append(pltpu.make_async_copy(bias_ref.at[:, rows], bias_hbm.at[:, place], sems.at[2 * index + 2]))
+        outward.append(pltpu.make_async_copy(load_ref.at[:, rows], load_hbm.at[:, place], sems.at[2 * index]))
+        outward.append(pltpu.make_async_copy(bias_ref.at[:, rows], bias_hbm.at[:, place], sems.at[2 * index + 1]))
         for copy in outward[-2:]:
             copy.start()
     for copy in outward:
@@ -175,7 +184,7 @@
             pltpu.VMEM((neurons, total), BF16),
             pltpu.VMEM((lats + EXTRA, neurons), BF16),
             pltpu.VMEM((lats, total), F32),
-            pltpu.SemaphoreType.DMA,
+            pltpu.SemaphoreType.DMA((neurons // chunk,)),
         ],
         compiler_params=params,
     )(pack, counts[0], *arrived)
@@ -196,7 +205,8 @@
                 pltpu.VMEM((count, total), F32),
                 pltpu.VMEM((lats, count), F32),
                 pltpu.VMEM((1, count), F32),
-                pltpu.SemaphoreType.DMA((1 + 2 * (count // chunk),)),
+                pltpu.SemaphoreType.DMA((count // chunk,)),
+                pltpu.SemaphoreType.DMA((2 * (count // chunk),)),
             ],
             input_output_aliases={4 + i: i for i in range(len(made))},
             compiler_params=params,

time: 28 us -> 28.1 us (level)
  no operation moved by 1% of the time
where the time goes in v18:
time: 28.1 us; the launch traced here: 27.8 us
  starting transfers between devices  11.4 us (41%)
  Pallas kernels  9.06 us (32%)
  waiting for transfers between devices  3.98 us (14%)
  other arithmetic  1.99 us (7%)
  between operations  1.43 us (5%)
    ppermute x10, starting transfers between devices, swap(): return lax.ppermute(value, axis, [(i, i ^ mask) for i in range(count)])  11.4 us
    pallas_call x2, Pallas kernels, make(): pl.pallas_call(functools.partial(load_kernel, lats, first, chunk, step),...  6.4 us
    ppermute x10, waiting for transfers between devices, swap(): return lax.ppermute(value, axis, [(i, i ^ mask) for i in range(count)])  3.98 us
    pallas_call x1, Pallas kernels, per_device(): pl.pallas_call(functools.partial(shift_kernel, neuron_count, order, 'neur...  2.66 us
    add x1, other arithmetic, per_device(): pack = pack + jnp.pad(latents, ((0, 8), (neurons, 0))).astype(F32)  1.07 us
    add x1, other arithmetic, per_device(): value = decode(code) + decode(arrived[0])  0.65 us
  transfers between devices with their start and end apart: 10, of which 3 were waited for; matrix products, arithmetic and copies ran while one was open for 4% of the time, Pallas kernels for 23%

profile of v18, /device:TPU:0, one launch (start us, length us, event | category | flops | bytes accessed | tf_op | source)
XLA Modules:
  0.0 27.8 jit_solution(7149501349849271305)
XLA Ops:
  0.6 3.0 %collective-permute-start = (bf16[64,256]{1,0:T(8,128)(2,1)}, bf16[64,256]{1,0:T(8,128)(2,1)S(1)}, u32[]{:S(2)}, u32[]{:S(2)}) collective-permute-start(bf16[64,256]{1,0:T(8,128)(2,1)} %param.7), channel_id=1, source_target_pairs={{0,2},{1,3},{2,0},{3,1},{4,6},{5,7},{6,4},{7,5},{8,10},{9,11},{10,... | collective-permute-start | bytes 98312 | tf_op jit(solution)/shard_map/ppermute | solution.py:163
  3.7 0.0 collective-permute-start.2
  3.7 0.2 collective-permute-start.1
  4.5 1.1 %convert_add_fusion.refs_0_ = f32[72,1536]{1,0:T(8,128)S(1)} fusion(s32[1,64]{1,0:T(1,128)} %param.10, f32[1,1280]{1,0:T(1,128)} %param.9, bf16[64,256]{1,0:T(8,128)(2,1)} %param.7, bf16[64,1280]{1,0:T(8,128)(2,1)} %bitcast.15, s32[]{:T(128)} %bitcast.10, pred[72]{0:T(512)(128)(4,1)S(1)} %iota_compare_fusion), kind=kLoop, calls=%fused_computation | loop fusion | flops 774144 | bytes 644428 | tf_op jit(solution)/shard_map/add | solution.py:172
  5.6 0.2 collective-permute-done.refs_2_
  5.8 1.5 %collective-permute-done.2.refs_4_ = bf16[64,256]{1,0:T(8,128)(2,1)S(1)} collective-permute-done((bf16[64,256]{1,0:T(8,128)(2,1)}, bf16[64,256]{1,0:T(8,128)(2,1)S(1)}, u32[]{:S(2)}, u32[]{:S(2)}) %collective-permute-start.2) | collective-permute-done | bytes 32800 | tf_op jit(solution)/shard_map/ppermute | solution.py:163
  7.3 0.0 collective-permute-done.1.refs_3_
  7.3 2.7 %shard_map.85 = (f32[64,256]{1,0:T(8,128)S(1)}, f32[64,256]{1,0:T(8,128)S(1)}, bf16[64,256]{1,0:T(8,128)(2,1)S(1)}, bf16[64,256]{1,0:T(8,128)(2,1)S(1)}, bf16[12...) custom-call(f32[72,1536]{1,0:T(8,128)S(1)} %convert_add_fusion.refs_0_, bf16[1280,1024]{1,0:T(8,128)(2,1)} %bitcast.11, ...), custom_call_target="tpu_custom_call" | custom-call | tf_op jit(solution)/shard_map/pallas_call | solution.py:174
  10.0 0.1 collective-permute-start.5
  10.0 0.7 %collective-permute-start.3 = (bf16[64,256]{1,0:T(8,128)(2,1)S(1)}, bf16[64,256]{1,0:T(8,128)(2,1)S(1)}, u32[]{:S(2)}, u32[]{:S(2)}) collective-permute-start(bf16[64,256]{1,0:T(8,128)(2,1)S(1)} %get-tuple-element.39), channel_id=1, source_target_pairs={{0,2},{1,3},{2,0},{3,1},{4,6},{5,7},{6,4},{7,5},{8,10},{9,11},{10,... | collective-permute-start | bytes 98312 | tf_op jit(solution)/shard_map/ppermute | solution.py:163
  10.7 1.2 %collective-permute-start.4 = (bf16[64,256]{1,0:T(8,128)(2,1)S(1)}, bf16[64,256]{1,0:T(8,128)(2,1)S(1)}, u32[]{:S(2)}, u32[]{:S(2)}) collective-permute-start(bf16[64,256]{1,0:T(8,128)(2,1)S(1)} %get-tuple-element.40), channel_id=1, source_target_pairs={{0,3},{1,2},{2,1},{3,0},{4,7},{5,6},{6,5},{7,4},{8,11},{9,10},{10,... | collective-permute-start | bytes 98312 | tf_op jit(solution)/shard_map/ppermute | solution.py:163
  11.9 2.8 %shard_map.86 = (f32[64,1280]{1,0:T(8,128)}, f32[1,1280]{1,0:T(1,128)}) custom-call(f32[72,1536]{1,0:T(8,128)S(1)} %convert_add_fusion.refs_0_, bf16[1280,80]{1,0:T(8,128)(2,1)S(1)} %get-tuple-element.50.refs_1_, bf16[80,1024]{1,0:T(8,128)(2,1)S(1)} %get-tuple-element.43.refs_2_, bf16[1280,1024]{1,0:T(8,128)(2,1)} %bitcast.12), custom_call_target="tpu_custom_call" | custom-call | flops 134217728 | bytes 1048576 | tf_op jit(solution)/shard_map/pallas_call | solution.py:198
  14.7 0.0 collective-permute-done.3
  14.7 0.0 collective-permute-done.4
  14.7 0.0 collective-permute-done.5
  14.9 2.6 %collective-permute-start.8 = (f16[72,256]{1,0:T(8,128)(2,1)S(1)}, f16[72,256]{1,0:T(8,128)(2,1)S(1)}, u32[]{:S(2)}, u32[]{:S(2)}) collective-permute-start(f16[72,256]{1,0:T(8,128)(2,1)S(1)} %pad_maximum_fusion), channel_id=1, source_target_pairs={{0,12},{4,8},{8,4},{12,0},{16,28},{20,24},{24,20},{28,16},{1,13},{... | collective-permute-start | bytes 110600 | tf_op jit(solution)/shard_map/ppermute | solution.py:163
  17.4 0.4 %collective-permute-start.7 = (f16[72,256]{1,0:T(8,128)(2,1)S(1)}, f16[72,256]{1,0:T(8,128)(2,1)S(1)}, u32[]{:S(2)}, u32[]{:S(2)}) collective-permute-start(f16[72,256]{1,0:T(8,128)(2,1)S(1)} %pad_maximum_fusion), channel_id=1, source_target_pairs={{0,8},{4,12},{8,0},{12,4},{16,24},{20,28},{24,16},{28,20},{1,9},{5... | collective-permute-start | bytes 110600 | tf_op jit(solution)/shard_map/ppermute | solution.py:163
  17.9 0.5 %collective-permute-start.6 = (f16[72,256]{1,0:T(8,128)(2,1)S(1)}, f16[72,256]{1,0:T(8,128)(2,1)S(1)}, u32[]{:S(2)}, u32[]{:S(2)}) collective-permute-start(f16[72,256]{1,0:T(8,128)(2,1)S(1)} %pad_maximum_fusion), channel_id=1, source_target_pairs={{0,4},{4,0},{8,12},{12,8},{16,20},{20,16},{24,28},{28,24},{1,5},{5... | collective-permute-start | bytes 110600 | tf_op jit(solution)/shard_map/ppermute | solution.py:163
  18.4 3.6 %shard_map.87 = (f32[64,1280]{1,0:T(8,128)}, f32[1,1280]{1,0:T(1,128)}) custom-call(f32[72,1536]{1,0:T(8,128)S(1)} %convert_add_fusion.refs_0_, bf16[1280,80]{1,0:T(8,128)(2,1)S(1)} %get-tuple-element.50.refs_1_, bf16[80,1024]{1,0:T(8,128)(2,1)S(1)} %get-tuple-element.43.refs_2_, ...), custom_call_target="tpu_custom_call", output_to_operand_aliasing={{0}: (4, {}), {1}: (5, {})} | custom-call | flops 201326592 | bytes 1572864 | tf_op jit(solution)/shard_map/pallas_call | solution.py:198
  22.0 0.0 collective-permute-done.8
  22.1 0.0 collective-permute-done.7
  22.1 0.0 collective-permute-done.6
  22.1 0.1 abs_reduce_fusion
  22.3 2.7 %collective-permute-start.9 = (f16[72,256]{1,0:T(8,128)(2,1)S(1)}, f16[72,256]{1,0:T(8,128)(2,1)S(1)}, u32[]{:S(2)}, u32[]{:S(2)}) collective-permute-start(f16[72,256]{1,0:T(8,128)(2,1)S(1)} %pad_maximum_fusion.1), channel_id=1, source_target_pairs={{0,16},{4,20},{8,24},{12,28},{16,0},{20,4},{24,8},{28,12},{1,17},{... | collective-permute-start | bytes 110600 | tf_op jit(solution)/shard_map/ppermute | solution.py:163
  24.9 2.3 %collective-permute-done.9 = f16[72,256]{1,0:T(8,128)(2,1)S(1)} collective-permute-done((f16[72,256]{1,0:T(8,128)(2,1)S(1)}, f16[72,256]{1,0:T(8,128)(2,1)S(1)}, u32[]{:S(2)}, u32[]{:S(2)}) %collective-permute-start.9) | collective-permute-done | bytes 36896 | tf_op jit(solution)/shard_map/ppermute | solution.py:163
  27.2 0.7 %multiply_add_fusion = f32[64,256]{1,0:T(8,128)} fusion(f16[72,256]{1,0:T(8,128)(2,1)S(1)} %pad_maximum_fusion.1, f32[256]{0:T(256)S(1)} %bitcast.25, f16[72,256]{1,0:T(8,128)(2,1)S(1)} %collective-permute-done.9, f32[256]{0:T(256)S(1)} %bitcast.24), kind=kLoop, calls=%fused_computation.1 | loop fusion | flops 81920 | bytes 133120 | tf_op jit(solution)/shard_map/add | solution.py:231
  (15 shorter events, 0.2 us)
Async XLA Ops:
  0.6 5.1 %collective-permute-start = (bf16[64,256]{1,0:T(8,128)(2,1)}, bf16[64,256]{1,0:T(8,128)(2,1)S(1)}, u32[]{:S(2)}, u32[]{:S(2)}) collective-permute-start(bf16[64,256]{1,0:T(8,128)(2,1)} %param.7), channel_id=1, source_target_pairs={{0,2},{1,3},{2,0},{3,1},{4,6},{5,7},{6,4},{7,5},{8,10},{9,11},{10,... | collective-permute-start | bytes 98312 | tf_op jit(solution)/shard_map/ppermute | solution.py:163
  3.7 3.6 %collective-permute-start.2 = (bf16[64,256]{1,0:T(8,128)(2,1)}, bf16[64,256]{1,0:T(8,128)(2,1)S(1)}, u32[]{:S(2)}, u32[]{:S(2)}) collective-permute-start(bf16[64,256]{1,0:T(8,128)(2,1)} %param.7), channel_id=1, source_target_pairs={{0,3},{1,2},{2,1},{3,0},{4,7},{5,6},{6,5},{7,4},{8,11},{9,10},{10,... | collective-permute-start | bytes 98312 | tf_op jit(solution)/shard_map/ppermute | solution.py:163
  3.7 3.6 %collective-permute-start.1 = (bf16[64,256]{1,0:T(8,128)(2,1)}, bf16[64,256]{1,0:T(8,128)(2,1)S(1)}, u32[]{:S(2)}, u32[]{:S(2)}) collective-permute-start(bf16[64,256]{1,0:T(8,128)(2,1)} %param.7), channel_id=1, source_target_pairs={{0,1},{1,0},{2,3},{3,2},{4,5},{5,4},{6,7},{7,6},{8,9},{9,8},{10,11... | collective-permute-start | bytes 98312 | tf_op jit(solution)/shard_map/ppermute | solution.py:163
  10.0 4.8 %collective-permute-start.5 = (f32[64,256]{1,0:T(8,128)S(1)}, f32[64,256]{1,0:T(8,128)S(1)}, u32[]{:S(2)}, u32[]{:S(2)}) collective-permute-start(f32[64,256]{1,0:T(8,128)S(1)} %get-tuple-element.41), channel_id=1, source_target_pairs={{0,1},{1,0},{2,3},{3,2},{4,5},{5,4},{6,7},{7,6},{8,9},{9,8},{10,11... | collective-permute-start | bytes 196616 | tf_op jit(solution)/shard_map/ppermute | solution.py:163
  10.0 4.7 %collective-permute-start.3 = (bf16[64,256]{1,0:T(8,128)(2,1)S(1)}, bf16[64,256]{1,0:T(8,128)(2,1)S(1)}, u32[]{:S(2)}, u32[]{:S(2)}) collective-permute-start(bf16[64,256]{1,0:T(8,128)(2,1)S(1)} %get-tuple-element.39), channel_id=1, source_target_pairs={{0,2},{1,3},{2,0},{3,1},{4,6},{5,7},{6,4},{7,5},{8,10},{9,11},{10,... | collective-permute-start | bytes 98312 | tf_op jit(solution)/shard_map/ppermute | solution.py:163
  10.7 4.0 %collective-permute-start.4 = (bf16[64,256]{1,0:T(8,128)(2,1)S(1)}, bf16[64,256]{1,0:T(8,128)(2,1)S(1)}, u32[]{:S(2)}, u32[]{:S(2)}) collective-permute-start(bf16[64,256]{1,0:T(8,128)(2,1)S(1)} %get-tuple-element.40), channel_id=1, source_target_pairs={{0,3},{1,2},{2,1},{3,0},{4,7},{5,6},{6,5},{7,4},{8,11},{9,10},{10,... | collective-permute-start | bytes 98312 | tf_op jit(solution)/shard_map/ppermute | solution.py:163
  14.9 7.2 %collective-permute-start.8 = (f16[72,256]{1,0:T(8,128)(2,1)S(1)}, f16[72,256]{1,0:T(8,128)(2,1)S(1)}, u32[]{:S(2)}, u32[]{:S(2)}) collective-permute-start(f16[72,256]{1,0:T(8,128)(2,1)S(1)} %pad_maximum_fusion), channel_id=1, source_target_pairs={{0,12},{4,8},{8,4},{12,0},{16,28},{20,24},{24,20},{28,16},{1,13},{... | collective-permute-start | bytes 110600 | tf_op jit(solution)/shard_map/ppermute | solution.py:163
  17.4 4.6 %collective-permute-start.7 = (f16[72,256]{1,0:T(8,128)(2,1)S(1)}, f16[72,256]{1,0:T(8,128)(2,1)S(1)}, u32[]{:S(2)}, u32[]{:S(2)}) collective-permute-start(f16[72,256]{1,0:T(8,128)(2,1)S(1)} %pad_maximum_fusion), channel_id=1, source_target_pairs={{0,8},{4,12},{8,0},{12,4},{16,24},{20,28},{24,16},{28,20},{1,9},{5... | collective-permute-start | bytes 110600 | tf_op jit(solution)/shard_map/ppermute | solution.py:163
  17.9 4.2 %collective-permute-start.6 = (f16[72,256]{1,0:T(8,128)(2,1)S(1)}, f16[72,256]{1,0:T(8,128)(2,1)S(1)}, u32[]{:S(2)}, u32[]{:S(2)}) collective-permute-start(f16[72,256]{1,0:T(8,128)(2,1)S(1)} %pad_maximum_fusion), channel_id=1, source_target_pairs={{0,4},{4,0},{8,12},{12,8},{16,20},{20,16},{24,28},{28,24},{1,5},{5... | collective-permute-start | bytes 110600 | tf_op jit(solution)/shard_map/ppermute | solution.py:163
  22.3 4.9 %collective-permute-start.9 = (f16[72,256]{1,0:T(8,128)(2,1)S(1)}, f16[72,256]{1,0:T(8,128)(2,1)S(1)}, u32[]{:S(2)}, u32[]{:S(2)}) collective-permute-start(f16[72,256]{1,0:T(8,128)(2,1)S(1)} %pad_maximum_fusion.1), channel_id=1, source_target_pairs={{0,16},{4,20},{8,24},{12,28},{16,0},{20,4},{24,8},{28,12},{1,17},{... | collective-permute-start | bytes 110600 | tf_op jit(solution)/shard_map/ppermute | solution.py:163

commit v19 on v16

--- a/solution.py
+++ b/solution.py
@@ -29,7 +29,7 @@
     return jnp.exp(eta)
 
 
-def shift_kernel(parts, order, axis, chunk, step, *refs):
+def shift_kernel(parts, order, targets, axis, chunk, step, *refs):
     pack_ref, counts_hbm = refs[:2]
     arrived = refs[2 : 1 + parts]
     outs = refs[1 + parts : 1 + 2 * parts]
@@ -88,9 +88,9 @@
         tiles.append(jnp.where(bins[:, span] < length, grad_shift[:, span], 0.0))
     for j, tile in enumerate(shift_tiles(tiles, delay, False)):
         grad_shift[:, j * LANES : (j + 1) * LANES] = tile
-    for k in range(parts):
+    for k, out in zip(targets, outs):
         start = pl.multiple_of((me ^ k) * width, width)
-        outs[k][...] = grad_shift[:, pl.ds(start, width)].astype(outs[k].dtype)
+        out[...] = grad_shift[:, pl.ds(start, width)].astype(out.dtype)
 
 
 def load_kernel(lats, first, chunk, step, *refs):
@@ -154,7 +154,7 @@
     def swap(value, axis, count, mask):
         return lax.ppermute(value, axis, [(i, i ^ mask) for i in range(count)])
 
-    order = sorted(range(1, neuron_count), key=lambda k: (k != 2, k))
+    order = [*range(2, neuron_count), 1]
     arrived = [swap(latents, "neuron", neuron_count, k) for k in order]
     row = lax.broadcasted_iota(jnp.int32, (lats + 8, neurons + width), 0)
     lines = jnp.pad(delays, ((lats + 1, 6), (0, neurons + width - lats)))
@@ -163,16 +163,17 @@
     pack = pack + jnp.pad(loadings[0], ((0, 8), (0, width))).astype(F32)
     pack = pack + jnp.pad(latents, ((0, 8), (neurons, 0))).astype(F32)
 
+    targets = [0, *order]
     *outs, load_ext, shifted = pl.pallas_call(
-        functools.partial(shift_kernel, neuron_count, order, "neuron", chunk, step),
-        out_shape=[jax.ShapeDtypeStruct((lats, width), BF16 if k > 1 else F32) for k in range(neuron_count)]
+        functools.partial(shift_kernel, neuron_count, order, targets, "neuron", chunk, step),
+        out_shape=[jax.ShapeDtypeStruct((lats, width), BF16 if k else F32) for k in targets]
         + [jax.ShapeDtypeStruct((lats + EXTRA, neurons), BF16), jax.ShapeDtypeStruct((lats + EXTRA, total), BF16)],
         in_specs=[vmem, hbm] + [vmem] * (neuron_count - 1),
         out_specs=[vmem] * (neuron_count + 2),
         scratch_shapes=[
             pltpu.VMEM((lats, total), BF16),
             pltpu.VMEM((neurons, total), BF16),
-            pltpu.VMEM((4 * chunk, total), F32),
+            pltpu.VMEM((2 * chunk, total), F32),
             pltpu.VMEM((neurons, total), BF16),
             pltpu.VMEM((lats, total), F32),
             pltpu.SemaphoreType.DMA,
@@ -207,7 +208,7 @@
         return before, out
 
     outs, made = make(outs)
-    arrived = [swap(outs[k], "neuron", neuron_count, k) for k in [*range(2, neuron_count), 1]]
+    arrived = [swap(out, "neuron", neuron_count, k) for k, out in zip(targets[1:], outs[1:])]
     arrived, made = lax.optimization_barrier((arrived, made))
     value = functools.reduce(jnp.add, [outs[0]] + [block.astype(F32) for block in arrived])
     mask = 1

time: 27.8 us -> 28.3 us (1.018)
  no operation moved by 1% of the time
where the time goes in v19:
time: 28.3 us; the launch traced here: 28.1 us
  starting transfers between devices  11.6 us (41%)
  Pallas kernels  9.09 us (32%)
  waiting for transfers between devices  3.89 us (14%)
  other arithmetic  1.99 us (7%)
  between operations  1.42 us (5%)
    ppermute x10, starting transfers between devices, swap(): return lax.ppermute(value, axis, [(i, i ^ mask) for i in range(count)])  11.6 us
    pallas_call x2, Pallas kernels, make(): pl.pallas_call(functools.partial(load_kernel, lats, first, chunk, step),...  6.07 us
    ppermute x10, waiting for transfers between devices, swap(): return lax.ppermute(value, axis, [(i, i ^ mask) for i in range(count)])  3.89 us
    pallas_call x1, Pallas kernels, per_device(): pl.pallas_call(functools.partial(shift_kernel, neuron_count, order, targe...  3.01 us
    add x1, other arithmetic, per_device(): pack = pack + jnp.pad(latents, ((0, 8), (neurons, 0))).astype(F32)  1.07 us
    add x1, other arithmetic, per_device(): value = decode(code) + decode(arrived[0])  0.65 us
  transfers between devices with their start and end apart: 10, of which 3 were waited for; matrix products, arithmetic and copies ran while one was open for 4% of the time, Pallas kernels for 22%

profile of v19, /device:TPU:0, one launch (start us, length us, event | category | flops | bytes accessed | tf_op | source)
XLA Modules:
  0.0 28.1 jit_solution(4996089829713821702)
XLA Ops:
  0.6 3.0 %collective-permute-start = (bf16[64,256]{1,0:T(8,128)(2,1)}, bf16[64,256]{1,0:T(8,128)(2,1)S(1)}, u32[]{:S(2)}, u32[]{:S(2)}) collective-permute-start(bf16[64,256]{1,0:T(8,128)(2,1)} %param.7), channel_id=1, source_target_pairs={{0,2},{1,3},{2,0},{3,1},{4,6},{5,7},{6,4},{7,5},{8,10},{9,11},{10,... | collective-permute-start | bytes 98312 | tf_op jit(solution)/shard_map/ppermute | solution.py:155
  3.7 0.0 collective-permute-start.2
  3.7 0.2 collective-permute-start.1
  4.5 1.1 %convert_add_fusion.refs_0_ = f32[72,1536]{1,0:T(8,128)S(1)} fusion(s32[1,64]{1,0:T(1,128)} %param.10, f32[1,1280]{1,0:T(1,128)} %param.9, bf16[64,256]{1,0:T(8,128)(2,1)} %param.7, bf16[64,1280]{1,0:T(8,128)(2,1)} %bitcast.15, s32[]{:T(128)} %bitcast.10, pred[72]{0:T(512)(128)(4,1)S(1)} %iota_compare_fusion), kind=kLoop, calls=%fused_computation | loop fusion | flops 774144 | bytes 644428 | tf_op jit(solution)/shard_map/add | solution.py:164
  5.6 0.2 collective-permute-done.refs_2_
  5.8 0.0 collective-permute-done.2.refs_4_
  5.8 1.4 %collective-permute-done.1.refs_3_ = bf16[64,256]{1,0:T(8,128)(2,1)S(1)} collective-permute-done((bf16[64,256]{1,0:T(8,128)(2,1)}, bf16[64,256]{1,0:T(8,128)(2,1)S(1)}, u32[]{:S(2)}, u32[]{:S(2)}) %collective-permute-start.1) | collective-permute-done | bytes 32800 | tf_op jit(solution)/shard_map/ppermute | solution.py:155
  7.2 3.0 %shard_map.85 = (f32[64,256]{1,0:T(8,128)S(1)}, bf16[64,256]{1,0:T(8,128)(2,1)S(1)}, bf16[64,256]{1,0:T(8,128)(2,1)S(1)}, bf16[64,256]{1,0:T(8,128)(2,1)S(1)}, b...) custom-call(f32[72,1536]{1,0:T(8,128)S(1)} %convert_add_fusion.refs_0_, bf16[1280,1024]{1,0:T(8,128)(2,1)} %bitcast.11, ...), custom_call_target="tpu_custom_call" | custom-call | tf_op jit(solution)/shard_map/pallas_call | solution.py:167
  10.2 0.8 %collective-permute-start.3 = (bf16[64,256]{1,0:T(8,128)(2,1)S(1)}, bf16[64,256]{1,0:T(8,128)(2,1)S(1)}, u32[]{:S(2)}, u32[]{:S(2)}) collective-permute-start(bf16[64,256]{1,0:T(8,128)(2,1)S(1)} %get-tuple-element.39), channel_id=1, source_target_pairs={{0,2},{1,3},{2,0},{3,1},{4,6},{5,7},{6,4},{7,5},{8,10},{9,11},{10,... | collective-permute-start | bytes 98312 | tf_op jit(solution)/shard_map/ppermute | solution.py:155
  11.1 1.1 %collective-permute-start.4 = (bf16[64,256]{1,0:T(8,128)(2,1)S(1)}, bf16[64,256]{1,0:T(8,128)(2,1)S(1)}, u32[]{:S(2)}, u32[]{:S(2)}) collective-permute-start(bf16[64,256]{1,0:T(8,128)(2,1)S(1)} %get-tuple-element.40), channel_id=1, source_target_pairs={{0,3},{1,2},{2,1},{3,0},{4,7},{5,6},{6,5},{7,4},{8,11},{9,10},{10,... | collective-permute-start | bytes 98312 | tf_op jit(solution)/shard_map/ppermute | solution.py:155
  12.2 0.3 %collective-permute-start.5 = (bf16[64,256]{1,0:T(8,128)(2,1)S(1)}, bf16[64,256]{1,0:T(8,128)(2,1)S(1)}, u32[]{:S(2)}, u32[]{:S(2)}) collective-permute-start(bf16[64,256]{1,0:T(8,128)(2,1)S(1)} %get-tuple-element.41), channel_id=1, source_target_pairs={{0,1},{1,0},{2,3},{3,2},{4,5},{5,4},{6,7},{7,6},{8,9},{9,8},{10,11... | collective-permute-start | bytes 98312 | tf_op jit(solution)/shard_map/ppermute | solution.py:155
  12.4 2.5 %shard_map.86 = (f32[64,1280]{1,0:T(8,128)}, f32[1,1280]{1,0:T(1,128)}) custom-call(f32[72,1536]{1,0:T(8,128)S(1)} %convert_add_fusion.refs_0_, bf16[80,1280]{1,0:T(8,128)(2,1)S(1)} %get-tuple-element.50.refs_1_, bf16[80,1024]{1,0:T(8,128)(2,1)S(1)} %get-tuple-element.43.refs_2_, bf16[1280,1024]{1,0:T(8,128)(2,1)} %bitcast.12), custom_call_target="tpu_custom_call" | custom-call | flops 134217728 | bytes 1048576 | tf_op jit(solution)/shard_map/pallas_call | solution.py:190
  15.0 0.0 collective-permute-done.3
  15.0 0.0 collective-permute-done.4
  15.0 0.0 collective-permute-done.5
  15.1 2.6 %collective-permute-start.8 = (f16[72,256]{1,0:T(8,128)(2,1)S(1)}, f16[72,256]{1,0:T(8,128)(2,1)S(1)}, u32[]{:S(2)}, u32[]{:S(2)}) collective-permute-start(f16[72,256]{1,0:T(8,128)(2,1)S(1)} %pad_maximum_fusion), channel_id=1, source_target_pairs={{0,12},{4,8},{8,4},{12,0},{16,28},{20,24},{24,20},{28,16},{1,13},{... | collective-permute-start | bytes 110600 | tf_op jit(solution)/shard_map/ppermute | solution.py:155
  17.7 0.4 %collective-permute-start.7 = (f16[72,256]{1,0:T(8,128)(2,1)S(1)}, f16[72,256]{1,0:T(8,128)(2,1)S(1)}, u32[]{:S(2)}, u32[]{:S(2)}) collective-permute-start(f16[72,256]{1,0:T(8,128)(2,1)S(1)} %pad_maximum_fusion), channel_id=1, source_target_pairs={{0,8},{4,12},{8,0},{12,4},{16,24},{20,28},{24,16},{28,20},{1,9},{5... | collective-permute-start | bytes 110600 | tf_op jit(solution)/shard_map/ppermute | solution.py:155
  18.2 0.5 %collective-permute-start.6 = (f16[72,256]{1,0:T(8,128)(2,1)S(1)}, f16[72,256]{1,0:T(8,128)(2,1)S(1)}, u32[]{:S(2)}, u32[]{:S(2)}) collective-permute-start(f16[72,256]{1,0:T(8,128)(2,1)S(1)} %pad_maximum_fusion), channel_id=1, source_target_pairs={{0,4},{4,0},{8,12},{12,8},{16,20},{20,16},{24,28},{28,24},{1,5},{5... | collective-permute-start | bytes 110600 | tf_op jit(solution)/shard_map/ppermute | solution.py:155
  18.7 3.5 %shard_map.87 = (f32[64,1280]{1,0:T(8,128)}, f32[1,1280]{1,0:T(1,128)}) custom-call(f32[72,1536]{1,0:T(8,128)S(1)} %convert_add_fusion.refs_0_, bf16[80,1280]{1,0:T(8,128)(2,1)S(1)} %get-tuple-element.50.refs_1_, bf16[80,1024]{1,0:T(8,128)(2,1)S(1)} %get-tuple-element.43.refs_2_, ...), custom_call_target="tpu_custom_call", output_to_operand_aliasing={{0}: (4, {}), {1}: (5, {})} | custom-call | flops 201326592 | bytes 1572864 | tf_op jit(solution)/shard_map/pallas_call | solution.py:190
  22.3 0.0 collective-permute-done.8
  22.3 0.0 collective-permute-done.7
  22.3 0.0 collective-permute-done.6
  22.5 2.6 %collective-permute-start.9 = (f16[72,256]{1,0:T(8,128)(2,1)S(1)}, f16[72,256]{1,0:T(8,128)(2,1)S(1)}, u32[]{:S(2)}, u32[]{:S(2)}) collective-permute-start(f16[72,256]{1,0:T(8,128)(2,1)S(1)} %pad_maximum_fusion.1), channel_id=1, source_target_pairs={{0,16},{4,20},{8,24},{12,28},{16,0},{20,4},{24,8},{28,12},{1,17},{... | collective-permute-start | bytes 110600 | tf_op jit(solution)/shard_map/ppermute | solution.py:155
  25.1 2.3 %collective-permute-done.9 = f16[72,256]{1,0:T(8,128)(2,1)S(1)} collective-permute-done((f16[72,256]{1,0:T(8,128)(2,1)S(1)}, f16[72,256]{1,0:T(8,128)(2,1)S(1)}, u32[]{:S(2)}, u32[]{:S(2)}) %collective-permute-start.9) | collective-permute-done | bytes 36896 | tf_op jit(solution)/shard_map/ppermute | solution.py:155
  27.4 0.7 %multiply_add_fusion = f32[64,256]{1,0:T(8,128)} fusion(f16[72,256]{1,0:T(8,128)(2,1)S(1)} %pad_maximum_fusion.1, f32[256]{0:T(256)S(1)} %bitcast.25, f16[72,256]{1,0:T(8,128)(2,1)S(1)} %collective-permute-done.9, f32[256]{0:T(256)S(1)} %bitcast.24), kind=kLoop, calls=%fused_computation.1 | loop fusion | flops 81920 | bytes 133120 | tf_op jit(solution)/shard_map/add | solution.py:222
  (16 shorter events, 0.3 us)
Async XLA Ops:
  0.6 5.1 %collective-permute-start = (bf16[64,256]{1,0:T(8,128)(2,1)}, bf16[64,256]{1,0:T(8,128)(2,1)S(1)}, u32[]{:S(2)}, u32[]{:S(2)}) collective-permute-start(bf16[64,256]{1,0:T(8,128)(2,1)} %param.7), channel_id=1, source_target_pairs={{0,2},{1,3},{2,0},{3,1},{4,6},{5,7},{6,4},{7,5},{8,10},{9,11},{10,... | collective-permute-start | bytes 98312 | tf_op jit(solution)/shard_map/ppermute | solution.py:155
  3.7 2.1 %collective-permute-start.2 = (bf16[64,256]{1,0:T(8,128)(2,1)}, bf16[64,256]{1,0:T(8,128)(2,1)S(1)}, u32[]{:S(2)}, u32[]{:S(2)}) collective-permute-start(bf16[64,256]{1,0:T(8,128)(2,1)} %param.7), channel_id=1, source_target_pairs={{0,1},{1,0},{2,3},{3,2},{4,5},{5,4},{6,7},{7,6},{8,9},{9,8},{10,11... | collective-permute-start | bytes 98312 | tf_op jit(solution)/shard_map/ppermute | solution.py:155
  3.7 3.6 %collective-permute-start.1 = (bf16[64,256]{1,0:T(8,128)(2,1)}, bf16[64,256]{1,0:T(8,128)(2,1)S(1)}, u32[]{:S(2)}, u32[]{:S(2)}) collective-permute-start(bf16[64,256]{1,0:T(8,128)(2,1)} %param.7), channel_id=1, source_target_pairs={{0,3},{1,2},{2,1},{3,0},{4,7},{5,6},{6,5},{7,4},{8,11},{9,10},{10,... | collective-permute-start | bytes 98312 | tf_op jit(solution)/shard_map/ppermute | solution.py:155
  10.2 4.8 %collective-permute-start.3 = (bf16[64,256]{1,0:T(8,128)(2,1)S(1)}, bf16[64,256]{1,0:T(8,128)(2,1)S(1)}, u32[]{:S(2)}, u32[]{:S(2)}) collective-permute-start(bf16[64,256]{1,0:T(8,128)(2,1)S(1)} %get-tuple-element.39), channel_id=1, source_target_pairs={{0,2},{1,3},{2,0},{3,1},{4,6},{5,7},{6,4},{7,5},{8,10},{9,11},{10,... | collective-permute-start | bytes 98312 | tf_op jit(solution)/shard_map/ppermute | solution.py:155
  11.1 3.9 %collective-permute-start.4 = (bf16[64,256]{1,0:T(8,128)(2,1)S(1)}, bf16[64,256]{1,0:T(8,128)(2,1)S(1)}, u32[]{:S(2)}, u32[]{:S(2)}) collective-permute-start(bf16[64,256]{1,0:T(8,128)(2,1)S(1)} %get-tuple-element.40), channel_id=1, source_target_pairs={{0,3},{1,2},{2,1},{3,0},{4,7},{5,6},{6,5},{7,4},{8,11},{9,10},{10,... | collective-permute-start | bytes 98312 | tf_op jit(solution)/shard_map/ppermute | solution.py:155
  12.2 2.9 %collective-permute-start.5 = (bf16[64,256]{1,0:T(8,128)(2,1)S(1)}, bf16[64,256]{1,0:T(8,128)(2,1)S(1)}, u32[]{:S(2)}, u32[]{:S(2)}) collective-permute-start(bf16[64,256]{1,0:T(8,128)(2,1)S(1)} %get-tuple-element.41), channel_id=1, source_target_pairs={{0,1},{1,0},{2,3},{3,2},{4,5},{5,4},{6,7},{7,6},{8,9},{9,8},{10,11... | collective-permute-start | bytes 98312 | tf_op jit(solution)/shard_map/ppermute | solution.py:155
  15.1 7.1 %collective-permute-start.8 = (f16[72,256]{1,0:T(8,128)(2,1)S(1)}, f16[72,256]{1,0:T(8,128)(2,1)S(1)}, u32[]{:S(2)}, u32[]{:S(2)}) collective-permute-start(f16[72,256]{1,0:T(8,128)(2,1)S(1)} %pad_maximum_fusion), channel_id=1, source_target_pairs={{0,12},{4,8},{8,4},{12,0},{16,28},{20,24},{24,20},{28,16},{1,13},{... | collective-permute-start | bytes 110600 | tf_op jit(solution)/shard_map/ppermute | solution.py:155
  17.7 4.6 %collective-permute-start.7 = (f16[72,256]{1,0:T(8,128)(2,1)S(1)}, f16[72,256]{1,0:T(8,128)(2,1)S(1)}, u32[]{:S(2)}, u32[]{:S(2)}) collective-permute-start(f16[72,256]{1,0:T(8,128)(2,1)S(1)} %pad_maximum_fusion), channel_id=1, source_target_pairs={{0,8},{4,12},{8,0},{12,4},{16,24},{20,28},{24,16},{28,20},{1,9},{5... | collective-permute-start | bytes 110600 | tf_op jit(solution)/shard_map/ppermute | solution.py:155
  18.2 4.1 %collective-permute-start.6 = (f16[72,256]{1,0:T(8,128)(2,1)S(1)}, f16[72,256]{1,0:T(8,128)(2,1)S(1)}, u32[]{:S(2)}, u32[]{:S(2)}) collective-permute-start(f16[72,256]{1,0:T(8,128)(2,1)S(1)} %pad_maximum_fusion), channel_id=1, source_target_pairs={{0,4},{4,0},{8,12},{12,8},{16,20},{20,16},{24,28},{28,24},{1,5},{5... | collective-permute-start | bytes 110600 | tf_op jit(solution)/shard_map/ppermute | solution.py:155
  22.5 4.9 %collective-permute-start.9 = (f16[72,256]{1,0:T(8,128)(2,1)S(1)}, f16[72,256]{1,0:T(8,128)(2,1)S(1)}, u32[]{:S(2)}, u32[]{:S(2)}) collective-permute-start(f16[72,256]{1,0:T(8,128)(2,1)S(1)} %pad_maximum_fusion.1), channel_id=1, source_target_pairs={{0,16},{4,20},{8,24},{12,28},{16,0},{20,4},{24,8},{28,12},{1,17},{... | collective-permute-start | bytes 110600 | tf_op jit(solution)/shard_map/ppermute | solution.py:155

commit v20 on v16

--- a/solution.py
+++ b/solution.py
@@ -36,7 +36,6 @@
     load_ext, shifted, whole, counts_ref, held, resid_low, grad_shift, counts_sem = refs[1 + 2 * parts :]
     me = lax.axis_index(axis)
     lats, total = grad_shift.shape
-    early = held.shape[0]
     neurons = counts_ref.shape[0]
     width = total // parts
     counts_copy = pltpu.make_async_copy(counts_hbm, counts_ref, counts_sem)
@@ -71,12 +70,10 @@
         for begin in range(0, total, step)
     ]
     for rows, span in blocks:
-        if rows.start < early:
-            held[rows, span] = expected(load_ext[:, rows], shifted[:, span])
+        held[rows, span] = expected(load_ext[:, rows], shifted[:, span])
     counts_copy.wait()
     for rows, span in blocks:
-        rate = held[rows, span] if rows.start < early else expected(load_ext[:, rows], shifted[:, span])
-        resid_low[rows, span] = (rate - counts_ref[rows, span].astype(F32)).astype(BF16)
+        resid_low[rows, span] = (held[rows, span] - counts_ref[rows, span].astype(F32)).astype(BF16)
     for begin in range(0, total, step):
         span = slice(begin, begin + step)
         grad_shift[:, span] = jnp.dot(load_ext[0:lats, :], resid_low[:, span], preferred_element_type=F32)
@@ -172,7 +169,7 @@
         scratch_shapes=[
             pltpu.VMEM((lats, total), BF16),
             pltpu.VMEM((neurons, total), BF16),
-            pltpu.VMEM((4 * chunk, total), F32),
+            pltpu.VMEM((neurons, total), F32),
             pltpu.VMEM((neurons, total), BF16),
             pltpu.VMEM((lats, total), F32),
             pltpu.SemaphoreType.DMA,
@@ -213,14 +210,19 @@
     mask = 1
     while mask < region_count:
         masks = [mask, 2 * mask, 3 * mask] if 2 * mask < region_count else [mask]
-        code = lax.optimization_barrier(encode(value))
+        if len(masks) == 3:
+            value = lax.reduce_precision(value, 8, 7)
+            sent, read = value.astype(BF16), lambda block: block.astype(F32)
+        else:
+            sent, read = lax.optimization_barrier(encode(value)), decode
+            value = decode(sent)
         if shares:
-            code, made = make(code)
-        arrived = [swap(code, "region", region_count, k) for k in masks]
+            (value, sent), made = make((value, sent))
+        arrived = [swap(sent, "region", region_count, k) for k in masks]
         arrived, made = lax.optimization_barrier((arrived, made))
-        value = decode(code) + decode(arrived[0])
+        value = value + read(arrived[0])
         if len(masks) == 3:
-            value = value + (decode(arrived[1]) + decode(arrived[2]))
+            value = value + (read(arrived[1]) + read(arrived[2]))
         mask *= 1 + len(masks)
     grad_load, grad_bias = made
     return (value, grad_load[None], grad_bias)

time: 27.8 us -> 28.3 us (1.018)
  Pallas kernels: 8.82 us -> 9.46 us
    pallas_call x1, Pallas kernels: 2.75 us -> 3.4 us  [per_device(): pl.pallas_call(functools.partial(shift_kernel, neuron_count, order, 'neur...]
where the time goes in v20:
time: 28.3 us; the launch traced here: 28.1 us
  starting transfers between devices  11.4 us (40%)
  Pallas kernels  9.46 us (33%)
  waiting for transfers between devices  3.93 us (14%)
  other arithmetic  1.86 us (7%)
  between operations  1.4 us (5%)
    ppermute x10, starting transfers between devices, swap(): return lax.ppermute(value, axis, [(i, i ^ mask) for i in range(count)])  11.4 us
    pallas_call x2, Pallas kernels, make(): pl.pallas_call(functools.partial(load_kernel, lats, first, chunk, step),...  6.07 us
    ppermute x10, waiting for transfers between devices, swap(): return lax.ppermute(value, axis, [(i, i ^ mask) for i in range(count)])  3.93 us
    pallas_call x1, Pallas kernels, per_device(): pl.pallas_call(functools.partial(shift_kernel, neuron_count, order, 'neur...  3.4 us
    add x1, other arithmetic, per_device(): pack = pack + jnp.pad(latents, ((0, 8), (neurons, 0))).astype(F32)  1.07 us
    add x1, other arithmetic, per_device(): value = value + read(arrived[0])  0.65 us
  transfers between devices with their start and end apart: 10, of which 3 were waited for; matrix products, arithmetic and copies ran while one was open for 4% of the time, Pallas kernels for 22%

profile of v20, /device:TPU:0, one launch (start us, length us, event | category | flops | bytes accessed | tf_op | source)
XLA Modules:
  0.0 28.1 jit_solution(864674403873079932)
XLA Ops:
  0.6 3.0 %collective-permute-start = (bf16[64,256]{1,0:T(8,128)(2,1)}, bf16[64,256]{1,0:T(8,128)(2,1)S(1)}, u32[]{:S(2)}, u32[]{:S(2)}) collective-permute-start(bf16[64,256]{1,0:T(8,128)(2,1)} %param.7), channel_id=1, source_target_pairs={{0,2},{1,3},{2,0},{3,1},{4,6},{5,7},{6,4},{7,5},{8,10},{9,11},{10,... | collective-permute-start | bytes 98312 | tf_op jit(solution)/shard_map/ppermute | solution.py:152
  3.7 0.0 collective-permute-start.2
  3.7 0.2 collective-permute-start.1
  4.5 1.1 %convert_add_fusion.refs_0_ = f32[72,1536]{1,0:T(8,128)S(1)} fusion(s32[1,64]{1,0:T(1,128)} %param.10, f32[1,1280]{1,0:T(1,128)} %param.9, bf16[64,256]{1,0:T(8,128)(2,1)} %param.7, bf16[64,1280]{1,0:T(8,128)(2,1)} %bitcast.11, s32[]{:T(128)} %bitcast.6, pred[72]{0:T(512)(128)(4,1)S(1)} %iota_compare_fusion), kind=kLoop, calls=%fused_computation | loop fusion | flops 774144 | bytes 644428 | tf_op jit(solution)/shard_map/add | solution.py:161
  5.6 0.2 collective-permute-done.refs_2_
  5.8 1.5 %collective-permute-done.2.refs_4_ = bf16[64,256]{1,0:T(8,128)(2,1)S(1)} collective-permute-done((bf16[64,256]{1,0:T(8,128)(2,1)}, bf16[64,256]{1,0:T(8,128)(2,1)S(1)}, u32[]{:S(2)}, u32[]{:S(2)}) %collective-permute-start.2) | collective-permute-done | bytes 32800 | tf_op jit(solution)/shard_map/ppermute | solution.py:152
  7.3 0.0 collective-permute-done.1.refs_3_
  7.3 3.4 %shard_map.85 = (f32[64,256]{1,0:T(8,128)S(1)}, f32[64,256]{1,0:T(8,128)S(1)}, bf16[64,256]{1,0:T(8,128)(2,1)S(1)}, bf16[64,256]{1,0:T(8,128)(2,1)S(1)}, bf16[80...) custom-call(f32[72,1536]{1,0:T(8,128)S(1)} %convert_add_fusion.refs_0_, bf16[1280,1024]{1,0:T(8,128)(2,1)} %bitcast.7, ...), custom_call_target="tpu_custom_call" | custom-call | tf_op jit(solution)/shard_map/pallas_call | solution.py:163
  10.7 0.1 collective-permute-start.5
  10.8 0.7 %collective-permute-start.3 = (bf16[64,256]{1,0:T(8,128)(2,1)S(1)}, bf16[64,256]{1,0:T(8,128)(2,1)S(1)}, u32[]{:S(2)}, u32[]{:S(2)}) collective-permute-start(bf16[64,256]{1,0:T(8,128)(2,1)S(1)} %get-tuple-element.40), channel_id=1, source_target_pairs={{0,2},{1,3},{2,0},{3,1},{4,6},{5,7},{6,4},{7,5},{8,10},{9,11},{10,... | collective-permute-start | bytes 98312 | tf_op jit(solution)/shard_map/ppermute | solution.py:152
  11.4 1.2 %collective-permute-start.4 = (bf16[64,256]{1,0:T(8,128)(2,1)S(1)}, bf16[64,256]{1,0:T(8,128)(2,1)S(1)}, u32[]{:S(2)}, u32[]{:S(2)}) collective-permute-start(bf16[64,256]{1,0:T(8,128)(2,1)S(1)} %get-tuple-element.41), channel_id=1, source_target_pairs={{0,3},{1,2},{2,1},{3,0},{4,7},{5,6},{6,5},{7,4},{8,11},{9,10},{10,... | collective-permute-start | bytes 98312 | tf_op jit(solution)/shard_map/ppermute | solution.py:152
  12.6 2.5 %shard_map.86 = (f32[64,1280]{1,0:T(8,128)}, f32[1,1280]{1,0:T(1,128)}) custom-call(f32[72,1536]{1,0:T(8,128)S(1)} %convert_add_fusion.refs_0_, bf16[80,1280]{1,0:T(8,128)(2,1)S(1)} %get-tuple-element.52.refs_1_, bf16[80,1024]{1,0:T(8,128)(2,1)S(1)} %get-tuple-element.44.refs_2_, bf16[1280,1024]{1,0:T(8,128)(2,1)} %bitcast.8), custom_call_target="tpu_custom_call" | custom-call | flops 134217728 | bytes 1048576 | tf_op jit(solution)/shard_map/pallas_call | solution.py:186
  15.2 0.0 collective-permute-done.3
  15.2 0.0 collective-permute-done.4
  15.2 0.0 collective-permute-done.5
  15.2 2.6 %collective-permute-start.8 = (bf16[64,256]{1,0:T(8,128)(2,1)S(1)}, bf16[64,256]{1,0:T(8,128)(2,1)S(1)}, u32[]{:S(2)}, u32[]{:S(2)}) collective-permute-start(bf16[64,256]{1,0:T(8,128)(2,1)S(1)} %get-tuple-element.51), channel_id=1, source_target_pairs={{0,12},{4,8},{8,4},{12,0},{16,28},{20,24},{24,20},{28,16},{1,13},{... | collective-permute-start | bytes 98312 | tf_op jit(solution)/shard_map/ppermute | solution.py:152
  17.9 0.5 %collective-permute-start.7 = (bf16[64,256]{1,0:T(8,128)(2,1)S(1)}, bf16[64,256]{1,0:T(8,128)(2,1)S(1)}, u32[]{:S(2)}, u32[]{:S(2)}) collective-permute-start(bf16[64,256]{1,0:T(8,128)(2,1)S(1)} %get-tuple-element.51), channel_id=1, source_target_pairs={{0,8},{4,12},{8,0},{12,4},{16,24},{20,28},{24,16},{28,20},{1,9},{5... | collective-permute-start | bytes 98312 | tf_op jit(solution)/shard_map/ppermute | solution.py:152
  18.3 0.5 %collective-permute-start.6 = (bf16[64,256]{1,0:T(8,128)(2,1)S(1)}, bf16[64,256]{1,0:T(8,128)(2,1)S(1)}, u32[]{:S(2)}, u32[]{:S(2)}) collective-permute-start(bf16[64,256]{1,0:T(8,128)(2,1)S(1)} %get-tuple-element.51), channel_id=1, source_target_pairs={{0,4},{4,0},{8,12},{12,8},{16,20},{20,16},{24,28},{28,24},{1,5},{5... | collective-permute-start | bytes 98312 | tf_op jit(solution)/shard_map/ppermute | solution.py:152
  18.8 3.5 %shard_map.87 = (f32[64,1280]{1,0:T(8,128)}, f32[1,1280]{1,0:T(1,128)}) custom-call(f32[72,1536]{1,0:T(8,128)S(1)} %convert_add_fusion.refs_0_, bf16[80,1280]{1,0:T(8,128)(2,1)S(1)} %get-tuple-element.52.refs_1_, bf16[80,1024]{1,0:T(8,128)(2,1)S(1)} %get-tuple-element.44.refs_2_, ...), custom_call_target="tpu_custom_call", output_to_operand_aliasing={{0}: (4, {}), {1}: (5, {})} | custom-call | flops 201326592 | bytes 1572864 | tf_op jit(solution)/shard_map/pallas_call | solution.py:186
  22.3 0.0 collective-permute-done.8
  22.4 0.0 collective-permute-done.7
  22.4 0.0 collective-permute-done.6
  22.5 2.7 %collective-permute-start.9 = (f16[72,256]{1,0:T(8,128)(2,1)S(1)}, f16[72,256]{1,0:T(8,128)(2,1)S(1)}, u32[]{:S(2)}, u32[]{:S(2)}) collective-permute-start(f16[72,256]{1,0:T(8,128)(2,1)S(1)} %pad_maximum_fusion), channel_id=1, source_target_pairs={{0,16},{4,20},{8,24},{12,28},{16,0},{20,4},{24,8},{28,12},{1,17},{... | collective-permute-start | bytes 110600 | tf_op jit(solution)/shard_map/ppermute | solution.py:152
  25.2 2.2 %collective-permute-done.9 = f16[72,256]{1,0:T(8,128)(2,1)S(1)} collective-permute-done((f16[72,256]{1,0:T(8,128)(2,1)S(1)}, f16[72,256]{1,0:T(8,128)(2,1)S(1)}, u32[]{:S(2)}, u32[]{:S(2)}) %collective-permute-start.9) | collective-permute-done | bytes 36896 | tf_op jit(solution)/shard_map/ppermute | solution.py:152
  27.4 0.7 %multiply_add_fusion = f32[64,256]{1,0:T(8,128)} fusion(f16[72,256]{1,0:T(8,128)(2,1)S(1)} %pad_maximum_fusion, f32[256]{0:T(256)S(1)} %bitcast.13, f16[72,256]{1,0:T(8,128)(2,1)S(1)} %collective-permute-done.9, f32[256]{0:T(256)S(1)} %bitcast.12), kind=kLoop, calls=%fused_computation.1 | loop fusion | flops 81920 | bytes 133120 | tf_op jit(solution)/shard_map/add | solution.py:223
  (9 shorter events, 0.1 us)
Async XLA Ops:
  0.6 5.1 %collective-permute-start = (bf16[64,256]{1,0:T(8,128)(2,1)}, bf16[64,256]{1,0:T(8,128)(2,1)S(1)}, u32[]{:S(2)}, u32[]{:S(2)}) collective-permute-start(bf16[64,256]{1,0:T(8,128)(2,1)} %param.7), channel_id=1, source_target_pairs={{0,2},{1,3},{2,0},{3,1},{4,6},{5,7},{6,4},{7,5},{8,10},{9,11},{10,... | collective-permute-start | bytes 98312 | tf_op jit(solution)/shard_map/ppermute | solution.py:152
  3.7 3.6 %collective-permute-start.2 = (bf16[64,256]{1,0:T(8,128)(2,1)}, bf16[64,256]{1,0:T(8,128)(2,1)S(1)}, u32[]{:S(2)}, u32[]{:S(2)}) collective-permute-start(bf16[64,256]{1,0:T(8,128)(2,1)} %param.7), channel_id=1, source_target_pairs={{0,3},{1,2},{2,1},{3,0},{4,7},{5,6},{6,5},{7,4},{8,11},{9,10},{10,... | collective-permute-start | bytes 98312 | tf_op jit(solution)/shard_map/ppermute | solution.py:152
  3.7 3.6 %collective-permute-start.1 = (bf16[64,256]{1,0:T(8,128)(2,1)}, bf16[64,256]{1,0:T(8,128)(2,1)S(1)}, u32[]{:S(2)}, u32[]{:S(2)}) collective-permute-start(bf16[64,256]{1,0:T(8,128)(2,1)} %param.7), channel_id=1, source_target_pairs={{0,1},{1,0},{2,3},{3,2},{4,5},{5,4},{6,7},{7,6},{8,9},{9,8},{10,11... | collective-permute-start | bytes 98312 | tf_op jit(solution)/shard_map/ppermute | solution.py:152
  10.7 4.5 %collective-permute-start.5 = (f32[64,256]{1,0:T(8,128)S(1)}, f32[64,256]{1,0:T(8,128)S(1)}, u32[]{:S(2)}, u32[]{:S(2)}) collective-permute-start(f32[64,256]{1,0:T(8,128)S(1)} %get-tuple-element.42), channel_id=1, source_target_pairs={{0,1},{1,0},{2,3},{3,2},{4,5},{5,4},{6,7},{7,6},{8,9},{9,8},{10,11... | collective-permute-start | bytes 196616 | tf_op jit(solution)/shard_map/ppermute | solution.py:152
  10.8 4.4 %collective-permute-start.3 = (bf16[64,256]{1,0:T(8,128)(2,1)S(1)}, bf16[64,256]{1,0:T(8,128)(2,1)S(1)}, u32[]{:S(2)}, u32[]{:S(2)}) collective-permute-start(bf16[64,256]{1,0:T(8,128)(2,1)S(1)} %get-tuple-element.40), channel_id=1, source_target_pairs={{0,2},{1,3},{2,0},{3,1},{4,6},{5,7},{6,4},{7,5},{8,10},{9,11},{10,... | collective-permute-start | bytes 98312 | tf_op jit(solution)/shard_map/ppermute | solution.py:152
  11.4 3.8 %collective-permute-start.4 = (bf16[64,256]{1,0:T(8,128)(2,1)S(1)}, bf16[64,256]{1,0:T(8,128)(2,1)S(1)}, u32[]{:S(2)}, u32[]{:S(2)}) collective-permute-start(bf16[64,256]{1,0:T(8,128)(2,1)S(1)} %get-tuple-element.41), channel_id=1, source_target_pairs={{0,3},{1,2},{2,1},{3,0},{4,7},{5,6},{6,5},{7,4},{8,11},{9,10},{10,... | collective-permute-start | bytes 98312 | tf_op jit(solution)/shard_map/ppermute | solution.py:152
  15.2 7.1 %collective-permute-start.8 = (bf16[64,256]{1,0:T(8,128)(2,1)S(1)}, bf16[64,256]{1,0:T(8,128)(2,1)S(1)}, u32[]{:S(2)}, u32[]{:S(2)}) collective-permute-start(bf16[64,256]{1,0:T(8,128)(2,1)S(1)} %get-tuple-element.51), channel_id=1, source_target_pairs={{0,12},{4,8},{8,4},{12,0},{16,28},{20,24},{24,20},{28,16},{1,13},{... | collective-permute-start | bytes 98312 | tf_op jit(solution)/shard_map/ppermute | solution.py:152
  17.9 4.5 %collective-permute-start.7 = (bf16[64,256]{1,0:T(8,128)(2,1)S(1)}, bf16[64,256]{1,0:T(8,128)(2,1)S(1)}, u32[]{:S(2)}, u32[]{:S(2)}) collective-permute-start(bf16[64,256]{1,0:T(8,128)(2,1)S(1)} %get-tuple-element.51), channel_id=1, source_target_pairs={{0,8},{4,12},{8,0},{12,4},{16,24},{20,28},{24,16},{28,20},{1,9},{5... | collective-permute-start | bytes 98312 | tf_op jit(solution)/shard_map/ppermute | solution.py:152
  18.3 4.0 %collective-permute-start.6 = (bf16[64,256]{1,0:T(8,128)(2,1)S(1)}, bf16[64,256]{1,0:T(8,128)(2,1)S(1)}, u32[]{:S(2)}, u32[]{:S(2)}) collective-permute-start(bf16[64,256]{1,0:T(8,128)(2,1)S(1)} %get-tuple-element.51), channel_id=1, source_target_pairs={{0,4},{4,0},{8,12},{12,8},{16,20},{20,16},{24,28},{28,24},{1,5},{5... | collective-permute-start | bytes 98312 | tf_op jit(solution)/shard_map/ppermute | solution.py:152
  22.5 4.9 %collective-permute-start.9 = (f16[72,256]{1,0:T(8,128)(2,1)S(1)}, f16[72,256]{1,0:T(8,128)(2,1)S(1)}, u32[]{:S(2)}, u32[]{:S(2)}) collective-permute-start(f16[72,256]{1,0:T(8,128)(2,1)S(1)} %pad_maximum_fusion), channel_id=1, source_target_pairs={{0,16},{4,20},{8,24},{12,28},{16,0},{20,4},{24,8},{28,12},{1,17},{... | collective-permute-start | bytes 110600 | tf_op jit(solution)/shard_map/ppermute | solution.py:152

commit v21 on v20

--- a/solution.py
+++ b/solution.py
@@ -36,6 +36,7 @@
     load_ext, shifted, whole, counts_ref, held, resid_low, grad_shift, counts_sem = refs[1 + 2 * parts :]
     me = lax.axis_index(axis)
     lats, total = grad_shift.shape
+    early = held.shape[0]
     neurons = counts_ref.shape[0]
     width = total // parts
     counts_copy = pltpu.make_async_copy(counts_hbm, counts_ref, counts_sem)
@@ -70,10 +71,12 @@
         for begin in range(0, total, step)
     ]
     for rows, span in blocks:
-        held[rows, span] = expected(load_ext[:, rows], shifted[:, span])
+        if rows.start < early:
+            held[rows, span] = expected(load_ext[:, rows], shifted[:, span])
     counts_copy.wait()
     for rows, span in blocks:
-        resid_low[rows, span] = (held[rows, span] - counts_ref[rows, span].astype(F32)).astype(BF16)
+        rate = held[rows, span] if rows.start < early else expected(load_ext[:, rows], shifted[:, span])
+        resid_low[rows, span] = (rate - counts_ref[rows, span].astype(F32)).astype(BF16)
     for begin in range(0, total, step):
         span = slice(begin, begin + step)
         grad_shift[:, span] = jnp.dot(load_ext[0:lats, :], resid_low[:, span], preferred_element_type=F32)
@@ -169,7 +172,7 @@
         scratch_shapes=[
             pltpu.VMEM((lats, total), BF16),
             pltpu.VMEM((neurons, total), BF16),
-            pltpu.VMEM((neurons, total), F32),
+            pltpu.VMEM((3 * chunk, total), F32),
             pltpu.VMEM((neurons, total), BF16),
             pltpu.VMEM((lats, total), F32),
             pltpu.SemaphoreType.DMA,

time: 28.3 us -> 27.8 us (0.982)
  Pallas kernels: 9.46 us -> 8.97 us
    pallas_call x1, Pallas kernels: 3.4 us -> 2.9 us  [per_device(): pl.pallas_call(functools.partial(shift_kernel, neuron_count, order, 'neur...]
where the time goes in v21:
time: 27.8 us; the launch traced here: 27.6 us
  starting transfers between devices  11.4 us (41%)
  Pallas kernels  8.97 us (32%)
  waiting for transfers between devices  3.92 us (14%)
  other arithmetic  1.86 us (7%)
  between operations  1.4 us (5%)
    ppermute x10, starting transfers between devices, swap(): return lax.ppermute(value, axis, [(i, i ^ mask) for i in range(count)])  11.4 us
    pallas_call x2, Pallas kernels, make(): pl.pallas_call(functools.partial(load_kernel, lats, first, chunk, step),...  6.07 us
    ppermute x10, waiting for transfers between devices, swap(): return lax.ppermute(value, axis, [(i, i ^ mask) for i in range(count)])  3.92 us
    pallas_call x1, Pallas kernels, per_device(): pl.pallas_call(functools.partial(shift_kernel, neuron_count, order, 'neur...  2.9 us
    add x1, other arithmetic, per_device(): pack = pack + jnp.pad(latents, ((0, 8), (neurons, 0))).astype(F32)  1.07 us
    add x1, other arithmetic, per_device(): value = value + read(arrived[0])  0.65 us
  transfers between devices with their start and end apart: 10, of which 3 were waited for; matrix products, arithmetic and copies ran while one was open for 4% of the time, Pallas kernels for 22%

profile of v21, /device:TPU:0, one launch (start us, length us, event | category | flops | bytes accessed | tf_op | source)
XLA Modules:
  0.0 27.6 jit_solution(9209400270731823503)
XLA Ops:
  0.6 3.0 %collective-permute-start = (bf16[64,256]{1,0:T(8,128)(2,1)}, bf16[64,256]{1,0:T(8,128)(2,1)S(1)}, u32[]{:S(2)}, u32[]{:S(2)}) collective-permute-start(bf16[64,256]{1,0:T(8,128)(2,1)} %param.7), channel_id=1, source_target_pairs={{0,2},{1,3},{2,0},{3,1},{4,6},{5,7},{6,4},{7,5},{8,10},{9,11},{10,... | collective-permute-start | bytes 98312 | tf_op jit(solution)/shard_map/ppermute | solution.py:155
  3.7 0.0 collective-permute-start.2
  3.7 0.2 collective-permute-start.1
  4.5 1.1 %convert_add_fusion.refs_0_ = f32[72,1536]{1,0:T(8,128)S(1)} fusion(s32[1,64]{1,0:T(1,128)} %param.10, f32[1,1280]{1,0:T(1,128)} %param.9, bf16[64,256]{1,0:T(8,128)(2,1)} %param.7, bf16[64,1280]{1,0:T(8,128)(2,1)} %bitcast.11, s32[]{:T(128)} %bitcast.6, pred[72]{0:T(512)(128)(4,1)S(1)} %iota_compare_fusion), kind=kLoop, calls=%fused_computation | loop fusion | flops 774144 | bytes 644428 | tf_op jit(solution)/shard_map/add | solution.py:164
  5.6 0.2 collective-permute-done.refs_2_
  5.8 1.5 %collective-permute-done.2.refs_4_ = bf16[64,256]{1,0:T(8,128)(2,1)S(1)} collective-permute-done((bf16[64,256]{1,0:T(8,128)(2,1)}, bf16[64,256]{1,0:T(8,128)(2,1)S(1)}, u32[]{:S(2)}, u32[]{:S(2)}) %collective-permute-start.2) | collective-permute-done | bytes 32800 | tf_op jit(solution)/shard_map/ppermute | solution.py:155
  7.3 0.0 collective-permute-done.1.refs_3_
  7.3 2.9 %shard_map.85 = (f32[64,256]{1,0:T(8,128)S(1)}, f32[64,256]{1,0:T(8,128)S(1)}, bf16[64,256]{1,0:T(8,128)(2,1)S(1)}, bf16[64,256]{1,0:T(8,128)(2,1)S(1)}, bf16[80...) custom-call(f32[72,1536]{1,0:T(8,128)S(1)} %convert_add_fusion.refs_0_, bf16[1280,1024]{1,0:T(8,128)(2,1)} %bitcast.7, ...), custom_call_target="tpu_custom_call" | custom-call | tf_op jit(solution)/shard_map/pallas_call | solution.py:166
  10.2 0.1 collective-permute-start.5
  10.3 0.7 %collective-permute-start.3 = (bf16[64,256]{1,0:T(8,128)(2,1)S(1)}, bf16[64,256]{1,0:T(8,128)(2,1)S(1)}, u32[]{:S(2)}, u32[]{:S(2)}) collective-permute-start(bf16[64,256]{1,0:T(8,128)(2,1)S(1)} %get-tuple-element.40), channel_id=1, source_target_pairs={{0,2},{1,3},{2,0},{3,1},{4,6},{5,7},{6,4},{7,5},{8,10},{9,11},{10,... | collective-permute-start | bytes 98312 | tf_op jit(solution)/shard_map/ppermute | solution.py:155
  10.9 1.2 %collective-permute-start.4 = (bf16[64,256]{1,0:T(8,128)(2,1)S(1)}, bf16[64,256]{1,0:T(8,128)(2,1)S(1)}, u32[]{:S(2)}, u32[]{:S(2)}) collective-permute-start(bf16[64,256]{1,0:T(8,128)(2,1)S(1)} %get-tuple-element.41), channel_id=1, source_target_pairs={{0,3},{1,2},{2,1},{3,0},{4,7},{5,6},{6,5},{7,4},{8,11},{9,10},{10,... | collective-permute-start | bytes 98312 | tf_op jit(solution)/shard_map/ppermute | solution.py:155
  12.1 2.5 %shard_map.86 = (f32[64,1280]{1,0:T(8,128)}, f32[1,1280]{1,0:T(1,128)}) custom-call(f32[72,1536]{1,0:T(8,128)S(1)} %convert_add_fusion.refs_0_, bf16[80,1280]{1,0:T(8,128)(2,1)S(1)} %get-tuple-element.52.refs_1_, bf16[80,1024]{1,0:T(8,128)(2,1)S(1)} %get-tuple-element.44.refs_2_, bf16[1280,1024]{1,0:T(8,128)(2,1)} %bitcast.8), custom_call_target="tpu_custom_call" | custom-call | flops 134217728 | bytes 1048576 | tf_op jit(solution)/shard_map/pallas_call | solution.py:189
  14.7 0.0 collective-permute-done.3
  14.7 0.0 collective-permute-done.4
  14.7 0.0 collective-permute-done.5
  14.8 2.6 %collective-permute-start.8 = (bf16[64,256]{1,0:T(8,128)(2,1)S(1)}, bf16[64,256]{1,0:T(8,128)(2,1)S(1)}, u32[]{:S(2)}, u32[]{:S(2)}) collective-permute-start(bf16[64,256]{1,0:T(8,128)(2,1)S(1)} %get-tuple-element.51), channel_id=1, source_target_pairs={{0,12},{4,8},{8,4},{12,0},{16,28},{20,24},{24,20},{28,16},{1,13},{... | collective-permute-start | bytes 98312 | tf_op jit(solution)/shard_map/ppermute | solution.py:155
  17.4 0.4 %collective-permute-start.7 = (bf16[64,256]{1,0:T(8,128)(2,1)S(1)}, bf16[64,256]{1,0:T(8,128)(2,1)S(1)}, u32[]{:S(2)}, u32[]{:S(2)}) collective-permute-start(bf16[64,256]{1,0:T(8,128)(2,1)S(1)} %get-tuple-element.51), channel_id=1, source_target_pairs={{0,8},{4,12},{8,0},{12,4},{16,24},{20,28},{24,16},{28,20},{1,9},{5... | collective-permute-start | bytes 98312 | tf_op jit(solution)/shard_map/ppermute | solution.py:155
  17.8 0.5 %collective-permute-start.6 = (bf16[64,256]{1,0:T(8,128)(2,1)S(1)}, bf16[64,256]{1,0:T(8,128)(2,1)S(1)}, u32[]{:S(2)}, u32[]{:S(2)}) collective-permute-start(bf16[64,256]{1,0:T(8,128)(2,1)S(1)} %get-tuple-element.51), channel_id=1, source_target_pairs={{0,4},{4,0},{8,12},{12,8},{16,20},{20,16},{24,28},{28,24},{1,5},{5... | collective-permute-start | bytes 98312 | tf_op jit(solution)/shard_map/ppermute | solution.py:155
  18.3 3.5 %shard_map.87 = (f32[64,1280]{1,0:T(8,128)}, f32[1,1280]{1,0:T(1,128)}) custom-call(f32[72,1536]{1,0:T(8,128)S(1)} %convert_add_fusion.refs_0_, bf16[80,1280]{1,0:T(8,128)(2,1)S(1)} %get-tuple-element.52.refs_1_, bf16[80,1024]{1,0:T(8,128)(2,1)S(1)} %get-tuple-element.44.refs_2_, ...), custom_call_target="tpu_custom_call", output_to_operand_aliasing={{0}: (4, {}), {1}: (5, {})} | custom-call | flops 201326592 | bytes 1572864 | tf_op jit(solution)/shard_map/pallas_call | solution.py:189
  21.8 0.0 collective-permute-done.8
  21.9 0.0 collective-permute-done.7
  21.9 0.0 collective-permute-done.6
  22.0 2.7 %collective-permute-start.9 = (f16[72,256]{1,0:T(8,128)(2,1)S(1)}, f16[72,256]{1,0:T(8,128)(2,1)S(1)}, u32[]{:S(2)}, u32[]{:S(2)}) collective-permute-start(f16[72,256]{1,0:T(8,128)(2,1)S(1)} %pad_maximum_fusion), channel_id=1, source_target_pairs={{0,16},{4,20},{8,24},{12,28},{16,0},{20,4},{24,8},{28,12},{1,17},{... | collective-permute-start | bytes 110600 | tf_op jit(solution)/shard_map/ppermute | solution.py:155
  24.7 2.2 %collective-permute-done.9 = f16[72,256]{1,0:T(8,128)(2,1)S(1)} collective-permute-done((f16[72,256]{1,0:T(8,128)(2,1)S(1)}, f16[72,256]{1,0:T(8,128)(2,1)S(1)}, u32[]{:S(2)}, u32[]{:S(2)}) %collective-permute-start.9) | collective-permute-done | bytes 36896 | tf_op jit(solution)/shard_map/ppermute | solution.py:155
  26.9 0.7 %multiply_add_fusion = f32[64,256]{1,0:T(8,128)} fusion(f16[72,256]{1,0:T(8,128)(2,1)S(1)} %pad_maximum_fusion, f32[256]{0:T(256)S(1)} %bitcast.13, f16[72,256]{1,0:T(8,128)(2,1)S(1)} %collective-permute-done.9, f32[256]{0:T(256)S(1)} %bitcast.12), kind=kLoop, calls=%fused_computation.1 | loop fusion | flops 81920 | bytes 133120 | tf_op jit(solution)/shard_map/add | solution.py:226
  (9 shorter events, 0.1 us)
Async XLA Ops:
  0.6 5.1 %collective-permute-start = (bf16[64,256]{1,0:T(8,128)(2,1)}, bf16[64,256]{1,0:T(8,128)(2,1)S(1)}, u32[]{:S(2)}, u32[]{:S(2)}) collective-permute-start(bf16[64,256]{1,0:T(8,128)(2,1)} %param.7), channel_id=1, source_target_pairs={{0,2},{1,3},{2,0},{3,1},{4,6},{5,7},{6,4},{7,5},{8,10},{9,11},{10,... | collective-permute-start | bytes 98312 | tf_op jit(solution)/shard_map/ppermute | solution.py:155
  3.7 3.6 %collective-permute-start.2 = (bf16[64,256]{1,0:T(8,128)(2,1)}, bf16[64,256]{1,0:T(8,128)(2,1)S(1)}, u32[]{:S(2)}, u32[]{:S(2)}) collective-permute-start(bf16[64,256]{1,0:T(8,128)(2,1)} %param.7), channel_id=1, source_target_pairs={{0,3},{1,2},{2,1},{3,0},{4,7},{5,6},{6,5},{7,4},{8,11},{9,10},{10,... | collective-permute-start | bytes 98312 | tf_op jit(solution)/shard_map/ppermute | solution.py:155
  3.7 3.6 %collective-permute-start.1 = (bf16[64,256]{1,0:T(8,128)(2,1)}, bf16[64,256]{1,0:T(8,128)(2,1)S(1)}, u32[]{:S(2)}, u32[]{:S(2)}) collective-permute-start(bf16[64,256]{1,0:T(8,128)(2,1)} %param.7), channel_id=1, source_target_pairs={{0,1},{1,0},{2,3},{3,2},{4,5},{5,4},{6,7},{7,6},{8,9},{9,8},{10,11... | collective-permute-start | bytes 98312 | tf_op jit(solution)/shard_map/ppermute | solution.py:155
  10.2 4.5 %collective-permute-start.5 = (f32[64,256]{1,0:T(8,128)S(1)}, f32[64,256]{1,0:T(8,128)S(1)}, u32[]{:S(2)}, u32[]{:S(2)}) collective-permute-start(f32[64,256]{1,0:T(8,128)S(1)} %get-tuple-element.42), channel_id=1, source_target_pairs={{0,1},{1,0},{2,3},{3,2},{4,5},{5,4},{6,7},{7,6},{8,9},{9,8},{10,11... | collective-permute-start | bytes 196616 | tf_op jit(solution)/shard_map/ppermute | solution.py:155
  10.3 4.4 %collective-permute-start.3 = (bf16[64,256]{1,0:T(8,128)(2,1)S(1)}, bf16[64,256]{1,0:T(8,128)(2,1)S(1)}, u32[]{:S(2)}, u32[]{:S(2)}) collective-permute-start(bf16[64,256]{1,0:T(8,128)(2,1)S(1)} %get-tuple-element.40), channel_id=1, source_target_pairs={{0,2},{1,3},{2,0},{3,1},{4,6},{5,7},{6,4},{7,5},{8,10},{9,11},{10,... | collective-permute-start | bytes 98312 | tf_op jit(solution)/shard_map/ppermute | solution.py:155
  10.9 3.8 %collective-permute-start.4 = (bf16[64,256]{1,0:T(8,128)(2,1)S(1)}, bf16[64,256]{1,0:T(8,128)(2,1)S(1)}, u32[]{:S(2)}, u32[]{:S(2)}) collective-permute-start(bf16[64,256]{1,0:T(8,128)(2,1)S(1)} %get-tuple-element.41), channel_id=1, source_target_pairs={{0,3},{1,2},{2,1},{3,0},{4,7},{5,6},{6,5},{7,4},{8,11},{9,10},{10,... | collective-permute-start | bytes 98312 | tf_op jit(solution)/shard_map/ppermute | solution.py:155
  14.8 7.1 %collective-permute-start.8 = (bf16[64,256]{1,0:T(8,128)(2,1)S(1)}, bf16[64,256]{1,0:T(8,128)(2,1)S(1)}, u32[]{:S(2)}, u32[]{:S(2)}) collective-permute-start(bf16[64,256]{1,0:T(8,128)(2,1)S(1)} %get-tuple-element.51), channel_id=1, source_target_pairs={{0,12},{4,8},{8,4},{12,0},{16,28},{20,24},{24,20},{28,16},{1,13},{... | collective-permute-start | bytes 98312 | tf_op jit(solution)/shard_map/ppermute | solution.py:155
  17.4 4.5 %collective-permute-start.7 = (bf16[64,256]{1,0:T(8,128)(2,1)S(1)}, bf16[64,256]{1,0:T(8,128)(2,1)S(1)}, u32[]{:S(2)}, u32[]{:S(2)}) collective-permute-start(bf16[64,256]{1,0:T(8,128)(2,1)S(1)} %get-tuple-element.51), channel_id=1, source_target_pairs={{0,8},{4,12},{8,0},{12,4},{16,24},{20,28},{24,16},{28,20},{1,9},{5... | collective-permute-start | bytes 98312 | tf_op jit(solution)/shard_map/ppermute | solution.py:155
  17.8 4.0 %collective-permute-start.6 = (bf16[64,256]{1,0:T(8,128)(2,1)S(1)}, bf16[64,256]{1,0:T(8,128)(2,1)S(1)}, u32[]{:S(2)}, u32[]{:S(2)}) collective-permute-start(bf16[64,256]{1,0:T(8,128)(2,1)S(1)} %get-tuple-element.51), channel_id=1, source_target_pairs={{0,4},{4,0},{8,12},{12,8},{16,20},{20,16},{24,28},{28,24},{1,5},{5... | collective-permute-start | bytes 98312 | tf_op jit(solution)/shard_map/ppermute | solution.py:155
  22.0 4.9 %collective-permute-start.9 = (f16[72,256]{1,0:T(8,128)(2,1)S(1)}, f16[72,256]{1,0:T(8,128)(2,1)S(1)}, u32[]{:S(2)}, u32[]{:S(2)}) collective-permute-start(f16[72,256]{1,0:T(8,128)(2,1)S(1)} %pad_maximum_fusion), channel_id=1, source_target_pairs={{0,16},{4,20},{8,24},{12,28},{16,0},{20,4},{24,8},{28,12},{1,17},{... | collective-permute-start | bytes 110600 | tf_op jit(solution)/shard_map/ppermute | solution.py:155

commit v22 on v16

--- a/solution.py
+++ b/solution.py
@@ -165,7 +165,7 @@
 
     *outs, load_ext, shifted = pl.pallas_call(
         functools.partial(shift_kernel, neuron_count, order, "neuron", chunk, step),
-        out_shape=[jax.ShapeDtypeStruct((lats, width), BF16 if k > 1 else F32) for k in range(neuron_count)]
+        out_shape=[jax.ShapeDtypeStruct((lats, width), BF16)] * neuron_count
         + [jax.ShapeDtypeStruct((lats + EXTRA, neurons), BF16), jax.ShapeDtypeStruct((lats + EXTRA, total), BF16)],
         in_specs=[vmem, hbm] + [vmem] * (neuron_count - 1),
         out_specs=[vmem] * (neuron_count + 2),
@@ -180,7 +180,7 @@
         compiler_params=params,
     )(pack, counts[0], *arrived)
 
-    shares = [(0, 2 * chunk), (2 * chunk, neurons - 2 * chunk)]
+    shares = [(0, 3 * chunk), (3 * chunk, neurons - 3 * chunk)]
     made = []
 
     def make(before):
@@ -206,11 +206,24 @@
         )(pack, start_load, shifted, counts[0], *made)
         return before, out
 
+    near = min(2, region_count)
     outs, made = make(outs)
-    arrived = [swap(outs[k], "neuron", neuron_count, k) for k in [*range(2, neuron_count), 1]]
+    arrived = {(0, 0): outs[0]}
+    for flip, k in [(f, k) for f in range(near) for k in range(neuron_count)][1:]:
+        pairs = [
+            (r * neuron_count + n, (r ^ flip) * neuron_count + (n ^ k))
+            for r in range(region_count)
+            for n in range(neuron_count)
+        ]
+        arrived[flip, k] = lax.ppermute(outs[k], ("region", "neuron"), pairs)
     arrived, made = lax.optimization_barrier((arrived, made))
-    value = functools.reduce(jnp.add, [outs[0]] + [block.astype(F32) for block in arrived])
-    mask = 1
+    pair_sums = [
+        functools.reduce(jnp.add, [arrived[flip, k].astype(F32) for flip in range(near)])
+        for k in range(neuron_count - 1, -1, -1)
+    ]
+    value = functools.reduce(jnp.add, pair_sums)
+
+    mask = near
     while mask < region_count:
         masks = [mask, 2 * mask, 3 * mask] if 2 * mask < region_count else [mask]
         code = lax.optimization_barrier(encode(value))

time: 27.8 us -> 29.7 us (1.068)
  starting transfers between devices: 11.4 us -> 14.6 us
  waiting for transfers between devices: 3.92 us -> 3.24 us
  Pallas kernels: 8.82 us -> 8.35 us
    ppermute x0 -> x7, starting transfers between devices: none -> 6.96 us  [per_device(): arrived[flip, k] = lax.ppermute(outs[k], ('region', 'neuron'), pairs)]
    ppermute x10 -> x6, starting transfers between devices: 11.4 us -> 7.68 us  [swap(): return lax.ppermute(value, axis, [(i, i ^ mask) for i in range(count)])]
    ppermute x10 -> x6, waiting for transfers between devices: 3.92 us -> 3.22 us  [swap(): return lax.ppermute(value, axis, [(i, i ^ mask) for i in range(count)])]
    pallas_call x2, Pallas kernels: 6.07 us -> 5.6 us  [make(): pl.pallas_call(functools.partial(load_kernel, lats, first, chunk, step),...]
  transfers between devices with their start and end apart: 10 -> 13, of which waited for: 3 -> 3; matrix products, arithmetic and copies ran while one was open for 4% -> 4% of each run, Pallas kernels for 22% -> 19%
where the time goes in v22:
time: 29.7 us; the launch traced here: 29.5 us
  starting transfers between devices  14.6 us (49%)
  Pallas kernels  8.35 us (28%)
  waiting for transfers between devices  3.24 us (11%)
  other arithmetic  1.87 us (6%)
  between operations  1.4 us (5%)
    ppermute x6, starting transfers between devices, swap(): return lax.ppermute(value, axis, [(i, i ^ mask) for i in range(count)])  7.68 us
    ppermute x7, starting transfers between devices, per_device(): arrived[flip, k] = lax.ppermute(outs[k], ('region', 'neuron'), pairs)  6.96 us
    pallas_call x2, Pallas kernels, make(): pl.pallas_call(functools.partial(load_kernel, lats, first, chunk, step),...  5.6 us
    ppermute x6, waiting for transfers between devices, swap(): return lax.ppermute(value, axis, [(i, i ^ mask) for i in range(count)])  3.22 us
    pallas_call x1, Pallas kernels, per_device(): pl.pallas_call(functools.partial(shift_kernel, neuron_count, order, 'neur...  2.75 us
    add x1, other arithmetic, per_device(): pack = pack + jnp.pad(latents, ((0, 8), (neurons, 0))).astype(F32)  1.07 us
    add x1, other arithmetic, per_device(): value = value + (decode(arrived[1]) + decode(arrived[2]))  0.66 us
  transfers between devices with their start and end apart: 13, of which 3 were waited for; matrix products, arithmetic and copies ran while one was open for 4% of the time, Pallas kernels for 19%

profile of v22, /device:TPU:0, one launch (start us, length us, event | category | flops | bytes accessed | tf_op | source)
XLA Modules:
  0.0 29.5 jit_solution(5444670400465849348)
XLA Ops:
  0.6 3.0 %collective-permute-start = (bf16[64,256]{1,0:T(8,128)(2,1)}, bf16[64,256]{1,0:T(8,128)(2,1)S(1)}, u32[]{:S(2)}, u32[]{:S(2)}) collective-permute-start(bf16[64,256]{1,0:T(8,128)(2,1)} %param.7), channel_id=1, source_target_pairs={{0,2},{1,3},{2,0},{3,1},{4,6},{5,7},{6,4},{7,5},{8,10},{9,11},{10,... | collective-permute-start | bytes 98312 | tf_op jit(solution)/shard_map/ppermute | solution.py:155
  3.7 0.0 collective-permute-start.2
  3.7 0.2 collective-permute-start.1
  4.5 1.1 %convert_add_fusion.refs_0_ = f32[72,1536]{1,0:T(8,128)S(1)} fusion(s32[1,64]{1,0:T(1,128)} %param.10, f32[1,1280]{1,0:T(1,128)} %param.9, bf16[64,256]{1,0:T(8,128)(2,1)} %param.7, bf16[64,1280]{1,0:T(8,128)(2,1)} %bitcast.13, s32[]{:T(128)} %bitcast.8, pred[72]{0:T(512)(128)(4,1)S(1)} %iota_compare_fusion), kind=kLoop, calls=%fused_computation | loop fusion | flops 774144 | bytes 644428 | tf_op jit(solution)/shard_map/add | solution.py:164
  5.6 0.2 collective-permute-done.refs_2_
  5.8 1.5 %collective-permute-done.2.refs_4_ = bf16[64,256]{1,0:T(8,128)(2,1)S(1)} collective-permute-done((bf16[64,256]{1,0:T(8,128)(2,1)}, bf16[64,256]{1,0:T(8,128)(2,1)S(1)}, u32[]{:S(2)}, u32[]{:S(2)}) %collective-permute-start.2) | collective-permute-done | bytes 32800 | tf_op jit(solution)/shard_map/ppermute | solution.py:155
  7.3 0.0 collective-permute-done.1.refs_3_
  7.3 2.8 %shard_map.85 = (bf16[64,256]{1,0:T(8,128)(2,1)S(1)}, bf16[64,256]{1,0:T(8,128)(2,1)S(1)}, bf16[64,256]{1,0:T(8,128)(2,1)S(1)}, bf16[64,256]{1,0:T(8,128)(2,1)S(...) custom-call(f32[72,1536]{1,0:T(8,128)S(1)} %convert_add_fusion.refs_0_, bf16[1280,1024]{1,0:T(8,128)(2,1)} %bitcast.9, ...), custom_call_target="tpu_custom_call" | custom-call | tf_op jit(solution)/shard_map/pallas_call | solution.py:166
  10.1 1.6 %collective-permute-start.6 = (bf16[64,256]{1,0:T(8,128)(2,1)S(1)}, bf16[64,256]{1,0:T(8,128)(2,1)S(1)}, u32[]{:S(2)}, u32[]{:S(2)}) collective-permute-start(bf16[64,256]{1,0:T(8,128)(2,1)S(1)} %get-tuple-element.54), channel_id=1, source_target_pairs={{0,4},{1,5},{2,6},{3,7},{4,0},{5,1},{6,2},{7,3},{8,12},{9,13},{10,... | collective-permute-start | bytes 98312 | tf_op jit(solution)/shard_map/ppermute | solution.py:218
  11.6 0.0 collective-permute-start.7
  11.6 0.7 %collective-permute-start.3 = (bf16[64,256]{1,0:T(8,128)(2,1)S(1)}, bf16[64,256]{1,0:T(8,128)(2,1)S(1)}, u32[]{:S(2)}, u32[]{:S(2)}) collective-permute-start(bf16[64,256]{1,0:T(8,128)(2,1)S(1)} %get-tuple-element.41), channel_id=1, source_target_pairs={{0,1},{1,0},{2,3},{3,2},{4,5},{5,4},{6,7},{7,6},{8,9},{9,8},{10,11... | collective-permute-start | bytes 98312 | tf_op jit(solution)/shard_map/ppermute | solution.py:218
  12.3 1.7 %collective-permute-start.8 = (bf16[64,256]{1,0:T(8,128)(2,1)S(1)}, bf16[64,256]{1,0:T(8,128)(2,1)S(1)}, u32[]{:S(2)}, u32[]{:S(2)}) collective-permute-start(bf16[64,256]{1,0:T(8,128)(2,1)S(1)} %get-tuple-element.42), channel_id=1, source_target_pairs={{0,6},{1,7},{2,4},{3,5},{4,2},{5,3},{6,0},{7,1},{8,14},{9,15},{10,... | collective-permute-start | bytes 98312 | tf_op jit(solution)/shard_map/ppermute | solution.py:218
  14.0 1.2 %collective-permute-start.4 = (bf16[64,256]{1,0:T(8,128)(2,1)S(1)}, bf16[64,256]{1,0:T(8,128)(2,1)S(1)}, u32[]{:S(2)}, u32[]{:S(2)}) collective-permute-start(bf16[64,256]{1,0:T(8,128)(2,1)S(1)} %get-tuple-element.42), channel_id=1, source_target_pairs={{0,2},{1,3},{2,0},{3,1},{4,6},{5,7},{6,4},{7,5},{8,10},{9,11},{10,... | collective-permute-start | bytes 98312 | tf_op jit(solution)/shard_map/ppermute | solution.py:218
  15.2 0.0 collective-permute-done.6
  15.2 0.0 collective-permute-start.9
  15.2 0.0 collective-permute-done.7
  15.2 1.8 %collective-permute-start.5 = (bf16[64,256]{1,0:T(8,128)(2,1)S(1)}, bf16[64,256]{1,0:T(8,128)(2,1)S(1)}, u32[]{:S(2)}, u32[]{:S(2)}) collective-permute-start(bf16[64,256]{1,0:T(8,128)(2,1)S(1)} %get-tuple-element.43), channel_id=1, source_target_pairs={{0,3},{1,2},{2,1},{3,0},{4,7},{5,6},{6,5},{7,4},{8,11},{9,10},{10,... | collective-permute-start | bytes 98312 | tf_op jit(solution)/shard_map/ppermute | solution.py:218
  17.0 3.1 %shard_map.86 = (f32[64,1280]{1,0:T(8,128)}, f32[1,1280]{1,0:T(1,128)}) custom-call(f32[72,1536]{1,0:T(8,128)S(1)} %convert_add_fusion.refs_0_, bf16[80,1280]{1,0:T(8,128)(2,1)S(1)} %get-tuple-element.57.refs_1_, bf16[80,1024]{1,0:T(8,128)(2,1)S(1)} %get-tuple-element.45.refs_2_, bf16[1280,1024]{1,0:T(8,128)(2,1)} %bitcast.10), custom_call_target="tpu_custom_call" | custom-call | flops 201326592 | bytes 1572864 | tf_op jit(solution)/shard_map/pallas_call | solution.py:189
  20.1 0.0 collective-permute-done.3
  20.1 0.0 collective-permute-done.8
  20.1 0.0 collective-permute-done.4
  20.1 0.0 collective-permute-done.9
  20.1 0.0 collective-permute-done.5
  20.2 0.1 abs_reduce_fusion
  20.3 3.7 %collective-permute-start.12 = (f16[72,256]{1,0:T(8,128)(2,1)S(1)}, f16[72,256]{1,0:T(8,128)(2,1)S(1)}, u32[]{:S(2)}, u32[]{:S(2)}) collective-permute-start(f16[72,256]{1,0:T(8,128)(2,1)S(1)} %pad_maximum_fusion), channel_id=1, source_target_pairs={{0,24},{4,28},{8,16},{12,20},{16,8},{20,12},{24,0},{28,4},{1,25},{... | collective-permute-start | bytes 110600 | tf_op jit(solution)/shard_map/ppermute | solution.py:155
  23.9 0.0 collective-permute-start.11
  24.0 0.8 %collective-permute-start.10 = (f16[72,256]{1,0:T(8,128)(2,1)S(1)}, f16[72,256]{1,0:T(8,128)(2,1)S(1)}, u32[]{:S(2)}, u32[]{:S(2)}) collective-permute-start(f16[72,256]{1,0:T(8,128)(2,1)S(1)} %pad_maximum_fusion), channel_id=1, source_target_pairs={{0,8},{4,12},{8,0},{12,4},{16,24},{20,28},{24,16},{28,20},{1,9},{5... | collective-permute-start | bytes 110600 | tf_op jit(solution)/shard_map/ppermute | solution.py:155
  24.7 2.5 %shard_map.87 = (f32[64,1280]{1,0:T(8,128)}, f32[1,1280]{1,0:T(1,128)}) custom-call(f32[72,1536]{1,0:T(8,128)S(1)} %convert_add_fusion.refs_0_, bf16[80,1280]{1,0:T(8,128)(2,1)S(1)} %get-tuple-element.57.refs_1_, bf16[80,1024]{1,0:T(8,128)(2,1)S(1)} %get-tuple-element.45.refs_2_, ...), custom_call_target="tpu_custom_call", output_to_operand_aliasing={{0}: (4, {}), {1}: (5, {})} | custom-call | flops 134217728 | bytes 1048576 | tf_op jit(solution)/shard_map/pallas_call | solution.py:189
  27.3 0.0 collective-permute-done.12
  27.3 1.5 %collective-permute-done.11 = f16[72,256]{1,0:T(8,128)(2,1)S(1)} collective-permute-done((f16[72,256]{1,0:T(8,128)(2,1)S(1)}, f16[72,256]{1,0:T(8,128)(2,1)S(1)}, u32[]{:S(2)}, u32[]{:S(2)}) %collective-permute-start.11) | collective-permute-done | bytes 36896 | tf_op jit(solution)/shard_map/ppermute | solution.py:155
  28.8 0.0 collective-permute-done.10
  28.8 0.7 %add_add_fusion = f32[64,256]{1,0:T(8,128)} fusion(f32[256]{0:T(256)S(1)} %bitcast.16, f16[72,256]{1,0:T(8,128)(2,1)S(1)} %collective-permute-done.12, f32[256]{0:T(256)S(1)} %bitcast.17, f16[72,256]{1,0:T(8,128)(2,1)S(1)} %collective-permute-done.11, f32[256]{0:T(256)S(1)} %bitcast.15, f16[72,256]{1,0:T(8,128)(2,1)S(1)} %collective-permute-done.10, ...), kind=kLoop, calls=%fused_computation.1 | loop fusion | flops 180224 | bytes 200704 | tf_op jit(solution)/shard_map/add | solution.py:236
  (8 shorter events, 0.1 us)
Async XLA Ops:
  0.6 5.1 %collective-permute-start = (bf16[64,256]{1,0:T(8,128)(2,1)}, bf16[64,256]{1,0:T(8,128)(2,1)S(1)}, u32[]{:S(2)}, u32[]{:S(2)}) collective-permute-start(bf16[64,256]{1,0:T(8,128)(2,1)} %param.7), channel_id=1, source_target_pairs={{0,2},{1,3},{2,0},{3,1},{4,6},{5,7},{6,4},{7,5},{8,10},{9,11},{10,... | collective-permute-start | bytes 98312 | tf_op jit(solution)/shard_map/ppermute | solution.py:155
  3.7 3.6 %collective-permute-start.2 = (bf16[64,256]{1,0:T(8,128)(2,1)}, bf16[64,256]{1,0:T(8,128)(2,1)S(1)}, u32[]{:S(2)}, u32[]{:S(2)}) collective-permute-start(bf16[64,256]{1,0:T(8,128)(2,1)} %param.7), channel_id=1, source_target_pairs={{0,3},{1,2},{2,1},{3,0},{4,7},{5,6},{6,5},{7,4},{8,11},{9,10},{10,... | collective-permute-start | bytes 98312 | tf_op jit(solution)/shard_map/ppermute | solution.py:155
  3.7 3.6 %collective-permute-start.1 = (bf16[64,256]{1,0:T(8,128)(2,1)}, bf16[64,256]{1,0:T(8,128)(2,1)S(1)}, u32[]{:S(2)}, u32[]{:S(2)}) collective-permute-start(bf16[64,256]{1,0:T(8,128)(2,1)} %param.7), channel_id=1, source_target_pairs={{0,1},{1,0},{2,3},{3,2},{4,5},{5,4},{6,7},{7,6},{8,9},{9,8},{10,11... | collective-permute-start | bytes 98312 | tf_op jit(solution)/shard_map/ppermute | solution.py:155
  10.1 5.2 %collective-permute-start.6 = (bf16[64,256]{1,0:T(8,128)(2,1)S(1)}, bf16[64,256]{1,0:T(8,128)(2,1)S(1)}, u32[]{:S(2)}, u32[]{:S(2)}) collective-permute-start(bf16[64,256]{1,0:T(8,128)(2,1)S(1)} %get-tuple-element.54), channel_id=1, source_target_pairs={{0,4},{1,5},{2,6},{3,7},{4,0},{5,1},{6,2},{7,3},{8,12},{9,13},{10,... | collective-permute-start | bytes 98312 | tf_op jit(solution)/shard_map/ppermute | solution.py:218
  11.6 3.6 %collective-permute-start.7 = (bf16[64,256]{1,0:T(8,128)(2,1)S(1)}, bf16[64,256]{1,0:T(8,128)(2,1)S(1)}, u32[]{:S(2)}, u32[]{:S(2)}) collective-permute-start(bf16[64,256]{1,0:T(8,128)(2,1)S(1)} %get-tuple-element.41), channel_id=1, source_target_pairs={{0,5},{1,4},{2,7},{3,6},{4,1},{5,0},{6,3},{7,2},{8,13},{9,12},{10,... | collective-permute-start | bytes 98312 | tf_op jit(solution)/shard_map/ppermute | solution.py:218
  11.6 8.5 %collective-permute-start.3 = (bf16[64,256]{1,0:T(8,128)(2,1)S(1)}, bf16[64,256]{1,0:T(8,128)(2,1)S(1)}, u32[]{:S(2)}, u32[]{:S(2)}) collective-permute-start(bf16[64,256]{1,0:T(8,128)(2,1)S(1)} %get-tuple-element.41), channel_id=1, source_target_pairs={{0,1},{1,0},{2,3},{3,2},{4,5},{5,4},{6,7},{7,6},{8,9},{9,8},{10,11... | collective-permute-start | bytes 98312 | tf_op jit(solution)/shard_map/ppermute | solution.py:218
  12.3 7.8 %collective-permute-start.8 = (bf16[64,256]{1,0:T(8,128)(2,1)S(1)}, bf16[64,256]{1,0:T(8,128)(2,1)S(1)}, u32[]{:S(2)}, u32[]{:S(2)}) collective-permute-start(bf16[64,256]{1,0:T(8,128)(2,1)S(1)} %get-tuple-element.42), channel_id=1, source_target_pairs={{0,6},{1,7},{2,4},{3,5},{4,2},{5,3},{6,0},{7,1},{8,14},{9,15},{10,... | collective-permute-start | bytes 98312 | tf_op jit(solution)/shard_map/ppermute | solution.py:218
  14.0 6.2 %collective-permute-start.4 = (bf16[64,256]{1,0:T(8,128)(2,1)S(1)}, bf16[64,256]{1,0:T(8,128)(2,1)S(1)}, u32[]{:S(2)}, u32[]{:S(2)}) collective-permute-start(bf16[64,256]{1,0:T(8,128)(2,1)S(1)} %get-tuple-element.42), channel_id=1, source_target_pairs={{0,2},{1,3},{2,0},{3,1},{4,6},{5,7},{6,4},{7,5},{8,10},{9,11},{10,... | collective-permute-start | bytes 98312 | tf_op jit(solution)/shard_map/ppermute | solution.py:218
  15.2 4.9 %collective-permute-start.9 = (bf16[64,256]{1,0:T(8,128)(2,1)S(1)}, bf16[64,256]{1,0:T(8,128)(2,1)S(1)}, u32[]{:S(2)}, u32[]{:S(2)}) collective-permute-start(bf16[64,256]{1,0:T(8,128)(2,1)S(1)} %get-tuple-element.43), channel_id=1, source_target_pairs={{0,7},{1,6},{2,5},{3,4},{4,3},{5,2},{6,1},{7,0},{8,15},{9,14},{10,... | collective-permute-start | bytes 98312 | tf_op jit(solution)/shard_map/ppermute | solution.py:218
  15.2 4.9 %collective-permute-start.5 = (bf16[64,256]{1,0:T(8,128)(2,1)S(1)}, bf16[64,256]{1,0:T(8,128)(2,1)S(1)}, u32[]{:S(2)}, u32[]{:S(2)}) collective-permute-start(bf16[64,256]{1,0:T(8,128)(2,1)S(1)} %get-tuple-element.43), channel_id=1, source_target_pairs={{0,3},{1,2},{2,1},{3,0},{4,7},{5,6},{6,5},{7,4},{8,11},{9,10},{10,... | collective-permute-start | bytes 98312 | tf_op jit(solution)/shard_map/ppermute | solution.py:218
  20.3 7.0 %collective-permute-start.12 = (f16[72,256]{1,0:T(8,128)(2,1)S(1)}, f16[72,256]{1,0:T(8,128)(2,1)S(1)}, u32[]{:S(2)}, u32[]{:S(2)}) collective-permute-start(f16[72,256]{1,0:T(8,128)(2,1)S(1)} %pad_maximum_fusion), channel_id=1, source_target_pairs={{0,24},{4,28},{8,16},{12,20},{16,8},{20,12},{24,0},{28,4},{1,25},{... | collective-permute-start | bytes 110600 | tf_op jit(solution)/shard_map/ppermute | solution.py:155
  23.9 4.9 %collective-permute-start.11 = (f16[72,256]{1,0:T(8,128)(2,1)S(1)}, f16[72,256]{1,0:T(8,128)(2,1)S(1)}, u32[]{:S(2)}, u32[]{:S(2)}) collective-permute-start(f16[72,256]{1,0:T(8,128)(2,1)S(1)} %pad_maximum_fusion), channel_id=1, source_target_pairs={{0,16},{4,20},{8,24},{12,28},{16,0},{20,4},{24,8},{28,12},{1,17},{... | collective-permute-start | bytes 110600 | tf_op jit(solution)/shard_map/ppermute | solution.py:155
  24.0 4.9 %collective-permute-start.10 = (f16[72,256]{1,0:T(8,128)(2,1)S(1)}, f16[72,256]{1,0:T(8,128)(2,1)S(1)}, u32[]{:S(2)}, u32[]{:S(2)}) collective-permute-start(f16[72,256]{1,0:T(8,128)(2,1)S(1)} %pad_maximum_fusion), channel_id=1, source_target_pairs={{0,8},{4,12},{8,0},{12,4},{16,24},{20,28},{24,16},{28,20},{1,9},{5... | collective-permute-start | bytes 110600 | tf_op jit(solution)/shard_map/ppermute | solution.py:155

commit v23 on v21

--- a/solution.py
+++ b/solution.py
@@ -172,7 +172,7 @@
         scratch_shapes=[
             pltpu.VMEM((lats, total), BF16),
             pltpu.VMEM((neurons, total), BF16),
-            pltpu.VMEM((3 * chunk, total), F32),
+            pltpu.VMEM((4 * chunk, total), F32),
             pltpu.VMEM((neurons, total), BF16),
             pltpu.VMEM((lats, total), F32),
             pltpu.SemaphoreType.DMA,

time: 27.8 us -> 27.7 us (level)
  no operation moved by 1% of the time
where the time goes in v23:
time: 27.7 us; the launch traced here: 27.4 us
  starting transfers between devices  11.4 us (41%)
  Pallas kernels  8.81 us (32%)
  waiting for transfers between devices  3.92 us (14%)
  other arithmetic  1.86 us (7%)
  between operations  1.4 us (5%)
    ppermute x10, starting transfers between devices, swap(): return lax.ppermute(value, axis, [(i, i ^ mask) for i in range(count)])  11.4 us
    pallas_call x2, Pallas kernels, make(): pl.pallas_call(functools.partial(load_kernel, lats, first, chunk, step),...  6.06 us
    ppermute x10, waiting for transfers between devices, swap(): return lax.ppermute(value, axis, [(i, i ^ mask) for i in range(count)])  3.92 us
    pallas_call x1, Pallas kernels, per_device(): pl.pallas_call(functools.partial(shift_kernel, neuron_count, order, 'neur...  2.75 us
    add x1, other arithmetic, per_device(): pack = pack + jnp.pad(latents, ((0, 8), (neurons, 0))).astype(F32)  1.07 us
    add x1, other arithmetic, per_device(): value = value + read(arrived[0])  0.65 us
  transfers between devices with their start and end apart: 10, of which 3 were waited for; matrix products, arithmetic and copies ran while one was open for 4% of the time, Pallas kernels for 22%

profile of v23, /device:TPU:0, one launch (start us, length us, event | category | flops | bytes accessed | tf_op | source)
XLA Modules:
  0.0 27.4 jit_solution(1609250107383193752)
XLA Ops:
  0.6 3.0 %collective-permute-start = (bf16[64,256]{1,0:T(8,128)(2,1)}, bf16[64,256]{1,0:T(8,128)(2,1)S(1)}, u32[]{:S(2)}, u32[]{:S(2)}) collective-permute-start(bf16[64,256]{1,0:T(8,128)(2,1)} %param.7), channel_id=1, source_target_pairs={{0,2},{1,3},{2,0},{3,1},{4,6},{5,7},{6,4},{7,5},{8,10},{9,11},{10,... | collective-permute-start | bytes 98312 | tf_op jit(solution)/shard_map/ppermute | solution.py:155
  3.7 0.0 collective-permute-start.2
  3.7 0.2 collective-permute-start.1
  4.5 1.1 %convert_add_fusion.refs_0_ = f32[72,1536]{1,0:T(8,128)S(1)} fusion(s32[1,64]{1,0:T(1,128)} %param.10, f32[1,1280]{1,0:T(1,128)} %param.9, bf16[64,256]{1,0:T(8,128)(2,1)} %param.7, bf16[64,1280]{1,0:T(8,128)(2,1)} %bitcast.11, s32[]{:T(128)} %bitcast.6, pred[72]{0:T(512)(128)(4,1)S(1)} %iota_compare_fusion), kind=kLoop, calls=%fused_computation | loop fusion | flops 774144 | bytes 644428 | tf_op jit(solution)/shard_map/add | solution.py:164
  5.6 0.2 collective-permute-done.refs_2_
  5.8 1.5 %collective-permute-done.2.refs_4_ = bf16[64,256]{1,0:T(8,128)(2,1)S(1)} collective-permute-done((bf16[64,256]{1,0:T(8,128)(2,1)}, bf16[64,256]{1,0:T(8,128)(2,1)S(1)}, u32[]{:S(2)}, u32[]{:S(2)}) %collective-permute-start.2) | collective-permute-done | bytes 32800 | tf_op jit(solution)/shard_map/ppermute | solution.py:155
  7.3 0.0 collective-permute-done.1.refs_3_
  7.3 2.8 %shard_map.85 = (f32[64,256]{1,0:T(8,128)S(1)}, f32[64,256]{1,0:T(8,128)S(1)}, bf16[64,256]{1,0:T(8,128)(2,1)S(1)}, bf16[64,256]{1,0:T(8,128)(2,1)S(1)}, bf16[80...) custom-call(f32[72,1536]{1,0:T(8,128)S(1)} %convert_add_fusion.refs_0_, bf16[1280,1024]{1,0:T(8,128)(2,1)} %bitcast.7, ...), custom_call_target="tpu_custom_call" | custom-call | tf_op jit(solution)/shard_map/pallas_call | solution.py:166
  10.1 0.1 collective-permute-start.5
  10.1 0.6 %collective-permute-start.3 = (bf16[64,256]{1,0:T(8,128)(2,1)S(1)}, bf16[64,256]{1,0:T(8,128)(2,1)S(1)}, u32[]{:S(2)}, u32[]{:S(2)}) collective-permute-start(bf16[64,256]{1,0:T(8,128)(2,1)S(1)} %get-tuple-element.40), channel_id=1, source_target_pairs={{0,2},{1,3},{2,0},{3,1},{4,6},{5,7},{6,4},{7,5},{8,10},{9,11},{10,... | collective-permute-start | bytes 98312 | tf_op jit(solution)/shard_map/ppermute | solution.py:155
  10.8 1.2 %collective-permute-start.4 = (bf16[64,256]{1,0:T(8,128)(2,1)S(1)}, bf16[64,256]{1,0:T(8,128)(2,1)S(1)}, u32[]{:S(2)}, u32[]{:S(2)}) collective-permute-start(bf16[64,256]{1,0:T(8,128)(2,1)S(1)} %get-tuple-element.41), channel_id=1, source_target_pairs={{0,3},{1,2},{2,1},{3,0},{4,7},{5,6},{6,5},{7,4},{8,11},{9,10},{10,... | collective-permute-start | bytes 98312 | tf_op jit(solution)/shard_map/ppermute | solution.py:155
  12.0 2.5 %shard_map.86 = (f32[64,1280]{1,0:T(8,128)}, f32[1,1280]{1,0:T(1,128)}) custom-call(f32[72,1536]{1,0:T(8,128)S(1)} %convert_add_fusion.refs_0_, bf16[80,1280]{1,0:T(8,128)(2,1)S(1)} %get-tuple-element.52.refs_1_, bf16[80,1024]{1,0:T(8,128)(2,1)S(1)} %get-tuple-element.44.refs_2_, bf16[1280,1024]{1,0:T(8,128)(2,1)} %bitcast.8), custom_call_target="tpu_custom_call" | custom-call | flops 134217728 | bytes 1048576 | tf_op jit(solution)/shard_map/pallas_call | solution.py:189
  14.5 0.0 collective-permute-done.3
  14.5 0.0 collective-permute-done.4
  14.6 0.0 collective-permute-done.5
  14.6 2.6 %collective-permute-start.8 = (bf16[64,256]{1,0:T(8,128)(2,1)S(1)}, bf16[64,256]{1,0:T(8,128)(2,1)S(1)}, u32[]{:S(2)}, u32[]{:S(2)}) collective-permute-start(bf16[64,256]{1,0:T(8,128)(2,1)S(1)} %get-tuple-element.51), channel_id=1, source_target_pairs={{0,12},{4,8},{8,4},{12,0},{16,28},{20,24},{24,20},{28,16},{1,13},{... | collective-permute-start | bytes 98312 | tf_op jit(solution)/shard_map/ppermute | solution.py:155
  17.2 0.4 %collective-permute-start.7 = (bf16[64,256]{1,0:T(8,128)(2,1)S(1)}, bf16[64,256]{1,0:T(8,128)(2,1)S(1)}, u32[]{:S(2)}, u32[]{:S(2)}) collective-permute-start(bf16[64,256]{1,0:T(8,128)(2,1)S(1)} %get-tuple-element.51), channel_id=1, source_target_pairs={{0,8},{4,12},{8,0},{12,4},{16,24},{20,28},{24,16},{28,20},{1,9},{5... | collective-permute-start | bytes 98312 | tf_op jit(solution)/shard_map/ppermute | solution.py:155
  17.7 0.5 %collective-permute-start.6 = (bf16[64,256]{1,0:T(8,128)(2,1)S(1)}, bf16[64,256]{1,0:T(8,128)(2,1)S(1)}, u32[]{:S(2)}, u32[]{:S(2)}) collective-permute-start(bf16[64,256]{1,0:T(8,128)(2,1)S(1)} %get-tuple-element.51), channel_id=1, source_target_pairs={{0,4},{4,0},{8,12},{12,8},{16,20},{20,16},{24,28},{28,24},{1,5},{5... | collective-permute-start | bytes 98312 | tf_op jit(solution)/shard_map/ppermute | solution.py:155
  18.2 3.5 %shard_map.87 = (f32[64,1280]{1,0:T(8,128)}, f32[1,1280]{1,0:T(1,128)}) custom-call(f32[72,1536]{1,0:T(8,128)S(1)} %convert_add_fusion.refs_0_, bf16[80,1280]{1,0:T(8,128)(2,1)S(1)} %get-tuple-element.52.refs_1_, bf16[80,1024]{1,0:T(8,128)(2,1)S(1)} %get-tuple-element.44.refs_2_, ...), custom_call_target="tpu_custom_call", output_to_operand_aliasing={{0}: (4, {}), {1}: (5, {})} | custom-call | flops 201326592 | bytes 1572864 | tf_op jit(solution)/shard_map/pallas_call | solution.py:189
  21.7 0.0 collective-permute-done.8
  21.7 0.0 collective-permute-done.7
  21.7 0.0 collective-permute-done.6
  21.8 2.7 %collective-permute-start.9 = (f16[72,256]{1,0:T(8,128)(2,1)S(1)}, f16[72,256]{1,0:T(8,128)(2,1)S(1)}, u32[]{:S(2)}, u32[]{:S(2)}) collective-permute-start(f16[72,256]{1,0:T(8,128)(2,1)S(1)} %pad_maximum_fusion), channel_id=1, source_target_pairs={{0,16},{4,20},{8,24},{12,28},{16,0},{20,4},{24,8},{28,12},{1,17},{... | collective-permute-start | bytes 110600 | tf_op jit(solution)/shard_map/ppermute | solution.py:155
  24.6 2.2 %collective-permute-done.9 = f16[72,256]{1,0:T(8,128)(2,1)S(1)} collective-permute-done((f16[72,256]{1,0:T(8,128)(2,1)S(1)}, f16[72,256]{1,0:T(8,128)(2,1)S(1)}, u32[]{:S(2)}, u32[]{:S(2)}) %collective-permute-start.9) | collective-permute-done | bytes 36896 | tf_op jit(solution)/shard_map/ppermute | solution.py:155
  26.8 0.7 %multiply_add_fusion = f32[64,256]{1,0:T(8,128)} fusion(f16[72,256]{1,0:T(8,128)(2,1)S(1)} %pad_maximum_fusion, f32[256]{0:T(256)S(1)} %bitcast.13, f16[72,256]{1,0:T(8,128)(2,1)S(1)} %collective-permute-done.9, f32[256]{0:T(256)S(1)} %bitcast.12), kind=kLoop, calls=%fused_computation.1 | loop fusion | flops 81920 | bytes 133120 | tf_op jit(solution)/shard_map/add | solution.py:226
  (9 shorter events, 0.1 us)
Async XLA Ops:
  0.6 5.1 %collective-permute-start = (bf16[64,256]{1,0:T(8,128)(2,1)}, bf16[64,256]{1,0:T(8,128)(2,1)S(1)}, u32[]{:S(2)}, u32[]{:S(2)}) collective-permute-start(bf16[64,256]{1,0:T(8,128)(2,1)} %param.7), channel_id=1, source_target_pairs={{0,2},{1,3},{2,0},{3,1},{4,6},{5,7},{6,4},{7,5},{8,10},{9,11},{10,... | collective-permute-start | bytes 98312 | tf_op jit(solution)/shard_map/ppermute | solution.py:155
  3.7 3.6 %collective-permute-start.2 = (bf16[64,256]{1,0:T(8,128)(2,1)}, bf16[64,256]{1,0:T(8,128)(2,1)S(1)}, u32[]{:S(2)}, u32[]{:S(2)}) collective-permute-start(bf16[64,256]{1,0:T(8,128)(2,1)} %param.7), channel_id=1, source_target_pairs={{0,3},{1,2},{2,1},{3,0},{4,7},{5,6},{6,5},{7,4},{8,11},{9,10},{10,... | collective-permute-start | bytes 98312 | tf_op jit(solution)/shard_map/ppermute | solution.py:155
  3.7 3.6 %collective-permute-start.1 = (bf16[64,256]{1,0:T(8,128)(2,1)}, bf16[64,256]{1,0:T(8,128)(2,1)S(1)}, u32[]{:S(2)}, u32[]{:S(2)}) collective-permute-start(bf16[64,256]{1,0:T(8,128)(2,1)} %param.7), channel_id=1, source_target_pairs={{0,1},{1,0},{2,3},{3,2},{4,5},{5,4},{6,7},{7,6},{8,9},{9,8},{10,11... | collective-permute-start | bytes 98312 | tf_op jit(solution)/shard_map/ppermute | solution.py:155
  10.1 4.5 %collective-permute-start.5 = (f32[64,256]{1,0:T(8,128)S(1)}, f32[64,256]{1,0:T(8,128)S(1)}, u32[]{:S(2)}, u32[]{:S(2)}) collective-permute-start(f32[64,256]{1,0:T(8,128)S(1)} %get-tuple-element.42), channel_id=1, source_target_pairs={{0,1},{1,0},{2,3},{3,2},{4,5},{5,4},{6,7},{7,6},{8,9},{9,8},{10,11... | collective-permute-start | bytes 196616 | tf_op jit(solution)/shard_map/ppermute | solution.py:155
  10.1 4.4 %collective-permute-start.3 = (bf16[64,256]{1,0:T(8,128)(2,1)S(1)}, bf16[64,256]{1,0:T(8,128)(2,1)S(1)}, u32[]{:S(2)}, u32[]{:S(2)}) collective-permute-start(bf16[64,256]{1,0:T(8,128)(2,1)S(1)} %get-tuple-element.40), channel_id=1, source_target_pairs={{0,2},{1,3},{2,0},{3,1},{4,6},{5,7},{6,4},{7,5},{8,10},{9,11},{10,... | collective-permute-start | bytes 98312 | tf_op jit(solution)/shard_map/ppermute | solution.py:155
  10.8 3.8 %collective-permute-start.4 = (bf16[64,256]{1,0:T(8,128)(2,1)S(1)}, bf16[64,256]{1,0:T(8,128)(2,1)S(1)}, u32[]{:S(2)}, u32[]{:S(2)}) collective-permute-start(bf16[64,256]{1,0:T(8,128)(2,1)S(1)} %get-tuple-element.41), channel_id=1, source_target_pairs={{0,3},{1,2},{2,1},{3,0},{4,7},{5,6},{6,5},{7,4},{8,11},{9,10},{10,... | collective-permute-start | bytes 98312 | tf_op jit(solution)/shard_map/ppermute | solution.py:155
  14.6 7.1 %collective-permute-start.8 = (bf16[64,256]{1,0:T(8,128)(2,1)S(1)}, bf16[64,256]{1,0:T(8,128)(2,1)S(1)}, u32[]{:S(2)}, u32[]{:S(2)}) collective-permute-start(bf16[64,256]{1,0:T(8,128)(2,1)S(1)} %get-tuple-element.51), channel_id=1, source_target_pairs={{0,12},{4,8},{8,4},{12,0},{16,28},{20,24},{24,20},{28,16},{1,13},{... | collective-permute-start | bytes 98312 | tf_op jit(solution)/shard_map/ppermute | solution.py:155
  17.2 4.5 %collective-permute-start.7 = (bf16[64,256]{1,0:T(8,128)(2,1)S(1)}, bf16[64,256]{1,0:T(8,128)(2,1)S(1)}, u32[]{:S(2)}, u32[]{:S(2)}) collective-permute-start(bf16[64,256]{1,0:T(8,128)(2,1)S(1)} %get-tuple-element.51), channel_id=1, source_target_pairs={{0,8},{4,12},{8,0},{12,4},{16,24},{20,28},{24,16},{28,20},{1,9},{5... | collective-permute-start | bytes 98312 | tf_op jit(solution)/shard_map/ppermute | solution.py:155
  17.7 4.0 %collective-permute-start.6 = (bf16[64,256]{1,0:T(8,128)(2,1)S(1)}, bf16[64,256]{1,0:T(8,128)(2,1)S(1)}, u32[]{:S(2)}, u32[]{:S(2)}) collective-permute-start(bf16[64,256]{1,0:T(8,128)(2,1)S(1)} %get-tuple-element.51), channel_id=1, source_target_pairs={{0,4},{4,0},{8,12},{12,8},{16,20},{20,16},{24,28},{28,24},{1,5},{5... | collective-permute-start | bytes 98312 | tf_op jit(solution)/shard_map/ppermute | solution.py:155
  21.8 4.9 %collective-permute-start.9 = (f16[72,256]{1,0:T(8,128)(2,1)S(1)}, f16[72,256]{1,0:T(8,128)(2,1)S(1)}, u32[]{:S(2)}, u32[]{:S(2)}) collective-permute-start(f16[72,256]{1,0:T(8,128)(2,1)S(1)} %pad_maximum_fusion), channel_id=1, source_target_pairs={{0,16},{4,20},{8,24},{12,28},{16,0},{20,4},{24,8},{28,12},{1,17},{... | collective-permute-start | bytes 110600 | tf_op jit(solution)/shard_map/ppermute | solution.py:155

commit v24 on v23

--- a/solution.py
+++ b/solution.py
@@ -33,14 +33,19 @@
     pack_ref, counts_hbm = refs[:2]
     arrived = refs[2 : 1 + parts]
     outs = refs[1 + parts : 1 + 2 * parts]
-    load_ext, shifted, whole, counts_ref, held, resid_low, grad_shift, counts_sem = refs[1 + 2 * parts :]
+    load_ext, shifted, whole, counts_ref, held, resid_low, grad_shift, counts_sems = refs[1 + 2 * parts :]
     me = lax.axis_index(axis)
     lats, total = grad_shift.shape
     early = held.shape[0]
     neurons = counts_ref.shape[0]
     width = total // parts
-    counts_copy = pltpu.make_async_copy(counts_hbm, counts_ref, counts_sem)
-    counts_copy.start()
+    cut = early - chunk
+    places = [pl.ds(0, cut), pl.ds(cut, neurons - cut)]
+    copies = [
+        pltpu.make_async_copy(counts_hbm.at[place], counts_ref.at[place], counts_sems.at[index])
+        for index, place in enumerate(places)
+    ]
+    copies[0].start()
 
     for k in range(parts):
         start = pl.multiple_of((me ^ k) * width, width)
@@ -56,6 +61,8 @@
     row = lax.broadcasted_iota(jnp.int32, (EXTRA, total), 0)
     shifted[lats:, :] = jnp.where(row < 3, 1.0, 0.0).astype(BF16)
 
+    copies[1].start()
+
     load_ext[0:lats, :] = pack_ref[0:lats, 0:neurons].astype(BF16)
     bias = pack_ref[lats : lats + 1, 0:neurons]
     high = bias.astype(BF16).astype(F32)
@@ -73,13 +80,16 @@
     for rows, span in blocks:
         if rows.start < early:
             held[rows, span] = expected(load_ext[:, rows], shifted[:, span])
-    counts_copy.wait()
-    for rows, span in blocks:
-        rate = held[rows, span] if rows.start < early else expected(load_ext[:, rows], shifted[:, span])
-        resid_low[rows, span] = (rate - counts_ref[rows, span].astype(F32)).astype(BF16)
-    for begin in range(0, total, step):
-        span = slice(begin, begin + step)
-        grad_shift[:, span] = jnp.dot(load_ext[0:lats, :], resid_low[:, span], preferred_element_type=F32)
+    spans = [slice(begin, begin + step) for begin in range(0, total, step)]
+    for copy, place in zip(copies, [slice(0, cut), slice(cut, neurons)]):
+        copy.wait()
+        for rows, span in blocks:
+            if place.start <= rows.start < place.stop:
+                rate = held[rows, span] if rows.start < early else expected(load_ext[:, rows], shifted[:, span])
+                resid_low[rows, span] = (rate - counts_ref[rows, span].astype(F32)).astype(BF16)
+        for span in spans:
+            part = jnp.dot(load_ext[0:lats, place], resid_low[place, span], preferred_element_type=F32)
+            grad_shift[:, span] = grad_shift[:, span] + part if place.start else part
 
     bins = lax.broadcasted_iota(jnp.int32, (1, total), 1)
     tiles = []
@@ -103,10 +113,13 @@
     length = pack_ref[lats + 2 : lats + 3, 0:1].astype(jnp.int32)
     bins = lax.broadcasted_iota(jnp.int32, (1, total), 1)
     blocks = [(slice(begin, begin + chunk), range(0, total, step)) for begin in range(0, count, chunk)]
-    for rows, starts in blocks:
+
+    def rate(rows, span):
+        return expected(load_ext[:, first + rows.start : first + rows.stop], shifted[:, span])
+
+    for rows, starts in blocks[:-1]:
         for at in starts:
-            load_part = load_ext[:, first + rows.start : first + rows.stop]
-            held[rows, at : at + step] = expected(load_part, shifted[:, at : at + step])
+            held[rows, at : at + step] = rate(rows, slice(at, at + step))
     counts_copy.wait()
     outward = []
     for index, (rows, starts) in enumerate(blocks):
@@ -114,7 +127,8 @@
         grad = jnp.zeros((chunk, lats), F32)
         for at in starts:
             span = slice(at, at + step)
-            resid = jnp.where(bins[:, span] < length, held[rows, span] - counts_ref[rows, span].astype(F32), 0.0)
+            made = held[rows, span] if index < len(blocks) - 1 else rate(rows, span)
+            resid = jnp.where(bins[:, span] < length, made - counts_ref[rows, span].astype(F32), 0.0)
             for j in range(step // LANES):
                 sums = sums + resid[:, j * LANES : (j + 1) * LANES]
             grad = grad + lax.dot_general(
@@ -175,7 +189,7 @@
             pltpu.VMEM((4 * chunk, total), F32),
             pltpu.VMEM((neurons, total), BF16),
             pltpu.VMEM((lats, total), F32),
-            pltpu.SemaphoreType.DMA,
+            pltpu.SemaphoreType.DMA((2,)),
         ],
         compiler_params=params,
     )(pack, counts[0], *arrived)

time: 27.7 us -> 27.5 us (level)
  Pallas kernels: 8.81 us -> 8.53 us
    pallas_call x1, Pallas kernels: 2.75 us -> 2.45 us  [per_device(): pl.pallas_call(functools.partial(shift_kernel, neuron_count, order, 'neur...]
  transfers between devices with their start and end apart: 10 -> 10, of which waited for: 3 -> 4; matrix products, arithmetic and copies ran while one was open for 4% -> 4% of each run, Pallas kernels for 22% -> 22%
where the time goes in v24:
time: 27.5 us; the launch traced here: 27.2 us
  starting transfers between devices  11.4 us (41%)
  Pallas kernels  8.53 us (31%)
  waiting for transfers between devices  4.07 us (15%)
  other arithmetic  1.86 us (7%)
  between operations  1.39 us (5%)
    ppermute x10, starting transfers between devices, swap(): return lax.ppermute(value, axis, [(i, i ^ mask) for i in range(count)])  11.4 us
    pallas_call x2, Pallas kernels, make(): pl.pallas_call(functools.partial(load_kernel, lats, first, chunk, step),...  6.08 us
    ppermute x10, waiting for transfers between devices, swap(): return lax.ppermute(value, axis, [(i, i ^ mask) for i in range(count)])  4.07 us
    pallas_call x1, Pallas kernels, per_device(): pl.pallas_call(functools.partial(shift_kernel, neuron_count, order, 'neur...  2.45 us
    add x1, other arithmetic, per_device(): pack = pack + jnp.pad(latents, ((0, 8), (neurons, 0))).astype(F32)  1.07 us
    add x1, other arithmetic, per_device(): value = value + read(arrived[0])  0.65 us
  transfers between devices with their start and end apart: 10, of which 4 were waited for; matrix products, arithmetic and copies ran while one was open for 4% of the time, Pallas kernels for 22%

profile of v24, /device:TPU:0, one launch (start us, length us, event | category | flops | bytes accessed | tf_op | source)
XLA Modules:
  0.0 27.2 jit_solution(749358204673264509)
XLA Ops:
  0.6 3.0 %collective-permute-start = (bf16[64,256]{1,0:T(8,128)(2,1)}, bf16[64,256]{1,0:T(8,128)(2,1)S(1)}, u32[]{:S(2)}, u32[]{:S(2)}) collective-permute-start(bf16[64,256]{1,0:T(8,128)(2,1)} %param.7), channel_id=1, source_target_pairs={{0,2},{1,3},{2,0},{3,1},{4,6},{5,7},{6,4},{7,5},{8,10},{9,11},{10,... | collective-permute-start | bytes 98312 | tf_op jit(solution)/shard_map/ppermute | solution.py:169
  3.7 0.0 collective-permute-start.2
  3.7 0.2 collective-permute-start.1
  4.5 1.1 %convert_add_fusion.refs_0_ = f32[72,1536]{1,0:T(8,128)S(1)} fusion(s32[1,64]{1,0:T(1,128)} %param.10, f32[1,1280]{1,0:T(1,128)} %param.9, bf16[64,256]{1,0:T(8,128)(2,1)} %param.7, bf16[64,1280]{1,0:T(8,128)(2,1)} %bitcast.11, s32[]{:T(128)} %bitcast.6, pred[72]{0:T(512)(128)(4,1)S(1)} %iota_compare_fusion), kind=kLoop, calls=%fused_computation | loop fusion | flops 774144 | bytes 644428 | tf_op jit(solution)/shard_map/add | solution.py:178
  5.6 0.2 collective-permute-done.refs_2_
  5.8 1.5 %collective-permute-done.2.refs_4_ = bf16[64,256]{1,0:T(8,128)(2,1)S(1)} collective-permute-done((bf16[64,256]{1,0:T(8,128)(2,1)}, bf16[64,256]{1,0:T(8,128)(2,1)S(1)}, u32[]{:S(2)}, u32[]{:S(2)}) %collective-permute-start.2) | collective-permute-done | bytes 32800 | tf_op jit(solution)/shard_map/ppermute | solution.py:169
  7.3 0.0 collective-permute-done.1.refs_3_
  7.3 2.4 %shard_map.85 = (f32[64,256]{1,0:T(8,128)S(1)}, f32[64,256]{1,0:T(8,128)S(1)}, bf16[64,256]{1,0:T(8,128)(2,1)S(1)}, bf16[64,256]{1,0:T(8,128)(2,1)S(1)}, bf16[80...) custom-call(f32[72,1536]{1,0:T(8,128)S(1)} %convert_add_fusion.refs_0_, bf16[1280,1024]{1,0:T(8,128)(2,1)} %bitcast.7, ...), custom_call_target="tpu_custom_call" | custom-call | tf_op jit(solution)/shard_map/pallas_call | solution.py:180
  9.8 0.1 collective-permute-start.5
  9.8 0.7 %collective-permute-start.3 = (bf16[64,256]{1,0:T(8,128)(2,1)S(1)}, bf16[64,256]{1,0:T(8,128)(2,1)S(1)}, u32[]{:S(2)}, u32[]{:S(2)}) collective-permute-start(bf16[64,256]{1,0:T(8,128)(2,1)S(1)} %get-tuple-element.40), channel_id=1, source_target_pairs={{0,2},{1,3},{2,0},{3,1},{4,6},{5,7},{6,4},{7,5},{8,10},{9,11},{10,... | collective-permute-start | bytes 98312 | tf_op jit(solution)/shard_map/ppermute | solution.py:169
  10.5 1.2 %collective-permute-start.4 = (bf16[64,256]{1,0:T(8,128)(2,1)S(1)}, bf16[64,256]{1,0:T(8,128)(2,1)S(1)}, u32[]{:S(2)}, u32[]{:S(2)}) collective-permute-start(bf16[64,256]{1,0:T(8,128)(2,1)S(1)} %get-tuple-element.41), channel_id=1, source_target_pairs={{0,3},{1,2},{2,1},{3,0},{4,7},{5,6},{6,5},{7,4},{8,11},{9,10},{10,... | collective-permute-start | bytes 98312 | tf_op jit(solution)/shard_map/ppermute | solution.py:169
  11.7 2.8 %shard_map.86 = (f32[64,1280]{1,0:T(8,128)}, f32[1,1280]{1,0:T(1,128)}) custom-call(f32[72,1536]{1,0:T(8,128)S(1)} %convert_add_fusion.refs_0_, bf16[80,1280]{1,0:T(8,128)(2,1)S(1)} %get-tuple-element.52.refs_1_, bf16[80,1024]{1,0:T(8,128)(2,1)S(1)} %get-tuple-element.44.refs_2_, bf16[1280,1024]{1,0:T(8,128)(2,1)} %bitcast.8), custom_call_target="tpu_custom_call" | custom-call | flops 134217728 | bytes 1048576 | tf_op jit(solution)/shard_map/pallas_call | solution.py:203
  14.5 0.0 collective-permute-done.3
  14.5 0.0 collective-permute-done.4
  14.5 0.0 collective-permute-done.5
  14.6 2.6 %collective-permute-start.8 = (bf16[64,256]{1,0:T(8,128)(2,1)S(1)}, bf16[64,256]{1,0:T(8,128)(2,1)S(1)}, u32[]{:S(2)}, u32[]{:S(2)}) collective-permute-start(bf16[64,256]{1,0:T(8,128)(2,1)S(1)} %get-tuple-element.51), channel_id=1, source_target_pairs={{0,12},{4,8},{8,4},{12,0},{16,28},{20,24},{24,20},{28,16},{1,13},{... | collective-permute-start | bytes 98312 | tf_op jit(solution)/shard_map/ppermute | solution.py:169
  17.2 0.5 %collective-permute-start.7 = (bf16[64,256]{1,0:T(8,128)(2,1)S(1)}, bf16[64,256]{1,0:T(8,128)(2,1)S(1)}, u32[]{:S(2)}, u32[]{:S(2)}) collective-permute-start(bf16[64,256]{1,0:T(8,128)(2,1)S(1)} %get-tuple-element.51), channel_id=1, source_target_pairs={{0,8},{4,12},{8,0},{12,4},{16,24},{20,28},{24,16},{28,20},{1,9},{5... | collective-permute-start | bytes 98312 | tf_op jit(solution)/shard_map/ppermute | solution.py:169
  17.6 0.5 %collective-permute-start.6 = (bf16[64,256]{1,0:T(8,128)(2,1)S(1)}, bf16[64,256]{1,0:T(8,128)(2,1)S(1)}, u32[]{:S(2)}, u32[]{:S(2)}) collective-permute-start(bf16[64,256]{1,0:T(8,128)(2,1)S(1)} %get-tuple-element.51), channel_id=1, source_target_pairs={{0,4},{4,0},{8,12},{12,8},{16,20},{20,16},{24,28},{28,24},{1,5},{5... | collective-permute-start | bytes 98312 | tf_op jit(solution)/shard_map/ppermute | solution.py:169
  18.1 3.3 %shard_map.87 = (f32[64,1280]{1,0:T(8,128)}, f32[1,1280]{1,0:T(1,128)}) custom-call(f32[72,1536]{1,0:T(8,128)S(1)} %convert_add_fusion.refs_0_, bf16[80,1280]{1,0:T(8,128)(2,1)S(1)} %get-tuple-element.52.refs_1_, bf16[80,1024]{1,0:T(8,128)(2,1)S(1)} %get-tuple-element.44.refs_2_, ...), custom_call_target="tpu_custom_call", output_to_operand_aliasing={{0}: (4, {}), {1}: (5, {})} | custom-call | flops 201326592 | bytes 1572864 | tf_op jit(solution)/shard_map/pallas_call | solution.py:203
  21.4 0.0 collective-permute-done.8
  21.4 0.0 collective-permute-done.7
  21.4 0.1 collective-permute-done.6
  21.6 2.7 %collective-permute-start.9 = (f16[72,256]{1,0:T(8,128)(2,1)S(1)}, f16[72,256]{1,0:T(8,128)(2,1)S(1)}, u32[]{:S(2)}, u32[]{:S(2)}) collective-permute-start(f16[72,256]{1,0:T(8,128)(2,1)S(1)} %pad_maximum_fusion), channel_id=1, source_target_pairs={{0,16},{4,20},{8,24},{12,28},{16,0},{20,4},{24,8},{28,12},{1,17},{... | collective-permute-start | bytes 110600 | tf_op jit(solution)/shard_map/ppermute | solution.py:169
  24.3 2.3 %collective-permute-done.9 = f16[72,256]{1,0:T(8,128)(2,1)S(1)} collective-permute-done((f16[72,256]{1,0:T(8,128)(2,1)S(1)}, f16[72,256]{1,0:T(8,128)(2,1)S(1)}, u32[]{:S(2)}, u32[]{:S(2)}) %collective-permute-start.9) | collective-permute-done | bytes 36896 | tf_op jit(solution)/shard_map/ppermute | solution.py:169
  26.6 0.7 %multiply_add_fusion = f32[64,256]{1,0:T(8,128)} fusion(f16[72,256]{1,0:T(8,128)(2,1)S(1)} %pad_maximum_fusion, f32[256]{0:T(256)S(1)} %bitcast.13, f16[72,256]{1,0:T(8,128)(2,1)S(1)} %collective-permute-done.9, f32[256]{0:T(256)S(1)} %bitcast.12), kind=kLoop, calls=%fused_computation.1 | loop fusion | flops 81920 | bytes 133120 | tf_op jit(solution)/shard_map/add | solution.py:240
  (9 shorter events, 0.1 us)
Async XLA Ops:
  0.6 5.1 %collective-permute-start = (bf16[64,256]{1,0:T(8,128)(2,1)}, bf16[64,256]{1,0:T(8,128)(2,1)S(1)}, u32[]{:S(2)}, u32[]{:S(2)}) collective-permute-start(bf16[64,256]{1,0:T(8,128)(2,1)} %param.7), channel_id=1, source_target_pairs={{0,2},{1,3},{2,0},{3,1},{4,6},{5,7},{6,4},{7,5},{8,10},{9,11},{10,... | collective-permute-start | bytes 98312 | tf_op jit(solution)/shard_map/ppermute | solution.py:169
  3.7 3.6 %collective-permute-start.2 = (bf16[64,256]{1,0:T(8,128)(2,1)}, bf16[64,256]{1,0:T(8,128)(2,1)S(1)}, u32[]{:S(2)}, u32[]{:S(2)}) collective-permute-start(bf16[64,256]{1,0:T(8,128)(2,1)} %param.7), channel_id=1, source_target_pairs={{0,3},{1,2},{2,1},{3,0},{4,7},{5,6},{6,5},{7,4},{8,11},{9,10},{10,... | collective-permute-start | bytes 98312 | tf_op jit(solution)/shard_map/ppermute | solution.py:169
  3.7 3.6 %collective-permute-start.1 = (bf16[64,256]{1,0:T(8,128)(2,1)}, bf16[64,256]{1,0:T(8,128)(2,1)S(1)}, u32[]{:S(2)}, u32[]{:S(2)}) collective-permute-start(bf16[64,256]{1,0:T(8,128)(2,1)} %param.7), channel_id=1, source_target_pairs={{0,1},{1,0},{2,3},{3,2},{4,5},{5,4},{6,7},{7,6},{8,9},{9,8},{10,11... | collective-permute-start | bytes 98312 | tf_op jit(solution)/shard_map/ppermute | solution.py:169
  9.8 4.8 %collective-permute-start.5 = (f32[64,256]{1,0:T(8,128)S(1)}, f32[64,256]{1,0:T(8,128)S(1)}, u32[]{:S(2)}, u32[]{:S(2)}) collective-permute-start(f32[64,256]{1,0:T(8,128)S(1)} %get-tuple-element.42), channel_id=1, source_target_pairs={{0,1},{1,0},{2,3},{3,2},{4,5},{5,4},{6,7},{7,6},{8,9},{9,8},{10,11... | collective-permute-start | bytes 196616 | tf_op jit(solution)/shard_map/ppermute | solution.py:169
  9.8 4.7 %collective-permute-start.3 = (bf16[64,256]{1,0:T(8,128)(2,1)S(1)}, bf16[64,256]{1,0:T(8,128)(2,1)S(1)}, u32[]{:S(2)}, u32[]{:S(2)}) collective-permute-start(bf16[64,256]{1,0:T(8,128)(2,1)S(1)} %get-tuple-element.40), channel_id=1, source_target_pairs={{0,2},{1,3},{2,0},{3,1},{4,6},{5,7},{6,4},{7,5},{8,10},{9,11},{10,... | collective-permute-start | bytes 98312 | tf_op jit(solution)/shard_map/ppermute | solution.py:169
  10.5 4.0 %collective-permute-start.4 = (bf16[64,256]{1,0:T(8,128)(2,1)S(1)}, bf16[64,256]{1,0:T(8,128)(2,1)S(1)}, u32[]{:S(2)}, u32[]{:S(2)}) collective-permute-start(bf16[64,256]{1,0:T(8,128)(2,1)S(1)} %get-tuple-element.41), channel_id=1, source_target_pairs={{0,3},{1,2},{2,1},{3,0},{4,7},{5,6},{6,5},{7,4},{8,11},{9,10},{10,... | collective-permute-start | bytes 98312 | tf_op jit(solution)/shard_map/ppermute | solution.py:169
  14.6 6.8 %collective-permute-start.8 = (bf16[64,256]{1,0:T(8,128)(2,1)S(1)}, bf16[64,256]{1,0:T(8,128)(2,1)S(1)}, u32[]{:S(2)}, u32[]{:S(2)}) collective-permute-start(bf16[64,256]{1,0:T(8,128)(2,1)S(1)} %get-tuple-element.51), channel_id=1, source_target_pairs={{0,12},{4,8},{8,4},{12,0},{16,28},{20,24},{24,20},{28,16},{1,13},{... | collective-permute-start | bytes 98312 | tf_op jit(solution)/shard_map/ppermute | solution.py:169
  17.2 4.3 %collective-permute-start.7 = (bf16[64,256]{1,0:T(8,128)(2,1)S(1)}, bf16[64,256]{1,0:T(8,128)(2,1)S(1)}, u32[]{:S(2)}, u32[]{:S(2)}) collective-permute-start(bf16[64,256]{1,0:T(8,128)(2,1)S(1)} %get-tuple-element.51), channel_id=1, source_target_pairs={{0,8},{4,12},{8,0},{12,4},{16,24},{20,28},{24,16},{28,20},{1,9},{5... | collective-permute-start | bytes 98312 | tf_op jit(solution)/shard_map/ppermute | solution.py:169
  17.6 3.9 %collective-permute-start.6 = (bf16[64,256]{1,0:T(8,128)(2,1)S(1)}, bf16[64,256]{1,0:T(8,128)(2,1)S(1)}, u32[]{:S(2)}, u32[]{:S(2)}) collective-permute-start(bf16[64,256]{1,0:T(8,128)(2,1)S(1)} %get-tuple-element.51), channel_id=1, source_target_pairs={{0,4},{4,0},{8,12},{12,8},{16,20},{20,16},{24,28},{28,24},{1,5},{5... | collective-permute-start | bytes 98312 | tf_op jit(solution)/shard_map/ppermute | solution.py:169
  21.6 4.9 %collective-permute-start.9 = (f16[72,256]{1,0:T(8,128)(2,1)S(1)}, f16[72,256]{1,0:T(8,128)(2,1)S(1)}, u32[]{:S(2)}, u32[]{:S(2)}) collective-permute-start(f16[72,256]{1,0:T(8,128)(2,1)S(1)} %pad_maximum_fusion), channel_id=1, source_target_pairs={{0,16},{4,20},{8,24},{12,28},{16,0},{20,4},{24,8},{28,12},{1,17},{... | collective-permute-start | bytes 110600 | tf_op jit(solution)/shard_map/ppermute | solution.py:169

commit v25 on v24

--- a/solution.py
+++ b/solution.py
@@ -39,7 +39,7 @@
     early = held.shape[0]
     neurons = counts_ref.shape[0]
     width = total // parts
-    cut = early - chunk
+    cut = 2 * chunk
     places = [pl.ds(0, cut), pl.ds(cut, neurons - cut)]
     copies = [
         pltpu.make_async_copy(counts_hbm.at[place], counts_ref.at[place], counts_sems.at[index])
@@ -117,7 +117,8 @@
     def rate(rows, span):
         return expected(load_ext[:, first + rows.start : first + rows.stop], shifted[:, span])
 
-    for rows, starts in blocks[:-1]:
+    early = blocks[:-1] if len(blocks) > 2 else blocks
+    for rows, starts in early:
         for at in starts:
             held[rows, at : at + step] = rate(rows, slice(at, at + step))
     counts_copy.wait()
@@ -127,7 +128,7 @@
         grad = jnp.zeros((chunk, lats), F32)
         for at in starts:
             span = slice(at, at + step)
-            made = held[rows, span] if index < len(blocks) - 1 else rate(rows, span)
+            made = held[rows, span] if index < len(early) else rate(rows, span)
             resid = jnp.where(bins[:, span] < length, made - counts_ref[rows, span].astype(F32), 0.0)
             for j in range(step // LANES):
                 sums = sums + resid[:, j * LANES : (j + 1) * LANES]
@@ -186,7 +187,7 @@
         scratch_shapes=[
             pltpu.VMEM((lats, total), BF16),
             pltpu.VMEM((neurons, total), BF16),
-            pltpu.VMEM((4 * chunk, total), F32),
+            pltpu.VMEM((3 * chunk, total), F32),
             pltpu.VMEM((neurons, total), BF16),
             pltpu.VMEM((lats, total), F32),
             pltpu.SemaphoreType.DMA((2,)),

time: 27.5 us -> 27.5 us (level)
    pallas_call x2, Pallas kernels: 6.08 us -> 5.8 us  [make(): pl.pallas_call(functools.partial(load_kernel, lats, first, chunk, step),...]
  transfers between devices with their start and end apart: 10 -> 10, of which waited for: 4 -> 4; matrix products, arithmetic and copies ran while one was open for 4% -> 4% of each run, Pallas kernels for 22% -> 21%
where the time goes in v25:
time: 27.5 us; the launch traced here: 27.2 us
  starting transfers between devices  11.4 us (41%)
  Pallas kernels  8.47 us (31%)
  waiting for transfers between devices  4.13 us (15%)
  other arithmetic  1.86 us (7%)
  between operations  1.39 us (5%)
    ppermute x10, starting transfers between devices, swap(): return lax.ppermute(value, axis, [(i, i ^ mask) for i in range(count)])  11.4 us
    pallas_call x2, Pallas kernels, make(): pl.pallas_call(functools.partial(load_kernel, lats, first, chunk, step),...  5.8 us
    ppermute x10, waiting for transfers between devices, swap(): return lax.ppermute(value, axis, [(i, i ^ mask) for i in range(count)])  4.13 us
    pallas_call x1, Pallas kernels, per_device(): pl.pallas_call(functools.partial(shift_kernel, neuron_count, order, 'neur...  2.67 us
    add x1, other arithmetic, per_device(): pack = pack + jnp.pad(latents, ((0, 8), (neurons, 0))).astype(F32)  1.07 us
    add x1, other arithmetic, per_device(): value = value + read(arrived[0])  0.65 us
  transfers between devices with their start and end apart: 10, of which 4 were waited for; matrix products, arithmetic and copies ran while one was open for 4% of the time, Pallas kernels for 21%

profile of v25, /device:TPU:0, one launch (start us, length us, event | category | flops | bytes accessed | tf_op | source)
XLA Modules:
  0.0 27.2 jit_solution(12194684464110038267)
XLA Ops:
  0.6 3.0 %collective-permute-start = (bf16[64,256]{1,0:T(8,128)(2,1)}, bf16[64,256]{1,0:T(8,128)(2,1)S(1)}, u32[]{:S(2)}, u32[]{:S(2)}) collective-permute-start(bf16[64,256]{1,0:T(8,128)(2,1)} %param.7), channel_id=1, source_target_pairs={{0,2},{1,3},{2,0},{3,1},{4,6},{5,7},{6,4},{7,5},{8,10},{9,11},{10,... | collective-permute-start | bytes 98312 | tf_op jit(solution)/shard_map/ppermute | solution.py:170
  3.7 0.0 collective-permute-start.2
  3.7 0.2 collective-permute-start.1
  4.5 1.1 %convert_add_fusion.refs_0_ = f32[72,1536]{1,0:T(8,128)S(1)} fusion(s32[1,64]{1,0:T(1,128)} %param.10, f32[1,1280]{1,0:T(1,128)} %param.9, bf16[64,256]{1,0:T(8,128)(2,1)} %param.7, bf16[64,1280]{1,0:T(8,128)(2,1)} %bitcast.11, s32[]{:T(128)} %bitcast.6, pred[72]{0:T(512)(128)(4,1)S(1)} %iota_compare_fusion), kind=kLoop, calls=%fused_computation | loop fusion | flops 774144 | bytes 644428 | tf_op jit(solution)/shard_map/add | solution.py:179
  5.6 0.2 collective-permute-done.refs_2_
  5.8 1.5 %collective-permute-done.2.refs_4_ = bf16[64,256]{1,0:T(8,128)(2,1)S(1)} collective-permute-done((bf16[64,256]{1,0:T(8,128)(2,1)}, bf16[64,256]{1,0:T(8,128)(2,1)S(1)}, u32[]{:S(2)}, u32[]{:S(2)}) %collective-permute-start.2) | collective-permute-done | bytes 32800 | tf_op jit(solution)/shard_map/ppermute | solution.py:170
  7.3 0.0 collective-permute-done.1.refs_3_
  7.3 2.7 %shard_map.85 = (f32[64,256]{1,0:T(8,128)S(1)}, f32[64,256]{1,0:T(8,128)S(1)}, bf16[64,256]{1,0:T(8,128)(2,1)S(1)}, bf16[64,256]{1,0:T(8,128)(2,1)S(1)}, bf16[80...) custom-call(f32[72,1536]{1,0:T(8,128)S(1)} %convert_add_fusion.refs_0_, bf16[1280,1024]{1,0:T(8,128)(2,1)} %bitcast.7, ...), custom_call_target="tpu_custom_call" | custom-call | tf_op jit(solution)/shard_map/pallas_call | solution.py:181
  10.0 0.1 collective-permute-start.5
  10.1 0.7 %collective-permute-start.3 = (bf16[64,256]{1,0:T(8,128)(2,1)S(1)}, bf16[64,256]{1,0:T(8,128)(2,1)S(1)}, u32[]{:S(2)}, u32[]{:S(2)}) collective-permute-start(bf16[64,256]{1,0:T(8,128)(2,1)S(1)} %get-tuple-element.40), channel_id=1, source_target_pairs={{0,2},{1,3},{2,0},{3,1},{4,6},{5,7},{6,4},{7,5},{8,10},{9,11},{10,... | collective-permute-start | bytes 98312 | tf_op jit(solution)/shard_map/ppermute | solution.py:170
  10.7 1.2 %collective-permute-start.4 = (bf16[64,256]{1,0:T(8,128)(2,1)S(1)}, bf16[64,256]{1,0:T(8,128)(2,1)S(1)}, u32[]{:S(2)}, u32[]{:S(2)}) collective-permute-start(bf16[64,256]{1,0:T(8,128)(2,1)S(1)} %get-tuple-element.41), channel_id=1, source_target_pairs={{0,3},{1,2},{2,1},{3,0},{4,7},{5,6},{6,5},{7,4},{8,11},{9,10},{10,... | collective-permute-start | bytes 98312 | tf_op jit(solution)/shard_map/ppermute | solution.py:170
  11.9 2.5 %shard_map.86 = (f32[64,1280]{1,0:T(8,128)}, f32[1,1280]{1,0:T(1,128)}) custom-call(f32[72,1536]{1,0:T(8,128)S(1)} %convert_add_fusion.refs_0_, bf16[80,1280]{1,0:T(8,128)(2,1)S(1)} %get-tuple-element.52.refs_1_, bf16[80,1024]{1,0:T(8,128)(2,1)S(1)} %get-tuple-element.44.refs_2_, bf16[1280,1024]{1,0:T(8,128)(2,1)} %bitcast.8), custom_call_target="tpu_custom_call" | custom-call | flops 134217728 | bytes 1048576 | tf_op jit(solution)/shard_map/pallas_call | solution.py:204
  14.5 0.0 collective-permute-done.3
  14.5 0.0 collective-permute-done.4
  14.5 0.0 collective-permute-done.5
  14.5 2.6 %collective-permute-start.8 = (bf16[64,256]{1,0:T(8,128)(2,1)S(1)}, bf16[64,256]{1,0:T(8,128)(2,1)S(1)}, u32[]{:S(2)}, u32[]{:S(2)}) collective-permute-start(bf16[64,256]{1,0:T(8,128)(2,1)S(1)} %get-tuple-element.51), channel_id=1, source_target_pairs={{0,12},{4,8},{8,4},{12,0},{16,28},{20,24},{24,20},{28,16},{1,13},{... | collective-permute-start | bytes 98312 | tf_op jit(solution)/shard_map/ppermute | solution.py:170
  17.2 0.5 %collective-permute-start.7 = (bf16[64,256]{1,0:T(8,128)(2,1)S(1)}, bf16[64,256]{1,0:T(8,128)(2,1)S(1)}, u32[]{:S(2)}, u32[]{:S(2)}) collective-permute-start(bf16[64,256]{1,0:T(8,128)(2,1)S(1)} %get-tuple-element.51), channel_id=1, source_target_pairs={{0,8},{4,12},{8,0},{12,4},{16,24},{20,28},{24,16},{28,20},{1,9},{5... | collective-permute-start | bytes 98312 | tf_op jit(solution)/shard_map/ppermute | solution.py:170
  17.6 0.5 %collective-permute-start.6 = (bf16[64,256]{1,0:T(8,128)(2,1)S(1)}, bf16[64,256]{1,0:T(8,128)(2,1)S(1)}, u32[]{:S(2)}, u32[]{:S(2)}) collective-permute-start(bf16[64,256]{1,0:T(8,128)(2,1)S(1)} %get-tuple-element.51), channel_id=1, source_target_pairs={{0,4},{4,0},{8,12},{12,8},{16,20},{20,16},{24,28},{28,24},{1,5},{5... | collective-permute-start | bytes 98312 | tf_op jit(solution)/shard_map/ppermute | solution.py:170
  18.1 3.3 %shard_map.87 = (f32[64,1280]{1,0:T(8,128)}, f32[1,1280]{1,0:T(1,128)}) custom-call(f32[72,1536]{1,0:T(8,128)S(1)} %convert_add_fusion.refs_0_, bf16[80,1280]{1,0:T(8,128)(2,1)S(1)} %get-tuple-element.52.refs_1_, bf16[80,1024]{1,0:T(8,128)(2,1)S(1)} %get-tuple-element.44.refs_2_, ...), custom_call_target="tpu_custom_call", output_to_operand_aliasing={{0}: (4, {}), {1}: (5, {})} | custom-call | flops 201326592 | bytes 1572864 | tf_op jit(solution)/shard_map/pallas_call | solution.py:204
  21.3 0.0 collective-permute-done.8
  21.4 0.0 collective-permute-done.7
  21.4 0.2 collective-permute-done.6
  21.6 2.7 %collective-permute-start.9 = (f16[72,256]{1,0:T(8,128)(2,1)S(1)}, f16[72,256]{1,0:T(8,128)(2,1)S(1)}, u32[]{:S(2)}, u32[]{:S(2)}) collective-permute-start(f16[72,256]{1,0:T(8,128)(2,1)S(1)} %pad_maximum_fusion), channel_id=1, source_target_pairs={{0,16},{4,20},{8,24},{12,28},{16,0},{20,4},{24,8},{28,12},{1,17},{... | collective-permute-start | bytes 110600 | tf_op jit(solution)/shard_map/ppermute | solution.py:170
  24.3 2.3 %collective-permute-done.9 = f16[72,256]{1,0:T(8,128)(2,1)S(1)} collective-permute-done((f16[72,256]{1,0:T(8,128)(2,1)S(1)}, f16[72,256]{1,0:T(8,128)(2,1)S(1)}, u32[]{:S(2)}, u32[]{:S(2)}) %collective-permute-start.9) | collective-permute-done | bytes 36896 | tf_op jit(solution)/shard_map/ppermute | solution.py:170
  26.6 0.7 %multiply_add_fusion = f32[64,256]{1,0:T(8,128)} fusion(f16[72,256]{1,0:T(8,128)(2,1)S(1)} %pad_maximum_fusion, f32[256]{0:T(256)S(1)} %bitcast.13, f16[72,256]{1,0:T(8,128)(2,1)S(1)} %collective-permute-done.9, f32[256]{0:T(256)S(1)} %bitcast.12), kind=kLoop, calls=%fused_computation.1 | loop fusion | flops 81920 | bytes 133120 | tf_op jit(solution)/shard_map/add | solution.py:241
  (9 shorter events, 0.1 us)
Async XLA Ops:
  0.6 5.1 %collective-permute-start = (bf16[64,256]{1,0:T(8,128)(2,1)}, bf16[64,256]{1,0:T(8,128)(2,1)S(1)}, u32[]{:S(2)}, u32[]{:S(2)}) collective-permute-start(bf16[64,256]{1,0:T(8,128)(2,1)} %param.7), channel_id=1, source_target_pairs={{0,2},{1,3},{2,0},{3,1},{4,6},{5,7},{6,4},{7,5},{8,10},{9,11},{10,... | collective-permute-start | bytes 98312 | tf_op jit(solution)/shard_map/ppermute | solution.py:170
  3.7 3.6 %collective-permute-start.2 = (bf16[64,256]{1,0:T(8,128)(2,1)}, bf16[64,256]{1,0:T(8,128)(2,1)S(1)}, u32[]{:S(2)}, u32[]{:S(2)}) collective-permute-start(bf16[64,256]{1,0:T(8,128)(2,1)} %param.7), channel_id=1, source_target_pairs={{0,3},{1,2},{2,1},{3,0},{4,7},{5,6},{6,5},{7,4},{8,11},{9,10},{10,... | collective-permute-start | bytes 98312 | tf_op jit(solution)/shard_map/ppermute | solution.py:170
  3.7 3.6 %collective-permute-start.1 = (bf16[64,256]{1,0:T(8,128)(2,1)}, bf16[64,256]{1,0:T(8,128)(2,1)S(1)}, u32[]{:S(2)}, u32[]{:S(2)}) collective-permute-start(bf16[64,256]{1,0:T(8,128)(2,1)} %param.7), channel_id=1, source_target_pairs={{0,1},{1,0},{2,3},{3,2},{4,5},{5,4},{6,7},{7,6},{8,9},{9,8},{10,11... | collective-permute-start | bytes 98312 | tf_op jit(solution)/shard_map/ppermute | solution.py:170
  10.0 4.5 %collective-permute-start.5 = (f32[64,256]{1,0:T(8,128)S(1)}, f32[64,256]{1,0:T(8,128)S(1)}, u32[]{:S(2)}, u32[]{:S(2)}) collective-permute-start(f32[64,256]{1,0:T(8,128)S(1)} %get-tuple-element.42), channel_id=1, source_target_pairs={{0,1},{1,0},{2,3},{3,2},{4,5},{5,4},{6,7},{7,6},{8,9},{9,8},{10,11... | collective-permute-start | bytes 196616 | tf_op jit(solution)/shard_map/ppermute | solution.py:170
  10.1 4.4 %collective-permute-start.3 = (bf16[64,256]{1,0:T(8,128)(2,1)S(1)}, bf16[64,256]{1,0:T(8,128)(2,1)S(1)}, u32[]{:S(2)}, u32[]{:S(2)}) collective-permute-start(bf16[64,256]{1,0:T(8,128)(2,1)S(1)} %get-tuple-element.40), channel_id=1, source_target_pairs={{0,2},{1,3},{2,0},{3,1},{4,6},{5,7},{6,4},{7,5},{8,10},{9,11},{10,... | collective-permute-start | bytes 98312 | tf_op jit(solution)/shard_map/ppermute | solution.py:170
  10.7 3.8 %collective-permute-start.4 = (bf16[64,256]{1,0:T(8,128)(2,1)S(1)}, bf16[64,256]{1,0:T(8,128)(2,1)S(1)}, u32[]{:S(2)}, u32[]{:S(2)}) collective-permute-start(bf16[64,256]{1,0:T(8,128)(2,1)S(1)} %get-tuple-element.41), channel_id=1, source_target_pairs={{0,3},{1,2},{2,1},{3,0},{4,7},{5,6},{6,5},{7,4},{8,11},{9,10},{10,... | collective-permute-start | bytes 98312 | tf_op jit(solution)/shard_map/ppermute | solution.py:170
  14.5 6.8 %collective-permute-start.8 = (bf16[64,256]{1,0:T(8,128)(2,1)S(1)}, bf16[64,256]{1,0:T(8,128)(2,1)S(1)}, u32[]{:S(2)}, u32[]{:S(2)}) collective-permute-start(bf16[64,256]{1,0:T(8,128)(2,1)S(1)} %get-tuple-element.51), channel_id=1, source_target_pairs={{0,12},{4,8},{8,4},{12,0},{16,28},{20,24},{24,20},{28,16},{1,13},{... | collective-permute-start | bytes 98312 | tf_op jit(solution)/shard_map/ppermute | solution.py:170
  17.2 4.2 %collective-permute-start.7 = (bf16[64,256]{1,0:T(8,128)(2,1)S(1)}, bf16[64,256]{1,0:T(8,128)(2,1)S(1)}, u32[]{:S(2)}, u32[]{:S(2)}) collective-permute-start(bf16[64,256]{1,0:T(8,128)(2,1)S(1)} %get-tuple-element.51), channel_id=1, source_target_pairs={{0,8},{4,12},{8,0},{12,4},{16,24},{20,28},{24,16},{28,20},{1,9},{5... | collective-permute-start | bytes 98312 | tf_op jit(solution)/shard_map/ppermute | solution.py:170
  17.6 3.9 %collective-permute-start.6 = (bf16[64,256]{1,0:T(8,128)(2,1)S(1)}, bf16[64,256]{1,0:T(8,128)(2,1)S(1)}, u32[]{:S(2)}, u32[]{:S(2)}) collective-permute-start(bf16[64,256]{1,0:T(8,128)(2,1)S(1)} %get-tuple-element.51), channel_id=1, source_target_pairs={{0,4},{4,0},{8,12},{12,8},{16,20},{20,16},{24,28},{28,24},{1,5},{5... | collective-permute-start | bytes 98312 | tf_op jit(solution)/shard_map/ppermute | solution.py:170
  21.6 4.9 %collective-permute-start.9 = (f16[72,256]{1,0:T(8,128)(2,1)S(1)}, f16[72,256]{1,0:T(8,128)(2,1)S(1)}, u32[]{:S(2)}, u32[]{:S(2)}) collective-permute-start(f16[72,256]{1,0:T(8,128)(2,1)S(1)} %pad_maximum_fusion), channel_id=1, source_target_pairs={{0,16},{4,20},{8,24},{12,28},{16,0},{20,4},{24,8},{28,12},{1,17},{... | collective-permute-start | bytes 110600 | tf_op jit(solution)/shard_map/ppermute | solution.py:170

commit v26 on v25

--- a/solution.py
+++ b/solution.py
@@ -39,7 +39,7 @@
     early = held.shape[0]
     neurons = counts_ref.shape[0]
     width = total // parts
-    cut = 2 * chunk
+    cut = 3 * chunk
     places = [pl.ds(0, cut), pl.ds(cut, neurons - cut)]
     copies = [
         pltpu.make_async_copy(counts_hbm.at[place], counts_ref.at[place], counts_sems.at[index])
@@ -187,7 +187,7 @@
         scratch_shapes=[
             pltpu.VMEM((lats, total), BF16),
             pltpu.VMEM((neurons, total), BF16),
-            pltpu.VMEM((3 * chunk, total), F32),
+            pltpu.VMEM((4 * chunk, total), F32),
             pltpu.VMEM((neurons, total), BF16),
             pltpu.VMEM((lats, total), F32),
             pltpu.SemaphoreType.DMA((2,)),

time: 27.5 us -> 27.2 us (0.989)
  no operation moved by 1% of the time
where the time goes in v26:
time: 27.2 us; the launch traced here: 27 us
  starting transfers between devices  11.4 us (42%)
  Pallas kernels  8.24 us (30%)
  waiting for transfers between devices  4.13 us (15%)
  other arithmetic  1.86 us (7%)
  between operations  1.39 us (5%)
    ppermute x10, starting transfers between devices, swap(): return lax.ppermute(value, axis, [(i, i ^ mask) for i in range(count)])  11.4 us
    pallas_call x2, Pallas kernels, make(): pl.pallas_call(functools.partial(load_kernel, lats, first, chunk, step),...  5.8 us
    ppermute x10, waiting for transfers between devices, swap(): return lax.ppermute(value, axis, [(i, i ^ mask) for i in range(count)])  4.13 us
    pallas_call x1, Pallas kernels, per_device(): pl.pallas_call(functools.partial(shift_kernel, neuron_count, order, 'neur...  2.45 us
    add x1, other arithmetic, per_device(): pack = pack + jnp.pad(latents, ((0, 8), (neurons, 0))).astype(F32)  1.07 us
    add x1, other arithmetic, per_device(): value = value + read(arrived[0])  0.65 us
  transfers between devices with their start and end apart: 10, of which 4 were waited for; matrix products, arithmetic and copies ran while one was open for 4% of the time, Pallas kernels for 21%

profile of v26, /device:TPU:0, one launch (start us, length us, event | category | flops | bytes accessed | tf_op | source)
XLA Modules:
  0.0 27.0 jit_solution(12263141145336996573)
XLA Ops:
  0.6 3.0 %collective-permute-start = (bf16[64,256]{1,0:T(8,128)(2,1)}, bf16[64,256]{1,0:T(8,128)(2,1)S(1)}, u32[]{:S(2)}, u32[]{:S(2)}) collective-permute-start(bf16[64,256]{1,0:T(8,128)(2,1)} %param.7), channel_id=1, source_target_pairs={{0,2},{1,3},{2,0},{3,1},{4,6},{5,7},{6,4},{7,5},{8,10},{9,11},{10,... | collective-permute-start | bytes 98312 | tf_op jit(solution)/shard_map/ppermute | solution.py:170
  3.7 0.0 collective-permute-start.2
  3.7 0.2 collective-permute-start.1
  4.5 1.1 %convert_add_fusion.refs_0_ = f32[72,1536]{1,0:T(8,128)S(1)} fusion(s32[1,64]{1,0:T(1,128)} %param.10, f32[1,1280]{1,0:T(1,128)} %param.9, bf16[64,256]{1,0:T(8,128)(2,1)} %param.7, bf16[64,1280]{1,0:T(8,128)(2,1)} %bitcast.11, s32[]{:T(128)} %bitcast.6, pred[72]{0:T(512)(128)(4,1)S(1)} %iota_compare_fusion), kind=kLoop, calls=%fused_computation | loop fusion | flops 774144 | bytes 644428 | tf_op jit(solution)/shard_map/add | solution.py:179
  5.6 0.2 collective-permute-done.refs_2_
  5.8 1.5 %collective-permute-done.2.refs_4_ = bf16[64,256]{1,0:T(8,128)(2,1)S(1)} collective-permute-done((bf16[64,256]{1,0:T(8,128)(2,1)}, bf16[64,256]{1,0:T(8,128)(2,1)S(1)}, u32[]{:S(2)}, u32[]{:S(2)}) %collective-permute-start.2) | collective-permute-done | bytes 32800 | tf_op jit(solution)/shard_map/ppermute | solution.py:170
  7.3 0.0 collective-permute-done.1.refs_3_
  7.3 2.4 %shard_map.85 = (f32[64,256]{1,0:T(8,128)S(1)}, f32[64,256]{1,0:T(8,128)S(1)}, bf16[64,256]{1,0:T(8,128)(2,1)S(1)}, bf16[64,256]{1,0:T(8,128)(2,1)S(1)}, bf16[80...) custom-call(f32[72,1536]{1,0:T(8,128)S(1)} %convert_add_fusion.refs_0_, bf16[1280,1024]{1,0:T(8,128)(2,1)} %bitcast.7, ...), custom_call_target="tpu_custom_call" | custom-call | tf_op jit(solution)/shard_map/pallas_call | solution.py:181
  9.8 0.1 collective-permute-start.5
  9.8 0.7 %collective-permute-start.3 = (bf16[64,256]{1,0:T(8,128)(2,1)S(1)}, bf16[64,256]{1,0:T(8,128)(2,1)S(1)}, u32[]{:S(2)}, u32[]{:S(2)}) collective-permute-start(bf16[64,256]{1,0:T(8,128)(2,1)S(1)} %get-tuple-element.40), channel_id=1, source_target_pairs={{0,2},{1,3},{2,0},{3,1},{4,6},{5,7},{6,4},{7,5},{8,10},{9,11},{10,... | collective-permute-start | bytes 98312 | tf_op jit(solution)/shard_map/ppermute | solution.py:170
  10.5 1.2 %collective-permute-start.4 = (bf16[64,256]{1,0:T(8,128)(2,1)S(1)}, bf16[64,256]{1,0:T(8,128)(2,1)S(1)}, u32[]{:S(2)}, u32[]{:S(2)}) collective-permute-start(bf16[64,256]{1,0:T(8,128)(2,1)S(1)} %get-tuple-element.41), channel_id=1, source_target_pairs={{0,3},{1,2},{2,1},{3,0},{4,7},{5,6},{6,5},{7,4},{8,11},{9,10},{10,... | collective-permute-start | bytes 98312 | tf_op jit(solution)/shard_map/ppermute | solution.py:170
  11.7 2.5 %shard_map.86 = (f32[64,1280]{1,0:T(8,128)}, f32[1,1280]{1,0:T(1,128)}) custom-call(f32[72,1536]{1,0:T(8,128)S(1)} %convert_add_fusion.refs_0_, bf16[80,1280]{1,0:T(8,128)(2,1)S(1)} %get-tuple-element.52.refs_1_, bf16[80,1024]{1,0:T(8,128)(2,1)S(1)} %get-tuple-element.44.refs_2_, bf16[1280,1024]{1,0:T(8,128)(2,1)} %bitcast.8), custom_call_target="tpu_custom_call" | custom-call | flops 134217728 | bytes 1048576 | tf_op jit(solution)/shard_map/pallas_call | solution.py:204
  14.2 0.0 collective-permute-done.3
  14.2 0.0 collective-permute-done.4
  14.3 0.0 collective-permute-done.5
  14.3 2.6 %collective-permute-start.8 = (bf16[64,256]{1,0:T(8,128)(2,1)S(1)}, bf16[64,256]{1,0:T(8,128)(2,1)S(1)}, u32[]{:S(2)}, u32[]{:S(2)}) collective-permute-start(bf16[64,256]{1,0:T(8,128)(2,1)S(1)} %get-tuple-element.51), channel_id=1, source_target_pairs={{0,12},{4,8},{8,4},{12,0},{16,28},{20,24},{24,20},{28,16},{1,13},{... | collective-permute-start | bytes 98312 | tf_op jit(solution)/shard_map/ppermute | solution.py:170
  16.9 0.5 %collective-permute-start.7 = (bf16[64,256]{1,0:T(8,128)(2,1)S(1)}, bf16[64,256]{1,0:T(8,128)(2,1)S(1)}, u32[]{:S(2)}, u32[]{:S(2)}) collective-permute-start(bf16[64,256]{1,0:T(8,128)(2,1)S(1)} %get-tuple-element.51), channel_id=1, source_target_pairs={{0,8},{4,12},{8,0},{12,4},{16,24},{20,28},{24,16},{28,20},{1,9},{5... | collective-permute-start | bytes 98312 | tf_op jit(solution)/shard_map/ppermute | solution.py:170
  17.4 0.5 %collective-permute-start.6 = (bf16[64,256]{1,0:T(8,128)(2,1)S(1)}, bf16[64,256]{1,0:T(8,128)(2,1)S(1)}, u32[]{:S(2)}, u32[]{:S(2)}) collective-permute-start(bf16[64,256]{1,0:T(8,128)(2,1)S(1)} %get-tuple-element.51), channel_id=1, source_target_pairs={{0,4},{4,0},{8,12},{12,8},{16,20},{20,16},{24,28},{28,24},{1,5},{5... | collective-permute-start | bytes 98312 | tf_op jit(solution)/shard_map/ppermute | solution.py:170
  17.8 3.3 %shard_map.87 = (f32[64,1280]{1,0:T(8,128)}, f32[1,1280]{1,0:T(1,128)}) custom-call(f32[72,1536]{1,0:T(8,128)S(1)} %convert_add_fusion.refs_0_, bf16[80,1280]{1,0:T(8,128)(2,1)S(1)} %get-tuple-element.52.refs_1_, bf16[80,1024]{1,0:T(8,128)(2,1)S(1)} %get-tuple-element.44.refs_2_, ...), custom_call_target="tpu_custom_call", output_to_operand_aliasing={{0}: (4, {}), {1}: (5, {})} | custom-call | flops 201326592 | bytes 1572864 | tf_op jit(solution)/shard_map/pallas_call | solution.py:204
  21.1 0.0 collective-permute-done.8
  21.1 0.0 collective-permute-done.7
  21.1 0.1 collective-permute-done.6
  21.4 2.7 %collective-permute-start.9 = (f16[72,256]{1,0:T(8,128)(2,1)S(1)}, f16[72,256]{1,0:T(8,128)(2,1)S(1)}, u32[]{:S(2)}, u32[]{:S(2)}) collective-permute-start(f16[72,256]{1,0:T(8,128)(2,1)S(1)} %pad_maximum_fusion), channel_id=1, source_target_pairs={{0,16},{4,20},{8,24},{12,28},{16,0},{20,4},{24,8},{28,12},{1,17},{... | collective-permute-start | bytes 110600 | tf_op jit(solution)/shard_map/ppermute | solution.py:170
  24.1 2.3 %collective-permute-done.9 = f16[72,256]{1,0:T(8,128)(2,1)S(1)} collective-permute-done((f16[72,256]{1,0:T(8,128)(2,1)S(1)}, f16[72,256]{1,0:T(8,128)(2,1)S(1)}, u32[]{:S(2)}, u32[]{:S(2)}) %collective-permute-start.9) | collective-permute-done | bytes 36896 | tf_op jit(solution)/shard_map/ppermute | solution.py:170
  26.3 0.7 %multiply_add_fusion = f32[64,256]{1,0:T(8,128)} fusion(f16[72,256]{1,0:T(8,128)(2,1)S(1)} %pad_maximum_fusion, f32[256]{0:T(256)S(1)} %bitcast.13, f16[72,256]{1,0:T(8,128)(2,1)S(1)} %collective-permute-done.9, f32[256]{0:T(256)S(1)} %bitcast.12), kind=kLoop, calls=%fused_computation.1 | loop fusion | flops 81920 | bytes 133120 | tf_op jit(solution)/shard_map/add | solution.py:241
  (9 shorter events, 0.1 us)
Async XLA Ops:
  0.6 5.1 %collective-permute-start = (bf16[64,256]{1,0:T(8,128)(2,1)}, bf16[64,256]{1,0:T(8,128)(2,1)S(1)}, u32[]{:S(2)}, u32[]{:S(2)}) collective-permute-start(bf16[64,256]{1,0:T(8,128)(2,1)} %param.7), channel_id=1, source_target_pairs={{0,2},{1,3},{2,0},{3,1},{4,6},{5,7},{6,4},{7,5},{8,10},{9,11},{10,... | collective-permute-start | bytes 98312 | tf_op jit(solution)/shard_map/ppermute | solution.py:170
  3.7 3.6 %collective-permute-start.2 = (bf16[64,256]{1,0:T(8,128)(2,1)}, bf16[64,256]{1,0:T(8,128)(2,1)S(1)}, u32[]{:S(2)}, u32[]{:S(2)}) collective-permute-start(bf16[64,256]{1,0:T(8,128)(2,1)} %param.7), channel_id=1, source_target_pairs={{0,3},{1,2},{2,1},{3,0},{4,7},{5,6},{6,5},{7,4},{8,11},{9,10},{10,... | collective-permute-start | bytes 98312 | tf_op jit(solution)/shard_map/ppermute | solution.py:170
  3.7 3.6 %collective-permute-start.1 = (bf16[64,256]{1,0:T(8,128)(2,1)}, bf16[64,256]{1,0:T(8,128)(2,1)S(1)}, u32[]{:S(2)}, u32[]{:S(2)}) collective-permute-start(bf16[64,256]{1,0:T(8,128)(2,1)} %param.7), channel_id=1, source_target_pairs={{0,1},{1,0},{2,3},{3,2},{4,5},{5,4},{6,7},{7,6},{8,9},{9,8},{10,11... | collective-permute-start | bytes 98312 | tf_op jit(solution)/shard_map/ppermute | solution.py:170
  9.8 4.5 %collective-permute-start.5 = (f32[64,256]{1,0:T(8,128)S(1)}, f32[64,256]{1,0:T(8,128)S(1)}, u32[]{:S(2)}, u32[]{:S(2)}) collective-permute-start(f32[64,256]{1,0:T(8,128)S(1)} %get-tuple-element.42), channel_id=1, source_target_pairs={{0,1},{1,0},{2,3},{3,2},{4,5},{5,4},{6,7},{7,6},{8,9},{9,8},{10,11... | collective-permute-start | bytes 196616 | tf_op jit(solution)/shard_map/ppermute | solution.py:170
  9.8 4.4 %collective-permute-start.3 = (bf16[64,256]{1,0:T(8,128)(2,1)S(1)}, bf16[64,256]{1,0:T(8,128)(2,1)S(1)}, u32[]{:S(2)}, u32[]{:S(2)}) collective-permute-start(bf16[64,256]{1,0:T(8,128)(2,1)S(1)} %get-tuple-element.40), channel_id=1, source_target_pairs={{0,2},{1,3},{2,0},{3,1},{4,6},{5,7},{6,4},{7,5},{8,10},{9,11},{10,... | collective-permute-start | bytes 98312 | tf_op jit(solution)/shard_map/ppermute | solution.py:170
  10.5 3.8 %collective-permute-start.4 = (bf16[64,256]{1,0:T(8,128)(2,1)S(1)}, bf16[64,256]{1,0:T(8,128)(2,1)S(1)}, u32[]{:S(2)}, u32[]{:S(2)}) collective-permute-start(bf16[64,256]{1,0:T(8,128)(2,1)S(1)} %get-tuple-element.41), channel_id=1, source_target_pairs={{0,3},{1,2},{2,1},{3,0},{4,7},{5,6},{6,5},{7,4},{8,11},{9,10},{10,... | collective-permute-start | bytes 98312 | tf_op jit(solution)/shard_map/ppermute | solution.py:170
  14.3 6.8 %collective-permute-start.8 = (bf16[64,256]{1,0:T(8,128)(2,1)S(1)}, bf16[64,256]{1,0:T(8,128)(2,1)S(1)}, u32[]{:S(2)}, u32[]{:S(2)}) collective-permute-start(bf16[64,256]{1,0:T(8,128)(2,1)S(1)} %get-tuple-element.51), channel_id=1, source_target_pairs={{0,12},{4,8},{8,4},{12,0},{16,28},{20,24},{24,20},{28,16},{1,13},{... | collective-permute-start | bytes 98312 | tf_op jit(solution)/shard_map/ppermute | solution.py:170
  16.9 4.2 %collective-permute-start.7 = (bf16[64,256]{1,0:T(8,128)(2,1)S(1)}, bf16[64,256]{1,0:T(8,128)(2,1)S(1)}, u32[]{:S(2)}, u32[]{:S(2)}) collective-permute-start(bf16[64,256]{1,0:T(8,128)(2,1)S(1)} %get-tuple-element.51), channel_id=1, source_target_pairs={{0,8},{4,12},{8,0},{12,4},{16,24},{20,28},{24,16},{28,20},{1,9},{5... | collective-permute-start | bytes 98312 | tf_op jit(solution)/shard_map/ppermute | solution.py:170
  17.4 3.9 %collective-permute-start.6 = (bf16[64,256]{1,0:T(8,128)(2,1)S(1)}, bf16[64,256]{1,0:T(8,128)(2,1)S(1)}, u32[]{:S(2)}, u32[]{:S(2)}) collective-permute-start(bf16[64,256]{1,0:T(8,128)(2,1)S(1)} %get-tuple-element.51), channel_id=1, source_target_pairs={{0,4},{4,0},{8,12},{12,8},{16,20},{20,16},{24,28},{28,24},{1,5},{5... | collective-permute-start | bytes 98312 | tf_op jit(solution)/shard_map/ppermute | solution.py:170
  21.4 4.9 %collective-permute-start.9 = (f16[72,256]{1,0:T(8,128)(2,1)S(1)}, f16[72,256]{1,0:T(8,128)(2,1)S(1)}, u32[]{:S(2)}, u32[]{:S(2)}) collective-permute-start(f16[72,256]{1,0:T(8,128)(2,1)S(1)} %pad_maximum_fusion), channel_id=1, source_target_pairs={{0,16},{4,20},{8,24},{12,28},{16,0},{20,4},{24,8},{28,12},{1,17},{... | collective-permute-start | bytes 110600 | tf_op jit(solution)/shard_map/ppermute | solution.py:170

commit v27 on v26

--- a/solution.py
+++ b/solution.py
@@ -179,7 +179,7 @@
     pack = pack + jnp.pad(latents, ((0, 8), (neurons, 0))).astype(F32)
 
     *outs, load_ext, shifted = pl.pallas_call(
-        functools.partial(shift_kernel, neuron_count, order, "neuron", chunk, step),
+        functools.partial(shift_kernel, neuron_count, order, "neuron", chunk, 2 * step),
         out_shape=[jax.ShapeDtypeStruct((lats, width), BF16 if k > 1 else F32) for k in range(neuron_count)]
         + [jax.ShapeDtypeStruct((lats + EXTRA, neurons), BF16), jax.ShapeDtypeStruct((lats + EXTRA, total), BF16)],
         in_specs=[vmem, hbm] + [vmem] * (neuron_count - 1),
@@ -222,7 +222,7 @@
         return before, out
 
     outs, made = make(outs)
-    arrived = [swap(outs[k], "neuron", neuron_count, k) for k in [*range(2, neuron_count), 1]]
+    arrived = [swap(outs[k], "neuron", neuron_count, k) for k in range(neuron_count - 1, 0, -1)]
     arrived, made = lax.optimization_barrier((arrived, made))
     value = functools.reduce(jnp.add, [outs[0]] + [block.astype(F32) for block in arrived])
     mask = 1

time: 27.2 us -> 27.5 us (1.011)
    ppermute x10, starting transfers between devices: 11.4 us -> 11.6 us  [swap(): return lax.ppermute(value, axis, [(i, i ^ mask) for i in range(count)])]
where the time goes in v27:
time: 27.5 us; the launch traced here: 27.3 us
  starting transfers between devices  11.6 us (42%)
  Pallas kernels  8.24 us (30%)
  waiting for transfers between devices  4.15 us (15%)
  other arithmetic  1.86 us (7%)
  between operations  1.39 us (5%)
    ppermute x10, starting transfers between devices, swap(): return lax.ppermute(value, axis, [(i, i ^ mask) for i in range(count)])  11.6 us
    pallas_call x2, Pallas kernels, make(): pl.pallas_call(functools.partial(load_kernel, lats, first, chunk, step),...  5.79 us
    ppermute x10, waiting for transfers between devices, swap(): return lax.ppermute(value, axis, [(i, i ^ mask) for i in range(count)])  4.15 us
    pallas_call x1, Pallas kernels, per_device(): pl.pallas_call(functools.partial(shift_kernel, neuron_count, order, 'neur...  2.45 us
    add x1, other arithmetic, per_device(): pack = pack + jnp.pad(latents, ((0, 8), (neurons, 0))).astype(F32)  1.07 us
    add x1, other arithmetic, per_device(): value = value + read(arrived[0])  0.65 us
  transfers between devices with their start and end apart: 10, of which 4 were waited for; matrix products, arithmetic and copies ran while one was open for 4% of the time, Pallas kernels for 21%

profile of v27, /device:TPU:0, one launch (start us, length us, event | category | flops | bytes accessed | tf_op | source)
XLA Modules:
  0.0 27.3 jit_solution(16265747167137043341)
XLA Ops:
  0.6 3.0 %collective-permute-start = (bf16[64,256]{1,0:T(8,128)(2,1)}, bf16[64,256]{1,0:T(8,128)(2,1)S(1)}, u32[]{:S(2)}, u32[]{:S(2)}) collective-permute-start(bf16[64,256]{1,0:T(8,128)(2,1)} %param.7), channel_id=1, source_target_pairs={{0,2},{1,3},{2,0},{3,1},{4,6},{5,7},{6,4},{7,5},{8,10},{9,11},{10,... | collective-permute-start | bytes 98312 | tf_op jit(solution)/shard_map/ppermute | solution.py:170
  3.7 0.0 collective-permute-start.2
  3.7 0.2 collective-permute-start.1
  4.5 1.1 %convert_add_fusion.refs_0_ = f32[72,1536]{1,0:T(8,128)S(1)} fusion(s32[1,64]{1,0:T(1,128)} %param.10, f32[1,1280]{1,0:T(1,128)} %param.9, bf16[64,256]{1,0:T(8,128)(2,1)} %param.7, bf16[64,1280]{1,0:T(8,128)(2,1)} %bitcast.11, s32[]{:T(128)} %bitcast.6, pred[72]{0:T(512)(128)(4,1)S(1)} %iota_compare_fusion), kind=kLoop, calls=%fused_computation | loop fusion | flops 774144 | bytes 644428 | tf_op jit(solution)/shard_map/add | solution.py:179
  5.6 0.2 collective-permute-done.refs_2_
  5.8 1.5 %collective-permute-done.2.refs_4_ = bf16[64,256]{1,0:T(8,128)(2,1)S(1)} collective-permute-done((bf16[64,256]{1,0:T(8,128)(2,1)}, bf16[64,256]{1,0:T(8,128)(2,1)S(1)}, u32[]{:S(2)}, u32[]{:S(2)}) %collective-permute-start.2) | collective-permute-done | bytes 32800 | tf_op jit(solution)/shard_map/ppermute | solution.py:170
  7.3 0.0 collective-permute-done.1.refs_3_
  7.3 2.4 %shard_map.85 = (f32[64,256]{1,0:T(8,128)S(1)}, f32[64,256]{1,0:T(8,128)S(1)}, bf16[64,256]{1,0:T(8,128)(2,1)S(1)}, bf16[64,256]{1,0:T(8,128)(2,1)S(1)}, bf16[80...) custom-call(f32[72,1536]{1,0:T(8,128)S(1)} %convert_add_fusion.refs_0_, bf16[1280,1024]{1,0:T(8,128)(2,1)} %bitcast.7, ...), custom_call_target="tpu_custom_call" | custom-call | tf_op jit(solution)/shard_map/pallas_call | solution.py:181
  9.8 0.1 collective-permute-start.5
  9.8 0.6 %collective-permute-start.3 = (bf16[64,256]{1,0:T(8,128)(2,1)S(1)}, bf16[64,256]{1,0:T(8,128)(2,1)S(1)}, u32[]{:S(2)}, u32[]{:S(2)}) collective-permute-start(bf16[64,256]{1,0:T(8,128)(2,1)S(1)} %get-tuple-element.40), channel_id=1, source_target_pairs={{0,3},{1,2},{2,1},{3,0},{4,7},{5,6},{6,5},{7,4},{8,11},{9,10},{10,... | collective-permute-start | bytes 98312 | tf_op jit(solution)/shard_map/ppermute | solution.py:170
  10.4 1.5 %collective-permute-start.4 = (bf16[64,256]{1,0:T(8,128)(2,1)S(1)}, bf16[64,256]{1,0:T(8,128)(2,1)S(1)}, u32[]{:S(2)}, u32[]{:S(2)}) collective-permute-start(bf16[64,256]{1,0:T(8,128)(2,1)S(1)} %get-tuple-element.41), channel_id=1, source_target_pairs={{0,2},{1,3},{2,0},{3,1},{4,6},{5,7},{6,4},{7,5},{8,10},{9,11},{10,... | collective-permute-start | bytes 98312 | tf_op jit(solution)/shard_map/ppermute | solution.py:170
  12.0 2.5 %shard_map.86 = (f32[64,1280]{1,0:T(8,128)}, f32[1,1280]{1,0:T(1,128)}) custom-call(f32[72,1536]{1,0:T(8,128)S(1)} %convert_add_fusion.refs_0_, bf16[80,1280]{1,0:T(8,128)(2,1)S(1)} %get-tuple-element.52.refs_1_, bf16[80,1024]{1,0:T(8,128)(2,1)S(1)} %get-tuple-element.44.refs_2_, bf16[1280,1024]{1,0:T(8,128)(2,1)} %bitcast.8), custom_call_target="tpu_custom_call" | custom-call | flops 134217728 | bytes 1048576 | tf_op jit(solution)/shard_map/pallas_call | solution.py:204
  14.5 0.0 collective-permute-done.3
  14.5 0.0 collective-permute-done.4
  14.5 0.0 collective-permute-done.5
  14.6 2.7 %collective-permute-start.8 = (bf16[64,256]{1,0:T(8,128)(2,1)S(1)}, bf16[64,256]{1,0:T(8,128)(2,1)S(1)}, u32[]{:S(2)}, u32[]{:S(2)}) collective-permute-start(bf16[64,256]{1,0:T(8,128)(2,1)S(1)} %get-tuple-element.51), channel_id=1, source_target_pairs={{0,12},{4,8},{8,4},{12,0},{16,28},{20,24},{24,20},{28,16},{1,13},{... | collective-permute-start | bytes 98312 | tf_op jit(solution)/shard_map/ppermute | solution.py:170
  17.2 0.4 %collective-permute-start.7 = (bf16[64,256]{1,0:T(8,128)(2,1)S(1)}, bf16[64,256]{1,0:T(8,128)(2,1)S(1)}, u32[]{:S(2)}, u32[]{:S(2)}) collective-permute-start(bf16[64,256]{1,0:T(8,128)(2,1)S(1)} %get-tuple-element.51), channel_id=1, source_target_pairs={{0,8},{4,12},{8,0},{12,4},{16,24},{20,28},{24,16},{28,20},{1,9},{5... | collective-permute-start | bytes 98312 | tf_op jit(solution)/shard_map/ppermute | solution.py:170
  17.7 0.5 %collective-permute-start.6 = (bf16[64,256]{1,0:T(8,128)(2,1)S(1)}, bf16[64,256]{1,0:T(8,128)(2,1)S(1)}, u32[]{:S(2)}, u32[]{:S(2)}) collective-permute-start(bf16[64,256]{1,0:T(8,128)(2,1)S(1)} %get-tuple-element.51), channel_id=1, source_target_pairs={{0,4},{4,0},{8,12},{12,8},{16,20},{20,16},{24,28},{28,24},{1,5},{5... | collective-permute-start | bytes 98312 | tf_op jit(solution)/shard_map/ppermute | solution.py:170
  18.1 3.3 %shard_map.87 = (f32[64,1280]{1,0:T(8,128)}, f32[1,1280]{1,0:T(1,128)}) custom-call(f32[72,1536]{1,0:T(8,128)S(1)} %convert_add_fusion.refs_0_, bf16[80,1280]{1,0:T(8,128)(2,1)S(1)} %get-tuple-element.52.refs_1_, bf16[80,1024]{1,0:T(8,128)(2,1)S(1)} %get-tuple-element.44.refs_2_, ...), custom_call_target="tpu_custom_call", output_to_operand_aliasing={{0}: (4, {}), {1}: (5, {})} | custom-call | flops 201326592 | bytes 1572864 | tf_op jit(solution)/shard_map/pallas_call | solution.py:204
  21.4 0.0 collective-permute-done.8
  21.4 0.0 collective-permute-done.7
  21.4 0.2 collective-permute-done.6
  21.7 2.7 %collective-permute-start.9 = (f16[72,256]{1,0:T(8,128)(2,1)S(1)}, f16[72,256]{1,0:T(8,128)(2,1)S(1)}, u32[]{:S(2)}, u32[]{:S(2)}) collective-permute-start(f16[72,256]{1,0:T(8,128)(2,1)S(1)} %pad_maximum_fusion), channel_id=1, source_target_pairs={{0,16},{4,20},{8,24},{12,28},{16,0},{20,4},{24,8},{28,12},{1,17},{... | collective-permute-start | bytes 110600 | tf_op jit(solution)/shard_map/ppermute | solution.py:170
  24.4 2.3 %collective-permute-done.9 = f16[72,256]{1,0:T(8,128)(2,1)S(1)} collective-permute-done((f16[72,256]{1,0:T(8,128)(2,1)S(1)}, f16[72,256]{1,0:T(8,128)(2,1)S(1)}, u32[]{:S(2)}, u32[]{:S(2)}) %collective-permute-start.9) | collective-permute-done | bytes 36896 | tf_op jit(solution)/shard_map/ppermute | solution.py:170
  26.6 0.7 %multiply_add_fusion = f32[64,256]{1,0:T(8,128)} fusion(f16[72,256]{1,0:T(8,128)(2,1)S(1)} %pad_maximum_fusion, f32[256]{0:T(256)S(1)} %bitcast.13, f16[72,256]{1,0:T(8,128)(2,1)S(1)} %collective-permute-done.9, f32[256]{0:T(256)S(1)} %bitcast.12), kind=kLoop, calls=%fused_computation.1 | loop fusion | flops 81920 | bytes 133120 | tf_op jit(solution)/shard_map/add | solution.py:241
  (9 shorter events, 0.1 us)
Async XLA Ops:
  0.6 5.1 %collective-permute-start = (bf16[64,256]{1,0:T(8,128)(2,1)}, bf16[64,256]{1,0:T(8,128)(2,1)S(1)}, u32[]{:S(2)}, u32[]{:S(2)}) collective-permute-start(bf16[64,256]{1,0:T(8,128)(2,1)} %param.7), channel_id=1, source_target_pairs={{0,2},{1,3},{2,0},{3,1},{4,6},{5,7},{6,4},{7,5},{8,10},{9,11},{10,... | collective-permute-start | bytes 98312 | tf_op jit(solution)/shard_map/ppermute | solution.py:170
  3.7 3.6 %collective-permute-start.2 = (bf16[64,256]{1,0:T(8,128)(2,1)}, bf16[64,256]{1,0:T(8,128)(2,1)S(1)}, u32[]{:S(2)}, u32[]{:S(2)}) collective-permute-start(bf16[64,256]{1,0:T(8,128)(2,1)} %param.7), channel_id=1, source_target_pairs={{0,3},{1,2},{2,1},{3,0},{4,7},{5,6},{6,5},{7,4},{8,11},{9,10},{10,... | collective-permute-start | bytes 98312 | tf_op jit(solution)/shard_map/ppermute | solution.py:170
  3.7 3.6 %collective-permute-start.1 = (bf16[64,256]{1,0:T(8,128)(2,1)}, bf16[64,256]{1,0:T(8,128)(2,1)S(1)}, u32[]{:S(2)}, u32[]{:S(2)}) collective-permute-start(bf16[64,256]{1,0:T(8,128)(2,1)} %param.7), channel_id=1, source_target_pairs={{0,1},{1,0},{2,3},{3,2},{4,5},{5,4},{6,7},{7,6},{8,9},{9,8},{10,11... | collective-permute-start | bytes 98312 | tf_op jit(solution)/shard_map/ppermute | solution.py:170
  9.8 4.8 %collective-permute-start.5 = (f32[64,256]{1,0:T(8,128)S(1)}, f32[64,256]{1,0:T(8,128)S(1)}, u32[]{:S(2)}, u32[]{:S(2)}) collective-permute-start(f32[64,256]{1,0:T(8,128)S(1)} %get-tuple-element.42), channel_id=1, source_target_pairs={{0,1},{1,0},{2,3},{3,2},{4,5},{5,4},{6,7},{7,6},{8,9},{9,8},{10,11... | collective-permute-start | bytes 196616 | tf_op jit(solution)/shard_map/ppermute | solution.py:170
  9.8 4.7 %collective-permute-start.3 = (bf16[64,256]{1,0:T(8,128)(2,1)S(1)}, bf16[64,256]{1,0:T(8,128)(2,1)S(1)}, u32[]{:S(2)}, u32[]{:S(2)}) collective-permute-start(bf16[64,256]{1,0:T(8,128)(2,1)S(1)} %get-tuple-element.40), channel_id=1, source_target_pairs={{0,3},{1,2},{2,1},{3,0},{4,7},{5,6},{6,5},{7,4},{8,11},{9,10},{10,... | collective-permute-start | bytes 98312 | tf_op jit(solution)/shard_map/ppermute | solution.py:170
  10.4 4.1 %collective-permute-start.4 = (bf16[64,256]{1,0:T(8,128)(2,1)S(1)}, bf16[64,256]{1,0:T(8,128)(2,1)S(1)}, u32[]{:S(2)}, u32[]{:S(2)}) collective-permute-start(bf16[64,256]{1,0:T(8,128)(2,1)S(1)} %get-tuple-element.41), channel_id=1, source_target_pairs={{0,2},{1,3},{2,0},{3,1},{4,6},{5,7},{6,4},{7,5},{8,10},{9,11},{10,... | collective-permute-start | bytes 98312 | tf_op jit(solution)/shard_map/ppermute | solution.py:170
  14.6 6.8 %collective-permute-start.8 = (bf16[64,256]{1,0:T(8,128)(2,1)S(1)}, bf16[64,256]{1,0:T(8,128)(2,1)S(1)}, u32[]{:S(2)}, u32[]{:S(2)}) collective-permute-start(bf16[64,256]{1,0:T(8,128)(2,1)S(1)} %get-tuple-element.51), channel_id=1, source_target_pairs={{0,12},{4,8},{8,4},{12,0},{16,28},{20,24},{24,20},{28,16},{1,13},{... | collective-permute-start | bytes 98312 | tf_op jit(solution)/shard_map/ppermute | solution.py:170
  17.2 4.2 %collective-permute-start.7 = (bf16[64,256]{1,0:T(8,128)(2,1)S(1)}, bf16[64,256]{1,0:T(8,128)(2,1)S(1)}, u32[]{:S(2)}, u32[]{:S(2)}) collective-permute-start(bf16[64,256]{1,0:T(8,128)(2,1)S(1)} %get-tuple-element.51), channel_id=1, source_target_pairs={{0,8},{4,12},{8,0},{12,4},{16,24},{20,28},{24,16},{28,20},{1,9},{5... | collective-permute-start | bytes 98312 | tf_op jit(solution)/shard_map/ppermute | solution.py:170
  17.7 3.9 %collective-permute-start.6 = (bf16[64,256]{1,0:T(8,128)(2,1)S(1)}, bf16[64,256]{1,0:T(8,128)(2,1)S(1)}, u32[]{:S(2)}, u32[]{:S(2)}) collective-permute-start(bf16[64,256]{1,0:T(8,128)(2,1)S(1)} %get-tuple-element.51), channel_id=1, source_target_pairs={{0,4},{4,0},{8,12},{12,8},{16,20},{20,16},{24,28},{28,24},{1,5},{5... | collective-permute-start | bytes 98312 | tf_op jit(solution)/shard_map/ppermute | solution.py:170
  21.7 4.9 %collective-permute-start.9 = (f16[72,256]{1,0:T(8,128)(2,1)S(1)}, f16[72,256]{1,0:T(8,128)(2,1)S(1)}, u32[]{:S(2)}, u32[]{:S(2)}) collective-permute-start(f16[72,256]{1,0:T(8,128)(2,1)S(1)} %pad_maximum_fusion), channel_id=1, source_target_pairs={{0,16},{4,20},{8,24},{12,28},{16,0},{20,4},{24,8},{28,12},{1,17},{... | collective-permute-start | bytes 110600 | tf_op jit(solution)/shard_map/ppermute | solution.py:170

commit v28 on v26

--- a/solution.py
+++ b/solution.py
@@ -236,8 +236,9 @@
             value = decode(sent)
         if shares:
             (value, sent), made = make((value, sent))
-        arrived = [swap(sent, "region", region_count, k) for k in masks]
+        arrived = [swap(sent, "region", region_count, k) for k in masks[::-1]]
         arrived, made = lax.optimization_barrier((arrived, made))
+        arrived = arrived[::-1]
         value = value + read(arrived[0])
         if len(masks) == 3:
             value = value + (read(arrived[1]) + read(arrived[2]))

time: 27.2 us -> 28.6 us (1.051)
  waiting for transfers between devices: 4.13 us -> 5.46 us
    ppermute x10, waiting for transfers between devices: 4.13 us -> 5.46 us  [swap(): return lax.ppermute(value, axis, [(i, i ^ mask) for i in range(count)])]
  transfers between devices with their start and end apart: 10 -> 10, of which waited for: 4 -> 4; matrix products, arithmetic and copies ran while one was open for 4% -> 4% of each run, Pallas kernels for 21% -> 20%
where the time goes in v28:
time: 28.6 us; the launch traced here: 28.3 us
  starting transfers between devices  11.4 us (40%)
  Pallas kernels  8.24 us (29%)
  waiting for transfers between devices  5.46 us (19%)
  other arithmetic  1.86 us (7%)
  between operations  1.39 us (5%)
    ppermute x10, starting transfers between devices, swap(): return lax.ppermute(value, axis, [(i, i ^ mask) for i in range(count)])  11.4 us
    pallas_call x2, Pallas kernels, make(): pl.pallas_call(functools.partial(load_kernel, lats, first, chunk, step),...  5.8 us
    ppermute x10, waiting for transfers between devices, swap(): return lax.ppermute(value, axis, [(i, i ^ mask) for i in range(count)])  5.46 us
    pallas_call x1, Pallas kernels, per_device(): pl.pallas_call(functools.partial(shift_kernel, neuron_count, order, 'neur...  2.45 us
    add x1, other arithmetic, per_device(): pack = pack + jnp.pad(latents, ((0, 8), (neurons, 0))).astype(F32)  1.07 us
    add x1, other arithmetic, per_device(): value = value + read(arrived[0])  0.65 us
  transfers between devices with their start and end apart: 10, of which 4 were waited for; matrix products, arithmetic and copies ran while one was open for 4% of the time, Pallas kernels for 20%

profile of v28, /device:TPU:0, one launch (start us, length us, event | category | flops | bytes accessed | tf_op | source)
XLA Modules:
  0.0 28.3 jit_solution(1080206947882611500)
XLA Ops:
  0.6 3.0 %collective-permute-start = (bf16[64,256]{1,0:T(8,128)(2,1)}, bf16[64,256]{1,0:T(8,128)(2,1)S(1)}, u32[]{:S(2)}, u32[]{:S(2)}) collective-permute-start(bf16[64,256]{1,0:T(8,128)(2,1)} %param.7), channel_id=1, source_target_pairs={{0,2},{1,3},{2,0},{3,1},{4,6},{5,7},{6,4},{7,5},{8,10},{9,11},{10,... | collective-permute-start | bytes 98312 | tf_op jit(solution)/shard_map/ppermute | solution.py:170
  3.7 0.0 collective-permute-start.2
  3.7 0.2 collective-permute-start.1
  4.5 1.1 %convert_add_fusion.refs_0_ = f32[72,1536]{1,0:T(8,128)S(1)} fusion(s32[1,64]{1,0:T(1,128)} %param.10, f32[1,1280]{1,0:T(1,128)} %param.9, bf16[64,256]{1,0:T(8,128)(2,1)} %param.7, bf16[64,1280]{1,0:T(8,128)(2,1)} %bitcast.11, s32[]{:T(128)} %bitcast.6, pred[72]{0:T(512)(128)(4,1)S(1)} %iota_compare_fusion), kind=kLoop, calls=%fused_computation | loop fusion | flops 774144 | bytes 644428 | tf_op jit(solution)/shard_map/add | solution.py:179
  5.6 0.2 collective-permute-done.refs_2_
  5.8 1.5 %collective-permute-done.2.refs_4_ = bf16[64,256]{1,0:T(8,128)(2,1)S(1)} collective-permute-done((bf16[64,256]{1,0:T(8,128)(2,1)}, bf16[64,256]{1,0:T(8,128)(2,1)S(1)}, u32[]{:S(2)}, u32[]{:S(2)}) %collective-permute-start.2) | collective-permute-done | bytes 32800 | tf_op jit(solution)/shard_map/ppermute | solution.py:170
  7.3 0.0 collective-permute-done.1.refs_3_
  7.3 2.4 %shard_map.85 = (f32[64,256]{1,0:T(8,128)S(1)}, f32[64,256]{1,0:T(8,128)S(1)}, bf16[64,256]{1,0:T(8,128)(2,1)S(1)}, bf16[64,256]{1,0:T(8,128)(2,1)S(1)}, bf16[80...) custom-call(f32[72,1536]{1,0:T(8,128)S(1)} %convert_add_fusion.refs_0_, bf16[1280,1024]{1,0:T(8,128)(2,1)} %bitcast.7, ...), custom_call_target="tpu_custom_call" | custom-call | tf_op jit(solution)/shard_map/pallas_call | solution.py:181
  9.8 0.1 collective-permute-start.5
  9.8 0.7 %collective-permute-start.3 = (bf16[64,256]{1,0:T(8,128)(2,1)S(1)}, bf16[64,256]{1,0:T(8,128)(2,1)S(1)}, u32[]{:S(2)}, u32[]{:S(2)}) collective-permute-start(bf16[64,256]{1,0:T(8,128)(2,1)S(1)} %get-tuple-element.40), channel_id=1, source_target_pairs={{0,2},{1,3},{2,0},{3,1},{4,6},{5,7},{6,4},{7,5},{8,10},{9,11},{10,... | collective-permute-start | bytes 98312 | tf_op jit(solution)/shard_map/ppermute | solution.py:170
  10.5 1.2 %collective-permute-start.4 = (bf16[64,256]{1,0:T(8,128)(2,1)S(1)}, bf16[64,256]{1,0:T(8,128)(2,1)S(1)}, u32[]{:S(2)}, u32[]{:S(2)}) collective-permute-start(bf16[64,256]{1,0:T(8,128)(2,1)S(1)} %get-tuple-element.41), channel_id=1, source_target_pairs={{0,3},{1,2},{2,1},{3,0},{4,7},{5,6},{6,5},{7,4},{8,11},{9,10},{10,... | collective-permute-start | bytes 98312 | tf_op jit(solution)/shard_map/ppermute | solution.py:170
  11.7 2.5 %shard_map.86 = (f32[64,1280]{1,0:T(8,128)}, f32[1,1280]{1,0:T(1,128)}) custom-call(f32[72,1536]{1,0:T(8,128)S(1)} %convert_add_fusion.refs_0_, bf16[80,1280]{1,0:T(8,128)(2,1)S(1)} %get-tuple-element.52.refs_1_, bf16[80,1024]{1,0:T(8,128)(2,1)S(1)} %get-tuple-element.44.refs_2_, bf16[1280,1024]{1,0:T(8,128)(2,1)} %bitcast.8), custom_call_target="tpu_custom_call" | custom-call | flops 134217728 | bytes 1048576 | tf_op jit(solution)/shard_map/pallas_call | solution.py:204
  14.2 0.0 collective-permute-done.3
  14.2 0.0 collective-permute-done.4
  14.3 0.0 collective-permute-done.5
  14.3 1.6 %collective-permute-start.8 = (bf16[64,256]{1,0:T(8,128)(2,1)S(1)}, bf16[64,256]{1,0:T(8,128)(2,1)S(1)}, u32[]{:S(2)}, u32[]{:S(2)}) collective-permute-start(bf16[64,256]{1,0:T(8,128)(2,1)S(1)} %get-tuple-element.51), channel_id=1, source_target_pairs={{0,4},{4,0},{8,12},{12,8},{16,20},{20,16},{24,28},{28,24},{1,5},{5... | collective-permute-start | bytes 98312 | tf_op jit(solution)/shard_map/ppermute | solution.py:170
  15.9 1.6 %collective-permute-start.7 = (bf16[64,256]{1,0:T(8,128)(2,1)S(1)}, bf16[64,256]{1,0:T(8,128)(2,1)S(1)}, u32[]{:S(2)}, u32[]{:S(2)}) collective-permute-start(bf16[64,256]{1,0:T(8,128)(2,1)S(1)} %get-tuple-element.51), channel_id=1, source_target_pairs={{0,8},{4,12},{8,0},{12,4},{16,24},{20,28},{24,16},{28,20},{1,9},{5... | collective-permute-start | bytes 98312 | tf_op jit(solution)/shard_map/ppermute | solution.py:170
  17.5 0.4 %collective-permute-start.6 = (bf16[64,256]{1,0:T(8,128)(2,1)S(1)}, bf16[64,256]{1,0:T(8,128)(2,1)S(1)}, u32[]{:S(2)}, u32[]{:S(2)}) collective-permute-start(bf16[64,256]{1,0:T(8,128)(2,1)S(1)} %get-tuple-element.51), channel_id=1, source_target_pairs={{0,12},{4,8},{8,4},{12,0},{16,28},{20,24},{24,20},{28,16},{1,13},{... | collective-permute-start | bytes 98312 | tf_op jit(solution)/shard_map/ppermute | solution.py:170
  17.8 3.3 %shard_map.87 = (f32[64,1280]{1,0:T(8,128)}, f32[1,1280]{1,0:T(1,128)}) custom-call(f32[72,1536]{1,0:T(8,128)S(1)} %convert_add_fusion.refs_0_, bf16[80,1280]{1,0:T(8,128)(2,1)S(1)} %get-tuple-element.52.refs_1_, bf16[80,1024]{1,0:T(8,128)(2,1)S(1)} %get-tuple-element.44.refs_2_, ...), custom_call_target="tpu_custom_call", output_to_operand_aliasing={{0}: (4, {}), {1}: (5, {})} | custom-call | flops 201326592 | bytes 1572864 | tf_op jit(solution)/shard_map/pallas_call | solution.py:204
  21.1 0.0 collective-permute-done.8
  21.1 0.0 collective-permute-done.7
  21.1 1.2 %collective-permute-done.6 = bf16[64,256]{1,0:T(8,128)(2,1)S(1)} collective-permute-done((bf16[64,256]{1,0:T(8,128)(2,1)S(1)}, bf16[64,256]{1,0:T(8,128)(2,1)S(1)}, u32[]{:S(2)}, u32[]{:S(2)}) %collective-permute-start.6) | collective-permute-done | bytes 32800 | tf_op jit(solution)/shard_map/ppermute | solution.py:170
  22.4 2.7 %collective-permute-start.9 = (f16[72,256]{1,0:T(8,128)(2,1)S(1)}, f16[72,256]{1,0:T(8,128)(2,1)S(1)}, u32[]{:S(2)}, u32[]{:S(2)}) collective-permute-start(f16[72,256]{1,0:T(8,128)(2,1)S(1)} %pad_maximum_fusion), channel_id=1, source_target_pairs={{0,16},{4,20},{8,24},{12,28},{16,0},{20,4},{24,8},{28,12},{1,17},{... | collective-permute-start | bytes 110600 | tf_op jit(solution)/shard_map/ppermute | solution.py:170
  25.1 2.6 %collective-permute-done.9 = f16[72,256]{1,0:T(8,128)(2,1)S(1)} collective-permute-done((f16[72,256]{1,0:T(8,128)(2,1)S(1)}, f16[72,256]{1,0:T(8,128)(2,1)S(1)}, u32[]{:S(2)}, u32[]{:S(2)}) %collective-permute-start.9) | collective-permute-done | bytes 36896 | tf_op jit(solution)/shard_map/ppermute | solution.py:170
  27.7 0.7 %multiply_add_fusion = f32[64,256]{1,0:T(8,128)} fusion(f16[72,256]{1,0:T(8,128)(2,1)S(1)} %pad_maximum_fusion, f32[256]{0:T(256)S(1)} %bitcast.13, f16[72,256]{1,0:T(8,128)(2,1)S(1)} %collective-permute-done.9, f32[256]{0:T(256)S(1)} %bitcast.12), kind=kLoop, calls=%fused_computation.1 | loop fusion | flops 81920 | bytes 133120 | tf_op jit(solution)/shard_map/add | solution.py:242
  (9 shorter events, 0.1 us)
Async XLA Ops:
  0.6 5.1 %collective-permute-start = (bf16[64,256]{1,0:T(8,128)(2,1)}, bf16[64,256]{1,0:T(8,128)(2,1)S(1)}, u32[]{:S(2)}, u32[]{:S(2)}) collective-permute-start(bf16[64,256]{1,0:T(8,128)(2,1)} %param.7), channel_id=1, source_target_pairs={{0,2},{1,3},{2,0},{3,1},{4,6},{5,7},{6,4},{7,5},{8,10},{9,11},{10,... | collective-permute-start | bytes 98312 | tf_op jit(solution)/shard_map/ppermute | solution.py:170
  3.7 3.6 %collective-permute-start.2 = (bf16[64,256]{1,0:T(8,128)(2,1)}, bf16[64,256]{1,0:T(8,128)(2,1)S(1)}, u32[]{:S(2)}, u32[]{:S(2)}) collective-permute-start(bf16[64,256]{1,0:T(8,128)(2,1)} %param.7), channel_id=1, source_target_pairs={{0,3},{1,2},{2,1},{3,0},{4,7},{5,6},{6,5},{7,4},{8,11},{9,10},{10,... | collective-permute-start | bytes 98312 | tf_op jit(solution)/shard_map/ppermute | solution.py:170
  3.7 3.6 %collective-permute-start.1 = (bf16[64,256]{1,0:T(8,128)(2,1)}, bf16[64,256]{1,0:T(8,128)(2,1)S(1)}, u32[]{:S(2)}, u32[]{:S(2)}) collective-permute-start(bf16[64,256]{1,0:T(8,128)(2,1)} %param.7), channel_id=1, source_target_pairs={{0,1},{1,0},{2,3},{3,2},{4,5},{5,4},{6,7},{7,6},{8,9},{9,8},{10,11... | collective-permute-start | bytes 98312 | tf_op jit(solution)/shard_map/ppermute | solution.py:170
  9.8 4.5 %collective-permute-start.5 = (f32[64,256]{1,0:T(8,128)S(1)}, f32[64,256]{1,0:T(8,128)S(1)}, u32[]{:S(2)}, u32[]{:S(2)}) collective-permute-start(f32[64,256]{1,0:T(8,128)S(1)} %get-tuple-element.42), channel_id=1, source_target_pairs={{0,1},{1,0},{2,3},{3,2},{4,5},{5,4},{6,7},{7,6},{8,9},{9,8},{10,11... | collective-permute-start | bytes 196616 | tf_op jit(solution)/shard_map/ppermute | solution.py:170
  9.8 4.4 %collective-permute-start.3 = (bf16[64,256]{1,0:T(8,128)(2,1)S(1)}, bf16[64,256]{1,0:T(8,128)(2,1)S(1)}, u32[]{:S(2)}, u32[]{:S(2)}) collective-permute-start(bf16[64,256]{1,0:T(8,128)(2,1)S(1)} %get-tuple-element.40), channel_id=1, source_target_pairs={{0,2},{1,3},{2,0},{3,1},{4,6},{5,7},{6,4},{7,5},{8,10},{9,11},{10,... | collective-permute-start | bytes 98312 | tf_op jit(solution)/shard_map/ppermute | solution.py:170
  10.5 3.8 %collective-permute-start.4 = (bf16[64,256]{1,0:T(8,128)(2,1)S(1)}, bf16[64,256]{1,0:T(8,128)(2,1)S(1)}, u32[]{:S(2)}, u32[]{:S(2)}) collective-permute-start(bf16[64,256]{1,0:T(8,128)(2,1)S(1)} %get-tuple-element.41), channel_id=1, source_target_pairs={{0,3},{1,2},{2,1},{3,0},{4,7},{5,6},{6,5},{7,4},{8,11},{9,10},{10,... | collective-permute-start | bytes 98312 | tf_op jit(solution)/shard_map/ppermute | solution.py:170
  14.3 6.8 %collective-permute-start.8 = (bf16[64,256]{1,0:T(8,128)(2,1)S(1)}, bf16[64,256]{1,0:T(8,128)(2,1)S(1)}, u32[]{:S(2)}, u32[]{:S(2)}) collective-permute-start(bf16[64,256]{1,0:T(8,128)(2,1)S(1)} %get-tuple-element.51), channel_id=1, source_target_pairs={{0,4},{4,0},{8,12},{12,8},{16,20},{20,16},{24,28},{28,24},{1,5},{5... | collective-permute-start | bytes 98312 | tf_op jit(solution)/shard_map/ppermute | solution.py:170
  15.9 5.2 %collective-permute-start.7 = (bf16[64,256]{1,0:T(8,128)(2,1)S(1)}, bf16[64,256]{1,0:T(8,128)(2,1)S(1)}, u32[]{:S(2)}, u32[]{:S(2)}) collective-permute-start(bf16[64,256]{1,0:T(8,128)(2,1)S(1)} %get-tuple-element.51), channel_id=1, source_target_pairs={{0,8},{4,12},{8,0},{12,4},{16,24},{20,28},{24,16},{28,20},{1,9},{5... | collective-permute-start | bytes 98312 | tf_op jit(solution)/shard_map/ppermute | solution.py:170
  17.5 4.8 %collective-permute-start.6 = (bf16[64,256]{1,0:T(8,128)(2,1)S(1)}, bf16[64,256]{1,0:T(8,128)(2,1)S(1)}, u32[]{:S(2)}, u32[]{:S(2)}) collective-permute-start(bf16[64,256]{1,0:T(8,128)(2,1)S(1)} %get-tuple-element.51), channel_id=1, source_target_pairs={{0,12},{4,8},{8,4},{12,0},{16,28},{20,24},{24,20},{28,16},{1,13},{... | collective-permute-start | bytes 98312 | tf_op jit(solution)/shard_map/ppermute | solution.py:170
  22.4 5.2 %collective-permute-start.9 = (f16[72,256]{1,0:T(8,128)(2,1)S(1)}, f16[72,256]{1,0:T(8,128)(2,1)S(1)}, u32[]{:S(2)}, u32[]{:S(2)}) collective-permute-start(f16[72,256]{1,0:T(8,128)(2,1)S(1)} %pad_maximum_fusion), channel_id=1, source_target_pairs={{0,16},{4,20},{8,24},{12,28},{16,0},{20,4},{24,8},{28,12},{1,17},{... | collective-permute-start | bytes 110600 | tf_op jit(solution)/shard_map/ppermute | solution.py:170

commit v29 on v26

--- a/solution.py
+++ b/solution.py
@@ -169,7 +169,7 @@
     def swap(value, axis, count, mask):
         return lax.ppermute(value, axis, [(i, i ^ mask) for i in range(count)])
 
-    order = sorted(range(1, neuron_count), key=lambda k: (k != 2, k))
+    order = [1, *range(neuron_count - 1, 1, -1)]
     arrived = [swap(latents, "neuron", neuron_count, k) for k in order]
     row = lax.broadcasted_iota(jnp.int32, (lats + 8, neurons + width), 0)
     lines = jnp.pad(delays, ((lats + 1, 6), (0, neurons + width - lats)))
@@ -236,8 +236,10 @@
             value = decode(sent)
         if shares:
             (value, sent), made = make((value, sent))
-        arrived = [swap(sent, "region", region_count, k) for k in masks]
+        turns = sorted(masks, key=lambda k: (k != mask, -k))
+        arrived = [swap(sent, "region", region_count, k) for k in turns]
         arrived, made = lax.optimization_barrier((arrived, made))
+        arrived = [arrived[turns.index(k)] for k in masks]
         value = value + read(arrived[0])
         if len(masks) == 3:
             value = value + (read(arrived[1]) + read(arrived[2]))

time: 27.2 us -> 27.3 us (level)
  transfers between devices with their start and end apart: 10 -> 10, of which waited for: 4 -> 5; matrix products, arithmetic and copies ran while one was open for 4% -> 4% of each run, Pallas kernels for 21% -> 21%
where the time goes in v29:
time: 27.3 us; the launch traced here: 27.1 us
  starting transfers between devices  11.3 us (41%)
  Pallas kernels  8.25 us (30%)
  waiting for transfers between devices  4.28 us (16%)
  other arithmetic  1.86 us (7%)
  between operations  1.37 us (5%)
    ppermute x10, starting transfers between devices, swap(): return lax.ppermute(value, axis, [(i, i ^ mask) for i in range(count)])  11.3 us
    pallas_call x2, Pallas kernels, make(): pl.pallas_call(functools.partial(load_kernel, lats, first, chunk, step),...  5.8 us
    ppermute x10, waiting for transfers between devices, swap(): return lax.ppermute(value, axis, [(i, i ^ mask) for i in range(count)])  4.28 us
    pallas_call x1, Pallas kernels, per_device(): pl.pallas_call(functools.partial(shift_kernel, neuron_count, order, 'neur...  2.45 us
    add x1, other arithmetic, per_device(): pack = pack + jnp.pad(latents, ((0, 8), (neurons, 0))).astype(F32)  1.07 us
    add x1, other arithmetic, per_device(): value = value + read(arrived[0])  0.65 us
  transfers between devices with their start and end apart: 10, of which 5 were waited for; matrix products, arithmetic and copies ran while one was open for 4% of the time, Pallas kernels for 21%

profile of v29, /device:TPU:0, one launch (start us, length us, event | category | flops | bytes accessed | tf_op | source)
XLA Modules:
  0.0 27.1 jit_solution(11020125187169149013)
XLA Ops:
  0.6 0.5 %collective-permute-start = (bf16[64,256]{1,0:T(8,128)(2,1)}, bf16[64,256]{1,0:T(8,128)(2,1)S(1)}, u32[]{:S(2)}, u32[]{:S(2)}) collective-permute-start(bf16[64,256]{1,0:T(8,128)(2,1)} %param.7), channel_id=1, source_target_pairs={{0,1},{1,0},{2,3},{3,2},{4,5},{5,4},{6,7},{7,6},{8,9},{9,8},{10,11... | collective-permute-start | bytes 98312 | tf_op jit(solution)/shard_map/ppermute | solution.py:170
  1.1 2.6 %collective-permute-start.2 = (bf16[64,256]{1,0:T(8,128)(2,1)}, bf16[64,256]{1,0:T(8,128)(2,1)S(1)}, u32[]{:S(2)}, u32[]{:S(2)}) collective-permute-start(bf16[64,256]{1,0:T(8,128)(2,1)} %param.7), channel_id=1, source_target_pairs={{0,2},{1,3},{2,0},{3,1},{4,6},{5,7},{6,4},{7,5},{8,10},{9,11},{10,... | collective-permute-start | bytes 98312 | tf_op jit(solution)/shard_map/ppermute | solution.py:170
  3.7 0.1 collective-permute-start.1
  4.5 1.1 %convert_add_fusion.refs_0_ = f32[72,1536]{1,0:T(8,128)S(1)} fusion(s32[1,64]{1,0:T(1,128)} %param.10, f32[1,1280]{1,0:T(1,128)} %param.9, bf16[64,256]{1,0:T(8,128)(2,1)} %param.7, bf16[64,1280]{1,0:T(8,128)(2,1)} %bitcast.11, s32[]{:T(128)} %bitcast.6, pred[72]{0:T(512)(128)(4,1)S(1)} %iota_compare_fusion), kind=kLoop, calls=%fused_computation | loop fusion | flops 774144 | bytes 644428 | tf_op jit(solution)/shard_map/add | solution.py:179
  5.5 0.0 collective-permute-done.refs_2_
  5.6 0.4 %collective-permute-done.2.refs_4_ = bf16[64,256]{1,0:T(8,128)(2,1)S(1)} collective-permute-done((bf16[64,256]{1,0:T(8,128)(2,1)}, bf16[64,256]{1,0:T(8,128)(2,1)S(1)}, u32[]{:S(2)}, u32[]{:S(2)}) %collective-permute-start.2) | collective-permute-done | bytes 32800 | tf_op jit(solution)/shard_map/ppermute | solution.py:170
  5.9 1.4 %collective-permute-done.1.refs_3_ = bf16[64,256]{1,0:T(8,128)(2,1)S(1)} collective-permute-done((bf16[64,256]{1,0:T(8,128)(2,1)}, bf16[64,256]{1,0:T(8,128)(2,1)S(1)}, u32[]{:S(2)}, u32[]{:S(2)}) %collective-permute-start.1) | collective-permute-done | bytes 32800 | tf_op jit(solution)/shard_map/ppermute | solution.py:170
  7.3 2.5 %shard_map.85 = (f32[64,256]{1,0:T(8,128)S(1)}, f32[64,256]{1,0:T(8,128)S(1)}, bf16[64,256]{1,0:T(8,128)(2,1)S(1)}, bf16[64,256]{1,0:T(8,128)(2,1)S(1)}, bf16[80...) custom-call(f32[72,1536]{1,0:T(8,128)S(1)} %convert_add_fusion.refs_0_, bf16[1280,1024]{1,0:T(8,128)(2,1)} %bitcast.7, ...), custom_call_target="tpu_custom_call" | custom-call | tf_op jit(solution)/shard_map/pallas_call | solution.py:181
  9.8 0.2 collective-permute-start.5
  10.0 0.7 %collective-permute-start.3 = (bf16[64,256]{1,0:T(8,128)(2,1)S(1)}, bf16[64,256]{1,0:T(8,128)(2,1)S(1)}, u32[]{:S(2)}, u32[]{:S(2)}) collective-permute-start(bf16[64,256]{1,0:T(8,128)(2,1)S(1)} %get-tuple-element.40), channel_id=1, source_target_pairs={{0,2},{1,3},{2,0},{3,1},{4,6},{5,7},{6,4},{7,5},{8,10},{9,11},{10,... | collective-permute-start | bytes 98312 | tf_op jit(solution)/shard_map/ppermute | solution.py:170
  10.7 0.9 %collective-permute-start.4 = (bf16[64,256]{1,0:T(8,128)(2,1)S(1)}, bf16[64,256]{1,0:T(8,128)(2,1)S(1)}, u32[]{:S(2)}, u32[]{:S(2)}) collective-permute-start(bf16[64,256]{1,0:T(8,128)(2,1)S(1)} %get-tuple-element.41), channel_id=1, source_target_pairs={{0,3},{1,2},{2,1},{3,0},{4,7},{5,6},{6,5},{7,4},{8,11},{9,10},{10,... | collective-permute-start | bytes 98312 | tf_op jit(solution)/shard_map/ppermute | solution.py:170
  11.7 2.5 %shard_map.86 = (f32[64,1280]{1,0:T(8,128)}, f32[1,1280]{1,0:T(1,128)}) custom-call(f32[72,1536]{1,0:T(8,128)S(1)} %convert_add_fusion.refs_0_, bf16[80,1280]{1,0:T(8,128)(2,1)S(1)} %get-tuple-element.52.refs_1_, bf16[80,1024]{1,0:T(8,128)(2,1)S(1)} %get-tuple-element.44.refs_2_, bf16[1280,1024]{1,0:T(8,128)(2,1)} %bitcast.8), custom_call_target="tpu_custom_call" | custom-call | flops 134217728 | bytes 1048576 | tf_op jit(solution)/shard_map/pallas_call | solution.py:204
  14.2 0.0 collective-permute-done.3
  14.2 0.2 collective-permute-done.4
  14.4 0.0 collective-permute-done.5
  14.5 1.7 %collective-permute-start.8 = (bf16[64,256]{1,0:T(8,128)(2,1)S(1)}, bf16[64,256]{1,0:T(8,128)(2,1)S(1)}, u32[]{:S(2)}, u32[]{:S(2)}) collective-permute-start(bf16[64,256]{1,0:T(8,128)(2,1)S(1)} %get-tuple-element.51), channel_id=1, source_target_pairs={{0,8},{4,12},{8,0},{12,4},{16,24},{20,28},{24,16},{28,20},{1,9},{5... | collective-permute-start | bytes 98312 | tf_op jit(solution)/shard_map/ppermute | solution.py:170
  16.1 1.4 %collective-permute-start.7 = (bf16[64,256]{1,0:T(8,128)(2,1)S(1)}, bf16[64,256]{1,0:T(8,128)(2,1)S(1)}, u32[]{:S(2)}, u32[]{:S(2)}) collective-permute-start(bf16[64,256]{1,0:T(8,128)(2,1)S(1)} %get-tuple-element.51), channel_id=1, source_target_pairs={{0,12},{4,8},{8,4},{12,0},{16,28},{20,24},{24,20},{28,16},{1,13},{... | collective-permute-start | bytes 98312 | tf_op jit(solution)/shard_map/ppermute | solution.py:170
  17.5 0.5 %collective-permute-start.6 = (bf16[64,256]{1,0:T(8,128)(2,1)S(1)}, bf16[64,256]{1,0:T(8,128)(2,1)S(1)}, u32[]{:S(2)}, u32[]{:S(2)}) collective-permute-start(bf16[64,256]{1,0:T(8,128)(2,1)S(1)} %get-tuple-element.51), channel_id=1, source_target_pairs={{0,4},{4,0},{8,12},{12,8},{16,20},{20,16},{24,28},{28,24},{1,5},{5... | collective-permute-start | bytes 98312 | tf_op jit(solution)/shard_map/ppermute | solution.py:170
  18.0 3.3 %shard_map.87 = (f32[64,1280]{1,0:T(8,128)}, f32[1,1280]{1,0:T(1,128)}) custom-call(f32[72,1536]{1,0:T(8,128)S(1)} %convert_add_fusion.refs_0_, bf16[80,1280]{1,0:T(8,128)(2,1)S(1)} %get-tuple-element.52.refs_1_, bf16[80,1024]{1,0:T(8,128)(2,1)S(1)} %get-tuple-element.44.refs_2_, ...), custom_call_target="tpu_custom_call", output_to_operand_aliasing={{0}: (4, {}), {1}: (5, {})} | custom-call | flops 201326592 | bytes 1572864 | tf_op jit(solution)/shard_map/pallas_call | solution.py:204
  21.3 0.0 collective-permute-done.8
  21.3 0.0 collective-permute-done.7
  21.3 0.1 collective-permute-done.6
  21.5 2.7 %collective-permute-start.9 = (f16[72,256]{1,0:T(8,128)(2,1)S(1)}, f16[72,256]{1,0:T(8,128)(2,1)S(1)}, u32[]{:S(2)}, u32[]{:S(2)}) collective-permute-start(f16[72,256]{1,0:T(8,128)(2,1)S(1)} %pad_maximum_fusion), channel_id=1, source_target_pairs={{0,16},{4,20},{8,24},{12,28},{16,0},{20,4},{24,8},{28,12},{1,17},{... | collective-permute-start | bytes 110600 | tf_op jit(solution)/shard_map/ppermute | solution.py:170
  24.2 2.3 %collective-permute-done.9 = f16[72,256]{1,0:T(8,128)(2,1)S(1)} collective-permute-done((f16[72,256]{1,0:T(8,128)(2,1)S(1)}, f16[72,256]{1,0:T(8,128)(2,1)S(1)}, u32[]{:S(2)}, u32[]{:S(2)}) %collective-permute-start.9) | collective-permute-done | bytes 36896 | tf_op jit(solution)/shard_map/ppermute | solution.py:170
  26.4 0.7 %multiply_add_fusion = f32[64,256]{1,0:T(8,128)} fusion(f16[72,256]{1,0:T(8,128)(2,1)S(1)} %pad_maximum_fusion, f32[256]{0:T(256)S(1)} %bitcast.13, f16[72,256]{1,0:T(8,128)(2,1)S(1)} %collective-permute-done.9, f32[256]{0:T(256)S(1)} %bitcast.12), kind=kLoop, calls=%fused_computation.1 | loop fusion | flops 81920 | bytes 133120 | tf_op jit(solution)/shard_map/add | solution.py:243
  (9 shorter events, 0.1 us)
Async XLA Ops:
  0.6 4.9 %collective-permute-start = (bf16[64,256]{1,0:T(8,128)(2,1)}, bf16[64,256]{1,0:T(8,128)(2,1)S(1)}, u32[]{:S(2)}, u32[]{:S(2)}) collective-permute-start(bf16[64,256]{1,0:T(8,128)(2,1)} %param.7), channel_id=1, source_target_pairs={{0,1},{1,0},{2,3},{3,2},{4,5},{5,4},{6,7},{7,6},{8,9},{9,8},{10,11... | collective-permute-start | bytes 98312 | tf_op jit(solution)/shard_map/ppermute | solution.py:170
  1.1 4.8 %collective-permute-start.2 = (bf16[64,256]{1,0:T(8,128)(2,1)}, bf16[64,256]{1,0:T(8,128)(2,1)S(1)}, u32[]{:S(2)}, u32[]{:S(2)}) collective-permute-start(bf16[64,256]{1,0:T(8,128)(2,1)} %param.7), channel_id=1, source_target_pairs={{0,2},{1,3},{2,0},{3,1},{4,6},{5,7},{6,4},{7,5},{8,10},{9,11},{10,... | collective-permute-start | bytes 98312 | tf_op jit(solution)/shard_map/ppermute | solution.py:170
  3.7 3.6 %collective-permute-start.1 = (bf16[64,256]{1,0:T(8,128)(2,1)}, bf16[64,256]{1,0:T(8,128)(2,1)S(1)}, u32[]{:S(2)}, u32[]{:S(2)}) collective-permute-start(bf16[64,256]{1,0:T(8,128)(2,1)} %param.7), channel_id=1, source_target_pairs={{0,3},{1,2},{2,1},{3,0},{4,7},{5,6},{6,5},{7,4},{8,11},{9,10},{10,... | collective-permute-start | bytes 98312 | tf_op jit(solution)/shard_map/ppermute | solution.py:170
  9.8 4.7 %collective-permute-start.5 = (f32[64,256]{1,0:T(8,128)S(1)}, f32[64,256]{1,0:T(8,128)S(1)}, u32[]{:S(2)}, u32[]{:S(2)}) collective-permute-start(f32[64,256]{1,0:T(8,128)S(1)} %get-tuple-element.42), channel_id=1, source_target_pairs={{0,1},{1,0},{2,3},{3,2},{4,5},{5,4},{6,7},{7,6},{8,9},{9,8},{10,11... | collective-permute-start | bytes 196616 | tf_op jit(solution)/shard_map/ppermute | solution.py:170
  10.0 4.2 %collective-permute-start.3 = (bf16[64,256]{1,0:T(8,128)(2,1)S(1)}, bf16[64,256]{1,0:T(8,128)(2,1)S(1)}, u32[]{:S(2)}, u32[]{:S(2)}) collective-permute-start(bf16[64,256]{1,0:T(8,128)(2,1)S(1)} %get-tuple-element.40), channel_id=1, source_target_pairs={{0,2},{1,3},{2,0},{3,1},{4,6},{5,7},{6,4},{7,5},{8,10},{9,11},{10,... | collective-permute-start | bytes 98312 | tf_op jit(solution)/shard_map/ppermute | solution.py:170
  10.7 3.7 %collective-permute-start.4 = (bf16[64,256]{1,0:T(8,128)(2,1)S(1)}, bf16[64,256]{1,0:T(8,128)(2,1)S(1)}, u32[]{:S(2)}, u32[]{:S(2)}) collective-permute-start(bf16[64,256]{1,0:T(8,128)(2,1)S(1)} %get-tuple-element.41), channel_id=1, source_target_pairs={{0,3},{1,2},{2,1},{3,0},{4,7},{5,6},{6,5},{7,4},{8,11},{9,10},{10,... | collective-permute-start | bytes 98312 | tf_op jit(solution)/shard_map/ppermute | solution.py:170
  14.5 6.8 %collective-permute-start.8 = (bf16[64,256]{1,0:T(8,128)(2,1)S(1)}, bf16[64,256]{1,0:T(8,128)(2,1)S(1)}, u32[]{:S(2)}, u32[]{:S(2)}) collective-permute-start(bf16[64,256]{1,0:T(8,128)(2,1)S(1)} %get-tuple-element.51), channel_id=1, source_target_pairs={{0,8},{4,12},{8,0},{12,4},{16,24},{20,28},{24,16},{28,20},{1,9},{5... | collective-permute-start | bytes 98312 | tf_op jit(solution)/shard_map/ppermute | solution.py:170
  16.1 5.2 %collective-permute-start.7 = (bf16[64,256]{1,0:T(8,128)(2,1)S(1)}, bf16[64,256]{1,0:T(8,128)(2,1)S(1)}, u32[]{:S(2)}, u32[]{:S(2)}) collective-permute-start(bf16[64,256]{1,0:T(8,128)(2,1)S(1)} %get-tuple-element.51), channel_id=1, source_target_pairs={{0,12},{4,8},{8,4},{12,0},{16,28},{20,24},{24,20},{28,16},{1,13},{... | collective-permute-start | bytes 98312 | tf_op jit(solution)/shard_map/ppermute | solution.py:170
  17.5 3.9 %collective-permute-start.6 = (bf16[64,256]{1,0:T(8,128)(2,1)S(1)}, bf16[64,256]{1,0:T(8,128)(2,1)S(1)}, u32[]{:S(2)}, u32[]{:S(2)}) collective-permute-start(bf16[64,256]{1,0:T(8,128)(2,1)S(1)} %get-tuple-element.51), channel_id=1, source_target_pairs={{0,4},{4,0},{8,12},{12,8},{16,20},{20,16},{24,28},{28,24},{1,5},{5... | collective-permute-start | bytes 98312 | tf_op jit(solution)/shard_map/ppermute | solution.py:170
  21.5 4.9 %collective-permute-start.9 = (f16[72,256]{1,0:T(8,128)(2,1)S(1)}, f16[72,256]{1,0:T(8,128)(2,1)S(1)}, u32[]{:S(2)}, u32[]{:S(2)}) collective-permute-start(f16[72,256]{1,0:T(8,128)(2,1)S(1)} %pad_maximum_fusion), channel_id=1, source_target_pairs={{0,16},{4,20},{8,24},{12,28},{16,0},{20,4},{24,8},{28,12},{1,17},{... | collective-permute-start | bytes 110600 | tf_op jit(solution)/shard_map/ppermute | solution.py:170

commit v30 on v29

--- a/solution.py
+++ b/solution.py
@@ -180,7 +180,7 @@
 
     *outs, load_ext, shifted = pl.pallas_call(
         functools.partial(shift_kernel, neuron_count, order, "neuron", chunk, step),
-        out_shape=[jax.ShapeDtypeStruct((lats, width), BF16 if k > 1 else F32) for k in range(neuron_count)]
+        out_shape=[jax.ShapeDtypeStruct((lats, width), BF16 if k else F32) for k in range(neuron_count)]
         + [jax.ShapeDtypeStruct((lats + EXTRA, neurons), BF16), jax.ShapeDtypeStruct((lats + EXTRA, total), BF16)],
         in_specs=[vmem, hbm] + [vmem] * (neuron_count - 1),
         out_specs=[vmem] * (neuron_count + 2),
@@ -222,7 +222,7 @@
         return before, out
 
     outs, made = make(outs)
-    arrived = [swap(outs[k], "neuron", neuron_count, k) for k in [*range(2, neuron_count), 1]]
+    arrived = [swap(outs[k], "neuron", neuron_count, k) for k in range(1, neuron_count)]
     arrived, made = lax.optimization_barrier((arrived, made))
     value = functools.reduce(jnp.add, [outs[0]] + [block.astype(F32) for block in arrived])
     mask = 1

time: 27.3 us -> 27.3 us (level)
  no operation moved by 1% of the time
where the time goes in v30:
time: 27.3 us; the launch traced here: 27.1 us
  starting transfers between devices  11.3 us (41%)
  Pallas kernels  8.25 us (30%)
  waiting for transfers between devices  4.27 us (16%)
  other arithmetic  1.86 us (7%)
  between operations  1.38 us (5%)
    ppermute x10, starting transfers between devices, swap(): return lax.ppermute(value, axis, [(i, i ^ mask) for i in range(count)])  11.3 us
    pallas_call x2, Pallas kernels, make(): pl.pallas_call(functools.partial(load_kernel, lats, first, chunk, step),...  5.8 us
    ppermute x10, waiting for transfers between devices, swap(): return lax.ppermute(value, axis, [(i, i ^ mask) for i in range(count)])  4.27 us
    pallas_call x1, Pallas kernels, per_device(): pl.pallas_call(functools.partial(shift_kernel, neuron_count, order, 'neur...  2.45 us
    add x1, other arithmetic, per_device(): pack = pack + jnp.pad(latents, ((0, 8), (neurons, 0))).astype(F32)  1.07 us
    add x1, other arithmetic, per_device(): value = value + read(arrived[0])  0.65 us
  transfers between devices with their start and end apart: 10, of which 5 were waited for; matrix products, arithmetic and copies ran while one was open for 4% of the time, Pallas kernels for 21%

profile of v30, /device:TPU:0, one launch (start us, length us, event | category | flops | bytes accessed | tf_op | source)
XLA Modules:
  0.0 27.1 jit_solution(15053784034210801974)
XLA Ops:
  0.6 0.5 %collective-permute-start = (bf16[64,256]{1,0:T(8,128)(2,1)}, bf16[64,256]{1,0:T(8,128)(2,1)S(1)}, u32[]{:S(2)}, u32[]{:S(2)}) collective-permute-start(bf16[64,256]{1,0:T(8,128)(2,1)} %param.7), channel_id=1, source_target_pairs={{0,1},{1,0},{2,3},{3,2},{4,5},{5,4},{6,7},{7,6},{8,9},{9,8},{10,11... | collective-permute-start | bytes 98312 | tf_op jit(solution)/shard_map/ppermute | solution.py:170
  1.1 2.6 %collective-permute-start.2 = (bf16[64,256]{1,0:T(8,128)(2,1)}, bf16[64,256]{1,0:T(8,128)(2,1)S(1)}, u32[]{:S(2)}, u32[]{:S(2)}) collective-permute-start(bf16[64,256]{1,0:T(8,128)(2,1)} %param.7), channel_id=1, source_target_pairs={{0,2},{1,3},{2,0},{3,1},{4,6},{5,7},{6,4},{7,5},{8,10},{9,11},{10,... | collective-permute-start | bytes 98312 | tf_op jit(solution)/shard_map/ppermute | solution.py:170
  3.7 0.1 collective-permute-start.1
  4.5 1.1 %convert_add_fusion.refs_0_ = f32[72,1536]{1,0:T(8,128)S(1)} fusion(s32[1,64]{1,0:T(1,128)} %param.10, f32[1,1280]{1,0:T(1,128)} %param.9, bf16[64,256]{1,0:T(8,128)(2,1)} %param.7, bf16[64,1280]{1,0:T(8,128)(2,1)} %bitcast.11, s32[]{:T(128)} %bitcast.6, pred[72]{0:T(512)(128)(4,1)S(1)} %iota_compare_fusion), kind=kLoop, calls=%fused_computation | loop fusion | flops 774144 | bytes 644428 | tf_op jit(solution)/shard_map/add | solution.py:179
  5.5 0.0 collective-permute-done.refs_2_
  5.6 0.4 %collective-permute-done.2.refs_4_ = bf16[64,256]{1,0:T(8,128)(2,1)S(1)} collective-permute-done((bf16[64,256]{1,0:T(8,128)(2,1)}, bf16[64,256]{1,0:T(8,128)(2,1)S(1)}, u32[]{:S(2)}, u32[]{:S(2)}) %collective-permute-start.2) | collective-permute-done | bytes 32800 | tf_op jit(solution)/shard_map/ppermute | solution.py:170
  5.9 1.4 %collective-permute-done.1.refs_3_ = bf16[64,256]{1,0:T(8,128)(2,1)S(1)} collective-permute-done((bf16[64,256]{1,0:T(8,128)(2,1)}, bf16[64,256]{1,0:T(8,128)(2,1)S(1)}, u32[]{:S(2)}, u32[]{:S(2)}) %collective-permute-start.1) | collective-permute-done | bytes 32800 | tf_op jit(solution)/shard_map/ppermute | solution.py:170
  7.3 2.5 %shard_map.85 = (f32[64,256]{1,0:T(8,128)S(1)}, bf16[64,256]{1,0:T(8,128)(2,1)S(1)}, bf16[64,256]{1,0:T(8,128)(2,1)S(1)}, bf16[64,256]{1,0:T(8,128)(2,1)S(1)}, b...) custom-call(f32[72,1536]{1,0:T(8,128)S(1)} %convert_add_fusion.refs_0_, bf16[1280,1024]{1,0:T(8,128)(2,1)} %bitcast.7, ...), custom_call_target="tpu_custom_call" | custom-call | tf_op jit(solution)/shard_map/pallas_call | solution.py:181
  9.8 0.2 collective-permute-start.3
  10.0 0.7 %collective-permute-start.4 = (bf16[64,256]{1,0:T(8,128)(2,1)S(1)}, bf16[64,256]{1,0:T(8,128)(2,1)S(1)}, u32[]{:S(2)}, u32[]{:S(2)}) collective-permute-start(bf16[64,256]{1,0:T(8,128)(2,1)S(1)} %get-tuple-element.41), channel_id=1, source_target_pairs={{0,2},{1,3},{2,0},{3,1},{4,6},{5,7},{6,4},{7,5},{8,10},{9,11},{10,... | collective-permute-start | bytes 98312 | tf_op jit(solution)/shard_map/ppermute | solution.py:170
  10.7 0.9 %collective-permute-start.5 = (bf16[64,256]{1,0:T(8,128)(2,1)S(1)}, bf16[64,256]{1,0:T(8,128)(2,1)S(1)}, u32[]{:S(2)}, u32[]{:S(2)}) collective-permute-start(bf16[64,256]{1,0:T(8,128)(2,1)S(1)} %get-tuple-element.42), channel_id=1, source_target_pairs={{0,3},{1,2},{2,1},{3,0},{4,7},{5,6},{6,5},{7,4},{8,11},{9,10},{10,... | collective-permute-start | bytes 98312 | tf_op jit(solution)/shard_map/ppermute | solution.py:170
  11.7 2.5 %shard_map.86 = (f32[64,1280]{1,0:T(8,128)}, f32[1,1280]{1,0:T(1,128)}) custom-call(f32[72,1536]{1,0:T(8,128)S(1)} %convert_add_fusion.refs_0_, bf16[80,1280]{1,0:T(8,128)(2,1)S(1)} %get-tuple-element.52.refs_1_, bf16[80,1024]{1,0:T(8,128)(2,1)S(1)} %get-tuple-element.44.refs_2_, bf16[1280,1024]{1,0:T(8,128)(2,1)} %bitcast.8), custom_call_target="tpu_custom_call" | custom-call | flops 134217728 | bytes 1048576 | tf_op jit(solution)/shard_map/pallas_call | solution.py:204
  14.2 0.0 collective-permute-done.3
  14.2 0.0 collective-permute-done.4
  14.2 0.2 collective-permute-done.5
  14.5 1.7 %collective-permute-start.8 = (bf16[64,256]{1,0:T(8,128)(2,1)S(1)}, bf16[64,256]{1,0:T(8,128)(2,1)S(1)}, u32[]{:S(2)}, u32[]{:S(2)}) collective-permute-start(bf16[64,256]{1,0:T(8,128)(2,1)S(1)} %get-tuple-element.51), channel_id=1, source_target_pairs={{0,8},{4,12},{8,0},{12,4},{16,24},{20,28},{24,16},{28,20},{1,9},{5... | collective-permute-start | bytes 98312 | tf_op jit(solution)/shard_map/ppermute | solution.py:170
  16.1 1.4 %collective-permute-start.7 = (bf16[64,256]{1,0:T(8,128)(2,1)S(1)}, bf16[64,256]{1,0:T(8,128)(2,1)S(1)}, u32[]{:S(2)}, u32[]{:S(2)}) collective-permute-start(bf16[64,256]{1,0:T(8,128)(2,1)S(1)} %get-tuple-element.51), channel_id=1, source_target_pairs={{0,12},{4,8},{8,4},{12,0},{16,28},{20,24},{24,20},{28,16},{1,13},{... | collective-permute-start | bytes 98312 | tf_op jit(solution)/shard_map/ppermute | solution.py:170
  17.5 0.5 %collective-permute-start.6 = (bf16[64,256]{1,0:T(8,128)(2,1)S(1)}, bf16[64,256]{1,0:T(8,128)(2,1)S(1)}, u32[]{:S(2)}, u32[]{:S(2)}) collective-permute-start(bf16[64,256]{1,0:T(8,128)(2,1)S(1)} %get-tuple-element.51), channel_id=1, source_target_pairs={{0,4},{4,0},{8,12},{12,8},{16,20},{20,16},{24,28},{28,24},{1,5},{5... | collective-permute-start | bytes 98312 | tf_op jit(solution)/shard_map/ppermute | solution.py:170
  18.0 3.3 %shard_map.87 = (f32[64,1280]{1,0:T(8,128)}, f32[1,1280]{1,0:T(1,128)}) custom-call(f32[72,1536]{1,0:T(8,128)S(1)} %convert_add_fusion.refs_0_, bf16[80,1280]{1,0:T(8,128)(2,1)S(1)} %get-tuple-element.52.refs_1_, bf16[80,1024]{1,0:T(8,128)(2,1)S(1)} %get-tuple-element.44.refs_2_, ...), custom_call_target="tpu_custom_call", output_to_operand_aliasing={{0}: (4, {}), {1}: (5, {})} | custom-call | flops 201326592 | bytes 1572864 | tf_op jit(solution)/shard_map/pallas_call | solution.py:204
  21.3 0.0 collective-permute-done.8
  21.3 0.0 collective-permute-done.7
  21.3 0.1 collective-permute-done.6
  21.5 2.7 %collective-permute-start.9 = (f16[72,256]{1,0:T(8,128)(2,1)S(1)}, f16[72,256]{1,0:T(8,128)(2,1)S(1)}, u32[]{:S(2)}, u32[]{:S(2)}) collective-permute-start(f16[72,256]{1,0:T(8,128)(2,1)S(1)} %pad_maximum_fusion), channel_id=1, source_target_pairs={{0,16},{4,20},{8,24},{12,28},{16,0},{20,4},{24,8},{28,12},{1,17},{... | collective-permute-start | bytes 110600 | tf_op jit(solution)/shard_map/ppermute | solution.py:170
  24.2 2.3 %collective-permute-done.9 = f16[72,256]{1,0:T(8,128)(2,1)S(1)} collective-permute-done((f16[72,256]{1,0:T(8,128)(2,1)S(1)}, f16[72,256]{1,0:T(8,128)(2,1)S(1)}, u32[]{:S(2)}, u32[]{:S(2)}) %collective-permute-start.9) | collective-permute-done | bytes 36896 | tf_op jit(solution)/shard_map/ppermute | solution.py:170
  26.4 0.7 %multiply_add_fusion = f32[64,256]{1,0:T(8,128)} fusion(f16[72,256]{1,0:T(8,128)(2,1)S(1)} %pad_maximum_fusion, f32[256]{0:T(256)S(1)} %bitcast.13, f16[72,256]{1,0:T(8,128)(2,1)S(1)} %collective-permute-done.9, f32[256]{0:T(256)S(1)} %bitcast.12), kind=kLoop, calls=%fused_computation.1 | loop fusion | flops 81920 | bytes 133120 | tf_op jit(solution)/shard_map/add | solution.py:243
  (9 shorter events, 0.1 us)
Async XLA Ops:
  0.6 4.9 %collective-permute-start = (bf16[64,256]{1,0:T(8,128)(2,1)}, bf16[64,256]{1,0:T(8,128)(2,1)S(1)}, u32[]{:S(2)}, u32[]{:S(2)}) collective-permute-start(bf16[64,256]{1,0:T(8,128)(2,1)} %param.7), channel_id=1, source_target_pairs={{0,1},{1,0},{2,3},{3,2},{4,5},{5,4},{6,7},{7,6},{8,9},{9,8},{10,11... | collective-permute-start | bytes 98312 | tf_op jit(solution)/shard_map/ppermute | solution.py:170
  1.1 4.8 %collective-permute-start.2 = (bf16[64,256]{1,0:T(8,128)(2,1)}, bf16[64,256]{1,0:T(8,128)(2,1)S(1)}, u32[]{:S(2)}, u32[]{:S(2)}) collective-permute-start(bf16[64,256]{1,0:T(8,128)(2,1)} %param.7), channel_id=1, source_target_pairs={{0,2},{1,3},{2,0},{3,1},{4,6},{5,7},{6,4},{7,5},{8,10},{9,11},{10,... | collective-permute-start | bytes 98312 | tf_op jit(solution)/shard_map/ppermute | solution.py:170
  3.7 3.6 %collective-permute-start.1 = (bf16[64,256]{1,0:T(8,128)(2,1)}, bf16[64,256]{1,0:T(8,128)(2,1)S(1)}, u32[]{:S(2)}, u32[]{:S(2)}) collective-permute-start(bf16[64,256]{1,0:T(8,128)(2,1)} %param.7), channel_id=1, source_target_pairs={{0,3},{1,2},{2,1},{3,0},{4,7},{5,6},{6,5},{7,4},{8,11},{9,10},{10,... | collective-permute-start | bytes 98312 | tf_op jit(solution)/shard_map/ppermute | solution.py:170
  9.8 4.5 %collective-permute-start.3 = (bf16[64,256]{1,0:T(8,128)(2,1)S(1)}, bf16[64,256]{1,0:T(8,128)(2,1)S(1)}, u32[]{:S(2)}, u32[]{:S(2)}) collective-permute-start(bf16[64,256]{1,0:T(8,128)(2,1)S(1)} %get-tuple-element.40), channel_id=1, source_target_pairs={{0,1},{1,0},{2,3},{3,2},{4,5},{5,4},{6,7},{7,6},{8,9},{9,8},{10,11... | collective-permute-start | bytes 98312 | tf_op jit(solution)/shard_map/ppermute | solution.py:170
  10.0 4.2 %collective-permute-start.4 = (bf16[64,256]{1,0:T(8,128)(2,1)S(1)}, bf16[64,256]{1,0:T(8,128)(2,1)S(1)}, u32[]{:S(2)}, u32[]{:S(2)}) collective-permute-start(bf16[64,256]{1,0:T(8,128)(2,1)S(1)} %get-tuple-element.41), channel_id=1, source_target_pairs={{0,2},{1,3},{2,0},{3,1},{4,6},{5,7},{6,4},{7,5},{8,10},{9,11},{10,... | collective-permute-start | bytes 98312 | tf_op jit(solution)/shard_map/ppermute | solution.py:170
  10.7 3.7 %collective-permute-start.5 = (bf16[64,256]{1,0:T(8,128)(2,1)S(1)}, bf16[64,256]{1,0:T(8,128)(2,1)S(1)}, u32[]{:S(2)}, u32[]{:S(2)}) collective-permute-start(bf16[64,256]{1,0:T(8,128)(2,1)S(1)} %get-tuple-element.42), channel_id=1, source_target_pairs={{0,3},{1,2},{2,1},{3,0},{4,7},{5,6},{6,5},{7,4},{8,11},{9,10},{10,... | collective-permute-start | bytes 98312 | tf_op jit(solution)/shard_map/ppermute | solution.py:170
  14.5 6.8 %collective-permute-start.8 = (bf16[64,256]{1,0:T(8,128)(2,1)S(1)}, bf16[64,256]{1,0:T(8,128)(2,1)S(1)}, u32[]{:S(2)}, u32[]{:S(2)}) collective-permute-start(bf16[64,256]{1,0:T(8,128)(2,1)S(1)} %get-tuple-element.51), channel_id=1, source_target_pairs={{0,8},{4,12},{8,0},{12,4},{16,24},{20,28},{24,16},{28,20},{1,9},{5... | collective-permute-start | bytes 98312 | tf_op jit(solution)/shard_map/ppermute | solution.py:170
  16.1 5.2 %collective-permute-start.7 = (bf16[64,256]{1,0:T(8,128)(2,1)S(1)}, bf16[64,256]{1,0:T(8,128)(2,1)S(1)}, u32[]{:S(2)}, u32[]{:S(2)}) collective-permute-start(bf16[64,256]{1,0:T(8,128)(2,1)S(1)} %get-tuple-element.51), channel_id=1, source_target_pairs={{0,12},{4,8},{8,4},{12,0},{16,28},{20,24},{24,20},{28,16},{1,13},{... | collective-permute-start | bytes 98312 | tf_op jit(solution)/shard_map/ppermute | solution.py:170
  17.5 3.9 %collective-permute-start.6 = (bf16[64,256]{1,0:T(8,128)(2,1)S(1)}, bf16[64,256]{1,0:T(8,128)(2,1)S(1)}, u32[]{:S(2)}, u32[]{:S(2)}) collective-permute-start(bf16[64,256]{1,0:T(8,128)(2,1)S(1)} %get-tuple-element.51), channel_id=1, source_target_pairs={{0,4},{4,0},{8,12},{12,8},{16,20},{20,16},{24,28},{28,24},{1,5},{5... | collective-permute-start | bytes 98312 | tf_op jit(solution)/shard_map/ppermute | solution.py:170
  21.5 4.9 %collective-permute-start.9 = (f16[72,256]{1,0:T(8,128)(2,1)S(1)}, f16[72,256]{1,0:T(8,128)(2,1)S(1)}, u32[]{:S(2)}, u32[]{:S(2)}) collective-permute-start(f16[72,256]{1,0:T(8,128)(2,1)S(1)} %pad_maximum_fusion), channel_id=1, source_target_pairs={{0,16},{4,20},{8,24},{12,28},{16,0},{20,4},{24,8},{28,12},{1,17},{... | collective-permute-start | bytes 110600 | tf_op jit(solution)/shard_map/ppermute | solution.py:170

commit v31 on v29

--- a/solution.py
+++ b/solution.py
@@ -36,10 +36,9 @@
     load_ext, shifted, whole, counts_ref, held, resid_low, grad_shift, counts_sems = refs[1 + 2 * parts :]
     me = lax.axis_index(axis)
     lats, total = grad_shift.shape
-    early = held.shape[0]
     neurons = counts_ref.shape[0]
     width = total // parts
-    cut = 3 * chunk
+    cut, late = 3 * chunk, chunk
     places = [pl.ds(0, cut), pl.ds(cut, neurons - cut)]
     copies = [
         pltpu.make_async_copy(counts_hbm.at[place], counts_ref.at[place], counts_sems.at[index])
@@ -78,14 +77,14 @@
         for begin in range(0, total, step)
     ]
     for rows, span in blocks:
-        if rows.start < early:
+        if rows.start >= late:
             held[rows, span] = expected(load_ext[:, rows], shifted[:, span])
     spans = [slice(begin, begin + step) for begin in range(0, total, step)]
     for copy, place in zip(copies, [slice(0, cut), slice(cut, neurons)]):
         copy.wait()
         for rows, span in blocks:
             if place.start <= rows.start < place.stop:
-                rate = held[rows, span] if rows.start < early else expected(load_ext[:, rows], shifted[:, span])
+                rate = held[rows, span] if rows.start >= late else expected(load_ext[:, rows], shifted[:, span])
                 resid_low[rows, span] = (rate - counts_ref[rows, span].astype(F32)).astype(BF16)
         for span in spans:
             part = jnp.dot(load_ext[0:lats, place], resid_low[place, span], preferred_element_type=F32)
@@ -187,7 +186,7 @@
         scratch_shapes=[
             pltpu.VMEM((lats, total), BF16),
             pltpu.VMEM((neurons, total), BF16),
-            pltpu.VMEM((4 * chunk, total), F32),
+            pltpu.VMEM((neurons, total), F32),
             pltpu.VMEM((neurons, total), BF16),
             pltpu.VMEM((lats, total), F32),
             pltpu.SemaphoreType.DMA((2,)),

time: 27.3 us -> 27.4 us (level)
  no operation moved by 1% of the time
where the time goes in v31:
time: 27.4 us; the launch traced here: 27.1 us
  starting transfers between devices  11.3 us (41%)
  Pallas kernels  8.29 us (30%)
  waiting for transfers between devices  4.29 us (16%)
  other arithmetic  1.86 us (7%)
  between operations  1.37 us (5%)
    ppermute x10, starting transfers between devices, swap(): return lax.ppermute(value, axis, [(i, i ^ mask) for i in range(count)])  11.3 us
    pallas_call x2, Pallas kernels, make(): pl.pallas_call(functools.partial(load_kernel, lats, first, chunk, step),...  5.8 us
    ppermute x10, waiting for transfers between devices, swap(): return lax.ppermute(value, axis, [(i, i ^ mask) for i in range(count)])  4.29 us
    pallas_call x1, Pallas kernels, per_device(): pl.pallas_call(functools.partial(shift_kernel, neuron_count, order, 'neur...  2.5 us
    add x1, other arithmetic, per_device(): pack = pack + jnp.pad(latents, ((0, 8), (neurons, 0))).astype(F32)  1.07 us
    add x1, other arithmetic, per_device(): value = value + read(arrived[0])  0.65 us
  transfers between devices with their start and end apart: 10, of which 5 were waited for; matrix products, arithmetic and copies ran while one was open for 4% of the time, Pallas kernels for 21%

profile of v31, /device:TPU:0, one launch (start us, length us, event | category | flops | bytes accessed | tf_op | source)
XLA Modules:
  0.0 27.1 jit_solution(16175680853299090635)
XLA Ops:
  0.6 0.5 %collective-permute-start = (bf16[64,256]{1,0:T(8,128)(2,1)}, bf16[64,256]{1,0:T(8,128)(2,1)S(1)}, u32[]{:S(2)}, u32[]{:S(2)}) collective-permute-start(bf16[64,256]{1,0:T(8,128)(2,1)} %param.7), channel_id=1, source_target_pairs={{0,1},{1,0},{2,3},{3,2},{4,5},{5,4},{6,7},{7,6},{8,9},{9,8},{10,11... | collective-permute-start | bytes 98312 | tf_op jit(solution)/shard_map/ppermute | solution.py:169
  1.1 2.6 %collective-permute-start.2 = (bf16[64,256]{1,0:T(8,128)(2,1)}, bf16[64,256]{1,0:T(8,128)(2,1)S(1)}, u32[]{:S(2)}, u32[]{:S(2)}) collective-permute-start(bf16[64,256]{1,0:T(8,128)(2,1)} %param.7), channel_id=1, source_target_pairs={{0,2},{1,3},{2,0},{3,1},{4,6},{5,7},{6,4},{7,5},{8,10},{9,11},{10,... | collective-permute-start | bytes 98312 | tf_op jit(solution)/shard_map/ppermute | solution.py:169
  3.7 0.1 collective-permute-start.1
  4.5 1.1 %convert_add_fusion.refs_0_ = f32[72,1536]{1,0:T(8,128)S(1)} fusion(s32[1,64]{1,0:T(1,128)} %param.10, f32[1,1280]{1,0:T(1,128)} %param.9, bf16[64,256]{1,0:T(8,128)(2,1)} %param.7, bf16[64,1280]{1,0:T(8,128)(2,1)} %bitcast.11, s32[]{:T(128)} %bitcast.6, pred[72]{0:T(512)(128)(4,1)S(1)} %iota_compare_fusion), kind=kLoop, calls=%fused_computation | loop fusion | flops 774144 | bytes 644428 | tf_op jit(solution)/shard_map/add | solution.py:178
  5.5 0.0 collective-permute-done.refs_2_
  5.6 0.4 %collective-permute-done.2.refs_4_ = bf16[64,256]{1,0:T(8,128)(2,1)S(1)} collective-permute-done((bf16[64,256]{1,0:T(8,128)(2,1)}, bf16[64,256]{1,0:T(8,128)(2,1)S(1)}, u32[]{:S(2)}, u32[]{:S(2)}) %collective-permute-start.2) | collective-permute-done | bytes 32800 | tf_op jit(solution)/shard_map/ppermute | solution.py:169
  5.9 1.4 %collective-permute-done.1.refs_3_ = bf16[64,256]{1,0:T(8,128)(2,1)S(1)} collective-permute-done((bf16[64,256]{1,0:T(8,128)(2,1)}, bf16[64,256]{1,0:T(8,128)(2,1)S(1)}, u32[]{:S(2)}, u32[]{:S(2)}) %collective-permute-start.1) | collective-permute-done | bytes 32800 | tf_op jit(solution)/shard_map/ppermute | solution.py:169
  7.3 2.5 %shard_map.85 = (f32[64,256]{1,0:T(8,128)S(1)}, f32[64,256]{1,0:T(8,128)S(1)}, bf16[64,256]{1,0:T(8,128)(2,1)S(1)}, bf16[64,256]{1,0:T(8,128)(2,1)S(1)}, bf16[80...) custom-call(f32[72,1536]{1,0:T(8,128)S(1)} %convert_add_fusion.refs_0_, bf16[1280,1024]{1,0:T(8,128)(2,1)} %bitcast.7, ...), custom_call_target="tpu_custom_call" | custom-call | tf_op jit(solution)/shard_map/pallas_call | solution.py:180
  9.8 0.2 collective-permute-start.5
  10.0 0.8 %collective-permute-start.3 = (bf16[64,256]{1,0:T(8,128)(2,1)S(1)}, bf16[64,256]{1,0:T(8,128)(2,1)S(1)}, u32[]{:S(2)}, u32[]{:S(2)}) collective-permute-start(bf16[64,256]{1,0:T(8,128)(2,1)S(1)} %get-tuple-element.40), channel_id=1, source_target_pairs={{0,2},{1,3},{2,0},{3,1},{4,6},{5,7},{6,4},{7,5},{8,10},{9,11},{10,... | collective-permute-start | bytes 98312 | tf_op jit(solution)/shard_map/ppermute | solution.py:169
  10.8 0.9 %collective-permute-start.4 = (bf16[64,256]{1,0:T(8,128)(2,1)S(1)}, bf16[64,256]{1,0:T(8,128)(2,1)S(1)}, u32[]{:S(2)}, u32[]{:S(2)}) collective-permute-start(bf16[64,256]{1,0:T(8,128)(2,1)S(1)} %get-tuple-element.41), channel_id=1, source_target_pairs={{0,3},{1,2},{2,1},{3,0},{4,7},{5,6},{6,5},{7,4},{8,11},{9,10},{10,... | collective-permute-start | bytes 98312 | tf_op jit(solution)/shard_map/ppermute | solution.py:169
  11.7 2.5 %shard_map.86 = (f32[64,1280]{1,0:T(8,128)}, f32[1,1280]{1,0:T(1,128)}) custom-call(f32[72,1536]{1,0:T(8,128)S(1)} %convert_add_fusion.refs_0_, bf16[80,1280]{1,0:T(8,128)(2,1)S(1)} %get-tuple-element.52.refs_1_, bf16[80,1024]{1,0:T(8,128)(2,1)S(1)} %get-tuple-element.44.refs_2_, bf16[1280,1024]{1,0:T(8,128)(2,1)} %bitcast.8), custom_call_target="tpu_custom_call" | custom-call | flops 134217728 | bytes 1048576 | tf_op jit(solution)/shard_map/pallas_call | solution.py:203
  14.3 0.0 collective-permute-done.3
  14.3 0.2 collective-permute-done.4
  14.5 0.0 collective-permute-done.5
  14.5 1.6 %collective-permute-start.8 = (bf16[64,256]{1,0:T(8,128)(2,1)S(1)}, bf16[64,256]{1,0:T(8,128)(2,1)S(1)}, u32[]{:S(2)}, u32[]{:S(2)}) collective-permute-start(bf16[64,256]{1,0:T(8,128)(2,1)S(1)} %get-tuple-element.51), channel_id=1, source_target_pairs={{0,8},{4,12},{8,0},{12,4},{16,24},{20,28},{24,16},{28,20},{1,9},{5... | collective-permute-start | bytes 98312 | tf_op jit(solution)/shard_map/ppermute | solution.py:169
  16.1 1.4 %collective-permute-start.7 = (bf16[64,256]{1,0:T(8,128)(2,1)S(1)}, bf16[64,256]{1,0:T(8,128)(2,1)S(1)}, u32[]{:S(2)}, u32[]{:S(2)}) collective-permute-start(bf16[64,256]{1,0:T(8,128)(2,1)S(1)} %get-tuple-element.51), channel_id=1, source_target_pairs={{0,12},{4,8},{8,4},{12,0},{16,28},{20,24},{24,20},{28,16},{1,13},{... | collective-permute-start | bytes 98312 | tf_op jit(solution)/shard_map/ppermute | solution.py:169
  17.5 0.5 %collective-permute-start.6 = (bf16[64,256]{1,0:T(8,128)(2,1)S(1)}, bf16[64,256]{1,0:T(8,128)(2,1)S(1)}, u32[]{:S(2)}, u32[]{:S(2)}) collective-permute-start(bf16[64,256]{1,0:T(8,128)(2,1)S(1)} %get-tuple-element.51), channel_id=1, source_target_pairs={{0,4},{4,0},{8,12},{12,8},{16,20},{20,16},{24,28},{28,24},{1,5},{5... | collective-permute-start | bytes 98312 | tf_op jit(solution)/shard_map/ppermute | solution.py:169
  18.1 3.3 %shard_map.87 = (f32[64,1280]{1,0:T(8,128)}, f32[1,1280]{1,0:T(1,128)}) custom-call(f32[72,1536]{1,0:T(8,128)S(1)} %convert_add_fusion.refs_0_, bf16[80,1280]{1,0:T(8,128)(2,1)S(1)} %get-tuple-element.52.refs_1_, bf16[80,1024]{1,0:T(8,128)(2,1)S(1)} %get-tuple-element.44.refs_2_, ...), custom_call_target="tpu_custom_call", output_to_operand_aliasing={{0}: (4, {}), {1}: (5, {})} | custom-call | flops 201326592 | bytes 1572864 | tf_op jit(solution)/shard_map/pallas_call | solution.py:203
  21.3 0.0 collective-permute-done.8
  21.4 0.0 collective-permute-done.7
  21.4 0.1 collective-permute-done.6
  21.6 2.7 %collective-permute-start.9 = (f16[72,256]{1,0:T(8,128)(2,1)S(1)}, f16[72,256]{1,0:T(8,128)(2,1)S(1)}, u32[]{:S(2)}, u32[]{:S(2)}) collective-permute-start(f16[72,256]{1,0:T(8,128)(2,1)S(1)} %pad_maximum_fusion), channel_id=1, source_target_pairs={{0,16},{4,20},{8,24},{12,28},{16,0},{20,4},{24,8},{28,12},{1,17},{... | collective-permute-start | bytes 110600 | tf_op jit(solution)/shard_map/ppermute | solution.py:169
  24.2 2.3 %collective-permute-done.9 = f16[72,256]{1,0:T(8,128)(2,1)S(1)} collective-permute-done((f16[72,256]{1,0:T(8,128)(2,1)S(1)}, f16[72,256]{1,0:T(8,128)(2,1)S(1)}, u32[]{:S(2)}, u32[]{:S(2)}) %collective-permute-start.9) | collective-permute-done | bytes 36896 | tf_op jit(solution)/shard_map/ppermute | solution.py:169
  26.5 0.7 %multiply_add_fusion = f32[64,256]{1,0:T(8,128)} fusion(f16[72,256]{1,0:T(8,128)(2,1)S(1)} %pad_maximum_fusion, f32[256]{0:T(256)S(1)} %bitcast.13, f16[72,256]{1,0:T(8,128)(2,1)S(1)} %collective-permute-done.9, f32[256]{0:T(256)S(1)} %bitcast.12), kind=kLoop, calls=%fused_computation.1 | loop fusion | flops 81920 | bytes 133120 | tf_op jit(solution)/shard_map/add | solution.py:242
  (9 shorter events, 0.1 us)
Async XLA Ops:
  0.6 4.9 %collective-permute-start = (bf16[64,256]{1,0:T(8,128)(2,1)}, bf16[64,256]{1,0:T(8,128)(2,1)S(1)}, u32[]{:S(2)}, u32[]{:S(2)}) collective-permute-start(bf16[64,256]{1,0:T(8,128)(2,1)} %param.7), channel_id=1, source_target_pairs={{0,1},{1,0},{2,3},{3,2},{4,5},{5,4},{6,7},{7,6},{8,9},{9,8},{10,11... | collective-permute-start | bytes 98312 | tf_op jit(solution)/shard_map/ppermute | solution.py:169
  1.1 4.8 %collective-permute-start.2 = (bf16[64,256]{1,0:T(8,128)(2,1)}, bf16[64,256]{1,0:T(8,128)(2,1)S(1)}, u32[]{:S(2)}, u32[]{:S(2)}) collective-permute-start(bf16[64,256]{1,0:T(8,128)(2,1)} %param.7), channel_id=1, source_target_pairs={{0,2},{1,3},{2,0},{3,1},{4,6},{5,7},{6,4},{7,5},{8,10},{9,11},{10,... | collective-permute-start | bytes 98312 | tf_op jit(solution)/shard_map/ppermute | solution.py:169
  3.7 3.6 %collective-permute-start.1 = (bf16[64,256]{1,0:T(8,128)(2,1)}, bf16[64,256]{1,0:T(8,128)(2,1)S(1)}, u32[]{:S(2)}, u32[]{:S(2)}) collective-permute-start(bf16[64,256]{1,0:T(8,128)(2,1)} %param.7), channel_id=1, source_target_pairs={{0,3},{1,2},{2,1},{3,0},{4,7},{5,6},{6,5},{7,4},{8,11},{9,10},{10,... | collective-permute-start | bytes 98312 | tf_op jit(solution)/shard_map/ppermute | solution.py:169
  9.8 4.7 %collective-permute-start.5 = (f32[64,256]{1,0:T(8,128)S(1)}, f32[64,256]{1,0:T(8,128)S(1)}, u32[]{:S(2)}, u32[]{:S(2)}) collective-permute-start(f32[64,256]{1,0:T(8,128)S(1)} %get-tuple-element.42), channel_id=1, source_target_pairs={{0,1},{1,0},{2,3},{3,2},{4,5},{5,4},{6,7},{7,6},{8,9},{9,8},{10,11... | collective-permute-start | bytes 196616 | tf_op jit(solution)/shard_map/ppermute | solution.py:169
  10.0 4.2 %collective-permute-start.3 = (bf16[64,256]{1,0:T(8,128)(2,1)S(1)}, bf16[64,256]{1,0:T(8,128)(2,1)S(1)}, u32[]{:S(2)}, u32[]{:S(2)}) collective-permute-start(bf16[64,256]{1,0:T(8,128)(2,1)S(1)} %get-tuple-element.40), channel_id=1, source_target_pairs={{0,2},{1,3},{2,0},{3,1},{4,6},{5,7},{6,4},{7,5},{8,10},{9,11},{10,... | collective-permute-start | bytes 98312 | tf_op jit(solution)/shard_map/ppermute | solution.py:169
  10.8 3.7 %collective-permute-start.4 = (bf16[64,256]{1,0:T(8,128)(2,1)S(1)}, bf16[64,256]{1,0:T(8,128)(2,1)S(1)}, u32[]{:S(2)}, u32[]{:S(2)}) collective-permute-start(bf16[64,256]{1,0:T(8,128)(2,1)S(1)} %get-tuple-element.41), channel_id=1, source_target_pairs={{0,3},{1,2},{2,1},{3,0},{4,7},{5,6},{6,5},{7,4},{8,11},{9,10},{10,... | collective-permute-start | bytes 98312 | tf_op jit(solution)/shard_map/ppermute | solution.py:169
  14.5 6.8 %collective-permute-start.8 = (bf16[64,256]{1,0:T(8,128)(2,1)S(1)}, bf16[64,256]{1,0:T(8,128)(2,1)S(1)}, u32[]{:S(2)}, u32[]{:S(2)}) collective-permute-start(bf16[64,256]{1,0:T(8,128)(2,1)S(1)} %get-tuple-element.51), channel_id=1, source_target_pairs={{0,8},{4,12},{8,0},{12,4},{16,24},{20,28},{24,16},{28,20},{1,9},{5... | collective-permute-start | bytes 98312 | tf_op jit(solution)/shard_map/ppermute | solution.py:169
  16.1 5.2 %collective-permute-start.7 = (bf16[64,256]{1,0:T(8,128)(2,1)S(1)}, bf16[64,256]{1,0:T(8,128)(2,1)S(1)}, u32[]{:S(2)}, u32[]{:S(2)}) collective-permute-start(bf16[64,256]{1,0:T(8,128)(2,1)S(1)} %get-tuple-element.51), channel_id=1, source_target_pairs={{0,12},{4,8},{8,4},{12,0},{16,28},{20,24},{24,20},{28,16},{1,13},{... | collective-permute-start | bytes 98312 | tf_op jit(solution)/shard_map/ppermute | solution.py:169
  17.5 3.9 %collective-permute-start.6 = (bf16[64,256]{1,0:T(8,128)(2,1)S(1)}, bf16[64,256]{1,0:T(8,128)(2,1)S(1)}, u32[]{:S(2)}, u32[]{:S(2)}) collective-permute-start(bf16[64,256]{1,0:T(8,128)(2,1)S(1)} %get-tuple-element.51), channel_id=1, source_target_pairs={{0,4},{4,0},{8,12},{12,8},{16,20},{20,16},{24,28},{28,24},{1,5},{5... | collective-permute-start | bytes 98312 | tf_op jit(solution)/shard_map/ppermute | solution.py:169
  21.6 4.9 %collective-permute-start.9 = (f16[72,256]{1,0:T(8,128)(2,1)S(1)}, f16[72,256]{1,0:T(8,128)(2,1)S(1)}, u32[]{:S(2)}, u32[]{:S(2)}) collective-permute-start(f16[72,256]{1,0:T(8,128)(2,1)S(1)} %pad_maximum_fusion), channel_id=1, source_target_pairs={{0,16},{4,20},{8,24},{12,28},{16,0},{20,4},{24,8},{28,12},{1,17},{... | collective-permute-start | bytes 110600 | tf_op jit(solution)/shard_map/ppermute | solution.py:169

commit v32 on v29

--- a/solution.py
+++ b/solution.py
@@ -236,7 +236,7 @@
             value = decode(sent)
         if shares:
             (value, sent), made = make((value, sent))
-        turns = sorted(masks, key=lambda k: (k != mask, -k))
+        turns = sorted(masks, key=lambda k: (k == 3 * mask, -k))
         arrived = [swap(sent, "region", region_count, k) for k in turns]
         arrived, made = lax.optimization_barrier((arrived, made))
         arrived = [arrived[turns.index(k)] for k in masks]

time: 27.3 us -> 27.4 us (level)
  no operation moved by 1% of the time
where the time goes in v32:
time: 27.4 us; the launch traced here: 27.2 us
  starting transfers between devices  11.3 us (41%)
  Pallas kernels  8.25 us (30%)
  waiting for transfers between devices  4.42 us (16%)
  other arithmetic  1.86 us (7%)
  between operations  1.37 us (5%)
    ppermute x10, starting transfers between devices, swap(): return lax.ppermute(value, axis, [(i, i ^ mask) for i in range(count)])  11.3 us
    pallas_call x2, Pallas kernels, make(): pl.pallas_call(functools.partial(load_kernel, lats, first, chunk, step),...  5.8 us
    ppermute x10, waiting for transfers between devices, swap(): return lax.ppermute(value, axis, [(i, i ^ mask) for i in range(count)])  4.42 us
    pallas_call x1, Pallas kernels, per_device(): pl.pallas_call(functools.partial(shift_kernel, neuron_count, order, 'neur...  2.45 us
    add x1, other arithmetic, per_device(): pack = pack + jnp.pad(latents, ((0, 8), (neurons, 0))).astype(F32)  1.07 us
    add x1, other arithmetic, per_device(): value = value + read(arrived[0])  0.65 us
  transfers between devices with their start and end apart: 10, of which 5 were waited for; matrix products, arithmetic and copies ran while one was open for 4% of the time, Pallas kernels for 21%

profile of v32, /device:TPU:0, one launch (start us, length us, event | category | flops | bytes accessed | tf_op | source)
XLA Modules:
  0.0 27.2 jit_solution(8552484863236750311)
XLA Ops:
  0.6 0.5 %collective-permute-start = (bf16[64,256]{1,0:T(8,128)(2,1)}, bf16[64,256]{1,0:T(8,128)(2,1)S(1)}, u32[]{:S(2)}, u32[]{:S(2)}) collective-permute-start(bf16[64,256]{1,0:T(8,128)(2,1)} %param.7), channel_id=1, source_target_pairs={{0,1},{1,0},{2,3},{3,2},{4,5},{5,4},{6,7},{7,6},{8,9},{9,8},{10,11... | collective-permute-start | bytes 98312 | tf_op jit(solution)/shard_map/ppermute | solution.py:170
  1.1 2.6 %collective-permute-start.2 = (bf16[64,256]{1,0:T(8,128)(2,1)}, bf16[64,256]{1,0:T(8,128)(2,1)S(1)}, u32[]{:S(2)}, u32[]{:S(2)}) collective-permute-start(bf16[64,256]{1,0:T(8,128)(2,1)} %param.7), channel_id=1, source_target_pairs={{0,2},{1,3},{2,0},{3,1},{4,6},{5,7},{6,4},{7,5},{8,10},{9,11},{10,... | collective-permute-start | bytes 98312 | tf_op jit(solution)/shard_map/ppermute | solution.py:170
  3.7 0.1 collective-permute-start.1
  4.5 1.1 %convert_add_fusion.refs_0_ = f32[72,1536]{1,0:T(8,128)S(1)} fusion(s32[1,64]{1,0:T(1,128)} %param.10, f32[1,1280]{1,0:T(1,128)} %param.9, bf16[64,256]{1,0:T(8,128)(2,1)} %param.7, bf16[64,1280]{1,0:T(8,128)(2,1)} %bitcast.11, s32[]{:T(128)} %bitcast.6, pred[72]{0:T(512)(128)(4,1)S(1)} %iota_compare_fusion), kind=kLoop, calls=%fused_computation | loop fusion | flops 774144 | bytes 644428 | tf_op jit(solution)/shard_map/add | solution.py:179
  5.5 0.0 collective-permute-done.refs_2_
  5.6 0.4 %collective-permute-done.2.refs_4_ = bf16[64,256]{1,0:T(8,128)(2,1)S(1)} collective-permute-done((bf16[64,256]{1,0:T(8,128)(2,1)}, bf16[64,256]{1,0:T(8,128)(2,1)S(1)}, u32[]{:S(2)}, u32[]{:S(2)}) %collective-permute-start.2) | collective-permute-done | bytes 32800 | tf_op jit(solution)/shard_map/ppermute | solution.py:170
  5.9 1.4 %collective-permute-done.1.refs_3_ = bf16[64,256]{1,0:T(8,128)(2,1)S(1)} collective-permute-done((bf16[64,256]{1,0:T(8,128)(2,1)}, bf16[64,256]{1,0:T(8,128)(2,1)S(1)}, u32[]{:S(2)}, u32[]{:S(2)}) %collective-permute-start.1) | collective-permute-done | bytes 32800 | tf_op jit(solution)/shard_map/ppermute | solution.py:170
  7.3 2.5 %shard_map.85 = (f32[64,256]{1,0:T(8,128)S(1)}, f32[64,256]{1,0:T(8,128)S(1)}, bf16[64,256]{1,0:T(8,128)(2,1)S(1)}, bf16[64,256]{1,0:T(8,128)(2,1)S(1)}, bf16[80...) custom-call(f32[72,1536]{1,0:T(8,128)S(1)} %convert_add_fusion.refs_0_, bf16[1280,1024]{1,0:T(8,128)(2,1)} %bitcast.7, ...), custom_call_target="tpu_custom_call" | custom-call | tf_op jit(solution)/shard_map/pallas_call | solution.py:181
  9.8 0.2 collective-permute-start.5
  10.0 0.7 %collective-permute-start.3 = (bf16[64,256]{1,0:T(8,128)(2,1)S(1)}, bf16[64,256]{1,0:T(8,128)(2,1)S(1)}, u32[]{:S(2)}, u32[]{:S(2)}) collective-permute-start(bf16[64,256]{1,0:T(8,128)(2,1)S(1)} %get-tuple-element.40), channel_id=1, source_target_pairs={{0,2},{1,3},{2,0},{3,1},{4,6},{5,7},{6,4},{7,5},{8,10},{9,11},{10,... | collective-permute-start | bytes 98312 | tf_op jit(solution)/shard_map/ppermute | solution.py:170
  10.7 0.9 %collective-permute-start.4 = (bf16[64,256]{1,0:T(8,128)(2,1)S(1)}, bf16[64,256]{1,0:T(8,128)(2,1)S(1)}, u32[]{:S(2)}, u32[]{:S(2)}) collective-permute-start(bf16[64,256]{1,0:T(8,128)(2,1)S(1)} %get-tuple-element.41), channel_id=1, source_target_pairs={{0,3},{1,2},{2,1},{3,0},{4,7},{5,6},{6,5},{7,4},{8,11},{9,10},{10,... | collective-permute-start | bytes 98312 | tf_op jit(solution)/shard_map/ppermute | solution.py:170
  11.7 2.5 %shard_map.86 = (f32[64,1280]{1,0:T(8,128)}, f32[1,1280]{1,0:T(1,128)}) custom-call(f32[72,1536]{1,0:T(8,128)S(1)} %convert_add_fusion.refs_0_, bf16[80,1280]{1,0:T(8,128)(2,1)S(1)} %get-tuple-element.52.refs_1_, bf16[80,1024]{1,0:T(8,128)(2,1)S(1)} %get-tuple-element.44.refs_2_, bf16[1280,1024]{1,0:T(8,128)(2,1)} %bitcast.8), custom_call_target="tpu_custom_call" | custom-call | flops 134217728 | bytes 1048576 | tf_op jit(solution)/shard_map/pallas_call | solution.py:204
  14.2 0.0 collective-permute-done.3
  14.2 0.2 collective-permute-done.4
  14.4 0.0 collective-permute-done.5
  14.5 2.6 %collective-permute-start.8 = (bf16[64,256]{1,0:T(8,128)(2,1)S(1)}, bf16[64,256]{1,0:T(8,128)(2,1)S(1)}, u32[]{:S(2)}, u32[]{:S(2)}) collective-permute-start(bf16[64,256]{1,0:T(8,128)(2,1)S(1)} %get-tuple-element.51), channel_id=1, source_target_pairs={{0,12},{4,8},{8,4},{12,0},{16,28},{20,24},{24,20},{28,16},{1,13},{... | collective-permute-start | bytes 98312 | tf_op jit(solution)/shard_map/ppermute | solution.py:170
  17.0 0.5 %collective-permute-start.7 = (bf16[64,256]{1,0:T(8,128)(2,1)S(1)}, bf16[64,256]{1,0:T(8,128)(2,1)S(1)}, u32[]{:S(2)}, u32[]{:S(2)}) collective-permute-start(bf16[64,256]{1,0:T(8,128)(2,1)S(1)} %get-tuple-element.51), channel_id=1, source_target_pairs={{0,4},{4,0},{8,12},{12,8},{16,20},{20,16},{24,28},{28,24},{1,5},{5... | collective-permute-start | bytes 98312 | tf_op jit(solution)/shard_map/ppermute | solution.py:170
  17.6 0.4 %collective-permute-start.6 = (bf16[64,256]{1,0:T(8,128)(2,1)S(1)}, bf16[64,256]{1,0:T(8,128)(2,1)S(1)}, u32[]{:S(2)}, u32[]{:S(2)}) collective-permute-start(bf16[64,256]{1,0:T(8,128)(2,1)S(1)} %get-tuple-element.51), channel_id=1, source_target_pairs={{0,8},{4,12},{8,0},{12,4},{16,24},{20,28},{24,16},{28,20},{1,9},{5... | collective-permute-start | bytes 98312 | tf_op jit(solution)/shard_map/ppermute | solution.py:170
  18.0 3.3 %shard_map.87 = (f32[64,1280]{1,0:T(8,128)}, f32[1,1280]{1,0:T(1,128)}) custom-call(f32[72,1536]{1,0:T(8,128)S(1)} %convert_add_fusion.refs_0_, bf16[80,1280]{1,0:T(8,128)(2,1)S(1)} %get-tuple-element.52.refs_1_, bf16[80,1024]{1,0:T(8,128)(2,1)S(1)} %get-tuple-element.44.refs_2_, ...), custom_call_target="tpu_custom_call", output_to_operand_aliasing={{0}: (4, {}), {1}: (5, {})} | custom-call | flops 201326592 | bytes 1572864 | tf_op jit(solution)/shard_map/pallas_call | solution.py:204
  21.3 0.0 collective-permute-done.8
  21.3 0.0 collective-permute-done.7
  21.3 0.2 collective-permute-done.6
  21.6 2.6 %collective-permute-start.9 = (f16[72,256]{1,0:T(8,128)(2,1)S(1)}, f16[72,256]{1,0:T(8,128)(2,1)S(1)}, u32[]{:S(2)}, u32[]{:S(2)}) collective-permute-start(f16[72,256]{1,0:T(8,128)(2,1)S(1)} %pad_maximum_fusion), channel_id=1, source_target_pairs={{0,16},{4,20},{8,24},{12,28},{16,0},{20,4},{24,8},{28,12},{1,17},{... | collective-permute-start | bytes 110600 | tf_op jit(solution)/shard_map/ppermute | solution.py:170
  24.2 2.3 %collective-permute-done.9 = f16[72,256]{1,0:T(8,128)(2,1)S(1)} collective-permute-done((f16[72,256]{1,0:T(8,128)(2,1)S(1)}, f16[72,256]{1,0:T(8,128)(2,1)S(1)}, u32[]{:S(2)}, u32[]{:S(2)}) %collective-permute-start.9) | collective-permute-done | bytes 36896 | tf_op jit(solution)/shard_map/ppermute | solution.py:170
  26.5 0.7 %multiply_add_fusion = f32[64,256]{1,0:T(8,128)} fusion(f16[72,256]{1,0:T(8,128)(2,1)S(1)} %pad_maximum_fusion, f32[256]{0:T(256)S(1)} %bitcast.13, f16[72,256]{1,0:T(8,128)(2,1)S(1)} %collective-permute-done.9, f32[256]{0:T(256)S(1)} %bitcast.12), kind=kLoop, calls=%fused_computation.1 | loop fusion | flops 81920 | bytes 133120 | tf_op jit(solution)/shard_map/add | solution.py:243
  (9 shorter events, 0.1 us)
Async XLA Ops:
  0.6 4.9 %collective-permute-start = (bf16[64,256]{1,0:T(8,128)(2,1)}, bf16[64,256]{1,0:T(8,128)(2,1)S(1)}, u32[]{:S(2)}, u32[]{:S(2)}) collective-permute-start(bf16[64,256]{1,0:T(8,128)(2,1)} %param.7), channel_id=1, source_target_pairs={{0,1},{1,0},{2,3},{3,2},{4,5},{5,4},{6,7},{7,6},{8,9},{9,8},{10,11... | collective-permute-start | bytes 98312 | tf_op jit(solution)/shard_map/ppermute | solution.py:170
  1.1 4.8 %collective-permute-start.2 = (bf16[64,256]{1,0:T(8,128)(2,1)}, bf16[64,256]{1,0:T(8,128)(2,1)S(1)}, u32[]{:S(2)}, u32[]{:S(2)}) collective-permute-start(bf16[64,256]{1,0:T(8,128)(2,1)} %param.7), channel_id=1, source_target_pairs={{0,2},{1,3},{2,0},{3,1},{4,6},{5,7},{6,4},{7,5},{8,10},{9,11},{10,... | collective-permute-start | bytes 98312 | tf_op jit(solution)/shard_map/ppermute | solution.py:170
  3.7 3.6 %collective-permute-start.1 = (bf16[64,256]{1,0:T(8,128)(2,1)}, bf16[64,256]{1,0:T(8,128)(2,1)S(1)}, u32[]{:S(2)}, u32[]{:S(2)}) collective-permute-start(bf16[64,256]{1,0:T(8,128)(2,1)} %param.7), channel_id=1, source_target_pairs={{0,3},{1,2},{2,1},{3,0},{4,7},{5,6},{6,5},{7,4},{8,11},{9,10},{10,... | collective-permute-start | bytes 98312 | tf_op jit(solution)/shard_map/ppermute | solution.py:170
  9.8 4.7 %collective-permute-start.5 = (f32[64,256]{1,0:T(8,128)S(1)}, f32[64,256]{1,0:T(8,128)S(1)}, u32[]{:S(2)}, u32[]{:S(2)}) collective-permute-start(f32[64,256]{1,0:T(8,128)S(1)} %get-tuple-element.42), channel_id=1, source_target_pairs={{0,1},{1,0},{2,3},{3,2},{4,5},{5,4},{6,7},{7,6},{8,9},{9,8},{10,11... | collective-permute-start | bytes 196616 | tf_op jit(solution)/shard_map/ppermute | solution.py:170
  10.0 4.2 %collective-permute-start.3 = (bf16[64,256]{1,0:T(8,128)(2,1)S(1)}, bf16[64,256]{1,0:T(8,128)(2,1)S(1)}, u32[]{:S(2)}, u32[]{:S(2)}) collective-permute-start(bf16[64,256]{1,0:T(8,128)(2,1)S(1)} %get-tuple-element.40), channel_id=1, source_target_pairs={{0,2},{1,3},{2,0},{3,1},{4,6},{5,7},{6,4},{7,5},{8,10},{9,11},{10,... | collective-permute-start | bytes 98312 | tf_op jit(solution)/shard_map/ppermute | solution.py:170
  10.7 3.7 %collective-permute-start.4 = (bf16[64,256]{1,0:T(8,128)(2,1)S(1)}, bf16[64,256]{1,0:T(8,128)(2,1)S(1)}, u32[]{:S(2)}, u32[]{:S(2)}) collective-permute-start(bf16[64,256]{1,0:T(8,128)(2,1)S(1)} %get-tuple-element.41), channel_id=1, source_target_pairs={{0,3},{1,2},{2,1},{3,0},{4,7},{5,6},{6,5},{7,4},{8,11},{9,10},{10,... | collective-permute-start | bytes 98312 | tf_op jit(solution)/shard_map/ppermute | solution.py:170
  14.5 6.8 %collective-permute-start.8 = (bf16[64,256]{1,0:T(8,128)(2,1)S(1)}, bf16[64,256]{1,0:T(8,128)(2,1)S(1)}, u32[]{:S(2)}, u32[]{:S(2)}) collective-permute-start(bf16[64,256]{1,0:T(8,128)(2,1)S(1)} %get-tuple-element.51), channel_id=1, source_target_pairs={{0,12},{4,8},{8,4},{12,0},{16,28},{20,24},{24,20},{28,16},{1,13},{... | collective-permute-start | bytes 98312 | tf_op jit(solution)/shard_map/ppermute | solution.py:170
  17.0 4.3 %collective-permute-start.7 = (bf16[64,256]{1,0:T(8,128)(2,1)S(1)}, bf16[64,256]{1,0:T(8,128)(2,1)S(1)}, u32[]{:S(2)}, u32[]{:S(2)}) collective-permute-start(bf16[64,256]{1,0:T(8,128)(2,1)S(1)} %get-tuple-element.51), channel_id=1, source_target_pairs={{0,4},{4,0},{8,12},{12,8},{16,20},{20,16},{24,28},{28,24},{1,5},{5... | collective-permute-start | bytes 98312 | tf_op jit(solution)/shard_map/ppermute | solution.py:170
  17.6 3.9 %collective-permute-start.6 = (bf16[64,256]{1,0:T(8,128)(2,1)S(1)}, bf16[64,256]{1,0:T(8,128)(2,1)S(1)}, u32[]{:S(2)}, u32[]{:S(2)}) collective-permute-start(bf16[64,256]{1,0:T(8,128)(2,1)S(1)} %get-tuple-element.51), channel_id=1, source_target_pairs={{0,8},{4,12},{8,0},{12,4},{16,24},{20,28},{24,16},{28,20},{1,9},{5... | collective-permute-start | bytes 98312 | tf_op jit(solution)/shard_map/ppermute | solution.py:170
  21.6 4.9 %collective-permute-start.9 = (f16[72,256]{1,0:T(8,128)(2,1)S(1)}, f16[72,256]{1,0:T(8,128)(2,1)S(1)}, u32[]{:S(2)}, u32[]{:S(2)}) collective-permute-start(f16[72,256]{1,0:T(8,128)(2,1)S(1)} %pad_maximum_fusion), channel_id=1, source_target_pairs={{0,16},{4,20},{8,24},{12,28},{16,0},{20,4},{24,8},{28,12},{1,17},{... | collective-permute-start | bytes 110600 | tf_op jit(solution)/shard_map/ppermute | solution.py:170
